TPU v7x, 128 devices: a whole 4x4x4 slice. The times are simulated.
128 devices in a mesh: dp: 4 (over x), seq: 32 (over y, z, core).
Axes of the slice: x: 4, y: 4, z: 4, core: 2. Of those that a mesh axis runs over, the one named last changes fastest.
Arguments:
- block_input: bfloat16 [16384, 2048], P(('dp', 'seq')), may hold values from -6 to 6
- cotangent: bfloat16 [16384, 2048], P(('dp', 'seq')), may hold values from -6 to 6
- lengths: int32 [4, 4], P('dp'), may hold values from 1 to 4093, as said below
- norm_gain: float32 [2048], P('seq'), may hold values from 0.4 to 1.6
- q_down: bfloat16 [2048, 1024], P('seq'), may hold values from -0.125 to 0.125
- q_gain: float32 [1024], P('seq'), may hold values from 0.4 to 1.6
- q_up: bfloat16 [1024, 4096], P('seq'), may hold values from -0.1875 to 0.1875
- key_weight: bfloat16 [2048, 256], P('seq'), may hold values from -0.125 to 0.125
- value_weight: bfloat16 [2048, 256], P('seq'), may hold values from -0.125 to 0.125
- out_weight: bfloat16 [4096, 2048], P('seq'), may hold values from -0.375 to 0.375
- ffn_gain: float32 [2048], P('seq'), may hold values from 0.4 to 1.6
- gate_weight: bfloat16 [2048, 5632], P('seq'), may hold values from -0.125 to 0.125
- up_weight: bfloat16 [2048, 5632], P('seq'), may hold values from -0.125 to 0.125
- down_weight: bfloat16 [5632, 2048], P('seq'), may hold values from -0.078125 to 0.078125
Outputs:
- output: bfloat16 [16384, 2048], P(('dp', 'seq'))
- input_grad: float32 [16384, 2048], P(('dp', 'seq'))
- grad_norm_gain: float32 [2048], P('seq')
- grad_q_down: float32 [2048, 1024], P('seq')
- grad_q_gain: float32 [1024], P('seq')
- grad_q_up: float32 [1024, 4096], P('seq')
- grad_key_weight: float32 [2048, 256], P('seq')
- grad_value_weight: float32 [2048, 256], P('seq')
- grad_out_weight: float32 [4096, 2048], P('seq')
- grad_ffn_gain: float32 [2048], P('seq')
- grad_gate_weight: float32 [2048, 5632], P('seq')
- grad_up_weight: float32 [2048, 5632], P('seq')
- grad_down_weight: float32 [5632, 2048], P('seq')
Inputs may be any that keep to these rules, and one draw needn't show every extreme that they name: `lengths`: each row packs its 4 documents from slot 0 in order, padding after them. The second document begins on the first device of its row and ends on the last; the first document, the documents after the second and the padding each take fewer slots than one device holds.
All inputs are finite; a program needn't handle non-finite values.
Results may differ from a plain program's by a relative error of at most 0.04.
Values may be sent and summed in bfloat16 or wider, within the bound.
A program may use at most 320 MiB of HBM per device.

v0:
```python
import math

import jax
import jax.numpy as jnp
from jax import lax
from jax.sharding import PartitionSpec as P

EPSILON = 1e-06
MASKED = -1e30


def product(left, right):
    return jnp.dot(left, right, preferred_element_type=jnp.float32)


def weight_grad(left, right):
    return lax.dot_general(
        left, right, (((0,), (0,)), ((), ())), preferred_element_type=jnp.float32
    )


def back_through(left, right):
    return lax.dot_general(
        left, right, (((1,), (1,)), ((), ())), preferred_element_type=jnp.float32
    )


def normalize(values, gain):
    inverse = lax.rsqrt(jnp.mean(values * values, axis=-1, keepdims=True) + EPSILON)
    return (values * inverse * gain, inverse)


def norm_back(values, inverse, gain, grad):
    scaled = grad * gain
    grad_values = inverse * scaled - values * inverse * inverse * inverse * jnp.mean(
        scaled * values, axis=-1, keepdims=True
    )
    return (grad_values, jnp.sum(grad * values * inverse, axis=0))


def layout(lengths_row, slots):
    count = lengths_row.shape[0]
    ends = jnp.cumsum(lengths_row)
    starts = jnp.concatenate([ends - lengths_row, ends[-1:]])
    places = jnp.arange(slots, dtype=jnp.int32)
    segment = jnp.sum((places[:, None] >= ends[None, :]).astype(jnp.int32), axis=1)
    picked = segment[:, None] == jnp.arange(count + 1, dtype=jnp.int32)[None, :]
    start_of = jnp.sum(jnp.where(picked, starts[None, :], 0), axis=1)
    position = places - start_of
    live = (segment < count).astype(jnp.float32)
    return (segment, position, live)


def tables(position, size):
    half = size // 2
    freq = jnp.exp(jnp.arange(half, dtype=jnp.float32) * (-math.log(10000.0) / half))
    angle = position.astype(jnp.float32)[:, None] * freq[None, :]
    return (jnp.cos(angle), jnp.sin(angle))


def rotate(values, cosine, sine):
    half = values.shape[-1] // 2
    lower, upper = (values[..., :half], values[..., half:])
    return jnp.concatenate([lower * cosine - upper * sine, upper * cosine + lower * sine], axis=-1)


def unrotate(grad, cosine, sine):
    half = grad.shape[-1] // 2
    lower, upper = (grad[..., :half], grad[..., half:])
    return jnp.concatenate([lower * cosine + upper * sine, upper * cosine - lower * sine], axis=-1)


def on_device(
    block_input,
    cotangent,
    lengths,
    norm_gain,
    q_down,
    q_gain,
    q_up,
    key_weight,
    value_weight,
    out_weight,
    ffn_gain,
    gate_weight,
    up_weight,
    down_weight,
):
    seq_width = lax.axis_size("seq")
    local_rows = block_input.shape[0]
    slots = local_rows * seq_width
    offset = lax.axis_index("seq") * local_rows
    size = key_weight.shape[1]
    head_count = q_up.shape[1] // size
    factor = size ** (-0.5)
    key_block = math.gcd(slots, 512)
    block_count = (offset + local_rows + key_block - 1) // key_block
    segment_all, position_all, live_all = layout(lengths[0], slots)
    segment_mine = lax.dynamic_slice_in_dim(segment_all, offset, local_rows)
    position_mine = lax.dynamic_slice_in_dim(position_all, offset, local_rows)
    live_mine = lax.dynamic_slice_in_dim(live_all, offset, local_rows)
    slot_mine = offset + jnp.arange(local_rows, dtype=jnp.int32)
    cosine, sine = tables(position_mine, size)
    gain_one, down_full, latent_gain, up_full_q, key_full, value_full, out_full, gain_two = (
        lax.all_gather(norm_gain.astype(jnp.bfloat16), "seq", axis=0, tiled=True).astype(
            norm_gain.dtype
        ),
        lax.all_gather(q_down, "seq", axis=0, tiled=True),
        lax.all_gather(q_gain.astype(jnp.bfloat16), "seq", axis=0, tiled=True).astype(q_gain.dtype),
        lax.all_gather(q_up, "seq", axis=0, tiled=True),
        lax.all_gather(key_weight, "seq", axis=0, tiled=True),
        lax.all_gather(value_weight, "seq", axis=0, tiled=True),
        lax.all_gather(out_weight, "seq", axis=0, tiled=True),
        lax.all_gather(ffn_gain.astype(jnp.bfloat16), "seq", axis=0, tiled=True).astype(
            ffn_gain.dtype
        ),
    )
    gate_use, up_use, down_use = (
        lax.all_gather(gate_weight, "seq", axis=0, tiled=True),
        lax.all_gather(up_weight, "seq", axis=0, tiled=True),
        lax.all_gather(down_weight, "seq", axis=0, tiled=True),
    )
    inputs = block_input.astype(jnp.float32)
    normed_f, inverse_one = normalize(inputs, gain_one)
    normed = normed_f.astype(jnp.bfloat16)
    latent = product(normed, down_full)
    latent_f, inverse_latent = normalize(latent, latent_gain)
    latent_normed = latent_f.astype(jnp.bfloat16)
    query_raw = product(latent_normed, up_full_q).reshape(local_rows, head_count, size)
    queries = rotate(query_raw, cosine[:, None, :], sine[:, None, :]).astype(jnp.bfloat16)
    key_local = rotate(product(normed, key_full), cosine, sine).astype(jnp.bfloat16)
    value_local = product(normed, value_full).astype(jnp.bfloat16)
    key_rows, value_rows = (
        lax.all_gather(key_local, "seq", axis=0, tiled=True),
        lax.all_gather(value_local, "seq", axis=0, tiled=True),
    )

    def block_scores(block_index):
        start = block_index * key_block
        key_part = lax.dynamic_slice_in_dim(key_rows, start, key_block)
        value_part = lax.dynamic_slice_in_dim(value_rows, start, key_block)
        segment_part = lax.dynamic_slice_in_dim(segment_all, start, key_block)
        slot_part = start + jnp.arange(key_block, dtype=jnp.int32)
        allowed = (segment_mine[:, None] == segment_part[None, :]) & (
            slot_mine[:, None] >= slot_part[None, :]
        )
        raw = (
            jnp.einsum("thd,kd->thk", queries, key_part, preferred_element_type=jnp.float32)
            * factor
        )
        allowed = allowed[:, None, :]
        return (jnp.where(allowed, raw, MASKED), allowed, key_part, value_part, start)

    def find_peak(block_index, carry):
        peak, totals = carry
        scores, allowed, key_part, value_part, start = block_scores(block_index)
        new_peak = jnp.maximum(peak, jnp.max(scores, axis=-1))
        weights = jnp.where(allowed, jnp.exp(scores - new_peak[..., None]), 0.0)
        return (new_peak, totals * jnp.exp(peak - new_peak) + jnp.sum(weights, axis=-1))

    first_peak = jnp.full((local_rows, head_count), MASKED, jnp.float32)
    first_totals = jnp.zeros((local_rows, head_count), jnp.float32)
    peak, totals = lax.fori_loop(0, block_count, find_peak, (first_peak, first_totals))

    def probabilities(scores, allowed):
        return jnp.where(allowed, jnp.exp(scores - peak[..., None]), 0.0) / totals[..., None]

    def gather_out(block_index, accum):
        scores, allowed, key_part, value_part, start = block_scores(block_index)
        probs = probabilities(scores, allowed).astype(jnp.bfloat16)
        return accum + jnp.einsum(
            "thk,kd->thd", probs, value_part, preferred_element_type=jnp.float32
        )

    attended = lax.fori_loop(
        0, block_count, gather_out, jnp.zeros((local_rows, head_count, size), jnp.float32)
    )
    mixed = (attended.reshape(local_rows, head_count * size) * live_mine[:, None]).astype(
        jnp.bfloat16
    )
    middle = inputs + product(mixed, out_full)
    normed_two_f, inverse_two = normalize(middle, gain_two)
    normed_two = normed_two_f.astype(jnp.bfloat16)
    gate_pre = product(normed_two, gate_use)
    up_pre = product(normed_two, up_use)
    hidden = (jax.nn.silu(gate_pre) * up_pre).astype(jnp.bfloat16)
    branch_part = product(hidden, down_use)
    output = (middle + branch_part).astype(jnp.bfloat16)
    grad_result = cotangent.astype(jnp.float32)
    grad_branch_two = grad_result.astype(jnp.bfloat16)
    gate_use, up_use, down_use = (
        lax.all_gather(gate_weight, "seq", axis=0, tiled=True),
        lax.all_gather(up_weight, "seq", axis=0, tiled=True),
        lax.all_gather(down_weight, "seq", axis=0, tiled=True),
    )
    grad_down = weight_grad(hidden, grad_branch_two)
    grad_hidden = back_through(grad_branch_two, down_use)
    sigma = jax.nn.sigmoid(gate_pre)
    grad_gate_pre = (grad_hidden * up_pre * sigma * (1.0 + gate_pre * (1.0 - sigma))).astype(
        jnp.bfloat16
    )
    grad_up_pre = (grad_hidden * gate_pre * sigma).astype(jnp.bfloat16)
    grad_gate_w = weight_grad(normed_two, grad_gate_pre)
    grad_up_w = weight_grad(normed_two, grad_up_pre)
    grad_normed_part = back_through(grad_gate_pre, gate_use) + back_through(grad_up_pre, up_use)
    grad_mid_norm, grad_gain_two = norm_back(middle, inverse_two, gain_two, grad_normed_part)
    grad_middle = grad_result + grad_mid_norm
    ffn_part = (
        lax.psum_scatter(
            grad_gate_w.astype(jnp.bfloat16), "seq", scatter_dimension=0, tiled=True
        ).astype(jnp.float32),
        lax.psum_scatter(
            grad_up_w.astype(jnp.bfloat16), "seq", scatter_dimension=0, tiled=True
        ).astype(jnp.float32),
        lax.psum_scatter(
            grad_down.astype(jnp.bfloat16), "seq", scatter_dimension=0, tiled=True
        ).astype(jnp.float32),
    )
    gain_one, down_full, latent_gain, up_full_q, key_full, value_full, out_full = (
        lax.all_gather(norm_gain.astype(jnp.bfloat16), "seq", axis=0, tiled=True).astype(
            norm_gain.dtype
        ),
        lax.all_gather(q_down, "seq", axis=0, tiled=True),
        lax.all_gather(q_gain.astype(jnp.bfloat16), "seq", axis=0, tiled=True).astype(q_gain.dtype),
        lax.all_gather(q_up, "seq", axis=0, tiled=True),
        lax.all_gather(key_weight, "seq", axis=0, tiled=True),
        lax.all_gather(value_weight, "seq", axis=0, tiled=True),
        lax.all_gather(out_weight, "seq", axis=0, tiled=True),
    )
    grad_branch = grad_middle.astype(jnp.bfloat16)
    grad_out_w = weight_grad(mixed, grad_branch)
    grad_mixed = back_through(grad_branch, out_full).astype(jnp.bfloat16)
    grad_attended = (grad_mixed * live_mine[:, None].astype(jnp.bfloat16)).reshape(
        local_rows, head_count, size
    )
    delta = jnp.sum(grad_attended.astype(jnp.float32) * attended, axis=-1)

    def gather_back(block_index, carry):
        grad_queries, grad_keys, grad_values = carry
        scores, allowed, key_part, value_part, start = block_scores(block_index)
        probs = probabilities(scores, allowed)
        grad_probs = jnp.einsum(
            "thd,kd->thk", grad_attended, value_part, preferred_element_type=jnp.float32
        )
        grad_scores = (probs * (grad_probs - delta[..., None])).astype(jnp.bfloat16)
        grad_queries = (
            grad_queries
            + jnp.einsum("thk,kd->thd", grad_scores, key_part, preferred_element_type=jnp.float32)
            * factor
        )
        key_term = (
            jnp.einsum("thk,thd->kd", grad_scores, queries, preferred_element_type=jnp.float32)
            * factor
        )
        value_term = jnp.einsum(
            "thk,thd->kd",
            probs.astype(jnp.bfloat16),
            grad_attended,
            preferred_element_type=jnp.float32,
        )
        grad_keys = lax.dynamic_update_slice_in_dim(
            grad_keys, lax.dynamic_slice_in_dim(grad_keys, start, key_block) + key_term, start, 0
        )
        grad_values = lax.dynamic_update_slice_in_dim(
            grad_values,
            lax.dynamic_slice_in_dim(grad_values, start, key_block) + value_term,
            start,
            0,
        )
        return (grad_queries, grad_keys, grad_values)

    start_queries = jnp.zeros((local_rows, head_count, size), jnp.float32)
    start_rows = jnp.zeros((slots, size), jnp.float32)
    grad_queries, grad_keys, grad_values = lax.fori_loop(
        0, block_count, gather_back, (start_queries, start_rows, start_rows)
    )
    grad_key_local, grad_value_local = (
        lax.psum_scatter(
            grad_keys.astype(jnp.bfloat16), "seq", scatter_dimension=0, tiled=True
        ).astype(jnp.float32),
        lax.psum_scatter(
            grad_values.astype(jnp.bfloat16), "seq", scatter_dimension=0, tiled=True
        ).astype(jnp.float32),
    )
    grad_query_raw = (
        unrotate(grad_queries, cosine[:, None, :], sine[:, None, :])
        .reshape(local_rows, head_count * size)
        .astype(jnp.bfloat16)
    )
    grad_key_raw = unrotate(grad_key_local, cosine, sine).astype(jnp.bfloat16)
    grad_value_raw = grad_value_local.astype(jnp.bfloat16)
    grad_up_q = weight_grad(latent_normed, grad_query_raw)
    grad_key_w = weight_grad(normed, grad_key_raw)
    grad_value_w = weight_grad(normed, grad_value_raw)
    grad_latent_normed = back_through(grad_query_raw, up_full_q)
    grad_latent_f, grad_latent_gain = norm_back(
        latent, inverse_latent, latent_gain, grad_latent_normed
    )
    grad_latent = grad_latent_f.astype(jnp.bfloat16)
    grad_down_q = weight_grad(normed, grad_latent)
    grad_normed = (
        back_through(grad_latent, down_full)
        + back_through(grad_key_raw, key_full)
        + back_through(grad_value_raw, value_full)
    )
    grad_input_norm, grad_gain_one = norm_back(inputs, inverse_one, gain_one, grad_normed)
    input_grad = grad_middle + grad_input_norm
    attn_part = (
        lax.psum_scatter(
            grad_gain_one.astype(jnp.bfloat16), "seq", scatter_dimension=0, tiled=True
        ).astype(jnp.float32),
        lax.psum_scatter(
            grad_down_q.astype(jnp.bfloat16), "seq", scatter_dimension=0, tiled=True
        ).astype(jnp.float32),
        lax.psum_scatter(
            grad_latent_gain.astype(jnp.bfloat16), "seq", scatter_dimension=0, tiled=True
        ).astype(jnp.float32),
        lax.psum_scatter(
            grad_up_q.astype(jnp.bfloat16), "seq", scatter_dimension=0, tiled=True
        ).astype(jnp.float32),
        lax.psum_scatter(
            grad_key_w.astype(jnp.bfloat16), "seq", scatter_dimension=0, tiled=True
        ).astype(jnp.float32),
        lax.psum_scatter(
            grad_value_w.astype(jnp.bfloat16), "seq", scatter_dimension=0, tiled=True
        ).astype(jnp.float32),
        lax.psum_scatter(
            grad_out_w.astype(jnp.bfloat16), "seq", scatter_dimension=0, tiled=True
        ).astype(jnp.float32),
        lax.psum_scatter(
            grad_gain_two.astype(jnp.bfloat16), "seq", scatter_dimension=0, tiled=True
        ).astype(jnp.float32),
    )
    summed = (
        lax.psum(attn_part[0].astype(jnp.bfloat16), "dp").astype(jnp.float32),
        lax.psum(attn_part[1].astype(jnp.bfloat16), "dp").astype(jnp.float32),
        lax.psum(attn_part[2].astype(jnp.bfloat16), "dp").astype(jnp.float32),
        lax.psum(attn_part[3].astype(jnp.bfloat16), "dp").astype(jnp.float32),
        lax.psum(attn_part[4].astype(jnp.bfloat16), "dp").astype(jnp.float32),
        lax.psum(attn_part[5].astype(jnp.bfloat16), "dp").astype(jnp.float32),
        lax.psum(attn_part[6].astype(jnp.bfloat16), "dp").astype(jnp.float32),
        lax.psum(attn_part[7].astype(jnp.bfloat16), "dp").astype(jnp.float32),
        lax.psum(ffn_part[0].astype(jnp.bfloat16), "dp").astype(jnp.float32),
        lax.psum(ffn_part[1].astype(jnp.bfloat16), "dp").astype(jnp.float32),
        lax.psum(ffn_part[2].astype(jnp.bfloat16), "dp").astype(jnp.float32),
    )
    return (
        output,
        input_grad,
        summed[0],
        summed[1],
        summed[2],
        summed[3],
        summed[4],
        summed[5],
        summed[6],
        summed[7],
        summed[8],
        summed[9],
        summed[10],
    )


def solution(mesh):
    in_specs = (
        P(("dp", "seq"), None),
        P(("dp", "seq"), None),
        P("dp", None),
        P("seq"),
        P("seq", None),
        P("seq"),
        P("seq", None),
        P("seq", None),
        P("seq", None),
        P("seq", None),
        P("seq"),
        P("seq", None),
        P("seq", None),
        P("seq", None),
    )
    out_specs = (
        P(("dp", "seq"), None),
        P(("dp", "seq"), None),
        P("seq"),
        P("seq", None),
        P("seq"),
        P("seq", None),
        P("seq", None),
        P("seq", None),
        P("seq", None),
        P("seq"),
        P("seq", None),
        P("seq", None),
        P("seq", None),
    )
    return jax.shard_map(
        on_device, mesh=mesh, in_specs=in_specs, out_specs=out_specs, check_vma=False
    )
```

profile of v0, /device:TPU:1, one launch (start us, length us, event | category | flops | bytes accessed | tf_op | source)
XLA Modules:
  0.0 1978.1 jit_solution(18221061329906264266)
XLA Ops:
  15.3 125.9 %all-reduce.7 = (bf16[2048]{0:T(1024)(128)(2,1)S(1)}, bf16[1024]{0:T(1024)(128)(2,1)S(1)}, bf16[2048]{0:T(1024)(128)(2,1)S(1)}) all-reduce(bf16[2048]{0:T(1024)(128)(2,1)S(1)} %dynamic-update-slice, bf16[1024]{0:T(1024)(128)(2,1)S(1)} %dynamic-update-slice.1, ...), channel_id=1, replica_groups=mesh['dp'=4,'seq'=32] {'seq'}, use_global_device_ids=true, to_apply=%add | all-reduce | flops 5120 | bytes 20480
  154.7 3.0 multiply_reduce_fusion.6
  157.8 45.8 %all-gather.17.cloned.1.call-done = bf16[1024,4096]{1,0:T(8,128)(2,1)} async-done(((bf16[32,4096]{1,0:T(8,128)(2,1)}), bf16[1024,4096]{1,0:T(8,128)(2,1)}) %all-gather.17.cloned.1.call-update) | async-done | bytes 8388624 | tf_op jit(solution)/shard_map/all_gather | solution.py:110
  203.6 6.8 fusion.93
  211.5 38.4 %all-gather.13.cloned.1.call-done = bf16[4096,256]{1,0:T(8,128)(2,1)} async-done(((bf16[128,256]{1,0:T(8,128)(2,1)}), bf16[4096,256]{1,0:T(8,128)(2,1)}) %all-gather.13.cloned.1.call-update) | async-done | bytes 2097168 | tf_op jit(solution)/shard_map/all_gather | solution.py:134
  249.9 3.1 while.39
  252.9 42.9 %all-gather.21.cloned.1.call-done = bf16[4096,256]{1,0:T(8,128)(2,1)} async-done(((bf16[128,256]{1,0:T(8,128)(2,1)}), bf16[4096,256]{1,0:T(8,128)(2,1)}) %all-gather.21.cloned.1.call-update) | async-done | bytes 2097168 | tf_op jit(solution)/shard_map/all_gather | solution.py:135
  296.0 4.3 while.40
  296.6 3.6 convolution_add_fusion.6
  302.4 2.7 fusion.58
  305.1 64.9 %all-gather.23.cloned.1.call-done = bf16[4096,2048]{1,0:T(8,128)(2,1)} async-done(((bf16[128,2048]{1,0:T(8,128)(2,1)}), bf16[4096,2048]{1,0:T(8,128)(2,1)}) %all-gather.23.cloned.1.call-update) | async-done | bytes 16777232 | tf_op jit(solution)/shard_map/all_gather | solution.py:113
  370.0 8.5 multiply_reduce_fusion.3
  378.8 80.3 %all-gather.25.cloned.1.call-done = bf16[2048,5632]{1,0:T(8,128)(2,1)} async-done(((bf16[64,5632]{1,0:T(8,128)(2,1)}), bf16[2048,5632]{1,0:T(8,128)(2,1)}) %all-gather.25.cloned.1.call-update) | async-done | bytes 23068688 | tf_op jit(solution)/shard_map/all_gather | solution.py:119
  459.1 12.5 fusion.103
  471.5 76.5 %all-gather.27.cloned.1.call-done = bf16[2048,5632]{1,0:T(8,128)(2,1)} async-done(((bf16[64,5632]{1,0:T(8,128)(2,1)}), bf16[2048,5632]{1,0:T(8,128)(2,1)}) %all-gather.27.cloned.1.call-update) | async-done | bytes 23068688 | tf_op jit(solution)/shard_map/all_gather | solution.py:120
  548.1 12.3 fusion.104
  560.4 76.6 %all-gather.29.cloned.1.call-done = bf16[5632,2048]{1,0:T(8,128)(2,1)} async-done(((bf16[176,2048]{1,0:T(8,128)(2,1)}), bf16[5632,2048]{1,0:T(8,128)(2,1)}) %all-gather.29.cloned.1.call-update) | async-done | bytes 23068688 | tf_op jit(solution)/shard_map/all_gather | solution.py:121
  637.0 15.1 multiply_convert_fusion
  652.1 13.4 fusion.105
  665.5 14.2 multiply_reduce_fusion.1
  681.4 12.8 fusion.55
  702.0 12.8 while.41
  703.0 2.6 fusion.185
  707.5 2.6 fusion.187
  710.1 2.6 fusion.188
  714.8 3.7 convert_element_type.222
  718.7 3.9 convert_element_type.224
  722.6 161.9 %reduce-scatter.11.cloned.1.call-done = bf16[128,256]{1,0:T(8,128)(2,1)} async-done(((bf16[4096,256]{1,0:T(8,128)(2,1)}), bf16[128,256]{1,0:T(8,128)(2,1)}) %reduce-scatter.11.cloned.1.call-update) | async-done | bytes 65552 | tf_op jit(solution)/shard_map/reduce_scatter | solution.py:278
  889.2 76.9 %reduce-scatter.13.cloned.1.call-done = bf16[128,256]{1,0:T(8,128)(2,1)} async-done(((bf16[4096,256]{1,0:T(8,128)(2,1)}), bf16[128,256]{1,0:T(8,128)(2,1)}) %reduce-scatter.13.cloned.1.call-update) | async-done | bytes 65552 | tf_op jit(solution)/shard_map/reduce_scatter | solution.py:281
  970.8 6.4 multiply_reduce_fusion.4
  977.4 3.4 convolution_convert_fusion.6
  980.8 5.7 convolution_convert_fusion.4
  988.1 8.3 convolution_convert_fusion.3
  997.5 12.2 convolution_convert_fusion.2
  1010.2 12.2 convolution_convert_fusion.1
  1023.5 12.3 convolution_convert_fusion
  1039.7 2.7 fusion.69
  1042.4 121.2 %all-reduce.6 = (bf16[2048]{0:T(1024)(128)(2,1)S(1)}, bf16[1024]{0:T(1024)(128)(2,1)S(1)}, bf16[2048]{0:T(1024)(128)(2,1)S(1)}) all-reduce(bf16[2048]{0:T(1024)(128)(2,1)S(1)} %get-tuple-element.421, bf16[1024]{0:T(1024)(128)(2,1)S(1)} %get-tuple-element.423, ...), channel_id=4, replica_groups=mesh['dp'=4,'seq'=32] {'seq'}, use_global_device_ids=true, to_apply=%region_21.22.clone | all-reduce | flops 5120 | bytes 20480
  1165.6 46.6 %reduce-scatter.15.cloned.1.call-done = bf16[64,1024]{1,0:T(8,128)(2,1)} async-done(((bf16[2048,1024]{1,0:T(8,128)(2,1)}), bf16[64,1024]{1,0:T(8,128)(2,1)}) %reduce-scatter.15.cloned.1.call-update) | async-done | bytes 131088 | tf_op jit(solution)/shard_map/reduce_scatter | solution.py:312
  1212.2 96.1 %reduce-scatter.17.cloned.1.call-done = bf16[32,4096]{1,0:T(8,128)(2,1)} async-done(((bf16[1024,4096]{1,0:T(8,128)(2,1)}), bf16[32,4096]{1,0:T(8,128)(2,1)}) %reduce-scatter.17.cloned.1.call-update) | async-done | bytes 262160 | tf_op jit(solution)/shard_map/reduce_scatter | solution.py:318
  1308.3 118.8 %reduce-scatter.23.cloned.1.call-done = bf16[128,2048]{1,0:T(8,128)(2,1)} async-done(((bf16[4096,2048]{1,0:T(8,128)(2,1)}), bf16[128,2048]{1,0:T(8,128)(2,1)}) %reduce-scatter.23.cloned.1.call-update) | async-done | bytes 524304 | tf_op jit(solution)/shard_map/reduce_scatter | solution.py:327
  1427.1 138.2 %reduce-scatter.25.cloned.1.call-done = bf16[64,5632]{1,0:T(8,128)(2,1)} async-done(((bf16[2048,5632]{1,0:T(8,128)(2,1)}), bf16[64,5632]{1,0:T(8,128)(2,1)}) %reduce-scatter.25.cloned.1.call-update) | async-done | bytes 720912 | tf_op jit(solution)/shard_map/reduce_scatter | solution.py:209
  1565.2 137.6 %reduce-scatter.27.cloned.1.call-done = bf16[64,5632]{1,0:T(8,128)(2,1)} async-done(((bf16[2048,5632]{1,0:T(8,128)(2,1)}), bf16[64,5632]{1,0:T(8,128)(2,1)}) %reduce-scatter.27.cloned.1.call-update) | async-done | bytes 720912 | tf_op jit(solution)/shard_map/reduce_scatter | solution.py:212
  1702.9 137.0 %reduce-scatter.29.cloned.1.call-done = bf16[176,2048]{1,0:T(8,128)(2,1)} async-done(((bf16[5632,2048]{1,0:T(8,128)(2,1)}), bf16[176,2048]{1,0:T(8,128)(2,1)}) %reduce-scatter.29.cloned.1.call-update) | async-done | bytes 720912 | tf_op jit(solution)/shard_map/reduce_scatter | solution.py:215
  1840.0 12.0 fusion.57
  1853.3 28.4 %all-reduce.13.cloned.1.call-done = (bf16[64]{0:T(256)(128)(2,1)}, bf16[32]{0:T(256)(128)(2,1)}, bf16[64,256]{1,0:T(8,128)(2,1)}, bf16[64,256]{1,0:T(8,128)(2,1)}, bf16[64]{0:T(256)(128)(2,1)}) async-done(((bf16[64]{0:T(256)(128)(2,1)}, bf16[32]{0:T(256)(128)(2,1)}, bf16[64,256]{1,0:T(8,128)(2,1)}, bf16[64,256]{1,0:T(8,128)(2,1)}, bf16[64]{0:T(256)(128)(2,1)}), (bf16[64]{0:T(256)(128)(2,1)}, ...) | async-done | bytes 65872 | tf_op jit(solution)/shard_map/psum | solution.py:335
  1888.0 74.4 %all-reduce.15.cloned.1.call-done = (bf16[64,1024]{1,0:T(8,128)(2,1)}, bf16[32,4096]{1,0:T(8,128)(2,1)}, bf16[128,2048]{1,0:T(8,128)(2,1)}, bf16[64,5632]{1,0:T(...) async-done(((bf16[64,1024]{1,0:T(8,128)(2,1)}, bf16[32,4096]{1,0:T(8,128)(2,1)}, bf16[128,2048]{1,0:T(8,128)(2,1)}, bf16[64,5632]{1,0:T(8,128)(2,1)}, ...) | async-done | bytes 3080208 | tf_op jit(solution)/shard_map/psum | solution.py:336
  1962.4 2.4 convert_element_type.242
  (248 shorter events, 73.1 us)
Async XLA Ops:
  7.2 138.4 %all-gather.11.cloned.1.call-start = ((), (), s32[]{:S(2)}) async-start(), calls=%async_computation.10 | async-start | bytes 1081344 | tf_op jit(solution)/shard_map/all_gather | solution.py:111
  7.9 140.6 %all-gather.19.cloned.1.call-start = ((), (), s32[]{:S(2)}) async-start(), calls=%async_computation.14 | async-start | bytes 1081344 | tf_op jit(solution)/shard_map/all_gather | solution.py:112
  8.7 146.1 %copy-start = (bf16[128,2048]{1,0:T(8,128)(2,1)S(1)}, bf16[128,2048]{1,0:T(8,128)(2,1)}, u32[]{:S(2)}) copy-start(bf16[128,2048]{1,0:T(8,128)(2,1)} %param.20) | copy-start | bytes 1572868
  8.7 146.0 %all-gather.15.cloned.1.call-start = ((), (), s32[]{:S(2)}) async-start(), calls=%async_computation.12 | async-start | bytes 4325376 | tf_op jit(solution)/shard_map/all_gather | solution.py:108
  9.4 194.2 %all-gather.17.cloned.1.call-start = ((), (), s32[]{:S(2)}) async-start(), calls=%async_computation.13 | async-start | bytes 8650752 | tf_op jit(solution)/shard_map/all_gather | solution.py:110
  10.0 239.9 %all-gather.13.cloned.1.call-start = ((), (), s32[]{:S(2)}) async-start(), calls=%async_computation.11 | async-start | bytes 2162688 | tf_op jit(solution)/shard_map/all_gather | solution.py:134
  141.2 16.6 copy-start.24
  148.4 147.4 %all-gather.21.cloned.1.call-start = ((), (), s32[]{:S(2)}) async-start(), calls=%async_computation.15 | async-start | bytes 2162688 | tf_op jit(solution)/shard_map/all_gather | solution.py:135
  150.9 219.1 %all-gather.23.cloned.1.call-start = ((), (), s32[]{:S(2)}) async-start(), calls=%async_computation.16 | async-start | bytes 17301504 | tf_op jit(solution)/shard_map/all_gather | solution.py:113
  151.7 307.4 %all-gather.25.cloned.1.call-start = ((), (), s32[]{:S(2)}) async-start(), calls=%async_computation.17 | async-start | bytes 23789568 | tf_op jit(solution)/shard_map/all_gather | solution.py:119
  152.4 395.7 %all-gather.27.cloned.1.call-start = ((), (), s32[]{:S(2)}) async-start(), calls=%async_computation.18 | async-start | bytes 23789568 | tf_op jit(solution)/shard_map/all_gather | solution.py:120
  153.1 483.8 %all-gather.29.cloned.1.call-start = ((), (), s32[]{:S(2)}) async-start(), calls=%async_computation.19 | async-start | bytes 23789568 | tf_op jit(solution)/shard_map/all_gather | solution.py:121
  153.7 730.8 %reduce-scatter.11.cloned.1.call-start = ((), (), s32[]{:S(2)}) async-start(), calls=%async_computation.20 | async-start | bytes 2162688 | tf_op jit(solution)/shard_map/reduce_scatter | solution.py:278
  153.8 56.7 %copy-start.33 = (f32[1024]{0:T(1024)}, f32[1024]{0:T(1024)S(1)}, u32[]{:S(2)}) copy-start(f32[1024]{0:T(1024)S(1)} %convert_element_type.203) | copy-start | bytes 12292
  153.8 224.8 %copy-start.39 = (f32[2048]{0:T(1024)}, f32[2048]{0:T(1024)S(1)}, u32[]{:S(2)}) copy-start(f32[2048]{0:T(1024)S(1)} %convert_element_type.209) | copy-start | bytes 24580
  154.6 56.0 %copy-start.26 = (f32[128,128]{0,1:T(8,128)}, f32[128,128]{0,1:T(8,128)S(1)}, u32[]{:S(2)}) copy-start(f32[128,128]{0,1:T(8,128)S(1)} %copy.63) | copy-start | bytes 196612
  154.7 55.8 %copy-start.28 = (f32[128,128]{0,1:T(8,128)}, f32[128,128]{0,1:T(8,128)S(1)}, u32[]{:S(2)}) copy-start(f32[128,128]{0,1:T(8,128)S(1)} %copy.65) | copy-start | bytes 196612
  157.8 52.7 %copy-start.9 = (f32[128,1024]{1,0:T(8,128)}, f32[128,1024]{1,0:T(8,128)S(1)}, u32[]{:S(2)}) copy-start(f32[128,1024]{1,0:T(8,128)S(1)} %get-tuple-element.534) | copy-start | bytes 1572868
  157.8 52.7 %copy-start.44 = (f32[128]{0:T(128)}, f32[128]{0:T(128)S(1)}, u32[]{:S(2)}) copy-start(f32[128]{0:T(128)S(1)} %add_rsqrt_fusion.1) | copy-start | bytes 1540
  252.9 42.9 %copy-start.21 = (bf16[128,16,256]{2,0,1:T(8,128)(2,1)}, bf16[128,16,256]{2,0,1:T(8,128)(2,1)S(1)}, u32[]{:S(2)}) copy-start(bf16[128,16,256]{2,0,1:T(8,128)(2,1)S(1)} %get-tuple-element.971) | copy-start | bytes 3145732
  300.3 78.2 %copy-start.35 = (s32[4096]{0:T(1024)}, s32[4096]{0:T(1024)S(1)}, u32[]{:S(2)}) copy-start(s32[4096]{0:T(1024)S(1)} %get-tuple-element.1011) | copy-start | bytes 49156
  300.3 78.2 %copy-start.36 = (s32[128]{0:T(128)}, s32[128]{0:T(128)S(1)}, u32[]{:S(2)}) copy-start(s32[128]{0:T(128)S(1)} %get-tuple-element.1013) | copy-start | bytes 1540
  378.6 301.2 %copy-start.2 = (f32[128,2048]{1,0:T(8,128)}, f32[128,2048]{1,0:T(8,128)S(1)}, u32[]{:S(2)}) copy-start(f32[128,2048]{1,0:T(8,128)S(1)} %get-tuple-element.536) | copy-start | bytes 3145732
  378.6 93.0 %copy-start.48 = (f32[128]{0:T(128)}, f32[128]{0:T(128)S(1)}, u32[]{:S(2)}) copy-start(f32[128]{0:T(128)S(1)} %add_rsqrt_fusion) | copy-start | bytes 1540
  378.8 169.3 %copy-start.11 = (bf16[128,2048]{1,0:T(8,128)(2,1)}, bf16[128,2048]{1,0:T(8,128)(2,1)S(1)}, u32[]{:S(2)}) copy-start(bf16[128,2048]{1,0:T(8,128)(2,1)S(1)} %multiply_convert_fusion.3) | copy-start | bytes 1572868
  471.5 165.4 %copy-start.17 = (bf16[128,2048]{1,0:T(8,128)(2,1)S(1)}, bf16[128,2048]{1,0:T(8,128)(2,1)}, u32[]{:S(2)}) copy-start(bf16[128,2048]{1,0:T(8,128)(2,1)} %param.21) | copy-start | bytes 1572868
  718.6 247.6 %reduce-scatter.13.cloned.1.call-start = ((), (), s32[]{:S(2)}) async-start(), calls=%async_computation.21 | async-start | bytes 2162688 | tf_op jit(solution)/shard_map/reduce_scatter | solution.py:281
  718.6 166.8 %copy-start.47 = (f32[128]{0:T(128)S(1)}, f32[128]{0:T(128)}, u32[]{:S(2)}) copy-start(f32[128]{0:T(128)} %copy-done.46) | copy-start | bytes 1540
  718.6 166.8 %copy-start.51 = (f32[128]{0:T(128)S(1)}, f32[128]{0:T(128)}, u32[]{:S(2)}) copy-start(f32[128]{0:T(128)} %copy-done.50) | copy-start | bytes 1540
  718.6 167.1 %copy-start.1 = (bf16[128,2048]{1,0:T(8,128)(2,1)S(1)}, bf16[128,2048]{1,0:T(8,128)(2,1)}, u32[]{:S(2)}) copy-start(bf16[128,2048]{1,0:T(8,128)(2,1)} %param.20) | copy-start | bytes 1572868
  718.6 167.1 %copy-start.25 = (f32[2048]{0:T(1024)S(1)}, f32[2048]{0:T(1024)}, u32[]{:S(2)}) copy-start(f32[2048]{0:T(1024)} %copy-done.24) | copy-start | bytes 24580
  718.7 167.1 %copy-start.42 = (f32[128]{0:T(128)S(1)}, f32[128]{0:T(128)}, u32[]{:S(2)}) copy-start(f32[128]{0:T(128)} %copy-done.41) | copy-start | bytes 1540
  722.6 442.7 %reduce-scatter.19.cloned.1.call-start = ((), (), s32[]{:S(2)}) async-start(), calls=%async_computation.24 | async-start | bytes 1081344 | tf_op jit(solution)/shard_map/reduce_scatter | solution.py:321
  887.3 81.5 %copy-start.27 = (f32[128,128]{0,1:T(8,128)S(1)}, f32[128,128]{0,1:T(8,128)}, u32[]{:S(2)}) copy-start(f32[128,128]{0,1:T(8,128)} %copy-done.26) | copy-start | bytes 196612
  887.3 81.5 %copy-start.29 = (f32[128,128]{0,1:T(8,128)S(1)}, f32[128,128]{0,1:T(8,128)}, u32[]{:S(2)}) copy-start(f32[128,128]{0,1:T(8,128)} %copy-done.28) | copy-start | bytes 196612
  887.4 277.9 %reduce-scatter.21.cloned.1.call-start = ((), (), s32[]{:S(2)}) async-start(), calls=%async_computation.25 | async-start | bytes 1081344 | tf_op jit(solution)/shard_map/reduce_scatter | solution.py:324
  889.2 81.5 %copy-start.10 = (f32[128,1024]{1,0:T(8,128)S(1)}, f32[128,1024]{1,0:T(8,128)}, u32[]{:S(2)}) copy-start(f32[128,1024]{1,0:T(8,128)} %copy-done.9) | copy-start | bytes 1572868
  889.2 81.6 %copy-start.34 = (f32[1024]{0:T(1024)S(1)}, f32[1024]{0:T(1024)}, u32[]{:S(2)}) copy-start(f32[1024]{0:T(1024)} %copy-done.33) | copy-start | bytes 12292
  889.2 81.6 %copy-start.45 = (f32[128]{0:T(128)S(1)}, f32[128]{0:T(128)}, u32[]{:S(2)}) copy-start(f32[128]{0:T(128)} %copy-done.44) | copy-start | bytes 1540
  968.6 243.6 %reduce-scatter.15.cloned.1.call-start = ((), (), s32[]{:S(2)}) async-start(), calls=%async_computation.22 | async-start | bytes 4325376 | tf_op jit(solution)/shard_map/reduce_scatter | solution.py:312
  980.8 327.5 %reduce-scatter.17.cloned.1.call-start = ((), (), s32[]{:S(2)}) async-start(), calls=%async_computation.23 | async-start | bytes 8650752 | tf_op jit(solution)/shard_map/reduce_scatter | solution.py:318
  986.6 440.5 %reduce-scatter.23.cloned.1.call-start = ((), (), s32[]{:S(2)}) async-start(), calls=%async_computation.26 | async-start | bytes 17301504 | tf_op jit(solution)/shard_map/reduce_scatter | solution.py:327
  996.5 568.8 %reduce-scatter.25.cloned.1.call-start = ((), (), s32[]{:S(2)}) async-start(), calls=%async_computation.27 | async-start | bytes 23789568 | tf_op jit(solution)/shard_map/reduce_scatter | solution.py:209
  1009.7 693.2 %reduce-scatter.27.cloned.1.call-start = ((), (), s32[]{:S(2)}) async-start(), calls=%async_computation.28 | async-start | bytes 23789568 | tf_op jit(solution)/shard_map/reduce_scatter | solution.py:212
  1022.4 817.5 %reduce-scatter.29.cloned.1.call-start = ((), (), s32[]{:S(2)}) async-start(), calls=%async_computation.29 | async-start | bytes 23789568 | tf_op jit(solution)/shard_map/reduce_scatter | solution.py:215
  1035.8 845.9 %all-reduce.13.cloned.1.call-start = ((), (), s32[]{:S(2)}) async-start(), calls=%async_computation.30 | async-start | bytes 134144 | tf_op jit(solution)/shard_map/psum | solution.py:335
  1039.7 800.3 %copy-start.3 = (f32[128,2048]{1,0:T(8,128)S(1)}, f32[128,2048]{1,0:T(8,128)}, u32[]{:S(2)}) copy-start(f32[128,2048]{1,0:T(8,128)} %copy-done.2) | copy-start | bytes 3145732
  1165.3 797.1 %all-reduce.15.cloned.1.call-start = ((), (), s32[]{:S(2)}) async-start(), calls=%async_computation.31 | async-start | bytes 6160384 | tf_op jit(solution)/shard_map/psum | solution.py:336
  (27 other events, 204.2 us)
Sparse Core Ops, SparseCore 0:
  10.3 46.5 all-gather.10
  59.2 42.0 all-gather.18
  103.6 45.5 all-gather.14
  151.3 52.2 all-gather.16
  206.3 43.4 all-gather.12
  252.5 43.2 all-gather.20
  298.1 71.8 all-gather.22
  372.2 86.7 all-gather.24
  461.3 86.7 all-gather.26
  550.2 86.7 all-gather.28
  718.7 165.8 reduce-scatter.10
  887.9 78.1 reduce-scatter.12
  969.7 76.9 reduce-scatter.18
  1050.4 76.9 reduce-scatter.20
  1130.9 81.2 reduce-scatter.14
  1216.2 92.0 reduce-scatter.16
  1312.0 114.9 reduce-scatter.22
  1430.9 134.2 reduce-scatter.24
  1569.8 133.0 reduce-scatter.26
  1706.7 133.1 reduce-scatter.28
  1843.9 37.7 all-reduce.12
  1884.5 77.8 all-reduce.14
where the time goes:
time: 1990 us; the launch traced here: 1980 us
  waiting for transfers between devices  1450 us (73%)
  blocking collectives  247 us (12%)
  matrix products  202 us (10%)
  other arithmetic  42.6 us (2%)
    unnamed x2, blocking collectives  247 us
    reduce_scatter x1, waiting for transfers between devices, on_device(): lax.psum_scatter(grad_keys.astype(jnp.bfloat16), 'seq', scatter_dimension...  162 us
    reduce_scatter x1, waiting for transfers between devices, on_device(): lax.psum_scatter(grad_gate_w.astype(jnp.bfloat16), 'seq', scatter_dimensi...  138 us
    reduce_scatter x1, waiting for transfers between devices, on_device(): lax.psum_scatter(grad_up_w.astype(jnp.bfloat16), 'seq', scatter_dimension...  138 us
    reduce_scatter x1, waiting for transfers between devices, on_device(): lax.psum_scatter(grad_down.astype(jnp.bfloat16), 'seq', scatter_dimension...  137 us
    reduce_scatter x1, waiting for transfers between devices, on_device(): lax.psum_scatter(grad_out_w.astype(jnp.bfloat16), 'seq', scatter_dimensio...  119 us
    reduce_scatter x1, waiting for transfers between devices, on_device(): lax.psum_scatter(grad_up_q.astype(jnp.bfloat16), 'seq', scatter_dimension...  96.1 us
    all_gather x1, waiting for transfers between devices, on_device(): lax.all_gather(gate_weight, 'seq', axis=0, tiled=True)  80.3 us
  transfers between devices with their start and end apart: 22, of which 17 were waited for; matrix products, arithmetic and copies ran while one was open for 9% of the time, Pallas kernels for 0%

commit v1 on v0

v1 whole, which is shorter than its diff:
```python
import functools
import math

import jax
import jax.numpy as jnp
from jax import lax
from jax.experimental import pallas as pl
from jax.experimental.pallas import tpu as pltpu
from jax.sharding import Mesh
from jax.sharding import PartitionSpec as P

EPSILON = 1e-06
MASKED = -1e30
BF = jnp.bfloat16
F32 = jnp.float32
SIZE = 256
HALF = 128
BLOCK = 256
ROW = ("y", "z", "c")
HEADS = ("y", "c")
FEED = ("x", "c")


def dot(left, right):
    return jnp.dot(left, right, preferred_element_type=F32)


def dot_tn(left, right):
    return lax.dot_general(left, right, (((0,), (0,)), ((), ())), preferred_element_type=F32)


def dot_nt(left, right):
    return lax.dot_general(left, right, (((1,), (1,)), ((), ())), preferred_element_type=F32)


def norm_back(values, inverse, gain, grad):
    scaled = grad * gain
    grad_values = inverse * scaled - values * inverse * inverse * inverse * jnp.mean(
        scaled * values, axis=-1, keepdims=True
    )
    return grad_values, jnp.sum(grad * values * inverse, axis=0)


def places_of(lengths_row, slots):
    ends = jnp.cumsum(lengths_row)
    begins = jnp.concatenate([ends - lengths_row, ends[-1:]])
    begin = jnp.max(jnp.where(slots[:, None] >= begins[None, :], begins[None, :], 0), axis=1)
    live = (slots < ends[-1]).astype(F32)
    return begin, live


def tables(position):
    freq = jnp.exp(jnp.arange(HALF, dtype=F32) * (-math.log(10000.0) / HALF))
    angle = position.astype(F32)[:, None] * freq[None, :]
    return jnp.cos(angle), jnp.sin(angle)


def rotate(values, cosine, sine):
    lower, upper = values[..., :HALF], values[..., HALF:]
    return jnp.concatenate([lower * cosine - upper * sine, upper * cosine + lower * sine], axis=-1)


def unrotate(grad, cosine, sine):
    lower, upper = grad[..., :HALF], grad[..., HALF:]
    return jnp.concatenate([lower * cosine + upper * sine, upper * cosine - lower * sine], axis=-1)


def attend_kernel(q_ref, k_ref, vt_ref, begin_ref, slot_ref, out_ref, lse_ref, peak, total, accum):
    depth = lax.axis_index("z")
    segments = slot_ref.shape[0]
    rows = slot_ref.shape[2]
    tokens = rows // 2
    for seg in range(segments):
        query = q_ref[pl.ds(seg * tokens, tokens), :]
        query = jnp.concatenate([query[:, :SIZE], query[:, SIZE:]], axis=0).T
        begin = begin_ref[seg]
        slot = slot_ref[seg]
        peak[...] = jnp.full_like(peak, MASKED)
        total[...] = jnp.zeros_like(total)
        accum[...] = jnp.zeros_like(accum)
        count = segments * seg + depth + 1

        @pl.loop(0, count)
        def _(block):
            at = pl.multiple_of(block * BLOCK, BLOCK)
            scores = dot(k_ref[pl.ds(at, BLOCK), :], query)
            key = lax.broadcasted_iota(jnp.int32, scores.shape, 0) + at
            scores = jnp.where((key >= begin) & (key <= slot), scores, MASKED)
            before = peak[...]
            now = jnp.maximum(before, jnp.max(scores, axis=0, keepdims=True))
            weights = jnp.exp(scores - now)
            shrink = jnp.exp(before - now)
            peak[...] = now
            total[...] = total[...] * shrink + jnp.sum(weights, axis=0, keepdims=True)
            accum[...] = accum[...] * shrink + dot(vt_ref[:, pl.ds(at, BLOCK)], weights.astype(BF))

        lse_ref[seg] = peak[...] + jnp.log(total[...])
        result = (accum[...] / total[...]).T
        out_ref[pl.ds(seg * tokens, tokens), :] = jnp.concatenate(
            [result[:tokens], result[tokens:]], axis=1
        )


def attend(q, k, vt, begin, slot):
    segments, _, rows = slot.shape
    return pl.pallas_call(
        attend_kernel,
        name="attend",
        out_shape=(
            jax.ShapeDtypeStruct(q.shape, F32),
            jax.ShapeDtypeStruct((segments, 1, rows), F32),
        ),
        in_specs=[pl.BlockSpec(memory_space=pltpu.VMEM)] * 5,
        out_specs=[pl.BlockSpec(memory_space=pltpu.VMEM)] * 2,
        scratch_shapes=[
            pltpu.VMEM((1, rows), F32),
            pltpu.VMEM((1, rows), F32),
            pltpu.VMEM((SIZE, rows), F32),
        ],
        compiler_params=pltpu.CompilerParams(vmem_limit_bytes=48 << 20),
    )(q, k, vt, begin, slot)


def attend_back_kernel(
    q_ref, do_ref, o_ref, k_ref, kt_ref, v_ref, begin_ref, slot_ref, lse_ref,
    dq_ref, dk_ref, dv_ref, accum,
):
    depth = lax.axis_index("z")
    segments = slot_ref.shape[0]
    rows = slot_ref.shape[2]
    tokens = rows // 2
    dk_ref[...] = jnp.zeros_like(dk_ref)
    dv_ref[...] = jnp.zeros_like(dv_ref)
    for seg in range(segments):
        here = pl.ds(seg * tokens, tokens)

        def stacked(ref):
            value = ref[here, :]
            return jnp.concatenate([value[:, :SIZE], value[:, SIZE:]], axis=0)

        query = stacked(q_ref)
        grad = stacked(do_ref)
        query_t = query.T
        grad_t = grad.T
        delta = jnp.sum(
            grad_t.astype(F32) * stacked(o_ref).T.astype(F32), axis=0, keepdims=True
        )
        begin = begin_ref[seg]
        slot = slot_ref[seg]
        lse = lse_ref[seg]
        accum[...] = jnp.zeros_like(accum)
        count = segments * seg + depth + 1

        @pl.loop(0, count)
        def _(block):
            at = pl.multiple_of(block * BLOCK, BLOCK)
            keys = pl.ds(at, BLOCK)
            scores = dot(k_ref[keys, :], query_t)
            key = lax.broadcasted_iota(jnp.int32, scores.shape, 0) + at
            allowed = (key >= begin) & (key <= slot)
            probs = jnp.where(allowed, jnp.exp(scores - lse), 0.0)
            grad_probs = dot(v_ref[keys, :], grad_t)
            grad_scores = (probs * (grad_probs - delta)).astype(BF)
            dv_ref[keys, :] += dot(probs.astype(BF), grad)
            dk_ref[keys, :] += dot(grad_scores, query)
            accum[...] += dot(kt_ref[:, keys], grad_scores)

        result = accum[...].T * (SIZE ** -0.5)
        dq_ref[here, :] = jnp.concatenate([result[:tokens], result[tokens:]], axis=1)


def attend_back(q, do, o, k, kt, v, begin, slot, lse):
    segments, _, rows = slot.shape
    return pl.pallas_call(
        attend_back_kernel,
        name="attend_back",
        out_shape=(
            jax.ShapeDtypeStruct(q.shape, F32),
            jax.ShapeDtypeStruct(k.shape, F32),
            jax.ShapeDtypeStruct(k.shape, F32),
        ),
        in_specs=[pl.BlockSpec(memory_space=pltpu.VMEM)] * 9,
        out_specs=[pl.BlockSpec(memory_space=pltpu.VMEM)] * 3,
        scratch_shapes=[pltpu.VMEM((SIZE, rows), F32)],
        compiler_params=pltpu.CompilerParams(vmem_limit_bytes=48 << 20),
    )(q, do, o, k, kt, v, begin, slot, lse)


def gather(value, axes):
    return lax.all_gather(value, axes, axis=0, tiled=True)


def scatter_sum(value, axes):
    return lax.psum_scatter(value, axes, scatter_dimension=0, tiled=True)


def swap(value, axes):
    return lax.all_to_all(value, axes, 0, 0, tiled=True)


def on_device(
    block_input, cotangent, lengths, norm_gain, q_down, q_gain, q_up, key_weight, value_weight,
    out_weight, ffn_gain, gate_weight, up_weight, down_weight,
):
    rows, width = block_input.shape
    latent_width = q_down.shape[1]
    n_x, n_y, n_z, n_c = (lax.axis_size(a) for a in ("x", "y", "z", "c"))
    x, y, z, c = (lax.axis_index(a) for a in ("x", "y", "z", "c"))
    span = n_y * n_z * n_c
    members = n_y * n_c
    lengths_row = lengths[0]

    mine = (y * n_z + z) * n_c + c
    slots_mine = mine * rows + jnp.arange(rows, dtype=jnp.int32)
    begin_mine, _ = places_of(lengths_row, slots_mine)
    cosine, sine = tables(slots_mine - begin_mine)
    strip = n_c * rows
    slots_group = (
        (jnp.arange(n_y, dtype=jnp.int32)[:, None] * n_z + z) * strip
        + jnp.arange(strip, dtype=jnp.int32)[None, :]
    ).reshape(-1)
    begin_group, live_group = places_of(lengths_row, slots_group)
    cosine_group, sine_group = tables(slots_group - begin_group)
    begin_lanes = jnp.tile(begin_group.reshape(n_y, 1, strip), (1, 1, 2))
    slot_lanes = jnp.tile(slots_group.reshape(n_y, 1, strip), (1, 1, 2))

    shard = norm_gain.shape[0]
    extra = jnp.stack(
        [norm_gain, ffn_gain, jnp.pad(q_gain, (0, shard - q_gain.shape[0]))], axis=1
    ).astype(BF)
    first_width = latent_width + 2 * SIZE
    first = jnp.concatenate(
        [q_down, key_weight, value_weight, jnp.pad(extra, ((0, 0), (0, 125)))], axis=1
    )
    first_full = gather(first, ROW)
    extra_full = first_full[:, first_width : first_width + 3].astype(F32)
    first_full = first_full[:, :first_width]
    gain_one = extra_full[:, 0]
    gain_two = extra_full[:, 1]
    gain_latent = extra_full[:, 2].reshape(span, shard)[:, : q_gain.shape[0]].reshape(-1)

    per_heads = q_up.shape[1] // members
    q_rows = q_up.shape[0]
    up_part = swap(q_up.reshape(q_rows, members, per_heads).transpose(1, 0, 2), HEADS)
    up_heads = gather(up_part[None], "z")
    up_heads = (
        up_heads.reshape(n_z, n_y, n_c, q_rows, per_heads)
        .transpose(1, 0, 2, 3, 4)
        .reshape(span * q_rows, per_heads)
    )
    out_chip = gather(out_weight, ("z", "c"))
    out_heads = lax.dynamic_slice_in_dim(out_chip, c * per_heads, per_heads)

    wide = gate_weight.shape[1]
    down_rows = down_weight.shape[0]
    share = down_rows // n_x
    padded = -(-share // 16) * 16
    source = lax.broadcasted_iota(jnp.int32, (wide // 2, n_c * (span // 4) * padded), 0)
    target = lax.broadcasted_iota(jnp.int32, source.shape, 1)
    block_at = target // (padded * (span // 4)) + n_c * ((target // padded) % (span // 4))
    inside = target % padded
    picks = (
        (source == block_at * down_rows + x * share + inside) & (inside < share)
    ).astype(BF)

    def spread(weight):
        stacked = jnp.concatenate([weight[:, : wide // 2], weight[:, wide // 2 :]], axis=0)
        part = dot(stacked, picks).astype(BF)
        part = part.reshape(2, shard, n_c, -1).transpose(2, 1, 0, 3)
        return part.reshape(n_c, shard, -1)

    both = jnp.stack([spread(gate_weight), spread(up_weight)], axis=1)
    both = swap(both, "c")
    units = both.shape[-1]
    both = both.transpose(0, 2, 1, 3).reshape(n_c * shard, 2 * units)
    both_full = gather(both, ("y", "z"))
    gate_use, up_use = both_full[:, :units], both_full[:, units:]
    down_part = lax.dynamic_slice_in_dim(down_weight, x * share, share)
    down_part = jnp.pad(down_part, ((0, padded - share), (0, 0)))
    down_use = gather(down_part, ("y", "z"))

    inputs = block_input.astype(F32)
    inverse_one = lax.rsqrt(jnp.mean(inputs * inputs, axis=-1, keepdims=True) + EPSILON)
    normed = (inputs * inverse_one * gain_one).astype(BF)
    firsts = dot(normed, first_full)
    latent = firsts[:, :latent_width]
    inverse_latent = lax.rsqrt(jnp.mean(latent * latent, axis=-1, keepdims=True) + EPSILON)
    latent_normed = (latent * inverse_latent * gain_latent).astype(BF)
    key_mine = rotate(firsts[:, latent_width : latent_width + SIZE], cosine, sine).astype(BF)
    value_mine = firsts[:, latent_width + SIZE :].astype(BF)
    key_value = gather(jnp.concatenate([key_mine, value_mine], axis=1), ROW)
    keys, values = key_value[:, :SIZE], key_value[:, SIZE:]
    latent_group = gather(latent_normed, HEADS)
    group = latent_group.shape[0]
    queries = rotate(
        dot(latent_group, up_heads).reshape(group, 2, SIZE),
        cosine_group[:, None, :], sine_group[:, None, :],
    ).astype(BF) * (SIZE ** -0.5)
    queries = queries.astype(BF).reshape(group, per_heads)
    attended, lse = attend(queries, keys, values.T, begin_lanes, slot_lanes)
    mixed = (attended * live_group[:, None]).astype(BF)
    middle = inputs + scatter_sum(dot(mixed, out_heads).astype(BF), HEADS).astype(F32)

    inverse_two = lax.rsqrt(jnp.mean(middle * middle, axis=-1, keepdims=True) + EPSILON)
    normed_two = gather((middle * inverse_two * gain_two).astype(BF), FEED)
    grad_feed = gather(cotangent, FEED)
    gate_pre = dot(normed_two, gate_use)
    up_pre = dot(normed_two, up_use)
    sigma = jax.nn.sigmoid(gate_pre)
    hidden = (gate_pre * sigma * up_pre).astype(BF)
    grad_hidden = dot_nt(grad_feed, down_use)
    grad_gate_pre = (grad_hidden * up_pre * sigma * (1.0 + gate_pre * (1.0 - sigma))).astype(BF)
    grad_up_pre = (grad_hidden * gate_pre * sigma).astype(BF)
    grad_normed_two = scatter_sum(
        (dot_nt(grad_gate_pre, gate_use) + dot_nt(grad_up_pre, up_use)).astype(BF), FEED
    ).astype(F32)
    branch_two = scatter_sum(dot(hidden, down_use).astype(BF), FEED).astype(F32)
    output = (middle + branch_two).astype(BF)
    grad_result = cotangent.astype(F32)
    grad_mid_norm, grad_gain_two = norm_back(middle, inverse_two, gain_two, grad_normed_two)
    grad_middle = grad_result + grad_mid_norm
    grad_both = jnp.concatenate(
        [dot_tn(normed_two, grad_gate_pre), dot_tn(normed_two, grad_up_pre)], axis=1
    ).astype(BF)
    grad_both = scatter_sum(grad_both, ("y", "z"))
    grad_down = scatter_sum(dot_tn(hidden, grad_feed).astype(BF), ("y", "z"))
    grad_both = grad_both.reshape(n_c, shard, 2, units).transpose(0, 2, 1, 3)
    grad_both = swap(grad_both, "c")
    grad_both = gather(grad_both.reshape(1, n_c, 2, shard, units), "x")
    grad_down = gather(grad_down[None], "x")

    def collect(grads):
        parts = grads.reshape(n_x, n_c, shard, 2, units // 2).transpose(0, 3, 2, 1, 4)
        parts = parts.reshape(n_x, 2 * shard, n_c * units // 2)
        whole = 0.0
        for i in range(n_x):
            picked = (
                (source == block_at * down_rows + i * share + inside) & (inside < share)
            ).astype(BF)
            whole = whole + dot_nt(parts[i], picked)
        return jnp.concatenate([whole[:shard], whole[shard:]], axis=1)

    grad_gate = collect(grad_both[:, :, 0])
    grad_up = collect(grad_both[:, :, 1])
    grad_down = grad_down[:, :share].reshape(down_rows, width).astype(F32)

    grad_branch = gather(grad_middle.astype(BF), HEADS)
    grad_mixed = dot_nt(grad_branch, out_heads).astype(BF)
    grad_attended = grad_mixed * live_group[:, None].astype(BF)
    grad_out = dot_tn(mixed, grad_branch).astype(BF)
    grad_queries, grad_keys, grad_values = attend_back(
        queries, grad_attended, mixed, keys, keys.T, values, begin_lanes, slot_lanes, lse
    )
    grad_kv = scatter_sum(
        jnp.concatenate([grad_keys, grad_values], axis=1).astype(BF), ROW
    ).astype(F32)
    grad_query_raw = (
        unrotate(
            grad_queries.reshape(group, 2, SIZE),
            cosine_group[:, None, :], sine_group[:, None, :],
        )
        .reshape(group, per_heads)
        .astype(BF)
    )
    grad_key_raw = unrotate(grad_kv[:, :SIZE], cosine, sine).astype(BF)
    grad_value_raw = grad_kv[:, SIZE:].astype(BF)
    grad_up_heads = dot_tn(latent_group, grad_query_raw).astype(BF)
    grad_latent_normed = scatter_sum(dot_nt(grad_query_raw, up_heads).astype(BF), HEADS).astype(F32)
    grad_latent_f, grad_gain_latent = norm_back(
        latent, inverse_latent, gain_latent, grad_latent_normed
    )
    grad_firsts = jnp.concatenate(
        [grad_latent_f.astype(BF), grad_key_raw, grad_value_raw], axis=1
    )
    grad_normed = dot_nt(grad_firsts, first_full)
    grad_input_norm, grad_gain_one = norm_back(inputs, inverse_one, gain_one, grad_normed)
    input_grad = grad_middle + grad_input_norm

    normed_group = gather(normed, HEADS)
    tall = width // n_y
    normed_part = lax.dynamic_slice_in_dim(normed_group, y * tall, tall, axis=1)
    grad_firsts_group = gather(grad_firsts, HEADS)
    half_first = first_width // n_c
    first_part = lax.dynamic_slice_in_dim(grad_firsts_group, c * half_first, half_first, axis=1)
    grad_first = dot_tn(normed_part, first_part).astype(BF)

    out_rows = out_weight.shape[0]
    grad_out = grad_out.reshape(n_z // n_c, n_c, out_rows, width).transpose(1, 0, 2, 3)
    grad_out = swap(grad_out, "c").reshape(n_z, out_rows * width)
    grad_first = grad_first.reshape(n_z, n_c, shard, half_first).transpose(1, 0, 2, 3)
    grad_first = swap(grad_first, "c").transpose(1, 2, 0, 3).reshape(n_z, shard * first_width)
    grad_up_heads = grad_up_heads.reshape(n_y, n_z, n_c, q_rows, per_heads)
    grad_up_heads = grad_up_heads.transpose(0, 2, 1, 3, 4).reshape(members, n_z, q_rows, per_heads)
    grad_up_heads = swap(grad_up_heads, HEADS).transpose(1, 2, 0, 3).reshape(n_z, -1)
    pieces = jnp.concatenate([grad_out, grad_first, grad_up_heads], axis=1)
    pieces = lax.psum(scatter_sum(pieces, "z"), "x").astype(F32)[0]
    at_first = out_rows * width
    at_up = at_first + shard * first_width
    grad_out = pieces[:at_first].reshape(out_rows, width)
    grad_first = pieces[at_first:at_up].reshape(shard, first_width)
    grad_q_up = pieces[at_up:].reshape(q_rows, -1)

    gains = jnp.concatenate(
        [
            grad_gain_one.reshape(span, shard),
            grad_gain_two.reshape(span, shard),
            grad_gain_latent.reshape(span, -1),
        ],
        axis=1,
    )
    gains = lax.psum(scatter_sum(gains, ROW), "x")[0]
    return (
        output,
        input_grad,
        gains[:shard],
        grad_first[:, :latent_width],
        gains[2 * shard :],
        grad_q_up,
        grad_first[:, latent_width : latent_width + SIZE],
        grad_first[:, latent_width + SIZE :],
        grad_out,
        gains[shard : 2 * shard],
        grad_gate,
        grad_up,
        grad_down,
    )


def solution(mesh):
    sizes = (4, 4, 4, 2)
    grid = Mesh(mesh.devices.reshape(sizes), ("x", "y", "z", "c"))
    tokens = P(("x", "y", "z", "c"), None)
    wide, thin = P(ROW, None), P(ROW)
    in_specs = (
        tokens, tokens, P("x", None), thin, wide, thin, wide, wide, wide, wide, thin, wide, wide,
        wide,
    )
    out_specs = (
        tokens, tokens, thin, wide, thin, wide, wide, wide, wide, thin, wide, wide, wide,
    )
    return jax.shard_map(
        on_device, mesh=grid, in_specs=in_specs, out_specs=out_specs, check_vma=False
    )
```

time: 1990 us -> 1190 us (0.60)
  waiting for transfers between devices: 1450 us -> 663 us
  matrix products: 202 us -> 108 us
  blocking collectives: 247 us -> 158 us
  local copies, waits for them, and re-layouts: 19.9 us -> 105 us
  Pallas kernels: 0 us -> 44.8 us
  other arithmetic: 42.6 us -> 63.9 us
    reduce_scatter x10 -> x7, waiting for transfers between devices: 913 us -> 266 us  [scatter_sum(): return lax.psum_scatter(value, axes, scatter_dimension=0, tiled=True)]
    unnamed x2 -> x1, blocking collectives: 247 us -> 124 us
    all_gather x10 -> x13, waiting for transfers between devices: 425 us -> 321 us  [gather(): return lax.all_gather(value, axes, axis=0, tiled=True)]
    dot_general x30 -> x28, matrix products: 195 us -> 108 us  [the longest x14 44.8 us: dot_nt(): lax.dot_general(left, right, (((1,), (1,)), ((), ())), preferred_element_...]
    psum x2 -> x1, waiting for transfers between devices: 103 us -> 54 us  [on_device(): pieces = lax.psum(scatter_sum(pieces, 'z'), 'x').astype(F32)[0]]
    pallas_call x0 -> x2, Pallas kernels: none -> 44.8 us  [the longest x1 25.9 us: attend_back(): pl.pallas_call(attend_back_kernel, name='attend_back', out_shape=(jax.Sha...]
    slice x1 -> x26, local copies, waits for them, and re-layouts: 0.58 us -> 30.3 us  [the longest x1 10.8 us: on_device(): grad_out = pieces[:at_first].reshape(out_rows, width)]
    concatenate x4 -> x10, other arithmetic: 1.51 us -> 29.4 us  [the longest x1 17.1 us: on_device(): pieces = jnp.concatenate([grad_out, grad_first, grad_up_heads], axis=1)]
  transfers between devices with their start and end apart: 22 -> 25, of which waited for: 17 -> 21; matrix products, arithmetic and copies ran while one was open for 9% -> 17% of each run, Pallas kernels for 0% -> 2%
where the time goes in v1:
time: 1190 us; the launch traced here: 1180 us
  waiting for transfers between devices  663 us (56%)
  blocking collectives  158 us (13%)
  matrix products  108 us (9%)
  local copies, waits for them, and re-layouts  105 us (9%)
  other arithmetic  63.9 us (5%)
  Pallas kernels  44.8 us (4%)
  starting transfers between devices  17.5 us (1%)
  between operations  17.3 us (1%)
    all_gather x13, waiting for transfers between devices, gather(): return lax.all_gather(value, axes, axis=0, tiled=True)  321 us
    reduce_scatter x7, waiting for transfers between devices, scatter_sum(): return lax.psum_scatter(value, axes, scatter_dimension=0, tiled=True)  266 us
    unnamed x1, blocking collectives  124 us
    psum x1, waiting for transfers between devices, on_device(): pieces = lax.psum(scatter_sum(pieces, 'z'), 'x').astype(F32)[0]  54 us
    dot_general x14, matrix products, dot_nt(): lax.dot_general(left, right, (((1,), (1,)), ((), ())), preferred_element_...  44.8 us
    dot_general x8, matrix products, dot(): return jnp.dot(left, right, preferred_element_type=F32)  36.6 us
    unnamed x126, local copies, waits for them, and re-layouts  32 us
    dot_general x6, matrix products, dot_tn(): lax.dot_general(left, right, (((0,), (0,)), ((), ())), preferred_element_...  26.2 us
  transfers between devices with their start and end apart: 25, of which 21 were waited for; matrix products, arithmetic and copies ran while one was open for 17% of the time, Pallas kernels for 2%

profile of v1, /device:TPU:1, one launch (start us, length us, event | category | flops | bytes accessed | tf_op | source)
XLA Modules:
  0.0 1176.7 jit_solution(18312008169906152870)
XLA Ops:
  13.1 6.0 all-to-all-start
  20.4 5.3 all-to-all-done
  26.4 39.1 %all-gather.17.cloned.1.call-done = bf16[2048,1664]{1,0:T(8,128)(2,1)} async-done(((bf16[64,1664]{1,0:T(8,128)(2,1)}), bf16[2048,1664]{1,0:T(8,128)(2,1)}) %all-gather.17.cloned.1.call-update) | async-done | bytes 6815760 | tf_op jit(solution)/shard_map/all_gather | solution.py:190
  79.7 9.8 all-gather.39.cloned.1.call-done
  94.1 24.5 %all-gather.19.cloned.1.call-done = bf16[1024,1024]{1,0:T(8,128)(2,1)} async-done(((bf16[128,1024]{1,0:T(8,128)(2,1)}), bf16[1024,1024]{1,0:T(8,128)(2,1)}) %all-gather.19.cloned.1.call-update) | async-done | bytes 2097168 | tf_op jit(solution)/shard_map/all_gather | solution.py:190
  123.8 43.7 %all-gather.21.cloned.1.call-done = bf16[4096,512]{1,0:T(8,128)(2,1)} async-done(((bf16[128,512]{1,0:T(8,128)(2,1)}), bf16[4096,512]{1,0:T(8,128)(2,1)}) %all-gather.21.cloned.1.call-update) | async-done | bytes 4194320 | tf_op jit(solution)/shard_map/all_gather | solution.py:190
  167.5 5.1 fusion.120
  172.7 4.4 copy.173.vt_ref
  178.4 18.8 %attend.1 = (f32[1024,512]{1,0:T(8,128)S(1)}, f32[4,1,512]{2,1,0:T(1,128)S(1)}) custom-call(bf16[1024,512]{1,0:T(8,128)(2,1)S(1)} %copy-done.3, bf16[4096,256]{1,0:T(8,128)(2,1)S(1)} %get-tuple-element.40.k_ref, bf16[256,4096]{1,0:T(8,128)(2,1)} %copy.173.vt_ref, s32[4,1,512]{2,1,0:T(1,128)S(1)} %tile.20.begin_ref, s32[4,1,512]{2,1,0:T(1,128)S(1)} %tile.22.slot_ref), custom_call_target="tpu_custom_call" | custom-call | tf_op jit(solution)/shard_map/attend/pallas_call | solution.py:106
  200.7 5.9 convolution_convert_fusion
  213.2 3.9 all_to_all.30
  218.4 27.9 %reduce-scatter.10.cloned.1.call-done = bf16[128,2048]{1,0:T(8,128)(2,1)} async-done(((bf16[1024,2048]{1,0:T(8,128)(2,1)}), bf16[128,2048]{1,0:T(8,128)(2,1)}) %reduce-scatter.10.cloned.1.call-update) | async-done | bytes 524304 | tf_op jit(solution)/shard_map/reduce_scatter | solution.py:194
  250.0 12.2 %all-gather.29.cloned.1.call-done = bf16[768,2048]{1,0:T(8,128)(2,1)} async-done(((bf16[48,2048]{1,0:T(8,128)(2,1)}), bf16[768,2048]{1,0:T(8,128)(2,1)}) %all-gather.29.cloned.1.call-update) | async-done | bytes 3145744 | tf_op jit(solution)/shard_map/all_gather | solution.py:190
  262.2 33.0 %all-gather.31.cloned.1.call-done = bf16[1024,2048]{1,0:T(8,128)(2,1)} async-done(((bf16[128,2048]{1,0:T(8,128)(2,1)}), bf16[1024,2048]{1,0:T(8,128)(2,1)}) %all-gather.31.cloned.1.call-update) | async-done | bytes 4194320 | tf_op jit(solution)/shard_map/all_gather | solution.py:190
  295.2 8.3 fusion.128
  303.5 54.7 %all-gather.27.cloned.1.call-done = bf16[2048,1536]{1,0:T(8,128)(2,1)} async-done(((bf16[128,1536]{1,0:T(8,128)(2,1)}), bf16[2048,1536]{1,0:T(8,128)(2,1)}) %all-gather.27.cloned.1.call-update) | async-done | bytes 6291472 | tf_op jit(solution)/shard_map/all_gather | solution.py:190
  358.2 34.3 %all-gather.25.cloned.1.call-done = bf16[1024,2048]{1,0:T(8,128)(2,1)} async-done(((bf16[128,2048]{1,0:T(8,128)(2,1)}), bf16[1024,2048]{1,0:T(8,128)(2,1)}) %all-gather.25.cloned.1.call-update) | async-done | bytes 4194320 | tf_op jit(solution)/shard_map/all_gather | solution.py:190
  392.6 6.3 fusion.24
  399.6 5.7 fusion.22
  408.8 5.1 add_convert_fusion
  413.9 34.3 %reduce-scatter.14.cloned.1.call-done = bf16[128,2048]{1,0:T(8,128)(2,1)} async-done(((bf16[1024,2048]{1,0:T(8,128)(2,1)}), bf16[128,2048]{1,0:T(8,128)(2,1)}) %reduce-scatter.14.cloned.1.call-update) | async-done | bytes 524304 | tf_op jit(solution)/shard_map/reduce_scatter | solution.py:194
  452.6 4.1 copy.179.kt_ref
  456.7 30.1 %all-gather.33.cloned.1.call-done = bf16[1024,2048]{1,0:T(8,128)(2,1)} async-done(((bf16[128,2048]{1,0:T(8,128)(2,1)}), bf16[1024,2048]{1,0:T(8,128)(2,1)}) %all-gather.33.cloned.1.call-update) | async-done | bytes 4194320 | tf_op jit(solution)/shard_map/all_gather | solution.py:190
  486.7 5.3 fusion.43.do_ref
  492.1 25.9 %attend_back.1 = (f32[1024,512]{1,0:T(8,128)S(1)}, f32[4096,256]{1,0:T(8,128)}, f32[4096,256]{1,0:T(8,128)}) custom-call(bf16[1024,512]{1,0:T(8,128)(2,1)S(1)} %copy-done.4, bf16[1024,512]{1,0:T(8,128)(2,1)S(1)} %fusion.43.do_ref, bf16[1024,512]{1,0:T(8,128)(2,1)S(1)} %multiply_convert_fusion.1.o_ref, bf16[4096,256]{1,0:T(8,128)(2,1)} %copy-done.2, ...), custom_call_target="tpu_custom_call" | custom-call | tf_op jit(solution)/shard_map/attend_back/pallas_call | solution.py:174
  534.4 6.3 convolution_convert_fusion.3
  548.3 8.6 copy.201
  557.6 8.3 reduce-scatter.16.cloned.1.call-done
  568.3 83.6 %reduce-scatter.18.cloned.1.call-done = bf16[128,512]{1,0:T(8,128)(2,1)} async-done(((bf16[4096,512]{1,0:T(8,128)(2,1)}), bf16[128,512]{1,0:T(8,128)(2,1)}) %reduce-scatter.18.cloned.1.call-update) | async-done | bytes 131088 | tf_op jit(solution)/shard_map/reduce_scatter | solution.py:194
  654.8 7.8 convolution_convert_fusion.2
  662.7 74.3 %reduce-scatter.22.cloned.1.call-done = bf16[128,1536]{1,0:T(8,128)(2,1)} async-done(((bf16[2048,1536]{1,0:T(8,128)(2,1)}), bf16[128,1536]{1,0:T(8,128)(2,1)}) %reduce-scatter.22.cloned.1.call-update) | async-done | bytes 393232 | tf_op jit(solution)/shard_map/reduce_scatter | solution.py:194
  738.8 5.4 all-to-all-start.5
  752.2 6.5 all_to_all.31
  758.7 4.5 all-to-all-start.4
  766.9 14.9 %all-to-all-done.4 = bf16[8,4,32,512]{3,2,1,0:T(8,128)(2,1)} async-done(((bf16[8,4,32,512]{3,2,1,0:T(8,128)(2,1)}), bf16[8,4,32,512]{3,2,1,0:T(8,128)(2,1)}, u32[]{:S(2)}, u32[]{:S(2)}) %all-to-all-start.4) | async-done | bytes 1048608 | tf_op jit(solution)/shard_map/all_to_all | solution.py:198
  785.4 21.7 %all-gather.37.cloned.1.call-done = bf16[1024,1536]{1,0:T(8,128)(2,1)} async-done(((bf16[128,1536]{1,0:T(8,128)(2,1)}), bf16[1024,1536]{1,0:T(8,128)(2,1)}) %all-gather.37.cloned.1.call-update) | async-done | bytes 3145744 | tf_op jit(solution)/shard_map/all_gather | solution.py:190
  809.9 4.6 all_to_all.32
  818.8 17.1 %pad_maximum_fusion.2 = bf16[4,491520]{1,0:T(4,128)(2,1)} fusion(bf16[4,131072]{1,0:T(4,128)(2,1)} %bitcast.171, bf16[4,98304]{1,0:T(4,128)(2,1)} %reshape.345, bf16[4,262144]{1,0:T(4,128)(2,1)S(1)} %bitcast.170), kind=kLoop, calls=%fused_computation.32 | loop fusion | flops 11796480 | bytes 7864320 | tf_op jit(solution)/shard_map/concatenate | solution.py:395
  838.7 8.0 convolution_convert_fusion.1
  846.8 38.0 %reduce-scatter.20.cloned.1.call-done = bf16[48,2048]{1,0:T(8,128)(2,1)} async-done(((bf16[768,2048]{1,0:T(8,128)(2,1)}), bf16[48,2048]{1,0:T(8,128)(2,1)}) %reduce-scatter.20.cloned.1.call-update) | async-done | bytes 196624 | tf_op jit(solution)/shard_map/reduce_scatter | solution.py:194
  884.8 11.6 all-gather.2
  900.5 14.2 %all-gather.41.cloned.1.call-done = bf16[8,2,64,768]{3,2,1,0:T(8,128)(2,1)} async-done(((bf16[2,2,64,768]{3,2,1,0:T(8,128)(2,1)}), bf16[8,2,64,768]{3,2,1,0:T(8,128)(2,1)}) %all-gather.41.cloned.1.call-update) | async-done | bytes 1572880 | tf_op jit(solution)/shard_map/all_gather | solution.py:190
  947.3 5.2 fusion.63
  952.7 123.7 %all-reduce.3 = f32[32,160]{1,0:T(8,128)S(1)} all-reduce(f32[32,160]{1,0:T(8,128)S(1)} %pad_maximum_fusion.8), channel_id=10, replica_groups=mesh['x'=4,'y'=4,'z'=4,'c'=2] {'y','z','c'}, use_global_device_ids=true, to_apply=%region_17.18.clone | all-reduce | flops 5120 | bytes 40960
  1077.1 7.4 psum.14
  1085.0 5.7 constant_dynamic-slice_fusion.1
  1094.5 54.0 %all-reduce.8.cloned.1.call-done = bf16[1,491520]{1,0:T(2,128)(2,1)} async-done(((bf16[1,491520]{1,0:T(2,128)(2,1)}), bf16[1,491520]{1,0:T(2,128)(2,1)}) %all-reduce.8.cloned.1.call-update) | async-done | bytes 983056 | tf_op jit(solution)/shard_map/psum | solution.py:396
  1152.2 10.8 slice_reduce_fusion
  (316 shorter events, 163.2 us)
Async XLA Ops:
  8.0 198.7 %copy-start = (bf16[176,2048]{1,0:T(8,128)(2,1)S(1)}, bf16[176,2048]{1,0:T(8,128)(2,1)}, u32[]{:S(2)}) copy-start(bf16[176,2048]{1,0:T(8,128)(2,1)} %param.27) | copy-start | bytes 2162692
  8.0 60.2 %copy-start.6 = (bf16[128,2048]{1,0:T(8,128)(2,1)S(1)}, bf16[128,2048]{1,0:T(8,128)(2,1)}, u32[]{:S(2)}) copy-start(bf16[128,2048]{1,0:T(8,128)(2,1)} %param.14) | copy-start | bytes 1572868
  8.0 57.5 %all-gather.17.cloned.1.call-start = ((), (), s32[]{:S(2)}) async-start(), calls=%async_computation.13 | async-start | bytes 7028736 | tf_op jit(solution)/shard_map/all_gather | solution.py:190
  13.1 12.5 %all-to-all-start = ((bf16[8,32,512]{2,1,0:T(8,128)(2,1)}), bf16[8,32,512]{2,1,0:T(8,128)(2,1)S(1)}, u32[]{:S(2)}, u32[]{:S(2)}) async-start(bf16[8,32,512]{2,1,0:T(8,128)(2,1)} %copy.169), calls=%async_computation | async-start | bytes 524288 | tf_op jit(solution)/shard_map/all_to_all | solution.py:198
  19.1 70.5 %all-gather.39.cloned.1.call-start = ((), (), s32[]{:S(2)}) async-start(), calls=%async_computation.31 | async-start | bytes 1310720 | tf_op jit(solution)/shard_map/all_gather | solution.py:190
  20.4 52.1 %copy-start.38 = (f32[128]{0:T(128)}, f32[128]{0:T(128)S(1)}, u32[]{:S(2)}) copy-start(f32[128]{0:T(128)S(1)} %add_rsqrt_fusion.2) | copy-start | bytes 1540
  26.4 92.3 %all-gather.19.cloned.1.call-start = ((), (), s32[]{:S(2)}) async-start(), calls=%async_computation.14 | async-start | bytes 2359296 | tf_op jit(solution)/shard_map/all_gather | solution.py:190
  68.1 381.6 %copy-start.32 = (f32[2048]{0:T(1024)}, f32[2048]{0:T(1024)S(1)}, u32[]{:S(2)}) copy-start(f32[2048]{0:T(1024)S(1)} %get-tuple-element.29) | copy-start | bytes 24580
  72.5 49.3 %copy-start.11 = (f32[128,1536]{1,0:T(8,128)}, f32[128,1536]{1,0:T(8,128)S(1)}, u32[]{:S(2)}) copy-start(f32[128,1536]{1,0:T(8,128)S(1)} %fusion.16) | copy-start | bytes 2359300
  73.5 94.0 %all-gather.21.cloned.1.call-start = ((), (), s32[]{:S(2)}) async-start(), calls=%async_computation.15 | async-start | bytes 4325376 | tf_op jit(solution)/shard_map/all_gather | solution.py:190
  76.2 124.5 %all-gather.23.cloned.1.call-start = ((), (), s32[]{:S(2)}) async-start(), calls=%async_computation.16 | async-start | bytes 4718592 | tf_op jit(solution)/shard_map/all_gather | solution.py:190
  76.8 169.5 %reduce-scatter.10.cloned.1.call-start = ((), (), s32[]{:S(2)}) async-start(), calls=%async_computation.17 | async-start | bytes 4718592 | tf_op jit(solution)/shard_map/reduce_scatter | solution.py:194
  79.7 42.1 %copy-start.16 = (f32[1024,128]{0,1:T(8,128)}, f32[1024,128]{0,1:T(8,128)S(1)}, u32[]{:S(2)}) copy-start(f32[1024,128]{0,1:T(8,128)S(1)} %get-tuple-element.71) | copy-start | bytes 1572868
  79.7 42.1 %copy-start.18 = (f32[1024,128]{0,1:T(8,128)}, f32[1024,128]{0,1:T(8,128)S(1)}, u32[]{:S(2)}) copy-start(f32[1024,128]{0,1:T(8,128)S(1)} %get-tuple-element.72) | copy-start | bytes 1572868
  172.7 24.6 %copy-start.2 = (bf16[4096,256]{1,0:T(8,128)(2,1)}, bf16[4096,256]{1,0:T(8,128)(2,1)S(1)}, u32[]{:S(2)}) copy-start(bf16[4096,256]{1,0:T(8,128)(2,1)S(1)} %get-tuple-element.40.k_ref) | copy-start | bytes 6291460
  206.7 55.5 %all-gather.29.cloned.1.call-start = ((), (), s32[]{:S(2)}) async-start(), calls=%async_computation.20 | async-start | bytes 3342336 | tf_op jit(solution)/shard_map/all_gather | solution.py:190
  207.5 87.7 %all-gather.31.cloned.1.call-start = ((), (), s32[]{:S(2)}) async-start(), calls=%async_computation.22 | async-start | bytes 4718592 | tf_op jit(solution)/shard_map/all_gather | solution.py:190
  208.1 150.1 %all-gather.27.cloned.1.call-start = ((), (), s32[]{:S(2)}) async-start(), calls=%async_computation.19 | async-start | bytes 6684672 | tf_op jit(solution)/shard_map/all_gather | solution.py:190
  218.3 174.3 %all-gather.25.cloned.1.call-start = ((), (), s32[]{:S(2)}) async-start(), calls=%async_computation.18 | async-start | bytes 4718592 | tf_op jit(solution)/shard_map/all_gather | solution.py:190
  247.6 202.1 %copy-start.36 = (f32[128]{0:T(128)}, f32[128]{0:T(128)S(1)}, u32[]{:S(2)}) copy-start(f32[128]{0:T(128)S(1)} %add_rsqrt_fusion) | copy-start | bytes 1540
  249.7 198.6 %reduce-scatter.14.cloned.1.call-start = ((), (), s32[]{:S(2)}) async-start(), calls=%async_computation.23 | async-start | bytes 4718592 | tf_op jit(solution)/shard_map/reduce_scatter | solution.py:194
  413.9 34.4 %copy-start.8 = (bf16[128,2048]{1,0:T(8,128)(2,1)S(1)}, bf16[128,2048]{1,0:T(8,128)(2,1)}, u32[]{:S(2)}) copy-start(bf16[128,2048]{1,0:T(8,128)(2,1)} %reduce-scatter.10.cloned.1.call-done) | copy-start | bytes 1572868
  413.9 35.8 %copy-start.13 = (bf16[128,2048]{1,0:T(8,128)(2,1)S(1)}, bf16[128,2048]{1,0:T(8,128)(2,1)}, u32[]{:S(2)}) copy-start(bf16[128,2048]{1,0:T(8,128)(2,1)} %param.15) | copy-start | bytes 1572868
  413.9 72.8 %all-gather.33.cloned.1.call-start = ((), (), s32[]{:S(2)}) async-start(), calls=%async_computation.24 | async-start | bytes 4718592 | tf_op jit(solution)/shard_map/all_gather | solution.py:190
  449.7 42.3 %copy-start.40 = (f32[128]{0:T(128)}, f32[128]{0:T(128)S(1)}, u32[]{:S(2)}) copy-start(f32[128]{0:T(128)S(1)} %broadcast_multiply_fusion.2) | copy-start | bytes 1540
  452.1 113.9 %reduce-scatter.16.cloned.1.call-start = ((), (), s32[]{:S(2)}) async-start(), calls=%async_computation.25 | async-start | bytes 2359296 | tf_op jit(solution)/shard_map/reduce_scatter | solution.py:194
  528.1 123.8 %reduce-scatter.18.cloned.1.call-start = ((), (), s32[]{:S(2)}) async-start(), calls=%async_computation.26 | async-start | bytes 4325376 | tf_op jit(solution)/shard_map/reduce_scatter | solution.py:194
  534.2 202.8 %reduce-scatter.22.cloned.1.call-start = ((), (), s32[]{:S(2)}) async-start(), calls=%async_computation.33 | async-start | bytes 6684672 | tf_op jit(solution)/shard_map/reduce_scatter | solution.py:194
  556.9 228.5 %all-gather.35.cloned.1.call-start = ((), (), s32[]{:S(2)}) async-start(), calls=%async_computation.27 | async-start | bytes 4718592 | tf_op jit(solution)/shard_map/all_gather | solution.py:190
  557.6 249.5 %all-gather.37.cloned.1.call-start = ((), (), s32[]{:S(2)}) async-start(), calls=%async_computation.28 | async-start | bytes 3538944 | tf_op jit(solution)/shard_map/all_gather | solution.py:190
  568.3 94.4 %copy-start.25 = (bf16[128,1024]{1,0:T(8,128)(2,1)}, bf16[128,1024]{1,0:T(8,128)(2,1)S(1)}, u32[]{:S(2)}) copy-start(bf16[128,1024]{1,0:T(8,128)(2,1)S(1)} %fusion.74) | copy-start | bytes 786436
  654.8 230.0 %reduce-scatter.20.cloned.1.call-start = ((), (), s32[]{:S(2)}) async-start(), calls=%async_computation.30 | async-start | bytes 3342336 | tf_op jit(solution)/shard_map/reduce_scatter | solution.py:194
  662.6 81.5 %copy-start.28 = (bf16[1024,2,256]{0,2,1:T(8,128)(2,1)S(1)}, bf16[1024,2,256]{0,2,1:T(8,128)(2,1)}, u32[]{:S(2)}) copy-start(bf16[1024,2,256]{0,2,1:T(8,128)(2,1)} %copy-done.27) | copy-start | bytes 3145732
  738.8 13.4 %all-to-all-start.5 = ((bf16[2,2,64,768]{3,1,2,0:T(2,128)(2,1)}), bf16[2,2,64,768]{3,1,2,0:T(2,128)(2,1)S(1)}, u32[]{:S(2)}, u32[]{:S(2)}) async-start(bf16[2,2,64,768]{3,1,2,0:T(2,128)(2,1)} %bitcast.35), calls=%async_computation.10 | async-start | bytes 786432 | tf_op jit(solution)/shard_map/all_to_all | solution.py:198
  758.7 23.1 %all-to-all-start.4 = ((bf16[8,4,32,512]{3,2,1,0:T(8,128)(2,1)}), bf16[8,4,32,512]{3,2,1,0:T(8,128)(2,1)}, u32[]{:S(2)}, u32[]{:S(2)}) async-start(bf16[8,4,32,512]{3,2,1,0:T(8,128)(2,1)} %bitcast.174), calls=%async_computation.9 | async-start | bytes 2097152 | tf_op jit(solution)/shard_map/all_to_all | solution.py:198
  763.1 151.6 %all-gather.41.cloned.1.call-start = ((), (), s32[]{:S(2)}) async-start(), calls=%async_computation.32 | async-start | bytes 1966080 | tf_op jit(solution)/shard_map/all_gather | solution.py:190
  763.9 321.0 %all-reduce.10.cloned.1.call-start = ((), (), s32[]{:S(2)}) async-start(), calls=%async_computation.34 | async-start | bytes 7864320
  785.4 33.4 %copy-start.10 = (bf16[1,4,128,2048]{3,1,2,0:T(4,128)(2,1)S(1)}, bf16[1,4,128,2048]{3,1,2,0:T(4,128)(2,1)}, u32[]{:S(2)}) copy-start(bf16[1,4,128,2048]{3,1,2,0:T(4,128)(2,1)} %copy.210) | copy-start | bytes 6291460
  818.8 17.8 %copy-start.47 = (u32[128]{0:T(128)S(1)}, u32[128]{0:T(128)}, u32[]{:S(2)}) copy-start(u32[128]{0:T(128)} %constant.123) | copy-start | bytes 1540
  835.9 255.4 %reduce-scatter.12.cloned.1.call-start = ((), (), s32[]{:S(2)}) async-start(), calls=%async_computation.21 | async-start | bytes 4718592 | tf_op jit(solution)/shard_map/reduce_scatter | solution.py:194
  846.7 301.7 %all-reduce.8.cloned.1.call-start = ((), (), s32[]{:S(2)}) async-start(), calls=%async_computation.29 | async-start | bytes 3932160 | tf_op jit(solution)/shard_map/psum | solution.py:396
  952.5 138.9 %copy-start.9 = (bf16[128,2048]{1,0:T(8,128)(2,1)S(1)}, bf16[128,2048]{1,0:T(8,128)(2,1)}, u32[]{:S(2)}) copy-start(bf16[128,2048]{1,0:T(8,128)(2,1)} %reduce-scatter.10.cloned.1.call-done) | copy-start | bytes 1572868
  952.5 138.9 %copy-start.14 = (bf16[128,2048]{1,0:T(8,128)(2,1)S(1)}, bf16[128,2048]{1,0:T(8,128)(2,1)}, u32[]{:S(2)}) copy-start(bf16[128,2048]{1,0:T(8,128)(2,1)} %param.15) | copy-start | bytes 1572868
  952.5 138.9 %copy-start.15 = (bf16[128,2048]{1,0:T(8,128)(2,1)S(1)}, bf16[128,2048]{1,0:T(8,128)(2,1)}, u32[]{:S(2)}) copy-start(bf16[128,2048]{1,0:T(8,128)(2,1)} %reduce-scatter.14.cloned.1.call-done) | copy-start | bytes 1572868
  952.5 138.9 %copy-start.33 = (f32[2048]{0:T(1024)S(1)}, f32[2048]{0:T(1024)}, u32[]{:S(2)}) copy-start(f32[2048]{0:T(1024)} %copy-done.32) | copy-start | bytes 24580
  952.5 138.8 %copy-start.37 = (f32[128]{0:T(128)S(1)}, f32[128]{0:T(128)}, u32[]{:S(2)}) copy-start(f32[128]{0:T(128)} %copy-done.36) | copy-start | bytes 1540
  952.5 138.8 %copy-start.41 = (f32[128]{0:T(128)S(1)}, f32[128]{0:T(128)}, u32[]{:S(2)}) copy-start(f32[128]{0:T(128)} %copy-done.40) | copy-start | bytes 1540
  1148.5 20.4 %copy-start.1 = (bf16[176,2048]{1,0:T(8,128)(2,1)S(1)}, bf16[176,2048]{1,0:T(8,128)(2,1)}, u32[]{:S(2)}) copy-start(bf16[176,2048]{1,0:T(8,128)(2,1)} %param.27) | copy-start | bytes 2162692
  (30 other events, 120.2 us)
Sparse Core Ops, SparseCore 0:
  11.7 53.8 all-gather.16
  67.8 21.7 all-gather.38
  91.9 26.7 all-gather.18
  120.8 46.6 all-gather.20
  169.1 31.5 all-gather.22
  206.8 39.4 reduce-scatter.9
  452.2 34.4 all-gather.32
  528.2 37.6 reduce-scatter.15
  569.6 82.2 reduce-scatter.17
  655.5 81.3 reduce-scatter.21
  739.3 37.4 all-gather.34
  779.1 27.9 all-gather.36
  810.8 73.9 reduce-scatter.19
  887.0 27.6 all-gather.40
  917.0 88.8 all-reduce.9
  1008.4 35.0 reduce-scatter.11
  1090.8 57.5 all-reduce.7
Sparse Core Ops, SparseCore 1:
  209.9 52.2 all-gather.28
  263.7 31.4 all-gather.30
  297.3 60.9 all-gather.26
  360.5 32.0 all-gather.24
  414.0 34.2 reduce-scatter.13

commit v2 on v1

--- a/solution.py
+++ b/solution.py
@@ -55,6 +55,12 @@
     return jnp.cos(angle), jnp.sin(angle)
 
 
+def tables_across(position):
+    freq = jnp.exp(jnp.arange(HALF, dtype=F32) * (-math.log(10000.0) / HALF))
+    angle = position.astype(F32)[..., None, :] * freq[:, None]
+    return jnp.cos(angle), jnp.sin(angle)
+
+
 def rotate(values, cosine, sine):
     lower, upper = values[..., :HALF], values[..., HALF:]
     return jnp.concatenate([lower * cosine - upper * sine, upper * cosine + lower * sine], axis=-1)
@@ -65,25 +71,48 @@
     return jnp.concatenate([lower * cosine + upper * sine, upper * cosine - lower * sine], axis=-1)
 
 
-def attend_kernel(q_ref, k_ref, vt_ref, begin_ref, slot_ref, out_ref, lse_ref, peak, total, accum):
+def turned(source, target, count, columns):
+    @pl.loop(0, count)
+    def _(block):
+        at = pl.ds(pl.multiple_of(block * BLOCK, BLOCK), BLOCK)
+        target[:, at] = source[at, columns].T
+
+
+KEYS, VALUES = slice(0, SIZE), slice(SIZE, 2 * SIZE)
+
+
+def attend_kernel(
+    q_ref, kv_ref, begin_ref, slot_ref, live_ref, cos_ref, sin_ref,
+    out_ref, qt_ref, lse_ref, vt, peak, total, accum,
+):
     depth = lax.axis_index("z")
     segments = slot_ref.shape[0]
     rows = slot_ref.shape[2]
     tokens = rows // 2
+    turned(kv_ref, vt, segments * (segments - 1) + depth + 1, VALUES)
     for seg in range(segments):
-        query = q_ref[pl.ds(seg * tokens, tokens), :]
-        query = jnp.concatenate([query[:, :SIZE], query[:, SIZE:]], axis=0).T
+        here = pl.ds(seg * tokens, tokens)
+        cosine, sine = cos_ref[seg], sin_ref[seg]
+        for head in range(2):
+            raw = q_ref[here, head * SIZE : (head + 1) * SIZE].T
+            lower, upper = raw[:HALF], raw[HALF:]
+            turn = jnp.concatenate(
+                [lower * cosine - upper * sine, upper * cosine + lower * sine], axis=0
+            )
+            qt_ref[seg, :, head * tokens : (head + 1) * tokens] = (
+                turn.astype(BF) * (SIZE ** -0.5)
+            ).astype(BF)
+        query = qt_ref[seg]
         begin = begin_ref[seg]
         slot = slot_ref[seg]
         peak[...] = jnp.full_like(peak, MASKED)
         total[...] = jnp.zeros_like(total)
         accum[...] = jnp.zeros_like(accum)
-        count = segments * seg + depth + 1
-
-        @pl.loop(0, count)
+
+        @pl.loop(0, segments * seg + depth + 1)
         def _(block):
             at = pl.multiple_of(block * BLOCK, BLOCK)
-            scores = dot(k_ref[pl.ds(at, BLOCK), :], query)
+            scores = dot(kv_ref[pl.ds(at, BLOCK), KEYS], query)
             key = lax.broadcasted_iota(jnp.int32, scores.shape, 0) + at
             scores = jnp.where((key >= begin) & (key <= slot), scores, MASKED)
             before = peak[...]
@@ -92,45 +121,48 @@
             shrink = jnp.exp(before - now)
             peak[...] = now
             total[...] = total[...] * shrink + jnp.sum(weights, axis=0, keepdims=True)
-            accum[...] = accum[...] * shrink + dot(vt_ref[:, pl.ds(at, BLOCK)], weights.astype(BF))
+            accum[...] = accum[...] * shrink + dot(vt[:, pl.ds(at, BLOCK)], weights.astype(BF))
 
         lse_ref[seg] = peak[...] + jnp.log(total[...])
-        result = (accum[...] / total[...]).T
-        out_ref[pl.ds(seg * tokens, tokens), :] = jnp.concatenate(
-            [result[:tokens], result[tokens:]], axis=1
-        )
-
-
-def attend(q, k, vt, begin, slot):
+        result = accum[...] * (live_ref[seg] / total[...])
+        for head in range(2):
+            out_ref[here, head * SIZE : (head + 1) * SIZE] = (
+                result[:, head * tokens : (head + 1) * tokens].T.astype(BF)
+            )
+
+
+def attend(q, kv, begin, slot, live, cosine, sine):
     segments, _, rows = slot.shape
     return pl.pallas_call(
         attend_kernel,
         name="attend",
         out_shape=(
-            jax.ShapeDtypeStruct(q.shape, F32),
+            jax.ShapeDtypeStruct(q.shape, BF),
+            jax.ShapeDtypeStruct((segments, SIZE, rows), BF),
             jax.ShapeDtypeStruct((segments, 1, rows), F32),
         ),
-        in_specs=[pl.BlockSpec(memory_space=pltpu.VMEM)] * 5,
-        out_specs=[pl.BlockSpec(memory_space=pltpu.VMEM)] * 2,
+        in_specs=[pl.BlockSpec(memory_space=pltpu.VMEM)] * 7,
+        out_specs=[pl.BlockSpec(memory_space=pltpu.VMEM)] * 3,
         scratch_shapes=[
+            pltpu.VMEM((SIZE, kv.shape[0]), BF),
             pltpu.VMEM((1, rows), F32),
             pltpu.VMEM((1, rows), F32),
             pltpu.VMEM((SIZE, rows), F32),
         ],
         compiler_params=pltpu.CompilerParams(vmem_limit_bytes=48 << 20),
-    )(q, k, vt, begin, slot)
+    )(q, kv, begin, slot, live, cosine, sine)
 
 
 def attend_back_kernel(
-    q_ref, do_ref, o_ref, k_ref, kt_ref, v_ref, begin_ref, slot_ref, lse_ref,
-    dq_ref, dk_ref, dv_ref, accum,
+    qt_ref, do_ref, o_ref, kv_ref, begin_ref, slot_ref, lse_ref, cos_ref, sin_ref,
+    dq_ref, dkv_ref, kt, sums, accum,
 ):
     depth = lax.axis_index("z")
     segments = slot_ref.shape[0]
     rows = slot_ref.shape[2]
     tokens = rows // 2
-    dk_ref[...] = jnp.zeros_like(dk_ref)
-    dv_ref[...] = jnp.zeros_like(dv_ref)
+    sums[...] = jnp.zeros_like(sums)
+    turned(kv_ref, kt, segments * (segments - 1) + depth + 1, KEYS)
     for seg in range(segments):
         here = pl.ds(seg * tokens, tokens)
 
@@ -138,9 +170,9 @@
             value = ref[here, :]
             return jnp.concatenate([value[:, :SIZE], value[:, SIZE:]], axis=0)
 
-        query = stacked(q_ref)
+        query_t = qt_ref[seg]
+        query = query_t.T
         grad = stacked(do_ref)
-        query_t = query.T
         grad_t = grad.T
         delta = jnp.sum(
             grad_t.astype(F32) * stacked(o_ref).T.astype(F32), axis=0, keepdims=True
@@ -149,41 +181,599 @@
         slot = slot_ref[seg]
         lse = lse_ref[seg]
         accum[...] = jnp.zeros_like(accum)
-        count = segments * seg + depth + 1
-
-        @pl.loop(0, count)
+
+        @pl.loop(0, segments * seg + depth + 1)
         def _(block):
             at = pl.multiple_of(block * BLOCK, BLOCK)
             keys = pl.ds(at, BLOCK)
-            scores = dot(k_ref[keys, :], query_t)
+            scores = dot(kv_ref[keys, KEYS], query_t)
             key = lax.broadcasted_iota(jnp.int32, scores.shape, 0) + at
             allowed = (key >= begin) & (key <= slot)
             probs = jnp.where(allowed, jnp.exp(scores - lse), 0.0)
-            grad_probs = dot(v_ref[keys, :], grad_t)
+            grad_probs = dot(kv_ref[keys, VALUES], grad_t)
             grad_scores = (probs * (grad_probs - delta)).astype(BF)
-            dv_ref[keys, :] += dot(probs.astype(BF), grad)
-            dk_ref[keys, :] += dot(grad_scores, query)
-            accum[...] += dot(kt_ref[:, keys], grad_scores)
-
-        result = accum[...].T * (SIZE ** -0.5)
-        dq_ref[here, :] = jnp.concatenate([result[:tokens], result[tokens:]], axis=1)
-
-
-def attend_back(q, do, o, k, kt, v, begin, slot, lse):
+            sums[keys, VALUES] += dot(probs.astype(BF), grad)
+            sums[keys, KEYS] += dot(grad_scores, query)
+            accum[...] += dot(kt[:, keys], grad_scores)
+
+        cosine, sine = cos_ref[seg], sin_ref[seg]
+        for head in range(2):
+            part = accum[:, head * tokens : (head + 1) * tokens] * (SIZE ** -0.5)
+            lower, upper = part[:HALF], part[HALF:]
+            turn = jnp.concatenate(
+                [lower * cosine + upper * sine, upper * cosine - lower * sine], axis=0
+            )
+            dq_ref[here, head * SIZE : (head + 1) * SIZE] = turn.T.astype(BF)
+
+    dkv_ref[...] = sums[...].astype(BF)
+
+
+def attend_back(qt, do, o, kv, begin, slot, lse, cosine, sine):
     segments, _, rows = slot.shape
     return pl.pallas_call(
         attend_back_kernel,
         name="attend_back",
         out_shape=(
-            jax.ShapeDtypeStruct(q.shape, F32),
-            jax.ShapeDtypeStruct(k.shape, F32),
-            jax.ShapeDtypeStruct(k.shape, F32),
+            jax.ShapeDtypeStruct(do.shape, BF),
+            jax.ShapeDtypeStruct(kv.shape, BF),
         ),
         in_specs=[pl.BlockSpec(memory_space=pltpu.VMEM)] * 9,
-        out_specs=[pl.BlockSpec(memory_space=pltpu.VMEM)] * 3,
-        scratch_shapes=[pltpu.VMEM((SIZE, rows), F32)],
+        out_specs=[pl.BlockSpec(memory_space=pltpu.VMEM)] * 2,
+        scratch_shapes=[
+            pltpu.VMEM((SIZE, kv.shape[0]), BF),
+            pltpu.VMEM(kv.shape, F32),
+            pltpu.VMEM((SIZE, rows), F32),
+        ],
         compiler_params=pltpu.CompilerParams(vmem_limit_bytes=48 << 20),
-    )(q, do, o, k, kt, v, begin, slot, lse)
+    )(qt, do, o, kv, begin, slot, lse, cosine, sine)
+
+
+MESH_IDS = pl.DeviceIdType.MESH
+AXES = ("x", "y", "z", "c")
+ANYWHERE = pl.BlockSpec(memory_space=pl.ANY)
+IN_VMEM = pl.BlockSpec(memory_space=pltpu.VMEM)
+
+
+def place():
+    return {a: lax.axis_index(a) for a in AXES}
+
+
+def along(axis, step):
+    size = lax.axis_size(axis)
+    return lax.rem(lax.axis_index(axis) + (step + size), size)
+
+
+def device(axis, step):
+    here = place()
+    here[axis] = along(axis, step)
+    return tuple(here[a] for a in AXES)
+
+
+class Net:
+    def __init__(self, sends, arrivals, locals_):
+        self.sends, self.arrivals, self.locals_ = sends, arrivals, locals_
+        self.used = 0
+        self.near = 0
+        self.open = []
+
+    def send(self, source, target, axis, step):
+        copy = pltpu.make_async_remote_copy(
+            src_ref=source, dst_ref=target, send_sem=self.sends.at[self.used],
+            recv_sem=self.arrivals.at[self.used], device_id=device(axis, step),
+            device_id_type=MESH_IDS,
+        )
+        copy.start()
+        self.used += 1
+        self.open.append(copy)
+        return copy
+
+    def keep(self, source, target):
+        copy = pltpu.make_async_copy(source, target, self.locals_.at[self.near])
+        copy.start()
+        self.near += 1
+        return copy
+
+    def close(self):
+        for copy in self.open:
+            copy.wait_send()
+
+
+def greet(partners):
+    barrier = pltpu.get_barrier_semaphore()
+    for axis, step in partners:
+        pl.semaphore_signal(barrier, 1, device_id=device(axis, step), device_id_type=MESH_IDS)
+    pl.semaphore_wait(barrier, len(partners))
+
+
+def semaphores(sends, locals_):
+    return [
+        pltpu.SemaphoreType.DMA((sends,)),
+        pltpu.SemaphoreType.DMA((sends,)),
+        pltpu.SemaphoreType.DMA((max(locals_, 1),)),
+    ]
+
+
+def comm_call(body, name, number, outs, ins, scratch, sends, locals_, spaces, out_spaces):
+    return pl.pallas_call(
+        body,
+        name=name,
+        out_shape=outs,
+        in_specs=spaces,
+        out_specs=out_spaces,
+        scratch_shapes=list(scratch) + semaphores(sends, locals_),
+        compiler_params=pltpu.CompilerParams(
+            collective_id=number, has_side_effects=True, vmem_limit_bytes=56 << 20
+        ),
+    )(*ins)
+
+
+LINE = (1, 2, 3)
+
+
+class RowGather:
+    def __init__(self, net, value, out):
+        self.net, self.out = net, out
+        h = value.shape[0] // 2
+        self.parts = (pl.ds(0, h), pl.ds(h, h))
+        y, z, c = (lax.axis_index(a) for a in ROW)
+        self.mine = net.keep(value, out.at[y, z, c])
+        self.own = net.send(value, out.at[y, z, c], "c", 1)
+        self.first = [
+            [net.send(value.at[part], out.at[y, z, c, part], axis, d) for d in LINE]
+            for part, axis in zip(self.parts, ("z", "y"))
+        ]
+
+    def spread(self):
+        net, out = self.net, self.out
+        y, z, c = (lax.axis_index(a) for a in ROW)
+        self.mine.wait()
+        (a, b) = self.parts
+        for copy in self.first[0]:
+            copy.wait_recv()
+        self.second = [
+            [net.send(out.at[y, :, c, a], out.at[y, :, c, a], "y", d) for d in LINE]
+        ]
+        for copy in self.first[1]:
+            copy.wait_recv()
+        self.second.append(
+            [net.send(out.at[:, z, c, b], out.at[:, z, c, b], "z", d) for d in LINE]
+        )
+        self.shared = [self.own]
+        for d in LINE:
+            spot = out.at[y, along("z", -d), c, a]
+            self.shared.append(net.send(spot, spot, "c", 1))
+            spot = out.at[along("y", -d), z, c, b]
+            self.shared.append(net.send(spot, spot, "c", 1))
+
+    def finish(self):
+        net, out = self.net, self.out
+        y, z, c = (lax.axis_index(a) for a in ROW)
+        (a, b) = self.parts
+        for d in LINE:
+            self.second[0][d - 1].wait_recv()
+            spot = out.at[along("y", -d), :, c, a]
+            self.shared.append(net.send(spot, spot, "c", 1))
+            self.second[1][d - 1].wait_recv()
+            spot = out.at[:, along("z", -d), c, b]
+            self.shared.append(net.send(spot, spot, "c", 1))
+        for copy in self.shared:
+            copy.wait_recv()
+
+
+class RingGather:
+    def __init__(self, net, value, out, axis):
+        self.net, self.out, self.axis = net, out, axis
+        a, c = lax.axis_index(axis), lax.axis_index("c")
+        h = value.shape[0] // 2
+        self.parts = one, two = pl.ds(0, h), pl.ds(h, h)
+        self.mine = net.keep(value, out.at[a, c])
+        self.right = [net.send(value.at[p], out.at[a, c, p], axis, 1) for p in (one, two)]
+        self.left = [net.send(value.at[p], out.at[a, c, p], axis, -1) for p in (two, one)]
+        self.shared = [net.send(value, out.at[a, c], "c", 1)]
+
+    def spread(self):
+        net, out, axis = self.net, self.out, self.axis
+        c = lax.axis_index("c")
+        one, two = self.parts
+        before, after = along(axis, -1), along(axis, 1)
+        self.right[0].wait_recv()
+        spot = out.at[before, c, one]
+        self.far = [net.send(spot, spot, axis, 1)]
+        self.left[0].wait_recv()
+        spot = out.at[after, c, two]
+        self.far.append(net.send(spot, spot, axis, -1))
+        for copies, where in ((self.right, before), (self.left, after)):
+            copies[1].wait_recv()
+            spot = out.at[where, c]
+            self.shared.append(net.send(spot, spot, "c", 1))
+
+    def finish(self):
+        for copy in self.far:
+            copy.wait_recv()
+        spot = self.out.at[along(self.axis, 2), lax.axis_index("c")]
+        self.shared.append(self.net.send(spot, spot, "c", 1))
+        for copy in self.shared:
+            copy.wait_recv()
+        self.mine.wait()
+
+
+STEP = 16
+
+
+def rows_loop(count, body):
+    pl.loop(0, count // STEP)(lambda i: body(pl.ds(pl.multiple_of(i * STEP, STEP), STEP)))
+
+
+def shifted(rows, first):
+    return pl.ds(pl.multiple_of(rows.start + first, STEP), STEP)
+
+
+class RingSum:
+    def __init__(self, net, value, out, axis, near, relay, come, go):
+        self.net, self.value, self.out, self.axis = net, value, out, axis
+        self.near, self.relay, self.come, self.go = near, relay, come, go
+        c = lax.axis_index("c")
+        self.size = value.shape[2]
+        h = self.size // 2
+        self.parts = pl.ds(0, h), pl.ds(h, h)
+        self.swaps = {
+            s: net.send(value.at[along(axis, s), 1 - c], near.at[s], "c", 1) for s in (2, 1, 3, 0)
+        }
+
+    def pair(self, s, part=None):
+        value, near, go = self.value, self.near, self.go
+        where, c = along(self.axis, s), lax.axis_index("c")
+        first = 0 if part is None else part.start
+        count = self.size if part is None else part.size
+
+        def add(rows):
+            at = shifted(rows, first)
+            go[s, at] = (
+                value[where, c, at].astype(F32) + near[s, at].astype(F32)
+            ).astype(BF)
+
+        rows_loop(count, add)
+
+    def relay_far(self):
+        net = self.net
+        one, two = self.parts
+        self.swaps[2].wait_recv()
+        self.pair(2)
+        self.relays = [
+            net.send(self.go.at[2, one], self.relay.at[0], self.axis, 1),
+            net.send(self.go.at[2, two], self.relay.at[1], self.axis, -1),
+        ]
+
+    def spread(self):
+        net, go, relay, come = self.net, self.go, self.relay, self.come
+        one, two = self.parts
+        self.swaps[1].wait_recv()
+        self.pair(1)
+        self.ends = [net.send(go.at[1, two], come.at[0, two], self.axis, 1)]
+        self.swaps[3].wait_recv()
+        self.pair(3)
+        self.ends.append(net.send(go.at[3, one], come.at[1, one], self.axis, -1))
+        for i, (s, part, step) in enumerate(((1, one, 1), (3, two, -1))):
+            self.relays[i].wait_recv()
+
+            def add(rows, i=i, s=s, part=part):
+                at = shifted(rows, part.start)
+                go[s, at] = (go[s, at].astype(F32) + relay[i, rows].astype(F32)).astype(BF)
+
+            rows_loop(part.size, add)
+            self.ends.append(net.send(go.at[s, part], come.at[i, part], self.axis, step))
+
+    def finish(self):
+        value, near, come, out = self.value, self.near, self.come, self.out
+        where, c = lax.axis_index(self.axis), lax.axis_index("c")
+        self.swaps[0].wait_recv()
+        for copy in self.ends:
+            copy.wait_recv()
+
+        def add(rows):
+            out[rows] = (
+                value[where, c, rows].astype(F32) + near[0, rows].astype(F32)
+            ) + (come[0, rows].astype(F32) + come[1, rows].astype(F32))
+
+        rows_loop(self.size, add)
+
+
+def ring_sum_scratch(size, width):
+    return [
+        pltpu.VMEM((4, size, width), BF),
+        pltpu.VMEM((2, size // 2, width), BF),
+        pltpu.VMEM((2, size, width), BF),
+        pltpu.VMEM((4, size, width), BF),
+    ]
+
+
+class RowSum:
+    def __init__(self, net, value, out, near, go, first, mid, last):
+        self.net, self.value, self.out = net, value, out
+        self.near, self.go, self.first, self.mid, self.last = near, go, first, mid, last
+        c = lax.axis_index("c")
+        self.size = value.shape[3]
+        h = self.size // 2
+        self.parts = pl.ds(0, h), pl.ds(h, h)
+        self.swaps = [
+            net.send(value.at[i, :, 1 - c], near.at[i], "c", 1) for i in range(4)
+        ]
+
+    def start(self):
+        net, value, near, go = self.net, self.value, self.near, self.go
+        c = lax.axis_index("c")
+        for i in range(4):
+            self.swaps[i].wait_recv()
+            for j in range(4):
+
+                def add(rows, i=i, j=j):
+                    go[i, j, rows] = (
+                        value[i, j, c, rows].astype(F32) + near[i, j, rows].astype(F32)
+                    ).astype(BF)
+
+                rows_loop(self.size, add)
+        a, b = self.parts
+        self.ones = [
+            [net.send(go.at[along("y", d), :, a], self.first.at[0, d - 1], "y", d) for d in LINE],
+            [net.send(go.at[:, along("z", d), b], self.first.at[1, d - 1], "z", d) for d in LINE],
+        ]
+
+    def turn(self):
+        net, go, first, mid = self.net, self.go, self.first, self.mid
+        y, z = lax.axis_index("y"), lax.axis_index("z")
+        self.twos = []
+        for k, axis in enumerate(("z", "y")):
+            for copy in self.ones[k]:
+                copy.wait_recv()
+            for j in range(4):
+
+                def add(rows, k=k, j=j):
+                    at = shifted(rows, self.parts[k].start)
+                    own = go[y, j, at] if k == 0 else go[j, z, at]
+                    mid[k, j, rows] = (
+                        own.astype(F32) + first[k, 0, j, rows].astype(F32)
+                        + (first[k, 1, j, rows].astype(F32) + first[k, 2, j, rows].astype(F32))
+                    ).astype(BF)
+
+                rows_loop(self.parts[k].size, add)
+            self.twos.append(
+                [net.send(mid.at[k, along(axis, d)], self.last.at[k, d - 1], axis, d) for d in LINE]
+            )
+
+    def finish(self):
+        mid, last, out = self.mid, self.last, self.out
+        for k, axis in enumerate(("z", "y")):
+            for copy in self.twos[k]:
+                copy.wait_recv()
+            here = lax.axis_index(axis)
+
+            def add(rows, k=k, here=here):
+                at = shifted(rows, self.parts[k].start)
+                out[at] = (
+                    mid[k, here, rows].astype(F32) + last[k, 0, rows].astype(F32)
+                    + (last[k, 1, rows].astype(F32) + last[k, 2, rows].astype(F32))
+                )
+
+            rows_loop(self.parts[k].size, add)
+
+
+def row_sum_scratch(size, width):
+    h = size // 2
+    return [
+        pltpu.VMEM((4, 4, size, width), BF),
+        pltpu.VMEM((4, 4, size, width), BF),
+        pltpu.VMEM((2, 3, 4, h, width), BF),
+        pltpu.VMEM((2, 4, h, width), BF),
+        pltpu.VMEM((2, 3, h, width), BF),
+    ]
+
+
+Y_LINE = [("y", d) for d in LINE]
+Z_LINE = [("z", d) for d in LINE]
+X_RING = [("x", 1), ("x", -1)]
+Y_RING = [("y", 1), ("y", -1)]
+TWIN = [("c", 1)]
+
+
+def shape(*dims, kind=BF):
+    return jax.ShapeDtypeStruct(dims, kind)
+
+
+def first_weights(first, up, both):
+    def body(first_ref, up_ref, both_ref, first_out, up_out, both_out, transit, sends, arrivals, locals_):
+        net = Net(sends, arrivals, locals_)
+        y, z, c = (lax.axis_index(a) for a in ROW)
+        greet(Y_LINE + Z_LINE + TWIN)
+        row = RowGather(net, first_ref, first_out)
+        up_mine = net.keep(up_ref.at[y], transit.at[y, z])
+        ups = [net.send(up_ref.at[along("y", d)], transit.at[y, z], "y", d) for d in LINE]
+        both_mine = net.keep(both_ref.at[c], both_out.at[c])
+        both_come = net.send(both_ref.at[1 - c], both_out.at[c], "c", 1)
+        row.spread()
+        up_mine.wait()
+        for copy in ups:
+            copy.wait_recv()
+        ups = [net.send(transit.at[:, z], transit.at[:, z], "z", d) for d in LINE]
+        row.finish()
+        for copy in ups:
+            copy.wait_recv()
+        up_keep = net.keep(transit.at[:, :, c], up_out.at[:, :, c])
+        up_come = net.send(transit.at[:, :, 1 - c], up_out.at[:, :, c], "c", 1)
+        both_mine.wait()
+        both_come.wait_recv()
+        up_keep.wait()
+        up_come.wait_recv()
+        net.close()
+
+    _, per, high, thin = up.shape
+    outs = (
+        shape(4, 4, 2, *first.shape), shape(4, 4, 2, high, thin), shape(*both.shape),
+        shape(4, 4, 2, high, thin),
+    )
+    return comm_call(
+        body, "first_weights", 1, outs, (first, up, both), [], 40, 4, [ANYWHERE] * 3, [ANYWHERE] * 4,
+    )[:3]
+
+
+def keys_and_latents(key_value, latent):
+    def body(kv_ref, lat_ref, kv_out, lat_out, sends, arrivals, locals_):
+        net = Net(sends, arrivals, locals_)
+        greet(Y_LINE + Z_LINE + TWIN)
+        row = RowGather(net, kv_ref, kv_out)
+        ring = RingGather(net, lat_ref, lat_out, "y")
+        row.spread()
+        ring.spread()
+        row.finish()
+        ring.finish()
+        net.close()
+
+    outs = (shape(4, 4, 2, *key_value.shape), shape(4, 2, *latent.shape))
+    return comm_call(
+        body, "keys_and_latents", 2, outs, (key_value, latent), [], 40, 2, [ANYWHERE] * 2, [ANYWHERE] * 2,
+    )
+
+
+def heads_sum_and_cotangent(partial, cotangent):
+    def body(part_ref, cot_ref, out_ref, cot_out, near, relay, come, go, sends, arrivals, locals_):
+        net = Net(sends, arrivals, locals_)
+        greet(X_RING + Y_RING + TWIN)
+        ring = RingSum(net, part_ref, out_ref, "y", near, relay, come, go)
+        feed = RingGather(net, cot_ref, cot_out, "x")
+        ring.relay_far()
+        ring.spread()
+        feed.spread()
+        ring.finish()
+        feed.finish()
+        net.close()
+
+    size, width = cotangent.shape
+    outs = (shape(size, width, kind=F32), shape(4, 2, size, width))
+    return comm_call(
+        body, "heads_sum_and_cotangent", 3, outs, (partial, cotangent), ring_sum_scratch(size, width), 20, 2,
+        [IN_VMEM, ANYWHERE], [IN_VMEM, ANYWHERE],
+    )
+
+
+def feed_gather(normed_two, normed):
+    def body(two_ref, one_ref, two_out, one_out, sends, arrivals, locals_):
+        net = Net(sends, arrivals, locals_)
+        y, c = lax.axis_index("y"), lax.axis_index("c")
+        tall = one_ref.shape[1] // 4
+        greet(X_RING + Y_LINE + TWIN)
+        feed = RingGather(net, two_ref, two_out, "x")
+        mine = net.keep(one_ref.at[:, pl.ds(pl.multiple_of(y * tall, tall), tall)], one_out.at[y, c])
+        ones = [
+            net.send(
+                one_ref.at[:, pl.ds(pl.multiple_of(along("y", d) * tall, tall), tall)],
+                one_out.at[y, c], "y", d,
+            )
+            for d in LINE
+        ]
+        feed.spread()
+        mine.wait()
+        spot = one_out.at[y, c]
+        shared = [net.send(spot, spot, "c", 1)]
+        for d in LINE:
+            ones[d - 1].wait_recv()
+            spot = one_out.at[along("y", -d), c]
+            shared.append(net.send(spot, spot, "c", 1))
+        feed.finish()
+        for copy in shared:
+            copy.wait_recv()
+        net.close()
+
+    size, width = normed_two.shape
+    outs = (shape(4, 2, size, width), shape(4, 2, size, width // 4))
+    return comm_call(
+        body, "feed_gather", 4, outs, (normed_two, normed), [], 20, 2, [ANYWHERE] * 2, [ANYWHERE] * 2,
+    )
+
+
+def feed_sum(partial, partial_two):
+    def body(one_ref, two_ref, one_out, two_out, *rest):
+        net = Net(*rest[8:])
+        greet(X_RING + TWIN)
+        one = RingSum(net, one_ref, one_out, "x", *rest[:4])
+        two = RingSum(net, two_ref, two_out, "x", *rest[4:8])
+        one.relay_far()
+        one.spread()
+        two.relay_far()
+        two.spread()
+        one.finish()
+        two.finish()
+        net.close()
+
+    _, _, size, width = partial.shape
+    outs = (shape(size, width, kind=F32),) * 2
+    return comm_call(
+        body, "feed_sum", 5, outs, (partial, partial_two), ring_sum_scratch(size, width) * 2, 24, 0,
+        [IN_VMEM] * 2, [IN_VMEM] * 2,
+    )
+
+
+def heads_gather(value):
+    def body(ref, out, sends, arrivals, locals_):
+        net = Net(sends, arrivals, locals_)
+        greet(Y_RING + TWIN)
+        ring = RingGather(net, ref, out, "y")
+        ring.spread()
+        ring.finish()
+        net.close()
+
+    return comm_call(
+        body, "heads_gather", 6, shape(4, 2, *value.shape), (value,), [], 12, 2, [ANYWHERE], ANYWHERE,
+    )
+
+
+def keys_and_latents_sum(grad_kv, partial):
+    def body(kv_ref, part_ref, kv_out, part_out, *rest):
+        net = Net(*rest[9:])
+        greet(Y_LINE + Z_LINE + TWIN)
+        row = RowSum(net, kv_ref, kv_out, *rest[:5])
+        ring = RingSum(net, part_ref, part_out, "y", *rest[5:9])
+        row.start()
+        ring.relay_far()
+        ring.spread()
+        row.turn()
+        ring.finish()
+        row.finish()
+        net.close()
+
+    _, _, _, size, thin = grad_kv.shape
+    width = partial.shape[3]
+    outs = (shape(size, thin, kind=F32), shape(size, width, kind=F32))
+    return comm_call(
+        body, "keys_and_latents_sum", 7, outs, (grad_kv, partial),
+        row_sum_scratch(size, thin) + ring_sum_scratch(size, width), 28, 0, [IN_VMEM] * 2, [IN_VMEM] * 2,
+    )
+
+
+def firsts_gather(value):
+    def body(ref, out, sends, arrivals, locals_):
+        net = Net(sends, arrivals, locals_)
+        y, c = lax.axis_index("y"), lax.axis_index("c")
+        greet(Y_RING + TWIN)
+        mine = net.keep(ref.at[c], out.at[y, c])
+        come = net.send(ref.at[1 - c], out.at[y, c], "c", 1)
+        mine.wait()
+        spot = out.at[y, c]
+        ahead = [net.send(spot, spot, "y", 1), net.send(spot, spot, "y", -1)]
+        come.wait_recv()
+        spot = out.at[y, 1 - c]
+        ahead += [net.send(spot, spot, "y", 1), net.send(spot, spot, "y", -1)]
+        ahead[0].wait_recv()
+        spot = out.at[along("y", -1), c]
+        ahead.append(net.send(spot, spot, "y", 1))
+        ahead[3].wait_recv()
+        spot = out.at[along("y", 1), 1 - c]
+        ahead.append(net.send(spot, spot, "y", -1))
+        for i in (1, 2, 4, 5):
+            ahead[i].wait_recv()
+        net.close()
+
+    return comm_call(
+        body, "firsts_gather", 8, shape(4, *value.shape), (value,), [], 12, 2, [ANYWHERE], ANYWHERE,
+    )
 
 
 def gather(value, axes):
@@ -220,9 +810,10 @@
         + jnp.arange(strip, dtype=jnp.int32)[None, :]
     ).reshape(-1)
     begin_group, live_group = places_of(lengths_row, slots_group)
-    cosine_group, sine_group = tables(slots_group - begin_group)
+    cosine_group, sine_group = tables_across((slots_group - begin_group).reshape(n_y, strip))
     begin_lanes = jnp.tile(begin_group.reshape(n_y, 1, strip), (1, 1, 2))
     slot_lanes = jnp.tile(slots_group.reshape(n_y, 1, strip), (1, 1, 2))
+    live_lanes = jnp.tile(live_group.reshape(n_y, 1, strip), (1, 1, 2))
 
     shard = norm_gain.shape[0]
     extra = jnp.stack(
@@ -232,22 +823,8 @@
     first = jnp.concatenate(
         [q_down, key_weight, value_weight, jnp.pad(extra, ((0, 0), (0, 125)))], axis=1
     )
-    first_full = gather(first, ROW)
-    extra_full = first_full[:, first_width : first_width + 3].astype(F32)
-    first_full = first_full[:, :first_width]
-    gain_one = extra_full[:, 0]
-    gain_two = extra_full[:, 1]
-    gain_latent = extra_full[:, 2].reshape(span, shard)[:, : q_gain.shape[0]].reshape(-1)
-
     per_heads = q_up.shape[1] // members
     q_rows = q_up.shape[0]
-    up_part = swap(q_up.reshape(q_rows, members, per_heads).transpose(1, 0, 2), HEADS)
-    up_heads = gather(up_part[None], "z")
-    up_heads = (
-        up_heads.reshape(n_z, n_y, n_c, q_rows, per_heads)
-        .transpose(1, 0, 2, 3, 4)
-        .reshape(span * q_rows, per_heads)
-    )
     out_chip = gather(out_weight, ("z", "c"))
     out_heads = lax.dynamic_slice_in_dim(out_chip, c * per_heads, per_heads)
 
@@ -269,10 +846,19 @@
         part = part.reshape(2, shard, n_c, -1).transpose(2, 1, 0, 3)
         return part.reshape(n_c, shard, -1)
 
-    both = jnp.stack([spread(gate_weight), spread(up_weight)], axis=1)
-    both = swap(both, "c")
-    units = both.shape[-1]
-    both = both.transpose(0, 2, 1, 3).reshape(n_c * shard, 2 * units)
+    both = jnp.concatenate([spread(gate_weight), spread(up_weight)], axis=2)
+    units = both.shape[-1] // 2
+    up_sent = q_up.reshape(q_rows, n_y, n_c, per_heads).transpose(1, 2, 0, 3)
+    first_full, up_heads, both = first_weights(first, up_sent, both)
+    first_full = first_full.reshape(span * shard, -1)
+    up_heads = up_heads.reshape(span * q_rows, per_heads)
+    both = both.reshape(n_c * shard, 2 * units)
+    extra_full = first_full[:, first_width : first_width + 3].astype(F32)
+    first_full = first_full[:, :first_width]
+    gain_one = extra_full[:, 0]
+    gain_two = extra_full[:, 1]
+    gain_latent = extra_full[:, 2].reshape(span, shard)[:, : q_gain.shape[0]].reshape(-1)
+
     both_full = gather(both, ("y", "z"))
     gate_use, up_use = both_full[:, :units], both_full[:, units:]
     down_part = lax.dynamic_slice_in_dim(down_weight, x * share, share)
@@ -288,22 +874,26 @@
     latent_normed = (latent * inverse_latent * gain_latent).astype(BF)
     key_mine = rotate(firsts[:, latent_width : latent_width + SIZE], cosine, sine).astype(BF)
     value_mine = firsts[:, latent_width + SIZE :].astype(BF)
-    key_value = gather(jnp.concatenate([key_mine, value_mine], axis=1), ROW)
-    keys, values = key_value[:, :SIZE], key_value[:, SIZE:]
-    latent_group = gather(latent_normed, HEADS)
-    group = latent_group.shape[0]
-    queries = rotate(
-        dot(latent_group, up_heads).reshape(group, 2, SIZE),
-        cosine_group[:, None, :], sine_group[:, None, :],
-    ).astype(BF) * (SIZE ** -0.5)
-    queries = queries.astype(BF).reshape(group, per_heads)
-    attended, lse = attend(queries, keys, values.T, begin_lanes, slot_lanes)
-    mixed = (attended * live_group[:, None]).astype(BF)
-    middle = inputs + scatter_sum(dot(mixed, out_heads).astype(BF), HEADS).astype(F32)
+    key_value, latent_group = keys_and_latents(
+        jnp.concatenate([key_mine, value_mine], axis=1), latent_normed
+    )
+    key_value = key_value.reshape(span * rows, 2 * SIZE)
+    group = members * rows
+    latent_group = latent_group.reshape(group, latent_width)
+    mixed, queries_t, lse = attend(
+        dot(latent_group, up_heads), key_value, begin_lanes, slot_lanes, live_lanes,
+        cosine_group, sine_group,
+    )
+    branch, grad_feed = heads_sum_and_cotangent(
+        dot(mixed, out_heads).astype(BF).reshape(n_y, n_c, rows, width), cotangent
+    )
+    grad_feed = grad_feed.reshape(group, width)
+    middle = inputs + branch
 
     inverse_two = lax.rsqrt(jnp.mean(middle * middle, axis=-1, keepdims=True) + EPSILON)
-    normed_two = gather((middle * inverse_two * gain_two).astype(BF), FEED)
-    grad_feed = gather(cotangent, FEED)
+    normed_two, normed_part = feed_gather((middle * inverse_two * gain_two).astype(BF), normed)
+    normed_two = normed_two.reshape(group, width)
+    normed_part = normed_part.reshape(group, -1)
     gate_pre = dot(normed_two, gate_use)
     up_pre = dot(normed_two, up_use)
     sigma = jax.nn.sigmoid(gate_pre)
@@ -311,10 +901,12 @@
     grad_hidden = dot_nt(grad_feed, down_use)
     grad_gate_pre = (grad_hidden * up_pre * sigma * (1.0 + gate_pre * (1.0 - sigma))).astype(BF)
     grad_up_pre = (grad_hidden * gate_pre * sigma).astype(BF)
-    grad_normed_two = scatter_sum(
-        (dot_nt(grad_gate_pre, gate_use) + dot_nt(grad_up_pre, up_use)).astype(BF), FEED
-    ).astype(F32)
-    branch_two = scatter_sum(dot(hidden, down_use).astype(BF), FEED).astype(F32)
+    grad_normed_two, branch_two = feed_sum(
+        (dot_nt(grad_gate_pre, gate_use) + dot_nt(grad_up_pre, up_use))
+        .astype(BF)
+        .reshape(n_x, n_c, rows, width),
+        dot(hidden, down_use).astype(BF).reshape(n_x, n_c, rows, width),
+    )
     output = (middle + branch_two).astype(BF)
     grad_result = cotangent.astype(F32)
     grad_mid_norm, grad_gain_two = norm_back(middle, inverse_two, gain_two, grad_normed_two)
@@ -344,28 +936,21 @@
     grad_up = collect(grad_both[:, :, 1])
     grad_down = grad_down[:, :share].reshape(down_rows, width).astype(F32)
 
-    grad_branch = gather(grad_middle.astype(BF), HEADS)
+    grad_branch = heads_gather(grad_middle.astype(BF)).reshape(group, width)
     grad_mixed = dot_nt(grad_branch, out_heads).astype(BF)
     grad_attended = grad_mixed * live_group[:, None].astype(BF)
     grad_out = dot_tn(mixed, grad_branch).astype(BF)
-    grad_queries, grad_keys, grad_values = attend_back(
-        queries, grad_attended, mixed, keys, keys.T, values, begin_lanes, slot_lanes, lse
-    )
-    grad_kv = scatter_sum(
-        jnp.concatenate([grad_keys, grad_values], axis=1).astype(BF), ROW
-    ).astype(F32)
-    grad_query_raw = (
-        unrotate(
-            grad_queries.reshape(group, 2, SIZE),
-            cosine_group[:, None, :], sine_group[:, None, :],
-        )
-        .reshape(group, per_heads)
-        .astype(BF)
+    grad_query_raw, grad_kv = attend_back(
+        queries_t, grad_attended, mixed, key_value, begin_lanes, slot_lanes, lse,
+        cosine_group, sine_group,
+    )
+    grad_kv, grad_latent_normed = keys_and_latents_sum(
+        grad_kv.reshape(n_y, n_z, n_c, rows, 2 * SIZE),
+        dot_nt(grad_query_raw, up_heads).astype(BF).reshape(n_y, n_c, rows, latent_width),
     )
     grad_key_raw = unrotate(grad_kv[:, :SIZE], cosine, sine).astype(BF)
     grad_value_raw = grad_kv[:, SIZE:].astype(BF)
     grad_up_heads = dot_tn(latent_group, grad_query_raw).astype(BF)
-    grad_latent_normed = scatter_sum(dot_nt(grad_query_raw, up_heads).astype(BF), HEADS).astype(F32)
     grad_latent_f, grad_gain_latent = norm_back(
         latent, inverse_latent, gain_latent, grad_latent_normed
     )
@@ -376,12 +961,10 @@
     grad_input_norm, grad_gain_one = norm_back(inputs, inverse_one, gain_one, grad_normed)
     input_grad = grad_middle + grad_input_norm
 
-    normed_group = gather(normed, HEADS)
-    tall = width // n_y
-    normed_part = lax.dynamic_slice_in_dim(normed_group, y * tall, tall, axis=1)
-    grad_firsts_group = gather(grad_firsts, HEADS)
     half_first = first_width // n_c
-    first_part = lax.dynamic_slice_in_dim(grad_firsts_group, c * half_first, half_first, axis=1)
+    first_part = firsts_gather(
+        grad_firsts.reshape(rows, n_c, half_first).transpose(1, 0, 2)
+    ).reshape(group, half_first)
     grad_first = dot_tn(normed_part, first_part).astype(BF)
 
     out_rows = out_weight.shape[0]

time: 1190 us -> 924 us (0.78)
  waiting for transfers between devices: 663 us -> 113 us
  Pallas kernels: 44.8 us -> 363 us
  local copies, waits for them, and re-layouts: 105 us -> 76.1 us
    pallas_call x0 -> x8, Pallas kernels: none -> 318 us  [comm_call(): pl.pallas_call(body, name=name, out_shape=outs, in_specs=spaces, out_spec...]
    all_gather x13 -> x4, waiting for transfers between devices: 321 us -> 16.8 us  [gather(): return lax.all_gather(value, axes, axis=0, tiled=True)]
    reduce_scatter x7 -> x2, waiting for transfers between devices: 266 us -> 24.3 us  [scatter_sum(): return lax.psum_scatter(value, axes, scatter_dimension=0, tiled=True)]
    unnamed x23 -> x9, waiting for transfers between devices: 2.06 us -> 63.7 us
    psum x1, waiting for transfers between devices: 54 us -> 0.01 us  [on_device(): pieces = lax.psum(scatter_sum(pieces, 'z'), 'x').astype(F32)[0]]
    concatenate x1, other arithmetic: 17.1 us -> 36.8 us  [on_device(): pieces = jnp.concatenate([grad_out, grad_first, grad_up_heads], axis=1)]
    all_to_all x3 -> x2, waiting for transfers between devices: 20.2 us -> 8.04 us  [swap(): return lax.all_to_all(value, axes, 0, 0, tiled=True)]
    transpose x5 -> x0, local copies, waits for them, and re-layouts: 12.1 us -> none  [the longest x1 4.44 us: on_device(): attended, lse = attend(queries, keys, values.T, begin_lanes, slot_lanes)]
  transfers between devices with their start and end apart: 25 -> 10, of which waited for: 21 -> 4; matrix products, arithmetic and copies ran while one was open for 17% -> 15% of each run, Pallas kernels for 2% -> 25%
where the time goes in v2:
time: 924 us; the launch traced here: 914 us
  Pallas kernels  363 us (39%)
  blocking collectives  161 us (17%)
  waiting for transfers between devices  113 us (12%)
  matrix products  103 us (11%)
  local copies, waits for them, and re-layouts  76.1 us (8%)
  other arithmetic  72.7 us (8%)
  between operations  15.6 us (2%)
  starting transfers between devices  10.1 us (1%)
    pallas_call x8, Pallas kernels, comm_call(): pl.pallas_call(body, name=name, out_shape=outs, in_specs=spaces, out_spec...  318 us
    unnamed x1, blocking collectives  122 us
    unnamed x9, waiting for transfers between devices  63.7 us
    dot_general x14, matrix products, dot_nt(): lax.dot_general(left, right, (((1,), (1,)), ((), ())), preferred_element_...  43 us
    concatenate x1, other arithmetic, on_device(): pieces = jnp.concatenate([grad_out, grad_first, grad_up_heads], axis=1)  36.8 us
    dot_general x8, matrix products, dot(): return jnp.dot(left, right, preferred_element_type=F32)  33.8 us
    unnamed x102, local copies, waits for them, and re-layouts  26.4 us
    dot_general x6, matrix products, dot_tn(): lax.dot_general(left, right, (((0,), (0,)), ((), ())), preferred_element_...  25.8 us
  transfers between devices with their start and end apart: 10, of which 4 were waited for; matrix products, arithmetic and copies ran while one was open for 15% of the time, Pallas kernels for 25%

profile of v2, /device:TPU:1, one launch (start us, length us, event | category | flops | bytes accessed | tf_op | source)
XLA Modules:
  0.0 913.7 jit_solution(4082120921773293509)
XLA Ops:
  20.0 75.4 %first_weights.1 = (bf16[4,4,2,64,1664]{4,3,2,1,0:T(8,128)(2,1)}, bf16[4,4,2,32,512]{4,3,2,1,0:T(8,128)(2,1)}, bf16[2,64,1536]{2,1,0:T(8,128)(2,1)}, bf16[4,4,2,32,512]{4,3,2,1,0:T(8,128)(2,1)}) custom-call(bf16[64,1664]{1,0:T(8,128)(2,1)} %fusion.52.first_ref, bf16[4,2,32,512]{3,2,1,0:T(8,128)(2,1)} %bitcast.182, ...), custom_call_target="tpu_custom_call" | custom-call | tf_op jit(solution)/shard_map/first_weights/pallas_call | solution.py:297
  99.9 4.0 fusion.16
  106.1 39.3 %keys_and_latents.1 = (bf16[4,4,2,128,512]{4,3,2,1,0:T(8,128)(2,1)}, bf16[4,2,128,1024]{3,2,1,0:T(8,128)(2,1)}) custom-call(bf16[128,512]{1,0:T(8,128)(2,1)} %pad_maximum_fusion.6.kv_ref, bf16[128,1024]{1,0:T(8,128)(2,1)} %multiply_convert_fusion.4.lat_ref), custom_call_target="tpu_custom_call" | custom-call | tf_op jit(solution)/shard_map/keys_and_latents/pallas_call | solution.py:297
  147.4 2.9 fusion.101.q_ref
  150.2 20.0 %attend.1 = (bf16[1024,512]{1,0:T(8,128)(2,1)S(1)}, bf16[4,256,512]{2,1,0:T(8,128)(2,1)S(1)}, f32[4,1,512]{2,1,0:T(1,128)S(1)}) custom-call(f32[1024,512]{1,0:T(8,128)S(1)} %fusion.101.q_ref, bf16[4096,512]{1,0:T(8,128)(2,1)} %bitcast.156, s32[4,1,512]{2,1,0:T(1,128)S(1)} %tile.28.begin_ref, s32[4,1,512]{2,1,0:T(1,128)S(1)} %tile.30.slot_ref, ...), custom_call_target="tpu_custom_call" | custom-call | tf_op jit(solution)/shard_map/attend/pallas_call | solution.py:136
  170.9 5.9 convolution_convert_fusion
  176.8 40.9 %heads_sum_and_cotangent.1 = (f32[128,2048]{1,0:T(8,128)}, bf16[4,2,128,2048]{3,2,1,0:T(8,128)(2,1)}) custom-call(bf16[4,2,128,2048]{3,2,1,0:T(8,128)(2,1)} %bitcast.165, bf16[128,2048]{1,0:T(8,128)(2,1)} %cot_ref.1), custom_call_target="tpu_custom_call" | custom-call | tf_op jit(solution)/shard_map/heads_sum_and_cotangent/pallas_call | solution.py:297
  221.1 26.7 %feed_gather.1 = (bf16[4,2,128,2048]{3,2,1,0:T(8,128)(2,1)}, bf16[4,2,128,512]{3,2,1,0:T(8,128)(2,1)}) custom-call(bf16[128,2048]{1,0:T(8,128)(2,1)} %multiply_convert_fusion.3.two_ref, bf16[128,2048]{1,0:T(8,128)(2,1)} %copy-done.18), custom_call_target="tpu_custom_call" | custom-call | tf_op jit(solution)/shard_map/feed_gather/pallas_call | solution.py:297
  247.8 8.3 fusion.102
  256.1 6.3 fusion.20
  263.2 5.6 multiply_convert_fusion
  268.7 5.4 convolution_convert_fusion.1
  274.2 3.4 fusion.18
  277.6 5.1 add_convert_fusion
  282.7 44.9 %feed_sum.1 = (f32[128,2048]{1,0:T(8,128)}, f32[128,2048]{1,0:T(8,128)}) custom-call(bf16[4,2,128,2048]{3,2,1,0:T(8,128)(2,1)} %bitcast.167, bf16[4,2,128,2048]{3,2,1,0:T(8,128)(2,1)} %bitcast.166), custom_call_target="tpu_custom_call" | custom-call | tf_op jit(solution)/shard_map/feed_sum/pallas_call | solution.py:297
  331.6 23.5 %heads_gather.1 = bf16[4,2,128,2048]{3,2,1,0:T(8,128)(2,1)} custom-call(bf16[128,2048]{1,0:T(8,128)(2,1)} %fusion.84.ref), custom_call_target="tpu_custom_call" | custom-call | tf_op jit(solution)/shard_map/heads_gather/pallas_call | solution.py:297
  355.1 4.7 convolution_convert_fusion.5
  362.2 25.1 %attend_back.1 = (bf16[1024,512]{1,0:T(8,128)(2,1)S(1)}, bf16[4096,512]{1,0:T(8,128)(2,1)}) custom-call(bf16[4,256,512]{2,1,0:T(8,128)(2,1)S(1)} %get-tuple-element.42.qt_ref, bf16[1024,512]{1,0:T(8,128)(2,1)S(1)} %fusion.31.do_ref, bf16[1024,512]{1,0:T(8,128)(2,1)S(1)} %get-tuple-element.35.o_ref, bf16[4096,512]{1,0:T(8,128)(2,1)} %bitcast.157, ...), custom_call_target="tpu_custom_call" | custom-call | tf_op jit(solution)/shard_map/attend_back/pallas_call | solution.py:213
  388.5 2.6 convolution_convert_fusion.6
  391.2 43.6 %keys_and_latents_sum.1 = (f32[128,512]{1,0:T(8,128)}, f32[128,1024]{1,0:T(8,128)}) custom-call(bf16[4,4,2,128,512]{4,3,2,1,0:T(8,128)(2,1)} %bitcast.162, bf16[4,2,128,1024]{3,2,1,0:T(8,128)(2,1)} %bitcast.175), custom_call_target="tpu_custom_call" | custom-call | tf_op jit(solution)/shard_map/keys_and_latents_sum/pallas_call | solution.py:297
  439.6 4.5 all-to-all-start
  448.4 23.8 %firsts_gather.1 = bf16[4,2,128,768]{3,2,1,0:T(8,128)(2,1)} custom-call(bf16[2,128,768]{2,1,0:T(8,128)(2,1)} %bitcast.180), custom_call_target="tpu_custom_call" | custom-call | tf_op jit(solution)/shard_map/firsts_gather/pallas_call | solution.py:297
  472.2 2.8 bitcast_convert_fusion
  475.9 6.8 all_to_all.20
  482.8 4.9 all-to-all-start.2
  487.7 3.0 copy.131
  492.3 2.5 reshape.368
  494.9 8.0 all-to-all-done.2
  505.6 36.8 %pad_maximum_fusion.1 = bf16[4,491520]{1,0:T(4,128)(2,1)} fusion(bf16[4,131072]{1,0:T(4,128)(2,1)S(1)} %bitcast.161, bf16[4,98304]{1,0:T(4,128)(2,1)S(1)} %copy-done.16, bf16[4,262144]{1,0:T(4,128)(2,1)S(1)} %bitcast.160), kind=kLoop, calls=%fused_computation.31 | loop fusion | flops 11796480 | bytes 7864320 | tf_op jit(solution)/shard_map/concatenate | solution.py:978
  543.5 6.3 convolution_convert_fusion.4
  549.8 3.7 convolution_convert_fusion.3
  553.6 3.7 pad_maximum_fusion
  557.3 8.7 copy.125
  566.1 62.9 %all-reduce.10.cloned.1.call-done = bf16[4,491520]{1,0:T(4,128)(2,1)} async-done(((bf16[4,491520]{1,0:T(4,128)(2,1)}), bf16[4,491520]{1,0:T(4,128)(2,1)}) %all-reduce.10.cloned.1.call-update) | async-done | bytes 3932176
  629.0 5.7 constant_dynamic-slice_fusion
  634.8 7.1 convolution_convert_fusion.2
  642.5 2.9 fusion.3
  645.5 6.3 fusion.44
  652.0 121.5 %all-reduce.3 = f32[32,160]{1,0:T(8,128)S(1)} all-reduce(f32[32,160]{1,0:T(8,128)S(1)} %pad_maximum_fusion.7), channel_id=4, replica_groups=mesh['x'=4,'y'=4,'z'=4,'c'=2] {'y','z','c'}, use_global_device_ids=true, to_apply=%region_12.13.clone | all-reduce | flops 5120 | bytes 40960
  774.2 8.4 psum.14
  785.5 12.5 %all_to_all.21 = bf16[2,2,64,768]{3,1,2,0:T(2,128)(2,1)S(1)} all-to-all(bf16[2,2,64,768]{3,1,2,0:T(2,128)(2,1)} %bitcast.179), channel_id=1, replica_groups=mesh['x'=4,'y'=4,'z'=4,'c'=2] {'c'}, dimensions={0} | all-to-all | bytes 786432 | tf_op jit(solution)/shard_map/all_to_all | solution.py:788
  798.9 3.3 fusion.40
  802.2 3.7 convert_element_type.161
  807.7 11.8 %slice_reduce_fusion = f32[262144]{0:T(1024)} fusion(f32[1,491520]{1,0:T(1,128)S(1)} %convert_element_type.161), kind=kLoop, calls=%fused_computation.84 | loop fusion | bytes 2097152 | tf_op jit(solution)/shard_map/slice | solution.py:982
  824.8 24.3 %reduce-scatter.5.cloned.1.call-done = bf16[48,2048]{1,0:T(8,128)(2,1)} async-done(((bf16[768,2048]{1,0:T(8,128)(2,1)}), bf16[48,2048]{1,0:T(8,128)(2,1)}) %reduce-scatter.5.cloned.1.call-update) | async-done | bytes 196624 | tf_op jit(solution)/shard_map/reduce_scatter | solution.py:784
  849.1 11.4 %all-gather.1 = bf16[192,2048]{1,0:T(8,128)(2,1)S(1)} all-gather(bf16[48,2048]{1,0:T(8,128)(2,1)} %reduce-scatter.5.cloned.1.call-done), channel_id=3, replica_groups=mesh['x'=4,'y'=4,'z'=4,'c'=2] {'x'}, dimensions={0}, use_global_device_ids=true | all-gather | bytes 983040 | tf_op jit(solution)/shard_map/all_gather | solution.py:780
  861.9 16.7 %all-gather.13.cloned.1.call-done = bf16[8,2,64,768]{3,2,1,0:T(8,128)(2,1)} async-done(((bf16[2,2,64,768]{3,2,1,0:T(8,128)(2,1)}), bf16[8,2,64,768]{3,2,1,0:T(8,128)(2,1)}) %all-gather.13.cloned.1.call-update) | async-done | bytes 1572880 | tf_op jit(solution)/shard_map/all_gather | solution.py:780
  883.4 2.9 reshape_squeeze.10
  (246 shorter events, 87.7 us)
Async XLA Ops:
  7.2 163.7 %all-gather.7.cloned.1.call-start = ((), (), s32[]{:S(2)}) async-start(), calls=%async_computation.6 | async-start | bytes 4718592 | tf_op jit(solution)/shard_map/all_gather | solution.py:780
  7.9 239.9 %all-gather.9.cloned.1.call-start = ((), (), s32[]{:S(2)}) async-start(), calls=%async_computation.7 | async-start | bytes 3342336 | tf_op jit(solution)/shard_map/all_gather | solution.py:780
  9.1 247.0 %all-gather.11.cloned.1.call-start = ((), (), s32[]{:S(2)}) async-start(), calls=%async_computation.8 | async-start | bytes 6684672 | tf_op jit(solution)/shard_map/all_gather | solution.py:780
  13.7 2.4 copy-start.20
  16.1 2.4 copy-start.22
  16.2 2.4 copy-start.23
  16.2 2.4 copy-start.24
  16.2 79.3 %copy-start.33 = (s32[1,4]{1,0:T(1,128)S(1)}, s32[1,4]{1,0:T(1,128)}, u32[]{:S(2)}) copy-start(s32[1,4]{1,0:T(1,128)} %param.16) | copy-start | bytes 52
  18.1 81.4 %copy-start.7 = (bf16[128,2048]{1,0:T(8,128)(2,1)S(1)}, bf16[128,2048]{1,0:T(8,128)(2,1)}, u32[]{:S(2)}) copy-start(bf16[128,2048]{1,0:T(8,128)(2,1)} %param.14) | copy-start | bytes 1572868
  99.9 4.1 copy-start.18
  99.9 47.4 %copy-start.31 = (bf16[4,4,2,32,512]{4,3,2,1,0:T(8,128)(2,1)S(1)}, bf16[4,4,2,32,512]{4,3,2,1,0:T(8,128)(2,1)}, u32[]{:S(2)}) copy-start(bf16[4,4,2,32,512]{4,3,2,1,0:T(8,128)(2,1)} %get-tuple-element.33) | copy-start | bytes 3145732
  104.0 41.5 %copy-start.11 = (f32[128,1536]{1,0:T(8,128)}, f32[128,1536]{1,0:T(8,128)S(1)}, u32[]{:S(2)}) copy-start(f32[128,1536]{1,0:T(8,128)S(1)} %fusion.16) | copy-start | bytes 2359300
  176.8 40.9 %copy-start.8 = (bf16[128,2048]{1,0:T(8,128)(2,1)S(1)}, bf16[128,2048]{1,0:T(8,128)(2,1)}, u32[]{:S(2)}) copy-start(bf16[128,2048]{1,0:T(8,128)(2,1)} %param.14) | copy-start | bytes 1572868
  256.1 6.3 copy-start.25
  256.1 6.3 copy-start.27
  256.1 7.1 copy-start.39
  263.2 5.6 copy-start.29
  268.7 5.4 copy-start.36
  268.7 5.4 copy-start.38
  274.2 3.5 copy-start.40
  282.7 44.9 %copy-start.3 = (f32[128,2048]{1,0:T(8,128)S(1)}, f32[128,2048]{1,0:T(8,128)}, u32[]{:S(2)}) copy-start(f32[128,2048]{1,0:T(8,128)} %copy-done.2) | copy-start | bytes 3145732
  282.7 46.4 %copy-start.12 = (bf16[128,2048]{1,0:T(8,128)(2,1)S(1)}, bf16[128,2048]{1,0:T(8,128)(2,1)}, u32[]{:S(2)}) copy-start(bf16[128,2048]{1,0:T(8,128)(2,1)} %cot_ref.1) | copy-start | bytes 1572868
  355.0 4.7 copy-start.14
  355.1 4.7 copy-start.26
  362.2 25.1 %copy-start.30 = (bf16[4,2,128,1024]{3,2,1,0:T(8,128)(2,1)S(1)}, bf16[4,2,128,1024]{3,2,1,0:T(8,128)(2,1)}, u32[]{:S(2)}) copy-start(bf16[4,2,128,1024]{3,2,1,0:T(8,128)(2,1)} %get-tuple-element.32) | copy-start | bytes 6291460
  438.0 6.1 copy-start.17
  439.6 36.3 %all-to-all-start = ((bf16[2,2,128,2048]{3,2,1,0:T(8,128)(2,1)}), bf16[2,2,128,2048]{3,2,1,0:T(8,128)(2,1)S(1)}, u32[]{:S(2)}, u32[]{:S(2)}) async-start(bf16[2,2,128,2048]{3,2,1,0:T(8,128)(2,1)} %bitcast.159), calls=%async_computation | async-start | bytes 4194304 | tf_op jit(solution)/shard_map/all_to_all | solution.py:788
  482.8 20.1 %all-to-all-start.2 = ((bf16[8,4,32,512]{3,2,1,0:T(8,128)(2,1)}), bf16[8,4,32,512]{3,2,1,0:T(8,128)(2,1)}, u32[]{:S(2)}, u32[]{:S(2)}) async-start(bf16[8,4,32,512]{3,2,1,0:T(8,128)(2,1)} %bitcast.168), calls=%async_computation.2 | async-start | bytes 2097152 | tf_op jit(solution)/shard_map/all_to_all | solution.py:788
  487.7 141.3 %all-reduce.10.cloned.1.call-start = ((), (), s32[]{:S(2)}) async-start(), calls=%async_computation.13 | async-start | bytes 7864320
  487.7 3.0 copy-start.15
  490.7 14.9 %copy-start.10 = (bf16[1,4,128,2048]{3,1,2,0:T(4,128)(2,1)S(1)}, bf16[1,4,128,2048]{3,1,2,0:T(4,128)(2,1)}, u32[]{:S(2)}) copy-start(bf16[1,4,128,2048]{3,1,2,0:T(4,128)(2,1)} %copy.131) | copy-start | bytes 6291460
  502.9 2.7 copy-start.16
  505.6 37.3 %copy-start.35 = (u32[128]{0:T(128)S(1)}, u32[128]{0:T(128)}, u32[]{:S(2)}) copy-start(u32[128]{0:T(128)} %constant.119) | copy-start | bytes 1540
  542.4 241.2 %reduce-scatter.7.cloned.1.call-start = ((), (), s32[]{:S(2)}) async-start(), calls=%async_computation.12 | async-start | bytes 6684672 | tf_op jit(solution)/shard_map/reduce_scatter | solution.py:784
  543.5 6.3 copy-start.28
  543.5 6.3 copy-start.41
  566.0 68.8 %copy-start.37 = (bf16[1024,768]{1,0:T(8,128)(2,1)S(1)}, bf16[1024,768]{1,0:T(8,128)(2,1)}, u32[]{:S(2)}) copy-start(bf16[1024,768]{1,0:T(8,128)(2,1)} %copy-done.36) | copy-start | bytes 4718596
  566.0 236.2 %all-reduce.8.cloned.1.call-start = ((), (), s32[]{:S(2)}) async-start(), calls=%async_computation.9 | async-start | bytes 3932160 | tf_op jit(solution)/shard_map/psum | solution.py:979
  634.7 7.2 copy-start.34
  634.7 214.4 %reduce-scatter.5.cloned.1.call-start = ((), (), s32[]{:S(2)}) async-start(), calls=%async_computation.10 | async-start | bytes 3342336 | tf_op jit(solution)/shard_map/reduce_scatter | solution.py:784
  641.8 3.7 copy-start.9
  641.9 236.7 %all-gather.13.cloned.1.call-start = ((), (), s32[]{:S(2)}) async-start(), calls=%async_computation.11 | async-start | bytes 1966080 | tf_op jit(solution)/shard_map/all_gather | solution.py:780
  645.5 153.4 %copy-start.4 = (f32[128,2048]{1,0:T(8,128)S(1)}, f32[128,2048]{1,0:T(8,128)}, u32[]{:S(2)}) copy-start(f32[128,2048]{1,0:T(8,128)} %copy-done.2) | copy-start | bytes 3145732
  645.5 153.4 %copy-start.6 = (f32[128,2048]{1,0:T(8,128)S(1)}, f32[128,2048]{1,0:T(8,128)}, u32[]{:S(2)}) copy-start(f32[128,2048]{1,0:T(8,128)} %get-tuple-element.41) | copy-start | bytes 3145732
  645.5 153.4 %copy-start.13 = (bf16[128,2048]{1,0:T(8,128)(2,1)S(1)}, bf16[128,2048]{1,0:T(8,128)(2,1)}, u32[]{:S(2)}) copy-start(bf16[128,2048]{1,0:T(8,128)(2,1)} %cot_ref.1) | copy-start | bytes 1572868
  882.2 6.9 copy-start.5
  896.1 2.0 copy-start.21
  902.0 4.4 copy-start.1
  (4 other events, 4.1 us)
Sparse Core Ops, SparseCore 0:
  9.7 60.8 all-gather.6
  73.4 54.7 all-gather.8
  130.4 77.7 all-gather.10
  542.6 86.3 all-reduce.9
  632.2 80.1 reduce-scatter.6
  714.7 56.7 all-reduce.7
  774.8 74.2 reduce-scatter.4
  851.3 27.2 all-gather.12

commit v3 on v2

--- a/solution.py
+++ b/solution.py
@@ -570,6 +570,7 @@
 
 Y_LINE = [("y", d) for d in LINE]
 Z_LINE = [("z", d) for d in LINE]
+X_LINE = [("x", d) for d in LINE]
 X_RING = [("x", 1), ("x", -1)]
 Y_RING = [("y", 1), ("y", -1)]
 TWIN = [("c", 1)]
@@ -579,40 +580,61 @@
     return jax.ShapeDtypeStruct(dims, kind)
 
 
-def first_weights(first, up, both):
-    def body(first_ref, up_ref, both_ref, first_out, up_out, both_out, transit, sends, arrivals, locals_):
+def first_weights(first, up, both, out):
+    def body(
+        first_ref, up_ref, both_ref, out_ref, first_out, up_out, both_out, out_out, transit, strip, sheet,
+        sends, arrivals, locals_,
+    ):
         net = Net(sends, arrivals, locals_)
-        y, z, c = (lax.axis_index(a) for a in ROW)
-        greet(Y_LINE + Z_LINE + TWIN)
+        x, y, z, c = (lax.axis_index(a) for a in AXES)
+        quarter = out_ref.shape[0] // 4
+        greet(X_LINE + Y_LINE + Z_LINE + TWIN)
         row = RowGather(net, first_ref, first_out)
+        piece = out_ref.at[pl.ds(pl.multiple_of(x * quarter, quarter), quarter)]
+        piece_mine = net.keep(piece, strip.at[z])
+        pieces = [net.send(piece, strip.at[z], "z", d) for d in LINE]
         up_mine = net.keep(up_ref.at[y], transit.at[y, z])
         ups = [net.send(up_ref.at[along("y", d)], transit.at[y, z], "y", d) for d in LINE]
         both_mine = net.keep(both_ref.at[c], both_out.at[c])
         both_come = net.send(both_ref.at[1 - c], both_out.at[c], "c", 1)
         row.spread()
+        piece_mine.wait()
+        for copy in pieces:
+            copy.wait_recv()
+        strip_mine = net.keep(strip, sheet.at[:, x])
+        strips = [net.send(strip, sheet.at[:, x], "x", d) for d in LINE]
         up_mine.wait()
         for copy in ups:
             copy.wait_recv()
         ups = [net.send(transit.at[:, z], transit.at[:, z], "z", d) for d in LINE]
         row.finish()
+        strip_mine.wait()
+        for copy in strips:
+            copy.wait_recv()
+        half = sheet.shape[0] // 2
+        sheet_keep = net.keep(sheet.at[pl.ds(half * c, half)], out_out.at[:, c])
+        sheet_come = net.send(sheet.at[pl.ds(half * (1 - c), half)], out_out.at[:, c], "c", 1)
         for copy in ups:
             copy.wait_recv()
         up_keep = net.keep(transit.at[:, :, c], up_out.at[:, :, c])
         up_come = net.send(transit.at[:, :, 1 - c], up_out.at[:, :, c], "c", 1)
-        both_mine.wait()
-        both_come.wait_recv()
-        up_keep.wait()
-        up_come.wait_recv()
+        for copy in (both_mine, up_keep, sheet_keep):
+            copy.wait()
+        for copy in (both_come, up_come, sheet_come):
+            copy.wait_recv()
         net.close()
 
     _, per, high, thin = up.shape
+    rows, width = out.shape
+    quarter = rows // 4
     outs = (
         shape(4, 4, 2, *first.shape), shape(4, 4, 2, high, thin), shape(*both.shape),
-        shape(4, 4, 2, high, thin),
+        shape(2, 2, 4, quarter, width), shape(4, 4, 2, high, thin), shape(4, quarter, width),
+        shape(4, 4, quarter, width),
     )
     return comm_call(
-        body, "first_weights", 1, outs, (first, up, both), [], 40, 4, [ANYWHERE] * 3, [ANYWHERE] * 4,
-    )[:3]
+        body, "first_weights", 1, outs, (first, up, both, out), [], 44, 8, [ANYWHERE] * 4, [ANYWHERE] * 7,
+    )[:4]
 
 
 def keys_and_latents(key_value, latent):
@@ -689,90 +711,278 @@
     )
 
 
-def feed_sum(partial, partial_two):
-    def body(one_ref, two_ref, one_out, two_out, *rest):
-        net = Net(*rest[8:])
+def feed_sum(partial):
+    def body(ref, out, *rest):
+        net = Net(*rest[4:])
         greet(X_RING + TWIN)
-        one = RingSum(net, one_ref, one_out, "x", *rest[:4])
-        two = RingSum(net, two_ref, two_out, "x", *rest[4:8])
-        one.relay_far()
-        one.spread()
-        two.relay_far()
-        two.spread()
-        one.finish()
-        two.finish()
-        net.close()
-
-    _, _, size, width = partial.shape
-    outs = (shape(size, width, kind=F32),) * 2
-    return comm_call(
-        body, "feed_sum", 5, outs, (partial, partial_two), ring_sum_scratch(size, width) * 2, 24, 0,
-        [IN_VMEM] * 2, [IN_VMEM] * 2,
-    )
-
-
-def heads_gather(value):
-    def body(ref, out, sends, arrivals, locals_):
-        net = Net(sends, arrivals, locals_)
-        greet(Y_RING + TWIN)
-        ring = RingGather(net, ref, out, "y")
+        ring = RingSum(net, ref, out, "x", *rest[:4])
+        ring.relay_far()
         ring.spread()
         ring.finish()
         net.close()
 
+    _, _, size, width = partial.shape
     return comm_call(
-        body, "heads_gather", 6, shape(4, 2, *value.shape), (value,), [], 12, 2, [ANYWHERE], ANYWHERE,
-    )
-
-
-def keys_and_latents_sum(grad_kv, partial):
-    def body(kv_ref, part_ref, kv_out, part_out, *rest):
-        net = Net(*rest[9:])
-        greet(Y_LINE + Z_LINE + TWIN)
+        body, "feed_sum", 5, shape(size, width, kind=F32), (partial,), ring_sum_scratch(size, width), 12, 0,
+        [IN_VMEM], IN_VMEM,
+    )
+
+
+def heads_gather_and_branch(value, partial):
+    def body(ref, part_ref, out, part_out, *rest):
+        net = Net(*rest[4:])
+        greet(X_RING + Y_RING + TWIN)
+        gathering = RingGather(net, ref, out, "y")
+        ring = RingSum(net, part_ref, part_out, "x", *rest[:4])
+        ring.relay_far()
+        gathering.spread()
+        ring.spread()
+        gathering.finish()
+        ring.finish()
+        net.close()
+
+    size, width = value.shape
+    return comm_call(
+        body, "heads_gather_and_branch", 6, (shape(4, 2, size, width), shape(size, width, kind=F32)),
+        (value, partial), ring_sum_scratch(size, width), 24, 2, [ANYWHERE, IN_VMEM], [ANYWHERE, IN_VMEM],
+    )
+
+
+def add_up(terms, out, rows):
+    total = terms[0][rows].astype(F32)
+    for term in terms[1:]:
+        total = total + term[rows].astype(F32)
+    out[rows] = total.astype(out.dtype)
+
+
+def add_all(terms, out):
+    rows_loop(out.shape[0], lambda rows: add_up(terms, out, rows))
+
+
+def keys_and_latents_sum(grad_kv, partial, grad_out, grad_up):
+    def body(kv_ref, part_ref, out_ref, up_ref, kv_out, part_out, out_out, up_out, *rest):
+        net = Net(*rest[12:])
+        stack, out_come, up_come = rest[9:12]
+        x, c = lax.axis_index("x"), lax.axis_index("c")
+        half = out_ref.shape[0]
+        quarter = out_out.shape[1]
+        lanes = up_out.shape[-1]
+
+        def strip(at):
+            return pl.ds(pl.multiple_of(at * quarter, quarter), quarter)
+
+        def lane(at):
+            return pl.ds(pl.multiple_of(at * lanes, lanes), lanes)
+
+        greet(X_LINE + Y_LINE + Z_LINE + TWIN)
+        mine = net.keep(out_ref.at[:, c], stack.at[pl.ds(half * c, half)])
+        come = net.send(out_ref.at[:, 1 - c], stack.at[pl.ds(half * c, half)], "c", 1)
         row = RowSum(net, kv_ref, kv_out, *rest[:5])
         ring = RingSum(net, part_ref, part_out, "y", *rest[5:9])
+        mine.wait()
+        come.wait_recv()
+        outs = [net.send(stack.at[:, strip(along("x", d))], out_come.at[d - 1], "x", d) for d in LINE]
         row.start()
+        ups = [
+            net.send(up_ref.at[:, :, :, :, lane(along("x", d))], up_come.at[d - 1], "x", d) for d in LINE
+        ]
         ring.relay_far()
         ring.spread()
         row.turn()
+        for copy in outs:
+            copy.wait_recv()
+        for i in range(4):
+            add_all([stack.at[i, strip(x)]] + [out_come.at[d, i] for d in range(3)], out_out.at[i])
+        for copy in ups:
+            copy.wait_recv()
+        for i in range(4):
+
+            @pl.loop(0, 8)
+            def _(k, i=i):
+                j, core = k // 2, k % 2
+                add_all(
+                    [up_ref.at[i, j, core, :, lane(x)]] + [up_come.at[d, i, j, core] for d in range(3)],
+                    up_out.at[i, j, core],
+                )
+
         ring.finish()
         row.finish()
         net.close()
 
     _, _, _, size, thin = grad_kv.shape
     width = partial.shape[3]
-    outs = (shape(size, thin, kind=F32), shape(size, width, kind=F32))
+    half, _, tall, wide = grad_out.shape
+    high, lanes = grad_up.shape[3], grad_up.shape[4] // 4
+    outs = (
+        shape(size, thin, kind=F32), shape(size, width, kind=F32), shape(4, tall // 4, wide),
+        shape(4, 4, 2, high, lanes),
+    )
+    scratch = [
+        pltpu.VMEM((2 * half, tall, wide), BF),
+        pltpu.VMEM((3, 4, tall // 4, wide), BF),
+        pltpu.VMEM((3, 4, 4, 2, high, lanes), BF),
+    ]
     return comm_call(
-        body, "keys_and_latents_sum", 7, outs, (grad_kv, partial),
-        row_sum_scratch(size, thin) + ring_sum_scratch(size, width), 28, 0, [IN_VMEM] * 2, [IN_VMEM] * 2,
-    )
-
-
-def firsts_gather(value):
-    def body(ref, out, sends, arrivals, locals_):
+        body, "keys_and_latents_sum", 7, outs, (grad_kv, partial, grad_out, grad_up),
+        row_sum_scratch(size, thin) + ring_sum_scratch(size, width) + scratch, 36, 1, [IN_VMEM] * 4,
+        [IN_VMEM] * 4,
+    )
+
+
+def firsts_gather(value, both, grad_out, grad_up):
+    def body(
+        ref, both_ref, out_ref, up_ref, gathered, both_out, out_out, up_out, out_come, up_come, up_sum, up_y,
+        sends, arrivals, locals_,
+    ):
         net = Net(sends, arrivals, locals_)
-        y, c = lax.axis_index("y"), lax.axis_index("c")
-        greet(Y_RING + TWIN)
-        mine = net.keep(ref.at[c], out.at[y, c])
-        come = net.send(ref.at[1 - c], out.at[y, c], "c", 1)
+        x, y, z, c = (lax.axis_index(a) for a in AXES)
+        greet(X_LINE + Y_LINE + Z_LINE + TWIN)
+        mine = net.keep(ref.at[c], gathered.at[y, c])
+        come = net.send(ref.at[1 - c], gathered.at[y, c], "c", 1)
+        both_mine = net.keep(both_ref.at[c], both_out.at[x, c])
+        both_come = net.send(both_ref.at[1 - c], both_out.at[x, c], "c", 1)
+        ups = [net.send(up_ref.at[:, along("z", d)], up_come.at[d - 1], "z", d) for d in LINE]
+        outs = [net.send(out_ref.at[along("z", d)], out_come.at[d - 1], "z", d) for d in LINE]
+
         mine.wait()
-        spot = out.at[y, c]
+        spot = gathered.at[y, c]
         ahead = [net.send(spot, spot, "y", 1), net.send(spot, spot, "y", -1)]
         come.wait_recv()
-        spot = out.at[y, 1 - c]
+        spot = gathered.at[y, 1 - c]
         ahead += [net.send(spot, spot, "y", 1), net.send(spot, spot, "y", -1)]
+        both_mine.wait()
+        both_come.wait_recv()
+        zero, one = both_out.at[x, 0], both_out.at[x, 1]
+        right = [net.send(spot, spot, "x", 1) for spot in (zero, one)]
+        left = [net.send(spot, spot, "x", -1) for spot in (one, zero)]
+
+        for copy in ups:
+            copy.wait_recv()
+        for i in range(4):
+            for core in range(2):
+                add_all(
+                    [up_ref.at[i, z, core]] + [up_come.at[d, i, core] for d in range(3)], up_sum.at[i, core]
+                )
+        ups = [net.send(up_sum.at[along("y", d)], up_y.at[y], "y", d) for d in LINE]
+        up_mine = net.keep(up_sum.at[y], up_y.at[y])
+
         ahead[0].wait_recv()
-        spot = out.at[along("y", -1), c]
+        spot = gathered.at[along("y", -1), c]
         ahead.append(net.send(spot, spot, "y", 1))
         ahead[3].wait_recv()
-        spot = out.at[along("y", 1), 1 - c]
+        spot = gathered.at[along("y", 1), 1 - c]
         ahead.append(net.send(spot, spot, "y", -1))
-        for i in (1, 2, 4, 5):
-            ahead[i].wait_recv()
+
+        for copy in outs:
+            copy.wait_recv()
+        add_all([out_ref.at[z]] + [out_come.at[d] for d in range(3)], out_out.at[x])
+        spot = out_out.at[x]
+        outs = [net.send(spot, spot, "x", d) for d in LINE]
+
+        up_mine.wait()
+        for copy in ups:
+            copy.wait_recv()
+        up_near = net.send(up_y.at[:, 1 - c], up_out.at[x, :, c], "c", 1)
+        up_mine = net.keep(up_y.at[:, c], up_out.at[x, :, c])
+
+        right[0].wait_recv()
+        spot = both_out.at[along("x", -1), 0]
+        far = [net.send(spot, spot, "x", 1)]
+        left[0].wait_recv()
+        spot = both_out.at[along("x", 1), 1]
+        far.append(net.send(spot, spot, "x", -1))
+
+        up_near.wait_recv()
+        up_mine.wait()
+        spot = up_out.at[x]
+        ups = [net.send(spot, spot, "x", d) for d in LINE]
+        for copy in [ahead[i] for i in (1, 2, 4, 5)] + [right[1], left[1]] + far + outs + ups:
+            copy.wait_recv()
         net.close()
 
+    _, tall, wide = grad_out.shape
+    _, _, _, high, lanes = grad_up.shape
+    outs = (
+        shape(4, *value.shape), shape(4, *both.shape), shape(4, tall, wide), shape(4, 4, 2, high, lanes),
+    )
+    scratch = [
+        pltpu.VMEM((3, tall, wide), BF),
+        pltpu.VMEM((3, 4, 2, high, lanes), BF),
+        pltpu.VMEM((4, 2, high, lanes), BF),
+        pltpu.VMEM((4, 2, high, lanes), BF),
+    ]
     return comm_call(
-        body, "firsts_gather", 8, shape(4, *value.shape), (value,), [], 12, 2, [ANYWHERE], ANYWHERE,
+        body, "firsts_gather", 8, outs, (value, both, grad_out, grad_up), scratch, 40, 4,
+        [ANYWHERE, ANYWHERE, IN_VMEM, IN_VMEM], [ANYWHERE, ANYWHERE, IN_VMEM, IN_VMEM],
+    )
+
+
+def last_sums(grad_first, gains, grad_down):
+    def body(
+        first_ref, gain_ref, down_ref, first_out, gain_out, down_out, wide, first_come, first_x,
+        gain_near, gain_one, gain_come, gain_two, gain_y, gain_three, gain_x, sends, arrivals, locals_,
+    ):
+        net = Net(sends, arrivals, locals_)
+        x, y, z, c = (lax.axis_index(a) for a in AXES)
+        greet(X_LINE + Y_LINE + Z_LINE + TWIN)
+        first_near = net.send(first_ref.at[:, 1 - c], wide.at[c], "c", 1)
+        first_mine = net.keep(first_ref.at[:, c], wide.at[c])
+        near = net.send(gain_ref.at[:, :, 1 - c], gain_near, "c", 1)
+        down_mine = net.keep(down_ref, down_out.at[x])
+        downs = [net.send(down_ref, down_out.at[x], "x", d) for d in LINE]
+        first_mine.wait()
+        first_near.wait_recv()
+        firsts = [net.send(wide.at[:, along("z", d)], first_come.at[d - 1], "z", d) for d in LINE]
+        near.wait_recv()
+        gain_one[...] = gain_ref[:, :, c] + gain_near[...]
+        comes = [net.send(gain_one.at[:, along("z", d)], gain_come.at[d - 1], "z", d) for d in LINE]
+        for copy in firsts:
+            copy.wait_recv()
+        for core in range(2):
+            add_all(
+                [wide.at[core, z]] + [first_come.at[d, core] for d in range(3)], first_x.at[x, core]
+            )
+        spot = first_x.at[x]
+        firsts = [net.send(spot, spot, "x", d) for d in LINE]
+        for copy in comes:
+            copy.wait_recv()
+        gain_two[...] = (gain_one[:, z] + gain_come[0]) + (gain_come[1] + gain_come[2])
+        comes = [net.send(gain_two.at[along("y", d)], gain_y.at[d - 1], "y", d) for d in LINE]
+        for copy in comes:
+            copy.wait_recv()
+        gain_three[...] = (gain_two[y] + gain_y[0]) + (gain_y[1] + gain_y[2])
+        gain_mine = net.keep(gain_three, gain_x.at[x])
+        comes = [net.send(gain_three, gain_x.at[x], "x", d) for d in LINE]
+        for copy in firsts:
+            copy.wait_recv()
+        for core in range(2):
+            add_all([first_x.at[i, core] for i in range(4)], first_out.at[core])
+        gain_mine.wait()
+        for copy in comes:
+            copy.wait_recv()
+        gain_out[...] = (gain_x[0] + gain_x[1]) + (gain_x[2] + gain_x[3])
+        down_mine.wait()
+        for copy in downs:
+            copy.wait_recv()
+        net.close()
+
+    _, _, high, lanes = grad_first.shape
+    outs = (shape(2, high, lanes, kind=F32), shape(8, 128, kind=F32), shape(4, *grad_down.shape))
+    scratch = [
+        pltpu.VMEM((2, 4, high, lanes), BF),
+        pltpu.VMEM((3, 2, high, lanes), BF),
+        pltpu.VMEM((4, 2, high, lanes), BF),
+        pltpu.VMEM((4, 4, 8, 128), F32),
+        pltpu.VMEM((4, 4, 8, 128), F32),
+        pltpu.VMEM((3, 4, 8, 128), F32),
+        pltpu.VMEM((4, 8, 128), F32),
+        pltpu.VMEM((3, 8, 128), F32),
+        pltpu.VMEM((8, 128), F32),
+        pltpu.VMEM((4, 8, 128), F32),
+    ]
+    return comm_call(
+        body, "last_sums", 9, outs, (grad_first, gains, grad_down), scratch, 24, 3,
+        [IN_VMEM, IN_VMEM, ANYWHERE], [IN_VMEM, IN_VMEM, ANYWHERE],
     )
 
 
@@ -782,10 +992,6 @@
 
 def scatter_sum(value, axes):
     return lax.psum_scatter(value, axes, scatter_dimension=0, tiled=True)
-
-
-def swap(value, axes):
-    return lax.all_to_all(value, axes, 0, 0, tiled=True)
 
 
 def on_device(
@@ -825,8 +1031,6 @@
     )
     per_heads = q_up.shape[1] // members
     q_rows = q_up.shape[0]
-    out_chip = gather(out_weight, ("z", "c"))
-    out_heads = lax.dynamic_slice_in_dim(out_chip, c * per_heads, per_heads)
 
     wide = gate_weight.shape[1]
     down_rows = down_weight.shape[0]
@@ -849,7 +1053,8 @@
     both = jnp.concatenate([spread(gate_weight), spread(up_weight)], axis=2)
     units = both.shape[-1] // 2
     up_sent = q_up.reshape(q_rows, n_y, n_c, per_heads).transpose(1, 2, 0, 3)
-    first_full, up_heads, both = first_weights(first, up_sent, both)
+    first_full, up_heads, both, out_heads = first_weights(first, up_sent, both, out_weight)
+    out_heads = out_heads.reshape(per_heads, width)
     first_full = first_full.reshape(span * shard, -1)
     up_heads = up_heads.reshape(span * q_rows, per_heads)
     both = both.reshape(n_c * shard, 2 * units)
@@ -863,6 +1068,7 @@
     gate_use, up_use = both_full[:, :units], both_full[:, units:]
     down_part = lax.dynamic_slice_in_dim(down_weight, x * share, share)
     down_part = jnp.pad(down_part, ((0, padded - share), (0, 0)))
+    down_part, _ = lax.optimization_barrier((down_part, both_full[:8, :128]))
     down_use = gather(down_part, ("y", "z"))
 
     inputs = block_input.astype(F32)
@@ -901,25 +1107,22 @@
     grad_hidden = dot_nt(grad_feed, down_use)
     grad_gate_pre = (grad_hidden * up_pre * sigma * (1.0 + gate_pre * (1.0 - sigma))).astype(BF)
     grad_up_pre = (grad_hidden * gate_pre * sigma).astype(BF)
-    grad_normed_two, branch_two = feed_sum(
-        (dot_nt(grad_gate_pre, gate_use) + dot_nt(grad_up_pre, up_use))
-        .astype(BF)
-        .reshape(n_x, n_c, rows, width),
-        dot(hidden, down_use).astype(BF).reshape(n_x, n_c, rows, width),
-    )
-    output = (middle + branch_two).astype(BF)
+    grad_both = jnp.concatenate(
+        [dot_tn(normed_two, grad_gate_pre).astype(BF), dot_tn(normed_two, grad_up_pre).astype(BF)],
+        axis=1,
+    )
+    grad_down = dot_tn(hidden, grad_feed).astype(BF)
+    branch_part = dot(hidden, down_use).astype(BF).reshape(n_x, n_c, rows, width)
+    partial = (dot_nt(grad_gate_pre, gate_use) + dot_nt(grad_up_pre, up_use)).astype(BF)
+    partial, grad_both, grad_down, branch_part = lax.optimization_barrier(
+        (partial, grad_both, grad_down, branch_part)
+    )
+    grad_both = scatter_sum(grad_both, ("y", "z"))
+    grad_down = scatter_sum(grad_down, ("y", "z"))
+    grad_normed_two = feed_sum(partial.reshape(n_x, n_c, rows, width))
     grad_result = cotangent.astype(F32)
     grad_mid_norm, grad_gain_two = norm_back(middle, inverse_two, gain_two, grad_normed_two)
     grad_middle = grad_result + grad_mid_norm
-    grad_both = jnp.concatenate(
-        [dot_tn(normed_two, grad_gate_pre), dot_tn(normed_two, grad_up_pre)], axis=1
-    ).astype(BF)
-    grad_both = scatter_sum(grad_both, ("y", "z"))
-    grad_down = scatter_sum(dot_tn(hidden, grad_feed).astype(BF), ("y", "z"))
-    grad_both = grad_both.reshape(n_c, shard, 2, units).transpose(0, 2, 1, 3)
-    grad_both = swap(grad_both, "c")
-    grad_both = gather(grad_both.reshape(1, n_c, 2, shard, units), "x")
-    grad_down = gather(grad_down[None], "x")
 
     def collect(grads):
         parts = grads.reshape(n_x, n_c, shard, 2, units // 2).transpose(0, 3, 2, 1, 4)
@@ -932,11 +1135,9 @@
             whole = whole + dot_nt(parts[i], picked)
         return jnp.concatenate([whole[:shard], whole[shard:]], axis=1)
 
-    grad_gate = collect(grad_both[:, :, 0])
-    grad_up = collect(grad_both[:, :, 1])
-    grad_down = grad_down[:, :share].reshape(down_rows, width).astype(F32)
-
-    grad_branch = heads_gather(grad_middle.astype(BF)).reshape(group, width)
+    grad_branch, branch_two = heads_gather_and_branch(grad_middle.astype(BF), branch_part)
+    grad_branch = grad_branch.reshape(group, width)
+    output = (middle + branch_two).astype(BF)
     grad_mixed = dot_nt(grad_branch, out_heads).astype(BF)
     grad_attended = grad_mixed * live_group[:, None].astype(BF)
     grad_out = dot_tn(mixed, grad_branch).astype(BF)
@@ -944,13 +1145,16 @@
         queries_t, grad_attended, mixed, key_value, begin_lanes, slot_lanes, lse,
         cosine_group, sine_group,
     )
-    grad_kv, grad_latent_normed = keys_and_latents_sum(
+    out_rows = out_weight.shape[0]
+    grad_up_heads = dot_tn(latent_group, grad_query_raw).astype(BF)
+    grad_kv, grad_latent_normed, grad_out, grad_up_heads = keys_and_latents_sum(
         grad_kv.reshape(n_y, n_z, n_c, rows, 2 * SIZE),
         dot_nt(grad_query_raw, up_heads).astype(BF).reshape(n_y, n_c, rows, latent_width),
+        grad_out.reshape(n_z // n_c, n_c, out_rows, width),
+        grad_up_heads.reshape(n_y, n_z, n_c, q_rows, per_heads),
     )
     grad_key_raw = unrotate(grad_kv[:, :SIZE], cosine, sine).astype(BF)
     grad_value_raw = grad_kv[:, SIZE:].astype(BF)
-    grad_up_heads = dot_tn(latent_group, grad_query_raw).astype(BF)
     grad_latent_f, grad_gain_latent = norm_back(
         latent, inverse_latent, gain_latent, grad_latent_normed
     )
@@ -962,27 +1166,12 @@
     input_grad = grad_middle + grad_input_norm
 
     half_first = first_width // n_c
-    first_part = firsts_gather(
-        grad_firsts.reshape(rows, n_c, half_first).transpose(1, 0, 2)
-    ).reshape(group, half_first)
+    first_part, grad_both, grad_out, grad_up_heads = firsts_gather(
+        grad_firsts.reshape(rows, n_c, half_first).transpose(1, 0, 2),
+        grad_both.reshape(n_c, shard, 2 * units), grad_out, grad_up_heads,
+    )
+    first_part = first_part.reshape(group, half_first)
     grad_first = dot_tn(normed_part, first_part).astype(BF)
-
-    out_rows = out_weight.shape[0]
-    grad_out = grad_out.reshape(n_z // n_c, n_c, out_rows, width).transpose(1, 0, 2, 3)
-    grad_out = swap(grad_out, "c").reshape(n_z, out_rows * width)
-    grad_first = grad_first.reshape(n_z, n_c, shard, half_first).transpose(1, 0, 2, 3)
-    grad_first = swap(grad_first, "c").transpose(1, 2, 0, 3).reshape(n_z, shard * first_width)
-    grad_up_heads = grad_up_heads.reshape(n_y, n_z, n_c, q_rows, per_heads)
-    grad_up_heads = grad_up_heads.transpose(0, 2, 1, 3, 4).reshape(members, n_z, q_rows, per_heads)
-    grad_up_heads = swap(grad_up_heads, HEADS).transpose(1, 2, 0, 3).reshape(n_z, -1)
-    pieces = jnp.concatenate([grad_out, grad_first, grad_up_heads], axis=1)
-    pieces = lax.psum(scatter_sum(pieces, "z"), "x").astype(F32)[0]
-    at_first = out_rows * width
-    at_up = at_first + shard * first_width
-    grad_out = pieces[:at_first].reshape(out_rows, width)
-    grad_first = pieces[at_first:at_up].reshape(shard, first_width)
-    grad_q_up = pieces[at_up:].reshape(q_rows, -1)
-
     gains = jnp.concatenate(
         [
             grad_gain_one.reshape(span, shard),
@@ -991,13 +1180,24 @@
         ],
         axis=1,
     )
-    gains = lax.psum(scatter_sum(gains, ROW), "x")[0]
+    shares = gains.shape[1]
+    gains = jnp.pad(gains, ((0, 0), (0, 8 * 128 - shares))).reshape(n_y, n_z, n_c, 8, 128)
+    grad_first, gains, grad_down = last_sums(
+        grad_first.reshape(n_z, n_c, shard, half_first), gains, grad_down
+    )
+    gains = gains.reshape(-1)
+    grad_first = jnp.concatenate([grad_first[0], grad_first[1]], axis=1)
+    grad_out = grad_out.reshape(out_rows, width).astype(F32)
+    grad_q_up = grad_up_heads.transpose(3, 1, 2, 0, 4).reshape(q_rows, -1).astype(F32)
+    grad_gate = collect(grad_both[..., :units])
+    grad_up = collect(grad_both[..., units:])
+    grad_down = grad_down[:, :share].reshape(down_rows, width).astype(F32)
     return (
         output,
         input_grad,
         gains[:shard],
         grad_first[:, :latent_width],
-        gains[2 * shard :],
+        gains[2 * shard : shares],
         grad_q_up,
         grad_first[:, latent_width : latent_width + SIZE],
         grad_first[:, latent_width + SIZE :],

time: 924 us -> 639 us (0.69)
  blocking collectives: 161 us -> 0 us
  waiting for transfers between devices: 113 us -> 0.6 us
  Pallas kernels: 363 us -> 430 us
  other arithmetic: 72.7 us -> 34.2 us
  local copies, waits for them, and re-layouts: 76.1 us -> 44.5 us
  starting transfers between devices: 10.1 us -> 0.16 us
    unnamed x1 -> x0, blocking collectives: 122 us -> none
    pallas_call x8 -> x9, Pallas kernels: 318 us -> 386 us  [comm_call(): pl.pallas_call(body, name=name, out_shape=outs, in_specs=spaces, out_spec...]
    unnamed x9 -> x4, waiting for transfers between devices: 63.7 us -> 0.57 us
    concatenate x3 -> x2, other arithmetic: 40.6 us -> 4.42 us  [the longest x1 3.7 us: on_device(): jnp.concatenate([dot_tn(normed_two, grad_gate_pre).astype(BF), dot_tn(nor...]
    reduce_scatter x2, waiting for transfers between devices: 24.3 us -> 0.01 us  [scatter_sum(): return lax.psum_scatter(value, axes, scatter_dimension=0, tiled=True)]
    all_to_all x2 -> x0, blocking collectives: 19.4 us -> none  [swap(): return lax.all_to_all(value, axes, 0, 0, tiled=True)]
    all_gather x4 -> x2, waiting for transfers between devices: 16.8 us -> 0.02 us  [gather(): return lax.all_gather(value, axes, axis=0, tiled=True)]
    unnamed x102 -> x112, local copies, waits for them, and re-layouts: 26.4 us -> 14.8 us
  transfers between devices with their start and end apart: 10 -> 4, of which waited for: 4 -> 0; matrix products, arithmetic and copies ran while one was open for 15% -> 13% of each run, Pallas kernels for 25% -> 64%
where the time goes in v3:
time: 639 us; the launch traced here: 629 us
  Pallas kernels  430 us (67%)
  matrix products  104 us (16%)
  local copies, waits for them, and re-layouts  44.5 us (7%)
  other arithmetic  34.2 us (5%)
  between operations  14.9 us (2%)
    pallas_call x9, Pallas kernels, comm_call(): pl.pallas_call(body, name=name, out_shape=outs, in_specs=spaces, out_spec...  386 us
    dot_general x14, matrix products, dot_nt(): lax.dot_general(left, right, (((1,), (1,)), ((), ())), preferred_element_...  47.1 us
    dot_general x8, matrix products, dot(): return jnp.dot(left, right, preferred_element_type=F32)  32.3 us
    dot_general x6, matrix products, dot_tn(): lax.dot_general(left, right, (((0,), (0,)), ((), ())), preferred_element_...  25 us
    pallas_call x1, Pallas kernels, attend_back(): pl.pallas_call(attend_back_kernel, name='attend_back', out_shape=(jax.Sha...  24.8 us
    pallas_call x1, Pallas kernels, attend(): pl.pallas_call(attend_kernel, name='attend', out_shape=(jax.ShapeDtypeStr...  20.2 us
    unnamed x112, local copies, waits for them, and re-layouts  14.8 us
  transfers between devices with their start and end apart: 4, of which 0 were waited for; matrix products, arithmetic and copies ran while one was open for 13% of the time, Pallas kernels for 64%

profile of v3, /device:TPU:1, one launch (start us, length us, event | category | flops | bytes accessed | tf_op | source)
XLA Modules:
  0.0 629.2 jit_solution(15829115091976146668)
XLA Ops:
  10.3 1.9 convolution_convert_fusion.10
  12.8 1.9 convolution_convert_fusion.9
  17.8 96.0 %first_weights.1 = (bf16[4,4,2,64,1664]{4,3,2,1,0:T(8,128)(2,1)}, bf16[4,4,2,32,512]{4,3,2,1,0:T(8,128)(2,1)}, bf16[2,64,1536]{2,1,0:T(8,128)(2,1)}, bf16[2,2,4,...) custom-call(bf16[64,1664]{1,0:T(8,128)(2,1)} %fusion.44.first_ref, ...), custom_call_target="tpu_custom_call" | custom-call | tf_op jit(solution)/shard_map/first_weights/pallas_call | solution.py:297
  116.7 4.0 fusion.16
  124.7 36.4 %keys_and_latents.1 = (bf16[4,4,2,128,512]{4,3,2,1,0:T(8,128)(2,1)}, bf16[4,2,128,1024]{3,2,1,0:T(8,128)(2,1)}) custom-call(bf16[128,512]{1,0:T(8,128)(2,1)} %pad_maximum_fusion.6.kv_ref, bf16[128,1024]{1,0:T(8,128)(2,1)} %multiply_convert_fusion.4.lat_ref), custom_call_target="tpu_custom_call" | custom-call | tf_op jit(solution)/shard_map/keys_and_latents/pallas_call | solution.py:297
  162.9 2.9 fusion.94.q_ref
  165.9 20.2 %attend.1 = (bf16[1024,512]{1,0:T(8,128)(2,1)S(1)}, bf16[4,256,512]{2,1,0:T(8,128)(2,1)S(1)}, f32[4,1,512]{2,1,0:T(1,128)S(1)}) custom-call(f32[1024,512]{1,0:T(8,128)S(1)} %fusion.94.q_ref, bf16[4096,512]{1,0:T(8,128)(2,1)} %bitcast.140, s32[4,1,512]{2,1,0:T(1,128)S(1)} %tile.28.begin_ref, s32[4,1,512]{2,1,0:T(1,128)S(1)} %tile.30.slot_ref, ...), custom_call_target="tpu_custom_call" | custom-call | tf_op jit(solution)/shard_map/attend/pallas_call | solution.py:136
  186.0 4.4 convolution_convert_fusion
  190.4 29.7 %heads_sum_and_cotangent.1 = (f32[128,2048]{1,0:T(8,128)}, bf16[4,2,128,2048]{3,2,1,0:T(8,128)(2,1)}) custom-call(bf16[4,2,128,2048]{3,2,1,0:T(8,128)(2,1)} %bitcast.144, bf16[128,2048]{1,0:T(8,128)(2,1)} %cot_ref.1), custom_call_target="tpu_custom_call" | custom-call | tf_op jit(solution)/shard_map/heads_sum_and_cotangent/pallas_call | solution.py:297
  223.6 25.9 %feed_gather.1 = (bf16[4,2,128,2048]{3,2,1,0:T(8,128)(2,1)}, bf16[4,2,128,512]{3,2,1,0:T(8,128)(2,1)}) custom-call(bf16[128,2048]{1,0:T(8,128)(2,1)} %multiply_convert_fusion.3.two_ref, bf16[128,2048]{1,0:T(8,128)(2,1)} %copy-done.18), custom_call_target="tpu_custom_call" | custom-call | tf_op jit(solution)/shard_map/feed_gather/pallas_call | solution.py:297
  249.5 8.2 %fusion.95 = f32[1024,768]{1,0:T(8,128)} fusion(bf16[1024,2048]{1,0:T(8,128)(2,1)} %bitcast.193, bf16[768,2048]{1,0:T(8,128)(2,1)} %all-gather.3.cloned.1.call-done), kind=kOutput, calls=%fused_computation.194 | convolution fusion | flops 3221225472 | bytes 10485760 | tf_op jit(solution)/shard_map/dot_general | solution.py:33
  257.7 6.3 fusion.20
  264.8 5.8 multiply_convert_fusion
  271.8 5.3 convolution_convert_fusion.2
  277.1 6.3 convolution_convert_fusion.4
  283.4 3.9 convolution_convert_fusion.3
  287.2 3.7 pad_maximum_fusion
  291.0 5.5 fusion.18
  296.5 5.0 convolution_convert_fusion.1
  301.5 5.1 add_convert_fusion
  306.6 8.8 %copy.74 = bf16[2048,1536]{1,0:T(8,128)(2,1)} copy(bf16[2048,1536]{0,1:T(8,128)(2,1)} %pad_maximum_fusion) | data formatting | bytes 12582912
  316.0 2.9 fusion.3
  319.6 26.2 %feed_sum.1 = f32[128,2048]{1,0:T(8,128)} custom-call(bf16[4,2,128,2048]{3,2,1,0:T(8,128)(2,1)} %bitcast.142), custom_call_target="tpu_custom_call" | custom-call | tf_op jit(solution)/shard_map/feed_sum/pallas_call | solution.py:297
  347.4 2.6 fusion.75.ref
  350.0 41.3 %heads_gather_and_branch.1 = (bf16[4,2,128,2048]{3,2,1,0:T(8,128)(2,1)}, f32[128,2048]{1,0:T(8,128)}) custom-call(bf16[128,2048]{1,0:T(8,128)(2,1)} %fusion.75.ref, bf16[4,2,128,2048]{3,2,1,0:T(8,128)(2,1)} %bitcast.143), custom_call_target="tpu_custom_call" | custom-call | tf_op jit(solution)/shard_map/heads_gather_and_branch/pallas_call | solution.py:297
  391.3 4.7 fusion.25.do_ref
  396.1 24.8 %attend_back.1 = (bf16[1024,512]{1,0:T(8,128)(2,1)S(1)}, bf16[4096,512]{1,0:T(8,128)(2,1)}) custom-call(bf16[4,256,512]{2,1,0:T(8,128)(2,1)S(1)} %get-tuple-element.58.qt_ref, bf16[1024,512]{1,0:T(8,128)(2,1)S(1)} %fusion.25.do_ref, bf16[1024,512]{1,0:T(8,128)(2,1)S(1)} %get-tuple-element.49.o_ref, bf16[4096,512]{1,0:T(8,128)(2,1)} %bitcast.141, ...), custom_call_target="tpu_custom_call" | custom-call | tf_op jit(solution)/shard_map/attend_back/pallas_call | solution.py:213
  420.8 2.6 convolution_convert_fusion.6
  423.4 2.3 convolution_convert_fusion.7
  425.7 3.7 convolution_convert_fusion.5
  429.4 60.2 %keys_and_latents_sum.1 = (f32[128,512]{1,0:T(8,128)}, f32[128,1024]{1,0:T(8,128)}, bf16[4,32,2048]{2,1,0:T(8,128)(2,1)}, bf16[4,4,2,32,128]{4,3,2,1,0:T(8,128)(2,1)}) custom-call(bf16[4,4,2,128,512]{4,3,2,1,0:T(8,128)(2,1)} %bitcast.145, bf16[4,2,128,1024]{3,2,1,0:T(8,128)(2,1)} %bitcast.148, bf16[2,2,128,2048]{3,2,1,0:T(8,128)(2,1)} %bitcast.149, ...), custom_call_target="tpu_custom_call" | custom-call | tf_op jit(solution)/shard_map/keys_and_latents_sum/pallas_call | solution.py:297
  496.2 6.2 fusion.36
  503.3 3.3 fusion.32
  506.7 42.1 %firsts_gather.1 = (bf16[4,2,128,768]{3,2,1,0:T(8,128)(2,1)}, bf16[4,2,64,1536]{3,2,1,0:T(8,128)(2,1)}, bf16[4,32,2048]{2,1,0:T(8,128)(2,1)}, bf16[4,4,2,32,128]{4,3,2,1,0:T(8,128)(2,1)}) custom-call(bf16[2,128,768]{2,1,0:T(8,128)(2,1)} %bitcast.151, bf16[2,64,1536]{2,1,0:T(8,128)(2,1)} %bitcast.169, bf16[4,32,2048]{2,1,0:T(8,128)(2,1)} %get-tuple-element.67.out_ref, ...), custom_call_target="tpu_custom_call" | custom-call | tf_op jit(solution)/shard_map/firsts_gather/pallas_call | solution.py:297
  548.7 3.6 bitcast_convert_fusion
  552.4 27.7 %last_sums.1 = (f32[2,64,768]{2,1,0:T(8,128)}, f32[8,128]{1,0:T(8,128)}, bf16[4,48,2048]{2,1,0:T(8,128)(2,1)}) custom-call(bf16[4,2,64,768]{3,2,1,0:T(8,128)(2,1)} %bitcast.164, f32[4,4,2,8,128]{4,3,2,1,0:T(8,128)} %bitcast.167, bf16[48,2048]{1,0:T(8,128)(2,1)} %reduce-scatter.5.cloned.1.call-done.down_ref), custom_call_target="tpu_custom_call" | custom-call | tf_op jit(solution)/shard_map/last_sums/pallas_call | solution.py:297
  582.6 2.8 fusion.84
  585.4 2.7 reshape.361
  588.1 1.9 copy.92
  592.4 1.9 convolution_add_fusion.2
  594.3 1.9 convolution_add_fusion.1
  596.3 1.9 convolution_add_fusion
  599.4 2.9 reshape.360
  602.3 1.9 copy.93
  606.6 1.9 convolution_add_fusion.5
  608.5 1.9 convolution_add_fusion.4
  610.5 1.9 convolution_add_fusion.3
  617.9 2.2 bitcast_convert_fusion.1
  (221 shorter events, 46.9 us)
Async XLA Ops:
  7.2 242.3 %all-gather.3.cloned.1.call-start = ((), (), s32[]{:S(2)}) async-start(), calls=%async_computation.2 | async-start | bytes 3342336 | tf_op jit(solution)/shard_map/all_gather | solution.py:990
  9.1 248.6 %all-gather.5.cloned.1.call-start = ((), (), s32[]{:S(2)}) async-start(), calls=%async_computation.3 | async-start | bytes 6684672 | tf_op jit(solution)/shard_map/all_gather | solution.py:990
  12.7 2.4 copy-start.41
  12.8 2.5 copy-start.28
  12.8 2.5 copy-start.29
  12.8 2.6 copy-start.24
  12.8 3.6 copy-start.25
  12.8 3.6 copy-start.26
  12.8 3.5 copy-start.27
  14.8 100.7 %copy-start.42 = (s32[1,4]{1,0:T(1,128)S(1)}, s32[1,4]{1,0:T(1,128)}, u32[]{:S(2)}) copy-start(s32[1,4]{1,0:T(1,128)} %param.16) | copy-start | bytes 52
  14.8 101.5 %copy-start.7 = (bf16[128,2048]{1,0:T(8,128)(2,1)S(1)}, bf16[128,2048]{1,0:T(8,128)(2,1)}, u32[]{:S(2)}) copy-start(bf16[128,2048]{1,0:T(8,128)(2,1)} %param.14) | copy-start | bytes 1572868
  113.9 392.7 %reduce-scatter.7.cloned.1.call-start = ((), (), s32[]{:S(2)}) async-start(), calls=%async_computation.5 | async-start | bytes 6684672 | tf_op jit(solution)/shard_map/reduce_scatter | solution.py:994
  116.6 4.0 copy-start.18
  116.7 46.3 %copy-start.39 = (bf16[4,4,2,32,512]{4,3,2,1,0:T(8,128)(2,1)S(1)}, bf16[4,4,2,32,512]{4,3,2,1,0:T(8,128)(2,1)}, u32[]{:S(2)}) copy-start(bf16[4,4,2,32,512]{4,3,2,1,0:T(8,128)(2,1)} %get-tuple-element.47) | copy-start | bytes 3145732
  120.7 40.4 %copy-start.10 = (f32[128,1536]{1,0:T(8,128)}, f32[128,1536]{1,0:T(8,128)S(1)}, u32[]{:S(2)}) copy-start(f32[128,1536]{1,0:T(8,128)S(1)} %fusion.16) | copy-start | bytes 2359300
  165.9 20.2 %copy-start.36 = (bf16[2,2,4,32,2048]{4,3,2,1,0:T(8,128)(2,1)S(1)}, bf16[2,2,4,32,2048]{4,3,2,1,0:T(8,128)(2,1)}, u32[]{:S(2)}) copy-start(bf16[2,2,4,32,2048]{4,3,2,1,0:T(8,128)(2,1)} %get-tuple-element.50) | copy-start | bytes 6291460
  190.4 29.7 %copy-start.8 = (bf16[128,2048]{1,0:T(8,128)(2,1)S(1)}, bf16[128,2048]{1,0:T(8,128)(2,1)}, u32[]{:S(2)}) copy-start(bf16[128,2048]{1,0:T(8,128)(2,1)} %param.14) | copy-start | bytes 1572868
  257.7 6.3 %copy-start.30 = (bf16[2048,1536]{1,0:T(8,128)(2,1)S(1)}, bf16[2048,1536]{1,0:T(8,128)(2,1)}, u32[]{:S(2)}) copy-start(bf16[2048,1536]{1,0:T(8,128)(2,1)} %all-gather.5.cloned.1.call-done) | copy-start | bytes 18874372
  257.7 6.3 %copy-start.32 = (bf16[4,2,128,2048]{3,2,1,0:T(8,128)(2,1)S(1)}, bf16[4,2,128,2048]{3,2,1,0:T(8,128)(2,1)}, u32[]{:S(2)}) copy-start(bf16[4,2,128,2048]{3,2,1,0:T(8,128)(2,1)} %get-tuple-element.53) | copy-start | bytes 12582916
  257.7 7.1 %copy-start.46 = (f32[1024,768]{1,0:T(8,128)S(1)}, f32[1024,768]{1,0:T(8,128)}, u32[]{:S(2)}) copy-start(f32[1024,768]{1,0:T(8,128)} %fusion.95) | copy-start | bytes 9437188
  264.8 7.0 %copy-start.31 = (bf16[4,2,128,2048]{3,2,1,0:T(8,128)(2,1)S(1)}, bf16[4,2,128,2048]{3,2,1,0:T(8,128)(2,1)}, u32[]{:S(2)}) copy-start(bf16[4,2,128,2048]{3,2,1,0:T(8,128)(2,1)} %get-tuple-element.52) | copy-start | bytes 12582916
  277.1 6.3 %copy-start.33 = (bf16[4,2,128,2048]{3,2,1,0:T(8,128)(2,1)S(1)}, bf16[4,2,128,2048]{3,2,1,0:T(8,128)(2,1)}, u32[]{:S(2)}) copy-start(bf16[4,2,128,2048]{3,2,1,0:T(8,128)(2,1)} %get-tuple-element.53) | copy-start | bytes 12582916
  277.1 6.3 %copy-start.47 = (bf16[1024,768]{1,0:T(8,128)(2,1)S(1)}, bf16[1024,768]{1,0:T(8,128)(2,1)}, u32[]{:S(2)}) copy-start(bf16[1024,768]{1,0:T(8,128)(2,1)} %get-tuple-element.87) | copy-start | bytes 4718596
  287.2 3.7 copy-start.45
  290.9 5.5 copy-start.35
  290.9 5.5 copy-start.44
  291.0 10.5 %slice-start = ((s8[6291456]{0:T(1024)(128)(4,1)}), s8[4194304]{0:T(1024)(128)(4,1)S(1)}, s32[]{:S(2)}) async-start(s8[6291456]{0:T(1024)(128)(4,1)} %bitcast.191), calls=%async_computation.6 | async-start | bytes 8388608
  296.5 5.0 slice-start.1
  315.4 237.0 %reduce-scatter.5.cloned.1.call-start = ((), (), s32[]{:S(2)}) async-start(), calls=%async_computation.4 | async-start | bytes 3342336 | tf_op jit(solution)/shard_map/reduce_scatter | solution.py:994
  316.0 29.9 %copy-start.3 = (f32[128,2048]{1,0:T(8,128)S(1)}, f32[128,2048]{1,0:T(8,128)}, u32[]{:S(2)}) copy-start(f32[128,2048]{1,0:T(8,128)} %copy-done.2) | copy-start | bytes 3145732
  318.9 28.5 %copy-start.12 = (bf16[128,2048]{1,0:T(8,128)(2,1)S(1)}, bf16[128,2048]{1,0:T(8,128)(2,1)}, u32[]{:S(2)}) copy-start(bf16[128,2048]{1,0:T(8,128)(2,1)} %cot_ref.1) | copy-start | bytes 1572868
  347.4 43.9 %copy-start.37 = (bf16[2,2,4,32,2048]{4,3,2,1,0:T(8,128)(2,1)S(1)}, bf16[2,2,4,32,2048]{4,3,2,1,0:T(8,128)(2,1)}, u32[]{:S(2)}) copy-start(bf16[2,2,4,32,2048]{4,3,2,1,0:T(8,128)(2,1)} %get-tuple-element.50) | copy-start | bytes 6291460
  396.1 24.8 %copy-start.40 = (bf16[4,4,2,32,512]{4,3,2,1,0:T(8,128)(2,1)S(1)}, bf16[4,4,2,32,512]{4,3,2,1,0:T(8,128)(2,1)}, u32[]{:S(2)}) copy-start(bf16[4,4,2,32,512]{4,3,2,1,0:T(8,128)(2,1)} %get-tuple-element.47) | copy-start | bytes 3145732
  420.8 2.6 copy-start.38
  429.4 61.2 %copy-start.11 = (f32[128,1536]{1,0:T(8,128)S(1)}, f32[128,1536]{1,0:T(8,128)}, u32[]{:S(2)}) copy-start(f32[128,1536]{1,0:T(8,128)} %copy-done.10) | copy-start | bytes 2359300
  489.6 6.6 %copy-start.9 = (bf16[128,2048]{1,0:T(8,128)(2,1)S(1)}, bf16[128,2048]{1,0:T(8,128)(2,1)}, u32[]{:S(2)}) copy-start(bf16[128,2048]{1,0:T(8,128)(2,1)} %param.14) | copy-start | bytes 1572868
  496.2 7.2 %copy-start.4 = (f32[128,2048]{1,0:T(8,128)S(1)}, f32[128,2048]{1,0:T(8,128)}, u32[]{:S(2)}) copy-start(f32[128,2048]{1,0:T(8,128)} %copy-done.2) | copy-start | bytes 3145732
  496.2 7.2 %copy-start.6 = (f32[128,2048]{1,0:T(8,128)S(1)}, f32[128,2048]{1,0:T(8,128)}, u32[]{:S(2)}) copy-start(f32[128,2048]{1,0:T(8,128)} %feed_sum.1) | copy-start | bytes 3145732
  496.2 7.2 %copy-start.13 = (bf16[128,2048]{1,0:T(8,128)(2,1)S(1)}, bf16[128,2048]{1,0:T(8,128)(2,1)}, u32[]{:S(2)}) copy-start(bf16[128,2048]{1,0:T(8,128)(2,1)} %cot_ref.1) | copy-start | bytes 1572868
  582.6 8.2 %copy-start.5 = (pred[2816,768]{1,0:T(32,128)(4,1)S(1)}, pred[2816,768]{1,0:T(32,128)(4,1)}, u32[]{:S(2)}) copy-start(pred[2816,768]{1,0:T(32,128)(4,1)} %fusion.3) | copy-start | bytes 6488068
  610.5 3.2 copy-start.20
  612.4 2.6 copy-start.22
  613.6 2.9 copy-start.23
  613.8 6.3 %copy-start.14 = (f32[64,2816]{1,0:T(8,128)S(1)}, f32[64,2816]{1,0:T(8,128)}, u32[]{:S(2)}) copy-start(f32[64,2816]{1,0:T(8,128)} %get-tuple-element.90) | copy-start | bytes 2162692
  615.0 5.0 copy-start.15
  615.1 6.2 copy-start.16
  616.5 6.0 copy-start.1
  617.9 3.4 copy-start.17
  (6 other events, 8.6 us)
Sparse Core Ops, SparseCore 0:
  10.8 71.8 all-gather.2
  114.0 69.7 all-gather.4
  315.5 91.0 reduce-scatter.6
  409.8 82.0 reduce-scatter.4

commit v4 on v3

v4 whole, which is shorter than its diff:
```python
import functools
import math

import jax
import jax.numpy as jnp
from jax import lax
from jax.experimental import pallas as pl
from jax.experimental.pallas import tpu as pltpu
from jax.sharding import Mesh
from jax.sharding import PartitionSpec as P

EPSILON = 1e-06
MASKED = -1e30
BF = jnp.bfloat16
F32 = jnp.float32
SIZE = 256
HALF = 128
BLOCK = 256
ROW = ("y", "z", "c")
HEADS = ("y", "c")
FEED = ("x", "c")


def dot(left, right):
    return jnp.dot(left, right, preferred_element_type=F32)


def dot_tn(left, right):
    return lax.dot_general(left, right, (((0,), (0,)), ((), ())), preferred_element_type=F32)


def dot_nt(left, right):
    return lax.dot_general(left, right, (((1,), (1,)), ((), ())), preferred_element_type=F32)


def norm_back(values, inverse, gain, grad):
    scaled = grad * gain
    grad_values = inverse * scaled - values * inverse * inverse * inverse * jnp.mean(
        scaled * values, axis=-1, keepdims=True
    )
    return grad_values, jnp.sum(grad * values * inverse, axis=0)


def places_of(lengths_row, slots):
    ends = jnp.cumsum(lengths_row)
    begins = jnp.concatenate([ends - lengths_row, ends[-1:]])
    begin = jnp.max(jnp.where(slots[:, None] >= begins[None, :], begins[None, :], 0), axis=1)
    live = (slots < ends[-1]).astype(F32)
    return begin, live


def tables(position):
    freq = jnp.exp(jnp.arange(HALF, dtype=F32) * (-math.log(10000.0) / HALF))
    angle = position.astype(F32)[:, None] * freq[None, :]
    return jnp.cos(angle), jnp.sin(angle)


def tables_across(position):
    freq = jnp.exp(jnp.arange(HALF, dtype=F32) * (-math.log(10000.0) / HALF))
    angle = position.astype(F32)[..., None, :] * freq[:, None]
    return jnp.cos(angle), jnp.sin(angle)


def rotate(values, cosine, sine):
    lower, upper = values[..., :HALF], values[..., HALF:]
    return jnp.concatenate([lower * cosine - upper * sine, upper * cosine + lower * sine], axis=-1)


def unrotate(grad, cosine, sine):
    lower, upper = grad[..., :HALF], grad[..., HALF:]
    return jnp.concatenate([lower * cosine + upper * sine, upper * cosine - lower * sine], axis=-1)


def turned(source, target, count, columns):
    @pl.loop(0, count)
    def _(block):
        at = pl.ds(pl.multiple_of(block * BLOCK, BLOCK), BLOCK)
        target[:, at] = source[at, columns].T


KEYS, VALUES = slice(0, SIZE), slice(SIZE, 2 * SIZE)


def attend_kernel(
    q_ref, kv_ref, begin_ref, slot_ref, live_ref, cos_ref, sin_ref,
    out_ref, qt_ref, lse_ref, vt, peak, total, accum,
):
    depth = lax.axis_index("z")
    segments = slot_ref.shape[0]
    rows = slot_ref.shape[2]
    tokens = rows // 2
    turned(kv_ref, vt, segments * (segments - 1) + depth + 1, VALUES)
    for seg in range(segments):
        here = pl.ds(seg * tokens, tokens)
        cosine, sine = cos_ref[seg], sin_ref[seg]
        for head in range(2):
            raw = q_ref[here, head * SIZE : (head + 1) * SIZE].T
            lower, upper = raw[:HALF], raw[HALF:]
            turn = jnp.concatenate(
                [lower * cosine - upper * sine, upper * cosine + lower * sine], axis=0
            )
            qt_ref[seg, :, head * tokens : (head + 1) * tokens] = (
                turn.astype(BF) * (SIZE ** -0.5)
            ).astype(BF)
        query = qt_ref[seg]
        begin = begin_ref[seg]
        slot = slot_ref[seg]
        peak[...] = jnp.full_like(peak, MASKED)
        total[...] = jnp.zeros_like(total)
        accum[...] = jnp.zeros_like(accum)

        @pl.loop(0, segments * seg + depth + 1)
        def _(block):
            at = pl.multiple_of(block * BLOCK, BLOCK)
            scores = dot(kv_ref[pl.ds(at, BLOCK), KEYS], query)
            key = lax.broadcasted_iota(jnp.int32, scores.shape, 0) + at
            scores = jnp.where((key >= begin) & (key <= slot), scores, MASKED)
            before = peak[...]
            now = jnp.maximum(before, jnp.max(scores, axis=0, keepdims=True))
            weights = jnp.exp(scores - now)
            shrink = jnp.exp(before - now)
            peak[...] = now
            total[...] = total[...] * shrink + jnp.sum(weights, axis=0, keepdims=True)
            accum[...] = accum[...] * shrink + dot(vt[:, pl.ds(at, BLOCK)], weights.astype(BF))

        lse_ref[seg] = peak[...] + jnp.log(total[...])
        result = accum[...] * (live_ref[seg] / total[...])
        for head in range(2):
            out_ref[here, head * SIZE : (head + 1) * SIZE] = (
                result[:, head * tokens : (head + 1) * tokens].T.astype(BF)
            )


def attend(q, kv, begin, slot, live, cosine, sine):
    segments, _, rows = slot.shape
    return pl.pallas_call(
        attend_kernel,
        name="attend",
        out_shape=(
            jax.ShapeDtypeStruct(q.shape, BF),
            jax.ShapeDtypeStruct((segments, SIZE, rows), BF),
            jax.ShapeDtypeStruct((segments, 1, rows), F32),
        ),
        in_specs=[pl.BlockSpec(memory_space=pltpu.VMEM)] * 7,
        out_specs=[pl.BlockSpec(memory_space=pltpu.VMEM)] * 3,
        scratch_shapes=[
            pltpu.VMEM((SIZE, kv.shape[0]), BF),
            pltpu.VMEM((1, rows), F32),
            pltpu.VMEM((1, rows), F32),
            pltpu.VMEM((SIZE, rows), F32),
        ],
        compiler_params=pltpu.CompilerParams(vmem_limit_bytes=48 << 20),
    )(q, kv, begin, slot, live, cosine, sine)


MESH_IDS = pl.DeviceIdType.MESH
AXES = ("x", "y", "z", "c")
ANYWHERE = pl.BlockSpec(memory_space=pl.ANY)
IN_VMEM = pl.BlockSpec(memory_space=pltpu.VMEM)


def place():
    return {a: lax.axis_index(a) for a in AXES}


def along(axis, step):
    size = lax.axis_size(axis)
    return lax.rem(lax.axis_index(axis) + (step + size), size)


def device(axis, step):
    here = place()
    here[axis] = along(axis, step)
    return tuple(here[a] for a in AXES)


class Net:
    def __init__(self, sends, arrivals, locals_):
        self.sends, self.arrivals, self.locals_ = sends, arrivals, locals_
        self.used = 0
        self.near = 0
        self.open = []

    def send(self, source, target, axis, step):
        copy = pltpu.make_async_remote_copy(
            src_ref=source, dst_ref=target, send_sem=self.sends.at[self.used],
            recv_sem=self.arrivals.at[self.used], device_id=device(axis, step),
            device_id_type=MESH_IDS,
        )
        copy.start()
        self.used += 1
        self.open.append(copy)
        return copy

    def keep(self, source, target):
        copy = pltpu.make_async_copy(source, target, self.locals_.at[self.near])
        copy.start()
        self.near += 1
        return copy

    def close(self):
        for copy in self.open:
            copy.wait_send()


def greet(partners):
    barrier = pltpu.get_barrier_semaphore()
    for axis, step in partners:
        pl.semaphore_signal(barrier, 1, device_id=device(axis, step), device_id_type=MESH_IDS)
    pl.semaphore_wait(barrier, len(partners))


def semaphores(sends, locals_):
    return [
        pltpu.SemaphoreType.DMA((sends,)),
        pltpu.SemaphoreType.DMA((sends,)),
        pltpu.SemaphoreType.DMA((max(locals_, 1),)),
    ]


def comm_call(body, name, number, outs, ins, scratch, sends, locals_, spaces, out_spaces):
    return pl.pallas_call(
        body,
        name=name,
        out_shape=outs,
        in_specs=spaces,
        out_specs=out_spaces,
        scratch_shapes=list(scratch) + semaphores(sends, locals_),
        compiler_params=pltpu.CompilerParams(
            collective_id=number, has_side_effects=True, vmem_limit_bytes=60 << 20
        ),
    )(*ins)


LINE = (1, 2, 3)


class RowGather:
    def __init__(self, net, value, out):
        self.net, self.out = net, out
        h = value.shape[0] // 2
        self.parts = (pl.ds(0, h), pl.ds(h, h))
        y, z, c = (lax.axis_index(a) for a in ROW)
        self.mine = net.keep(value, out.at[y, z, c])
        self.own = net.send(value, out.at[y, z, c], "c", 1)
        self.first = [
            [net.send(value.at[part], out.at[y, z, c, part], axis, d) for d in LINE]
            for part, axis in zip(self.parts, ("z", "y"))
        ]

    def spread(self):
        net, out = self.net, self.out
        y, z, c = (lax.axis_index(a) for a in ROW)
        self.mine.wait()
        (a, b) = self.parts
        for copy in self.first[0]:
            copy.wait_recv()
        self.second = [
            [net.send(out.at[y, :, c, a], out.at[y, :, c, a], "y", d) for d in LINE]
        ]
        for copy in self.first[1]:
            copy.wait_recv()
        self.second.append(
            [net.send(out.at[:, z, c, b], out.at[:, z, c, b], "z", d) for d in LINE]
        )
        self.shared = [self.own]
        for d in LINE:
            spot = out.at[y, along("z", -d), c, a]
            self.shared.append(net.send(spot, spot, "c", 1))
            spot = out.at[along("y", -d), z, c, b]
            self.shared.append(net.send(spot, spot, "c", 1))

    def finish(self):
        net, out = self.net, self.out
        y, z, c = (lax.axis_index(a) for a in ROW)
        (a, b) = self.parts
        for d in LINE:
            self.second[0][d - 1].wait_recv()
            spot = out.at[along("y", -d), :, c, a]
            self.shared.append(net.send(spot, spot, "c", 1))
            self.second[1][d - 1].wait_recv()
            spot = out.at[:, along("z", -d), c, b]
            self.shared.append(net.send(spot, spot, "c", 1))
        for copy in self.shared:
            copy.wait_recv()


class RingGather:
    def __init__(self, net, value, out, axis):
        self.net, self.out, self.axis = net, out, axis
        a, c = lax.axis_index(axis), lax.axis_index("c")
        h = value.shape[0] // 2
        self.parts = one, two = pl.ds(0, h), pl.ds(h, h)
        self.mine = net.keep(value, out.at[a, c])
        self.right = [net.send(value.at[p], out.at[a, c, p], axis, 1) for p in (one, two)]
        self.left = [net.send(value.at[p], out.at[a, c, p], axis, -1) for p in (two, one)]
        self.shared = [net.send(value, out.at[a, c], "c", 1)]

    def forward(self):
        net, out, axis = self.net, self.out, self.axis
        c = lax.axis_index("c")
        one, two = self.parts
        before, after = along(axis, -1), along(axis, 1)
        self.right[0].wait_recv()
        spot = out.at[before, c, one]
        self.far = [net.send(spot, spot, axis, 1)]
        self.left[0].wait_recv()
        spot = out.at[after, c, two]
        self.far.append(net.send(spot, spot, axis, -1))

    def share(self):
        c = lax.axis_index("c")
        for copies, step in ((self.right, -1), (self.left, 1)):
            copies[1].wait_recv()
            spot = self.out.at[along(self.axis, step), c]
            self.shared.append(self.net.send(spot, spot, "c", 1))

    def finish(self):
        for copy in self.far:
            copy.wait_recv()
        spot = self.out.at[along(self.axis, 2), lax.axis_index("c")]
        self.shared.append(self.net.send(spot, spot, "c", 1))
        for copy in self.shared:
            copy.wait_recv()
        self.mine.wait()


STEP = 16


def rows_loop(count, body):
    pl.loop(0, count // STEP)(lambda i: body(pl.ds(pl.multiple_of(i * STEP, STEP), STEP)))


def shifted(rows, first):
    return pl.ds(pl.multiple_of(rows.start + first, STEP), STEP)


class RingSum:
    def __init__(self, net, value, out, axis, near, relay, come, go):
        self.net, self.value, self.out, self.axis = net, value, out, axis
        self.near, self.relay, self.come, self.go = near, relay, come, go
        c = lax.axis_index("c")
        self.size = value.shape[2]
        h = self.size // 2
        self.parts = pl.ds(0, h), pl.ds(h, h)
        self.swaps = {
            s: net.send(value.at[along(axis, s), 1 - c], near.at[s], "c", 1) for s in (2, 1, 3, 0)
        }

    def pair(self, s, part=None):
        value, near, go = self.value, self.near, self.go
        where, c = along(self.axis, s), lax.axis_index("c")
        first = 0 if part is None else part.start
        count = self.size if part is None else part.size

        def add(rows):
            at = shifted(rows, first)
            go[s, at] = (
                value[where, c, at].astype(F32) + near[s, at].astype(F32)
            ).astype(BF)

        rows_loop(count, add)

    def relay_far(self):
        net = self.net
        one, two = self.parts
        self.swaps[2].wait_recv()
        self.pair(2)
        self.relays = [
            net.send(self.go.at[2, one], self.relay.at[0], self.axis, 1),
            net.send(self.go.at[2, two], self.relay.at[1], self.axis, -1),
        ]

    def issue(self):
        net, go, come = self.net, self.go, self.come
        one, two = self.parts
        self.swaps[1].wait_recv()
        self.pair(1)
        self.ends = [net.send(go.at[1, two], come.at[0, two], self.axis, 1)]
        self.swaps[3].wait_recv()
        self.pair(3)
        self.ends.append(net.send(go.at[3, one], come.at[1, one], self.axis, -1))

    def pass_on(self):
        net, go, relay, come = self.net, self.go, self.relay, self.come
        one, two = self.parts
        for i, (s, part, step) in enumerate(((1, one, 1), (3, two, -1))):
            self.relays[i].wait_recv()

            def add(rows, i=i, s=s, part=part):
                at = shifted(rows, part.start)
                go[s, at] = (go[s, at].astype(F32) + relay[i, rows].astype(F32)).astype(BF)

            rows_loop(part.size, add)
            self.ends.append(net.send(go.at[s, part], come.at[i, part], self.axis, step))

    def finish(self):
        value, near, come, out = self.value, self.near, self.come, self.out
        where, c = lax.axis_index(self.axis), lax.axis_index("c")
        self.swaps[0].wait_recv()
        for copy in self.ends:
            copy.wait_recv()

        def add(rows):
            out[rows] = (
                value[where, c, rows].astype(F32) + near[0, rows].astype(F32)
            ) + (come[0, rows].astype(F32) + come[1, rows].astype(F32))

        rows_loop(self.size, add)


def ring_sum_scratch(size, width):
    return [
        pltpu.VMEM((4, size, width), BF),
        pltpu.VMEM((2, size // 2, width), BF),
        pltpu.VMEM((2, size, width), BF),
        pltpu.VMEM((4, size, width), BF),
    ]


class RowSum:
    def __init__(self, net, value, out, near, go, first, mid, last):
        self.net, self.value, self.out = net, value, out
        self.near, self.go, self.first, self.mid, self.last = near, go, first, mid, last
        c = lax.axis_index("c")
        self.size = value.shape[3]
        h = self.size // 2
        self.parts = pl.ds(0, h), pl.ds(h, h)
        self.swaps = [
            net.send(value.at[i, :, 1 - c], near.at[i], "c", 1) for i in range(4)
        ]

    def start(self):
        net, value, near, go = self.net, self.value, self.near, self.go
        c = lax.axis_index("c")
        for i in range(4):
            self.swaps[i].wait_recv()
            for j in range(4):

                def add(rows, i=i, j=j):
                    go[i, j, rows] = (
                        value[i, j, c, rows].astype(F32) + near[i, j, rows].astype(F32)
                    ).astype(BF)

                rows_loop(self.size, add)
        a, b = self.parts
        self.ones = [
            [net.send(go.at[along("y", d), :, a], self.first.at[0, d - 1], "y", d) for d in LINE],
            [net.send(go.at[:, along("z", d), b], self.first.at[1, d - 1], "z", d) for d in LINE],
        ]

    def turn(self):
        net, go, first, mid = self.net, self.go, self.first, self.mid
        y, z = lax.axis_index("y"), lax.axis_index("z")
        self.twos = []
        for k, axis in enumerate(("z", "y")):
            for copy in self.ones[k]:
                copy.wait_recv()
            for j in range(4):

                def add(rows, k=k, j=j):
                    at = shifted(rows, self.parts[k].start)
                    own = go[y, j, at] if k == 0 else go[j, z, at]
                    mid[k, j, rows] = (
                        own.astype(F32) + first[k, 0, j, rows].astype(F32)
                        + (first[k, 1, j, rows].astype(F32) + first[k, 2, j, rows].astype(F32))
                    ).astype(BF)

                rows_loop(self.parts[k].size, add)
            self.twos.append(
                [net.send(mid.at[k, along(axis, d)], self.last.at[k, d - 1], axis, d) for d in LINE]
            )

    def finish(self):
        mid, last, out = self.mid, self.last, self.out
        for k, axis in enumerate(("z", "y")):
            for copy in self.twos[k]:
                copy.wait_recv()
            here = lax.axis_index(axis)

            def add(rows, k=k, here=here):
                at = shifted(rows, self.parts[k].start)
                out[at] = (
                    mid[k, here, rows].astype(F32) + last[k, 0, rows].astype(F32)
                    + (last[k, 1, rows].astype(F32) + last[k, 2, rows].astype(F32))
                )

            rows_loop(self.parts[k].size, add)


def row_sum_scratch(size, width):
    h = size // 2
    return [
        pltpu.VMEM((4, 4, size, width), BF),
        pltpu.VMEM((4, 4, size, width), BF),
        pltpu.VMEM((2, 3, 4, h, width), BF),
        pltpu.VMEM((2, 4, h, width), BF),
        pltpu.VMEM((2, 3, h, width), BF),
    ]


Y_LINE = [("y", d) for d in LINE]
Z_LINE = [("z", d) for d in LINE]
X_LINE = [("x", d) for d in LINE]
X_RING = [("x", 1), ("x", -1)]
Y_RING = [("y", 1), ("y", -1)]
TWIN = [("c", 1)]


def shape(*dims, kind=BF):
    return jax.ShapeDtypeStruct(dims, kind)


def first_weights(first, both, out, down):
    def body(
        first_ref, both_ref, out_ref, down_ref, first_out, both_out, out_out, down_out, strip, sheet,
        sends, arrivals, locals_,
    ):
        net = Net(sends, arrivals, locals_)
        x, y, z, c = (lax.axis_index(a) for a in AXES)
        quarter = out_ref.shape[0] // 4
        greet(X_LINE + Y_LINE + Z_LINE + TWIN)
        row = RowGather(net, first_ref, first_out)
        piece = out_ref.at[pl.ds(pl.multiple_of(x * quarter, quarter), quarter)]
        piece_mine = net.keep(piece, strip.at[z])
        pieces = [net.send(piece, strip.at[z], "z", d) for d in LINE]
        both_mine = net.keep(both_ref.at[c], both_out.at[c])
        both_come = net.send(both_ref.at[1 - c], both_out.at[c], "c", 1)
        down_mine = net.keep(down_ref, down_out)
        row.spread()
        piece_mine.wait()
        for copy in pieces:
            copy.wait_recv()
        strip_mine = net.keep(strip, sheet.at[:, x])
        strips = [net.send(strip, sheet.at[:, x], "x", d) for d in LINE]
        row.finish()
        strip_mine.wait()
        for copy in strips:
            copy.wait_recv()
        half = sheet.shape[0] // 2
        sheet_keep = net.keep(sheet.at[pl.ds(half * c, half)], out_out.at[:, c])
        sheet_come = net.send(sheet.at[pl.ds(half * (1 - c), half)], out_out.at[:, c], "c", 1)
        for copy in (both_mine, sheet_keep, down_mine):
            copy.wait()
        for copy in (both_come, sheet_come):
            copy.wait_recv()
        net.close()

    rows, width = out.shape
    quarter = rows // 4
    outs = (
        shape(4, 4, 2, *first.shape), shape(*both.shape), shape(2, 2, 4, quarter, width), shape(*down.shape),
    )
    scratch = [pltpu.VMEM((4, quarter, width), BF), pltpu.VMEM((4, 4, quarter, width), BF)]
    return comm_call(
        body, "first_weights", 1, outs, (first, both, out, down), scratch, 36, 8, [IN_VMEM] * 4, [ANYWHERE] * 4,
    )


def keys_and_latents(key_value, latent, up):
    def body(kv_ref, lat_ref, up_ref, kv_out, lat_out, up_out, transit, sends, arrivals, locals_):
        net = Net(sends, arrivals, locals_)
        y, z, c = (lax.axis_index(a) for a in ROW)
        greet(Y_LINE + Z_LINE + TWIN)
        up_mine = net.keep(up_ref.at[y], transit.at[y, z])
        ups = [net.send(up_ref.at[along("y", d)], transit.at[y, z], "y", d) for d in LINE]
        row = RowGather(net, kv_ref, kv_out)
        ring = RingGather(net, lat_ref, lat_out, "y")
        up_mine.wait()
        for copy in ups:
            copy.wait_recv()
        ups = [net.send(transit.at[:, z], transit.at[:, z], "z", d) for d in LINE]
        row.spread()
        ring.forward()
        ring.share()
        for copy in ups:
            copy.wait_recv()
        up_keep = net.keep(transit.at[:, :, c], up_out.at[:, :, c])
        up_come = net.send(transit.at[:, :, 1 - c], up_out.at[:, :, c], "c", 1)
        row.finish()
        ring.finish()
        up_keep.wait()
        up_come.wait_recv()
        net.close()

    _, _, high, thin = up.shape
    outs = (shape(4, 4, 2, *key_value.shape), shape(4, 2, *latent.shape), shape(4, 4, 2, high, thin))
    return comm_call(
        body, "keys_and_latents", 2, outs, (key_value, latent, up), [pltpu.VMEM((4, 4, 2, high, thin), BF)], 44, 4,
        [IN_VMEM] * 3, [ANYWHERE] * 3,
    )


def heads_sum_and_cotangent(partial, cotangent):
    def body(part_ref, cot_ref, out_ref, cot_out, near, relay, come, go, sends, arrivals, locals_):
        net = Net(sends, arrivals, locals_)
        greet(X_RING + Y_RING + TWIN)
        ring = RingSum(net, part_ref, out_ref, "y", near, relay, come, go)
        feed = RingGather(net, cot_ref, cot_out, "x")
        ring.relay_far()
        ring.issue()
        feed.forward()
        ring.pass_on()
        feed.share()
        ring.finish()
        feed.finish()
        net.close()

    size, width = cotangent.shape
    outs = (shape(size, width, kind=F32), shape(4, 2, size, width))
    return comm_call(
        body, "heads_sum_and_cotangent", 3, outs, (partial, cotangent), ring_sum_scratch(size, width), 20, 2,
        [IN_VMEM, IN_VMEM], [IN_VMEM, ANYWHERE],
    )


def add_up(terms, out, rows):
    total = terms[0][rows].astype(F32)
    for term in terms[1:]:
        total = total + term[rows].astype(F32)
    out[rows] = total.astype(out.dtype)


def add_all(terms, out):
    rows_loop(out.shape[0], lambda rows: add_up(terms, out, rows))


def feed_forward(normed_two, normed, grad_out, both, down):
    size, width = normed_two.shape
    units = down.shape[0]
    tall = width // 4
    lanes = width // 2
    high = units // 16

    def body(
        two_ref, one_ref, cot_hbm, both_hbm, down_hbm, sum_out, one_out, branch_out, gb_out, mid_out,
        two, cot, both, down, hidden, grads, part, near, go, come, gb, gd, down_come,
        sends, arrivals, locals_,
    ):
        net = Net(sends, arrivals, locals_)
        x, y, z, c = (lax.axis_index(a) for a in AXES)
        both_load = net.keep(both_hbm, both)
        down_load = net.keep(down_hbm, down)
        cot_load = net.keep(cot_hbm, cot)
        greet(X_LINE + Y_LINE + Z_LINE + TWIN)
        feed = RingGather(net, two_ref, two, "x")
        one_mine = net.keep(one_ref.at[:, pl.ds(pl.multiple_of(y * tall, tall), tall)], one_out.at[y, c])
        ones = [
            net.send(
                one_ref.at[:, pl.ds(pl.multiple_of(along("y", d) * tall, tall), tall)],
                one_out.at[y, c], "y", d,
            )
            for d in LINE
        ]

        def block(s):
            where = along("x", s)
            at = pl.ds(pl.multiple_of(where * 2 * size, 2 * size), 2 * size)
            value = two[where].reshape(2 * size, width)
            pre = dot(value, both[...])
            grad = dot_nt(cot[where].reshape(2 * size, width), down[...])
            gate, up = pre[:, :units], pre[:, units:]
            sigma = 1.0 / (1.0 + jnp.exp(-gate))
            gated = gate * sigma
            hidden[at, :] = (gated * up).astype(BF)
            grads[at, :units] = (grad * up * (sigma + gated * (1.0 - sigma))).astype(BF)
            grads[at, units:] = (grad * gated).astype(BF)
            part[where] = dot_nt(grads[at, :], both[...]).astype(BF).reshape(2, size, width)
            return net.send(part.at[where, 1 - c], near.at[s], "c", 1)

        def pair(s):
            where = along("x", s)
            swaps[s].wait_recv()
            add_all([part.at[where, c], near.at[s]], go.at[s - 1])
            return net.send(go.at[s - 1], come.at[s - 1], "x", s)

        swaps = {}
        feed.mine.wait()
        feed.shared[0].wait_recv()
        both_load.wait()
        down_load.wait()
        cot_load.wait()
        swaps[0] = block(0)
        feed.forward()
        feed.share()
        one_mine.wait()
        spot = one_out.at[y, c]
        shared = [net.send(spot, spot, "c", 1)]
        for d in LINE:
            ones[d - 1].wait_recv()
            spot = one_out.at[along("y", -d), c]
            shared.append(net.send(spot, spot, "c", 1))
        feed.shared[1].wait_recv()
        feed.shared[2].wait_recv()
        swaps[1] = block(1)
        for copy in feed.far:
            copy.wait_recv()
        spot = two.at[along("x", 2), c]
        last = net.send(spot, spot, "c", 1)
        swaps[3] = block(3)
        ends = [pair(1)]
        last.wait_recv()
        swaps[2] = block(2)
        ends.append(pair(3))
        ends.append(pair(2))
        early, net.open = net.open, []

        first = []
        for k, axis in enumerate(("y", "z")):
            columns = slice(k * lanes, (k + 1) * lanes)
            gd[k] = (
                dot_tn(hidden[...], cot[...].reshape(8 * size, width)[:, columns])
                .astype(BF)
                .reshape(4, 4, high, lanes)
            )
            for d in LINE:
                at = along(axis, d)
                source = gd.at[k, at] if k == 0 else gd.at[k, :, at]
                first.append(net.send(source, down_come.at[k, d - 1], axis, d))

        gb_copies = []
        for i in range(8):
            at = pl.ds(i * 2 * size, 2 * size)
            gb[i] = dot_tn(two[...].reshape(8 * size, width)[:, i * 2 * size : (i + 1) * 2 * size], grads[...]).astype(BF)
            gb_copies.append(net.keep(gb.at[i], gb_out.at[at]))
        for copy in early:
            copy.wait_send()

        @pl.loop(0, 4)
        def _(i):
            at = pl.ds(pl.multiple_of(i * 2 * size, 2 * size), 2 * size)
            two[i] = dot(hidden[at, :], down[...]).astype(BF).reshape(2, size, width)

        branch_copy = net.keep(two, branch_out)
        swaps[0].wait_recv()
        for copy in ends:
            copy.wait_recv()
        add_all([part.at[x, c], near.at[0], come.at[0], come.at[1], come.at[2]], sum_out)
        for copy in shared:
            copy.wait_recv()
        for copy in first:
            copy.wait_recv()
        for k in range(2):
            for i in range(4):
                own = gd.at[k, y, i] if k == 0 else gd.at[k, i, z]
                add_all([own] + [down_come.at[k, d, i] for d in range(3)], mid_out.at[k, i])
        for copy in gb_copies + [branch_copy]:
            copy.wait()
        net.close()

    outs = (
        shape(size, width, kind=F32), shape(4, 2, size, tall), shape(4, 2, size, width), shape(width, 2 * units),
        shape(2, 4, high, lanes),
    )
    scratch = [
        pltpu.VMEM((4, 2, size, width), BF),
        pltpu.VMEM((4, 2, size, width), BF),
        pltpu.VMEM((width, 2 * units), BF),
        pltpu.VMEM((units, width), BF),
        pltpu.VMEM((8 * size, units), BF),
        pltpu.VMEM((8 * size, 2 * units), BF),
        pltpu.VMEM((4, 2, size, width), BF),
        pltpu.VMEM((4, size, width), BF),
        pltpu.VMEM((3, size, width), BF),
        pltpu.VMEM((3, size, width), BF),
        pltpu.VMEM((8, 2 * size, 2 * units), BF),
        pltpu.VMEM((2, 4, 4, high, lanes), BF),
        pltpu.VMEM((2, 3, 4, high, lanes), BF),
    ]
    return comm_call(
        body, "feed_forward", 4, outs, (normed_two, normed, grad_out, both, down), scratch, 32, 14,
        [IN_VMEM] * 2 + [ANYWHERE] * 3, [IN_VMEM, ANYWHERE, ANYWHERE, ANYWHERE, IN_VMEM],
    )


class FirstStep:
    def __init__(self, net, value, columns, axis, own, come, out):
        self.own, self.come, self.out = own, come, out
        self.copies = []
        for d in (1, 2, 3, 0):
            at = along(axis, d)
            source = value.at[at, :, :, columns] if axis == "y" else value.at[:, at, :, columns]
            if d:
                self.copies.append(net.send(source, come.at[d - 1], axis, d))
            else:
                self.mine = net.keep(source, own)

    def finish(self):
        self.mine.wait()
        for copy in self.copies:
            copy.wait_recv()
        for i in range(4):
            add_all([self.own.at[i]] + [self.come.at[d, i] for d in range(3)], self.out.at[i])


class SecondStep:
    def __init__(self, net, mid, axis, come):
        self.mid, self.axis, self.come = mid, axis, come
        self.copies = [net.send(mid.at[along(axis, d)], come.at[d - 1], axis, d) for d in LINE]

    def finish(self, out):
        for copy in self.copies:
            copy.wait_recv()
        here = lax.axis_index(self.axis)
        add_all([self.mid.at[here]] + [self.come.at[d] for d in range(3)], out)


def heads_gather_and_branch(value, partial, mid, gb):
    size, width = value.shape
    _, _, high, lanes = mid.shape
    _, _, tall, wide = gb.shape
    third = wide // 3

    def body(ref, part_ref, mid_ref, gb_ref, out, part_out, mid_out, gb_out, *rest):
        net = Net(*rest[8:])
        greet(X_RING + Y_LINE + Z_LINE + TWIN)
        gathering = RingGather(net, ref, out, "y")
        ring = RingSum(net, part_ref, part_out, "x", *rest[:4])
        halves = [SecondStep(net, mid_ref.at[k], axis, rest[4 + k]) for k, axis in enumerate(("z", "y"))]
        step = FirstStep(net, gb_ref, pl.ds(third, third), "z", rest[6], rest[7], gb_out)
        ring.relay_far()
        ring.issue()
        gathering.forward()
        ring.pass_on()
        gathering.share()
        for k in range(2):
            halves[k].finish(mid_out.at[:, pl.ds(k * lanes, lanes)])
        gathering.finish()
        ring.finish()
        step.finish()
        net.close()

    outs = (
        shape(4, 2, size, width), shape(size, width, kind=F32), shape(high, 2 * lanes), shape(4, tall, third),
    )
    scratch = [
        pltpu.VMEM((3, high, lanes), BF),
        pltpu.VMEM((3, high, lanes), BF),
        pltpu.VMEM((4, tall, third), BF),
        pltpu.VMEM((3, 4, tall, third), BF),
    ]
    return comm_call(
        body, "heads_gather_and_branch", 6, outs, (value, partial, mid, gb),
        ring_sum_scratch(size, width) + scratch, 30, 3,
        [IN_VMEM] * 3 + [ANYWHERE], [ANYWHERE] + [IN_VMEM] * 3,
    )


def keys_and_latents_sum(grad_kv, partial, grad_up, grad_out, mids, grad_down):
    _, _, _, size, thin = grad_kv.shape
    width = partial.shape[3]
    high, lanes = grad_up.shape[3], grad_up.shape[4] // 4
    _, quarter, wide = grad_out.shape
    tall, third = mids[0].shape[1:]

    def body(
        kv_ref, part_ref, up_ref, out_ref, one_ref, two_ref, down_ref, kv_out, part_out, up_out, out_out, mid_out,
        down_out, *rest,
    ):
        net = Net(*rest[13:])
        up_come, out_come = rest[9:11]
        x, z = lax.axis_index("x"), lax.axis_index("z")

        def lane(at):
            return pl.ds(pl.multiple_of(at * lanes, lanes), lanes)

        greet(X_LINE + Y_LINE + Z_LINE + TWIN)
        row = RowSum(net, kv_ref, kv_out, *rest[:5])
        ring = RingSum(net, part_ref, part_out, "y", *rest[5:9])
        ups = [
            net.send(up_ref.at[:, :, :, :, lane(along("x", d))], up_come.at[d - 1], "x", d) for d in LINE
        ]
        outs = [net.send(out_ref.at[along("z", d)], out_come.at[d - 1], "z", d) for d in LINE]
        halves = [
            SecondStep(net, mid, axis, come)
            for mid, axis, come in ((one_ref, "z", rest[11]), (two_ref, "y", rest[12]))
        ]
        down_mine = net.keep(down_ref, down_out.at[x])
        downs = [net.send(down_ref, down_out.at[x], "x", d) for d in LINE]
        row.start()
        ring.relay_far()
        ring.issue()
        row.turn()
        ring.pass_on()
        for copy in outs:
            copy.wait_recv()
        add_all([out_ref.at[z]] + [out_come.at[d] for d in range(3)], out_out)
        for copy in ups:
            copy.wait_recv()
        for i in range(4):

            @pl.loop(0, 8)
            def _(k, i=i):
                j, core = k // 2, k % 2
                add_all(
                    [up_ref.at[i, j, core, :, lane(x)]] + [up_come.at[d, i, j, core] for d in range(3)],
                    up_out.at[i, j, core],
                )

        halves[0].finish(mid_out.at[:, pl.ds(0, third)])
        halves[1].finish(mid_out.at[:, pl.ds(2 * third, third)])
        ring.finish()
        row.finish()
        down_mine.wait()
        for copy in downs:
            copy.wait_recv()
        net.close()

    outs = (
        shape(size, thin, kind=F32), shape(size, width, kind=F32), shape(4, 4, 2, high, lanes),
        shape(quarter, wide), shape(tall, 3 * third), shape(4, *grad_down.shape),
    )
    scratch = [
        pltpu.VMEM((3, 4, 4, 2, high, lanes), BF),
        pltpu.VMEM((3, quarter, wide), BF),
        pltpu.VMEM((3, tall, third), BF),
        pltpu.VMEM((3, tall, third), BF),
    ]
    return comm_call(
        body, "keys_and_latents_sum", 7, outs, (grad_kv, partial, grad_up, grad_out, *mids, grad_down),
        row_sum_scratch(size, thin) + ring_sum_scratch(size, width) + scratch, 46, 2,
        [IN_VMEM] * 7, [IN_VMEM] * 5 + [ANYWHERE],
    )


def firsts_gather(value, both, grad_out, grad_up):
    def body(
        ref, both_ref, out_ref, up_ref, gathered, both_out, out_out, up_out, up_come, up_sum, up_y,
        sends, arrivals, locals_,
    ):
        net = Net(sends, arrivals, locals_)
        x, y, z, c = (lax.axis_index(a) for a in AXES)
        greet(X_LINE + Y_LINE + Z_LINE + TWIN)
        mine = net.keep(ref.at[c], gathered.at[y, c])
        come = net.send(ref.at[1 - c], gathered.at[y, c], "c", 1)
        both_mine = net.keep(both_ref.at[c], both_out.at[x, c])
        both_come = net.send(both_ref.at[1 - c], both_out.at[x, c], "c", 1)
        ups = [net.send(up_ref.at[:, along("z", d)], up_come.at[d - 1], "z", d) for d in LINE]
        outs = [net.send(out_ref, out_out.at[x], "x", d) for d in LINE]
        out_mine = net.keep(out_ref, out_out.at[x])

        mine.wait()
        spot = gathered.at[y, c]
        ahead = [net.send(spot, spot, "y", 1), net.send(spot, spot, "y", -1)]
        come.wait_recv()
        spot = gathered.at[y, 1 - c]
        ahead += [net.send(spot, spot, "y", 1), net.send(spot, spot, "y", -1)]
        both_mine.wait()
        both_come.wait_recv()
        zero, one = both_out.at[x, 0], both_out.at[x, 1]
        right = [net.send(spot, spot, "x", 1) for spot in (zero, one)]
        left = [net.send(spot, spot, "x", -1) for spot in (one, zero)]

        for copy in ups:
            copy.wait_recv()
        for i in range(4):
            for core in range(2):
                add_all(
                    [up_ref.at[i, z, core]] + [up_come.at[d, i, core] for d in range(3)], up_sum.at[i, core]
                )
        ups = [net.send(up_sum.at[along("y", d)], up_y.at[y], "y", d) for d in LINE]
        up_mine = net.keep(up_sum.at[y], up_y.at[y])

        ahead[0].wait_recv()
        spot = gathered.at[along("y", -1), c]
        ahead.append(net.send(spot, spot, "y", 1))
        ahead[3].wait_recv()
        spot = gathered.at[along("y", 1), 1 - c]
        ahead.append(net.send(spot, spot, "y", -1))

        up_mine.wait()
        for copy in ups:
            copy.wait_recv()
        up_near = net.send(up_y.at[:, 1 - c], up_out.at[x, :, c], "c", 1)
        up_mine = net.keep(up_y.at[:, c], up_out.at[x, :, c])

        right[0].wait_recv()
        spot = both_out.at[along("x", -1), 0]
        far = [net.send(spot, spot, "x", 1)]
        left[0].wait_recv()
        spot = both_out.at[along("x", 1), 1]
        far.append(net.send(spot, spot, "x", -1))

        up_near.wait_recv()
        up_mine.wait()
        spot = up_out.at[x]
        ups = [net.send(spot, spot, "x", d) for d in LINE]
        for copy in [ahead[i] for i in (1, 2, 4, 5)] + [right[1], left[1]] + far + outs + ups:
            copy.wait_recv()
        out_mine.wait()
        net.close()

    tall, wide = grad_out.shape
    _, _, _, high, lanes = grad_up.shape
    outs = (
        shape(4, *value.shape), shape(4, *both.shape), shape(4, tall, wide), shape(4, 4, 2, high, lanes),
    )
    scratch = [
        pltpu.VMEM((3, 4, 2, high, lanes), BF),
        pltpu.VMEM((4, 2, high, lanes), BF),
        pltpu.VMEM((4, 2, high, lanes), BF),
    ]
    return comm_call(
        body, "firsts_gather", 8, outs, (value, both, grad_out, grad_up), scratch, 40, 6,
        [IN_VMEM] * 4, [ANYWHERE, ANYWHERE, IN_VMEM, IN_VMEM],
    )


def last_sums(grad_first, gains):
    def body(
        first_ref, gain_ref, first_out, gain_out, wide, first_come, first_x,
        gain_near, gain_one, gain_come, gain_two, gain_y, gain_three, gain_x, sends, arrivals, locals_,
    ):
        net = Net(sends, arrivals, locals_)
        x, y, z, c = (lax.axis_index(a) for a in AXES)
        greet(X_LINE + Y_LINE + Z_LINE + TWIN)
        first_near = net.send(first_ref.at[:, 1 - c], wide.at[c], "c", 1)
        first_mine = net.keep(first_ref.at[:, c], wide.at[c])
        near = net.send(gain_ref.at[:, :, 1 - c], gain_near, "c", 1)
        first_mine.wait()
        first_near.wait_recv()
        firsts = [
            [net.send(wide.at[core, along("z", d)], first_come.at[d - 1, core], "z", d) for d in LINE]
            for core in range(2)
        ]
        near.wait_recv()
        gain_one[...] = gain_ref[:, :, c] + gain_near[...]
        comes = [net.send(gain_one.at[:, along("z", d)], gain_come.at[d - 1], "z", d) for d in LINE]
        def onward(core):
            for copy in firsts[core]:
                copy.wait_recv()
            add_all([wide.at[core, z]] + [first_come.at[d, core] for d in range(3)], first_x.at[x, core])
            spot = first_x.at[x, core]
            return [net.send(spot, spot, "x", d) for d in LINE]

        finals = [onward(0)]
        for copy in comes:
            copy.wait_recv()
        gain_two[...] = (gain_one[:, z] + gain_come[0]) + (gain_come[1] + gain_come[2])
        comes = [net.send(gain_two.at[along("y", d)], gain_y.at[d - 1], "y", d) for d in LINE]
        finals.append(onward(1))
        for copy in comes:
            copy.wait_recv()
        gain_three[...] = (gain_two[y] + gain_y[0]) + (gain_y[1] + gain_y[2])
        gain_mine = net.keep(gain_three, gain_x.at[x])
        comes = [net.send(gain_three, gain_x.at[x], "x", d) for d in LINE]
        for core in range(2):
            for copy in finals[core]:
                copy.wait_recv()
            add_all([first_x.at[i, core] for i in range(4)], first_out.at[core])
        gain_mine.wait()
        for copy in comes:
            copy.wait_recv()
        gain_out[...] = (gain_x[0] + gain_x[1]) + (gain_x[2] + gain_x[3])
        net.close()

    _, _, high, lanes = grad_first.shape
    outs = (shape(2, high, lanes, kind=F32), shape(8, 128, kind=F32))
    scratch = [
        pltpu.VMEM((2, 4, high, lanes), BF),
        pltpu.VMEM((3, 2, high, lanes), BF),
        pltpu.VMEM((4, 2, high, lanes), BF),
        pltpu.VMEM((4, 4, 8, 128), F32),
        pltpu.VMEM((4, 4, 8, 128), F32),
        pltpu.VMEM((3, 4, 8, 128), F32),
        pltpu.VMEM((4, 8, 128), F32),
        pltpu.VMEM((3, 8, 128), F32),
        pltpu.VMEM((8, 128), F32),
        pltpu.VMEM((4, 8, 128), F32),
    ]
    return comm_call(
        body, "last_sums", 9, outs, (grad_first, gains), scratch, 24, 2, [IN_VMEM] * 2, [IN_VMEM] * 2,
    )


def attend_back_kernel(
    qt_ref, do_ref, o_ref, kv_ref, begin_ref, slot_ref, lse_ref, cos_ref, sin_ref, go_ref, mid_ref, gb_ref,
    dq_ref, dkv_ref, go_out, one_out, two_out, mid_out,
    kt, sums, accum, gb_own, gb_come, mid_come, stack, go_come, sends, arrivals, locals_,
):
    net = Net(sends, arrivals, locals_)
    x, c = lax.axis_index("x"), lax.axis_index("c")
    greet(X_LINE + Y_LINE + Z_LINE + TWIN)
    half = go_ref.shape[0]
    third = mid_ref.shape[-1]
    quarter = go_out.shape[1]

    def strip(at):
        return pl.ds(pl.multiple_of(at * quarter, quarter), quarter)

    go_mine = net.keep(go_ref.at[:, c], stack.at[pl.ds(half * c, half)])
    go_near = net.send(go_ref.at[:, 1 - c], stack.at[pl.ds(half * c, half)], "c", 1)
    steps = [
        FirstStep(net, gb_ref, pl.ds(0, third), "y", gb_own.at[0], gb_come.at[0], one_out),
        FirstStep(net, gb_ref, pl.ds(2 * third, third), "z", gb_own.at[1], gb_come.at[1], two_out),
    ]
    second = SecondStep(net, mid_ref, "y", mid_come)
    go_mine.wait()
    go_near.wait_recv()
    go_sends = [net.send(stack.at[:, strip(along("x", d))], go_come.at[d - 1], "x", d) for d in LINE]
    depth = lax.axis_index("z")
    segments = slot_ref.shape[0]
    rows = slot_ref.shape[2]
    tokens = rows // 2
    sums[...] = jnp.zeros_like(sums)
    turned(kv_ref, kt, segments * (segments - 1) + depth + 1, KEYS)
    for seg in range(segments):
        here = pl.ds(seg * tokens, tokens)

        def stacked(ref):
            value = ref[here, :]
            return jnp.concatenate([value[:, :SIZE], value[:, SIZE:]], axis=0)

        query_t = qt_ref[seg]
        query = query_t.T
        grad = stacked(do_ref)
        grad_t = grad.T
        delta = jnp.sum(
            grad_t.astype(F32) * stacked(o_ref).T.astype(F32), axis=0, keepdims=True
        )
        begin = begin_ref[seg]
        slot = slot_ref[seg]
        lse = lse_ref[seg]
        accum[...] = jnp.zeros_like(accum)

        @pl.loop(0, segments * seg + depth + 1)
        def _(block):
            at = pl.multiple_of(block * BLOCK, BLOCK)
            keys = pl.ds(at, BLOCK)
            scores = dot(kv_ref[keys, KEYS], query_t)
            key = lax.broadcasted_iota(jnp.int32, scores.shape, 0) + at
            allowed = (key >= begin) & (key <= slot)
            probs = jnp.where(allowed, jnp.exp(scores - lse), 0.0)
            grad_probs = dot(kv_ref[keys, VALUES], grad_t)
            grad_scores = (probs * (grad_probs - delta)).astype(BF)
            sums[keys, VALUES] += dot(probs.astype(BF), grad)
            sums[keys, KEYS] += dot(grad_scores, query)
            accum[...] += dot(kt[:, keys], grad_scores)

        cosine, sine = cos_ref[seg], sin_ref[seg]
        for head in range(2):
            part = accum[:, head * tokens : (head + 1) * tokens] * (SIZE ** -0.5)
            lower, upper = part[:HALF], part[HALF:]
            turn = jnp.concatenate(
                [lower * cosine + upper * sine, upper * cosine - lower * sine], axis=0
            )
            dq_ref[here, head * SIZE : (head + 1) * SIZE] = turn.T.astype(BF)

    dkv_ref[...] = sums[...].astype(BF)
    second.finish(mid_out)
    for copy in go_sends:
        copy.wait_recv()
    for i in range(2 * half):
        add_all([stack.at[i, strip(x)]] + [go_come.at[d, i] for d in range(3)], go_out.at[i])
    for step in steps:
        step.finish()
    net.close()


def attend_back(qt, do, o, kv, begin, slot, lse, cosine, sine, grad_out, mid, gb):
    segments, _, rows = slot.shape
    half, _, tall, wide = grad_out.shape
    _, high, third = mid.shape
    part = jax.ShapeDtypeStruct((4, high, third), BF)
    return pl.pallas_call(
        attend_back_kernel,
        name="attend_back",
        out_shape=(
            jax.ShapeDtypeStruct(do.shape, BF),
            jax.ShapeDtypeStruct(kv.shape, BF),
            jax.ShapeDtypeStruct((2 * half, tall // 4, wide), BF),
            part,
            part,
            jax.ShapeDtypeStruct((high, third), BF),
        ),
        in_specs=[IN_VMEM] * 11 + [ANYWHERE],
        out_specs=[IN_VMEM] * 6,
        scratch_shapes=[
            pltpu.VMEM((SIZE, kv.shape[0]), BF),
            pltpu.VMEM(kv.shape, F32),
            pltpu.VMEM((SIZE, rows), F32),
            pltpu.VMEM((2, 4, high, third), BF),
            pltpu.VMEM((2, 3, 4, high, third), BF),
            pltpu.VMEM((3, high, third), BF),
            pltpu.VMEM((2 * half, tall, wide), BF),
            pltpu.VMEM((3, 2 * half, tall // 4, wide), BF),
        ] + semaphores(14, 3),
        compiler_params=pltpu.CompilerParams(
            collective_id=10, has_side_effects=True, vmem_limit_bytes=60 << 20
        ),
    )(qt, do, o, kv, begin, slot, lse, cosine, sine, grad_out, mid, gb)


def gather(value, axes):
    return lax.all_gather(value, axes, axis=0, tiled=True)


def on_device(
    block_input, cotangent, lengths, norm_gain, q_down, q_gain, q_up, key_weight, value_weight,
    out_weight, ffn_gain, gate_weight, up_weight, down_weight,
):
    rows, width = block_input.shape
    latent_width = q_down.shape[1]
    n_x, n_y, n_z, n_c = (lax.axis_size(a) for a in ("x", "y", "z", "c"))
    x, y, z, c = (lax.axis_index(a) for a in ("x", "y", "z", "c"))
    span = n_y * n_z * n_c
    members = n_y * n_c
    lengths_row = lengths[0]

    mine = (y * n_z + z) * n_c + c
    slots_mine = mine * rows + jnp.arange(rows, dtype=jnp.int32)
    begin_mine, _ = places_of(lengths_row, slots_mine)
    cosine, sine = tables(slots_mine - begin_mine)
    strip = n_c * rows
    slots_group = (
        (jnp.arange(n_y, dtype=jnp.int32)[:, None] * n_z + z) * strip
        + jnp.arange(strip, dtype=jnp.int32)[None, :]
    ).reshape(-1)
    begin_group, live_group = places_of(lengths_row, slots_group)
    cosine_group, sine_group = tables_across((slots_group - begin_group).reshape(n_y, strip))
    begin_lanes = jnp.tile(begin_group.reshape(n_y, 1, strip), (1, 1, 2))
    slot_lanes = jnp.tile(slots_group.reshape(n_y, 1, strip), (1, 1, 2))
    live_lanes = jnp.tile(live_group.reshape(n_y, 1, strip), (1, 1, 2))

    shard = norm_gain.shape[0]
    extra = jnp.stack(
        [norm_gain, ffn_gain, jnp.pad(q_gain, (0, shard - q_gain.shape[0]))], axis=1
    ).astype(BF)
    first_width = latent_width + 2 * SIZE
    first = jnp.concatenate(
        [q_down, key_weight, value_weight, jnp.pad(extra, ((0, 0), (0, 125)))], axis=1
    )
    per_heads = q_up.shape[1] // members
    q_rows = q_up.shape[0]

    wide = gate_weight.shape[1]
    down_rows = down_weight.shape[0]
    share = down_rows // n_x
    padded = -(-share // 16) * 16
    source = lax.broadcasted_iota(jnp.int32, (wide // 2, n_c * (span // 4) * padded), 0)
    target = lax.broadcasted_iota(jnp.int32, source.shape, 1)
    block_at = target // (padded * (span // 4)) + n_c * ((target // padded) % (span // 4))
    inside = target % padded
    picks = (
        (source == block_at * down_rows + x * share + inside) & (inside < share)
    ).astype(BF)

    def spread(weight):
        stacked = jnp.concatenate([weight[:, : wide // 2], weight[:, wide // 2 :]], axis=0)
        part = dot(stacked, picks).astype(BF)
        part = part.reshape(2, shard, n_c, -1).transpose(2, 1, 0, 3)
        return part.reshape(n_c, shard, -1)

    both = jnp.concatenate([spread(gate_weight), spread(up_weight)], axis=2)
    units = both.shape[-1] // 2
    down_part = lax.dynamic_slice_in_dim(down_weight, x * share, share)
    down_part = jnp.pad(down_part, ((0, padded - share), (0, 0)))
    first_full, both, out_heads, down_part = first_weights(first, both, out_weight, down_part)
    out_heads = out_heads.reshape(per_heads, width)
    first_full = first_full.reshape(span * shard, -1)
    both = both.reshape(n_c * shard, 2 * units)
    extra_full = first_full[:, first_width : first_width + 3].astype(F32)
    first_full = first_full[:, :first_width]
    gain_one = extra_full[:, 0]
    gain_two = extra_full[:, 1]
    gain_latent = extra_full[:, 2].reshape(span, shard)[:, : q_gain.shape[0]].reshape(-1)

    both_full = gather(both, ("y", "z"))
    down_use = gather(down_part, ("y", "z"))

    inputs = block_input.astype(F32)
    inverse_one = lax.rsqrt(jnp.mean(inputs * inputs, axis=-1, keepdims=True) + EPSILON)
    normed = (inputs * inverse_one * gain_one).astype(BF)
    firsts = dot(normed, first_full)
    latent = firsts[:, :latent_width]
    inverse_latent = lax.rsqrt(jnp.mean(latent * latent, axis=-1, keepdims=True) + EPSILON)
    latent_normed = (latent * inverse_latent * gain_latent).astype(BF)
    key_mine = rotate(firsts[:, latent_width : latent_width + SIZE], cosine, sine).astype(BF)
    value_mine = firsts[:, latent_width + SIZE :].astype(BF)
    key_value, latent_group, up_heads = keys_and_latents(
        jnp.concatenate([key_mine, value_mine], axis=1), latent_normed,
        q_up.reshape(q_rows, n_y, n_c, per_heads).transpose(1, 2, 0, 3),
    )
    up_heads = up_heads.reshape(span * q_rows, per_heads)
    key_value = key_value.reshape(span * rows, 2 * SIZE)
    group = members * rows
    latent_group = latent_group.reshape(group, latent_width)
    mixed, queries_t, lse = attend(
        dot(latent_group, up_heads), key_value, begin_lanes, slot_lanes, live_lanes,
        cosine_group, sine_group,
    )
    branch, grad_feed = heads_sum_and_cotangent(
        dot(mixed, out_heads).astype(BF).reshape(n_y, n_c, rows, width), cotangent
    )
    middle = inputs + branch

    inverse_two = lax.rsqrt(jnp.mean(middle * middle, axis=-1, keepdims=True) + EPSILON)
    grad_normed_two, normed_part, branch_part, grad_both, grad_down = feed_forward(
        (middle * inverse_two * gain_two).astype(BF), normed, grad_feed, both_full, down_use
    )
    normed_part = normed_part.reshape(group, -1)
    grad_result = cotangent.astype(F32)
    grad_mid_norm, grad_gain_two = norm_back(middle, inverse_two, gain_two, grad_normed_two)
    grad_middle = grad_result + grad_mid_norm

    def collect(grads):
        parts = grads.reshape(n_x, n_c, shard, 2, units // 2).transpose(0, 3, 2, 1, 4)
        parts = parts.reshape(n_x, 2 * shard, n_c * units // 2)
        whole = 0.0
        for i in range(n_x):
            picked = (
                (source == block_at * down_rows + i * share + inside) & (inside < share)
            ).astype(BF)
            whole = whole + dot_nt(parts[i], picked)
        return jnp.concatenate([whole[:shard], whole[shard:]], axis=1)

    grad_both = grad_both.reshape(n_y, n_z, n_c * shard, 2 * units)
    grad_branch, branch_two, grad_down, grad_mid = heads_gather_and_branch(
        grad_middle.astype(BF), branch_part, grad_down, grad_both
    )
    grad_branch = grad_branch.reshape(group, width)
    output = (middle + branch_two).astype(BF)
    grad_mixed = dot_nt(grad_branch, out_heads).astype(BF)
    grad_attended = grad_mixed * live_group[:, None].astype(BF)
    grad_out = dot_tn(mixed, grad_branch).astype(BF)
    out_rows = out_weight.shape[0]
    grad_query_raw, grad_kv, grad_out, grad_one, grad_two, grad_mid = attend_back(
        queries_t, grad_attended, mixed, key_value, begin_lanes, slot_lanes, lse,
        cosine_group, sine_group, grad_out.reshape(n_z // n_c, n_c, out_rows, width), grad_mid, grad_both,
    )
    grad_up_heads = dot_tn(latent_group, grad_query_raw).astype(BF)
    grad_kv, grad_latent_normed, grad_up_heads, grad_out, grad_both, grad_down = keys_and_latents_sum(
        grad_kv.reshape(n_y, n_z, n_c, rows, 2 * SIZE),
        dot_nt(grad_query_raw, up_heads).astype(BF).reshape(n_y, n_c, rows, latent_width),
        grad_up_heads.reshape(n_y, n_z, n_c, q_rows, per_heads),
        grad_out, (grad_one, grad_two), grad_down,
    )
    third = grad_mid.shape[1]
    grad_both = jnp.concatenate([grad_both[:, :third], grad_mid, grad_both[:, 2 * third :]], axis=1)
    grad_key_raw = unrotate(grad_kv[:, :SIZE], cosine, sine).astype(BF)
    grad_value_raw = grad_kv[:, SIZE:].astype(BF)
    grad_latent_f, grad_gain_latent = norm_back(
        latent, inverse_latent, gain_latent, grad_latent_normed
    )
    grad_firsts = jnp.concatenate(
        [grad_latent_f.astype(BF), grad_key_raw, grad_value_raw], axis=1
    )
    grad_normed = dot_nt(grad_firsts, first_full)
    grad_input_norm, grad_gain_one = norm_back(inputs, inverse_one, gain_one, grad_normed)
    input_grad = grad_middle + grad_input_norm

    half_first = first_width // n_c
    first_part, grad_both, grad_out, grad_up_heads = firsts_gather(
        grad_firsts.reshape(rows, n_c, half_first).transpose(1, 0, 2),
        grad_both.reshape(n_c, shard, 2 * units), grad_out, grad_up_heads,
    )
    first_part = first_part.reshape(group, half_first)
    grad_first = dot_tn(normed_part, first_part).astype(BF)
    gains = jnp.concatenate(
        [
            grad_gain_one.reshape(span, shard),
            grad_gain_two.reshape(span, shard),
            grad_gain_latent.reshape(span, -1),
        ],
        axis=1,
    )
    shares = gains.shape[1]
    gains = jnp.pad(gains, ((0, 0), (0, 8 * 128 - shares))).reshape(n_y, n_z, n_c, 8, 128)
    grad_first, gains = last_sums(grad_first.reshape(n_z, n_c, shard, half_first), gains)
    gains = gains.reshape(-1)
    grad_first = jnp.concatenate([grad_first[0], grad_first[1]], axis=1)
    grad_out = grad_out.reshape(out_rows, width).astype(F32)
    grad_q_up = grad_up_heads.transpose(3, 1, 2, 0, 4).reshape(q_rows, -1).astype(F32)
    grad_gate = collect(grad_both[..., :units])
    grad_up = collect(grad_both[..., units:])
    grad_down = grad_down[:, :share].reshape(down_rows, width).astype(F32)
    return (
        output,
        input_grad,
        gains[:shard],
        grad_first[:, :latent_width],
        gains[2 * shard : shares],
        grad_q_up,
        grad_first[:, latent_width : latent_width + SIZE],
        grad_first[:, latent_width + SIZE :],
        grad_out,
        gains[shard : 2 * shard],
        grad_gate,
        grad_up,
        grad_down,
    )


def solution(mesh):
    sizes = (4, 4, 4, 2)
    grid = Mesh(mesh.devices.reshape(sizes), ("x", "y", "z", "c"))
    tokens = P(("x", "y", "z", "c"), None)
    wide, thin = P(ROW, None), P(ROW)
    in_specs = (
        tokens, tokens, P("x", None), thin, wide, thin, wide, wide, wide, wide, thin, wide, wide,
        wide,
    )
    out_specs = (
        tokens, tokens, thin, wide, thin, wide, wide, wide, wide, thin, wide, wide, wide,
    )
    return jax.shard_map(
        on_device, mesh=grid, in_specs=in_specs, out_specs=out_specs, check_vma=False
    )
```

time: 639 us -> 557 us (0.87)
  matrix products: 104 us -> 59.7 us
  Pallas kernels: 430 us -> 403 us
  local copies, waits for them, and re-layouts: 44.5 us -> 32.6 us
    pallas_call x9 -> x8, Pallas kernels: 386 us -> 331 us  [comm_call(): pl.pallas_call(body, name=name, out_shape=outs, in_specs=spaces, out_spec...]
    dot_general x14 -> x11, matrix products: 47.1 us -> 30 us  [dot_nt(): lax.dot_general(left, right, (((1,), (1,)), ((), ())), preferred_element_...]
    dot_general x8 -> x5, matrix products: 32.3 us -> 15.7 us  [dot(): return jnp.dot(left, right, preferred_element_type=F32)]
    pallas_call x1, Pallas kernels: 24.8 us -> 40.5 us  [attend_back(): pl.pallas_call(attend_back_kernel, name='attend_back', out_shape=(jax.Sha...]
    unnamed x112 -> x77, local copies, waits for them, and re-layouts: 14.8 us -> 2.85 us
    pallas_call x1, Pallas kernels: 20.2 us -> 31.5 us  [attend(): pl.pallas_call(attend_kernel, name='attend', out_shape=(jax.ShapeDtypeStr...]
    dot_general x6 -> x3, matrix products: 25 us -> 13.9 us  [dot_tn(): lax.dot_general(left, right, (((0,), (0,)), ((), ())), preferred_element_...]
  transfers between devices with their start and end apart: 4 -> 2, of which waited for: 0 -> 0; matrix products, arithmetic and copies ran while one was open for 13% -> 5% of each run, Pallas kernels for 64% -> 22%
where the time goes in v4:
time: 557 us; the launch traced here: 547 us
  Pallas kernels  403 us (72%)
  matrix products  59.7 us (11%)
  other arithmetic  36.1 us (6%)
  local copies, waits for them, and re-layouts  32.6 us (6%)
  between operations  15.1 us (3%)
    pallas_call x8, Pallas kernels, comm_call(): pl.pallas_call(body, name=name, out_shape=outs, in_specs=spaces, out_spec...  331 us
    pallas_call x1, Pallas kernels, attend_back(): pl.pallas_call(attend_back_kernel, name='attend_back', out_shape=(jax.Sha...  40.5 us
    pallas_call x1, Pallas kernels, attend(): pl.pallas_call(attend_kernel, name='attend', out_shape=(jax.ShapeDtypeStr...  31.5 us
    dot_general x11, matrix products, dot_nt(): lax.dot_general(left, right, (((1,), (1,)), ((), ())), preferred_element_...  30 us
    dot_general x5, matrix products, dot(): return jnp.dot(left, right, preferred_element_type=F32)  15.7 us
    dot_general x3, matrix products, dot_tn(): lax.dot_general(left, right, (((0,), (0,)), ((), ())), preferred_element_...  13.9 us
  transfers between devices with their start and end apart: 2, of which 0 were waited for; matrix products, arithmetic and copies ran while one was open for 5% of the time, Pallas kernels for 22%

profile of v4, /device:TPU:1, one launch (start us, length us, event | category | flops | bytes accessed | tf_op | source)
XLA Modules:
  0.0 547.1 jit_solution(4153524505294288273)
XLA Ops:
  7.3 1.2 fusion.82
  8.5 1.9 convolution_convert_fusion.6
  11.0 1.9 convolution_convert_fusion.5
  15.8 48.9 %first_weights.1 = (bf16[4,4,2,64,1664]{4,3,2,1,0:T(8,128)(2,1)}, bf16[2,64,1536]{2,1,0:T(8,128)(2,1)}, bf16[2,2,4,32,2048]{4,3,2,1,0:T(8,128)(2,1)}, bf16[48,2048]{1,0:T(8,128)(2,1)}) custom-call(bf16[64,1664]{1,0:T(8,128)(2,1)} %fusion.37.first_ref, bf16[2,64,1536]{2,1,0:T(8,128)(2,1)} %pad_maximum_fusion.2.both_ref, bf16[128,2048]{1,0:T(8,128)(2,1)} %out_ref.1, ...), custom_call_target="tpu_custom_call" | custom-call | tf_op jit(solution)/shard_map/first_weights/pallas_call | solution.py:222
  68.2 4.0 fusion.16
  77.1 51.1 %keys_and_latents.1 = (bf16[4,4,2,128,512]{4,3,2,1,0:T(8,128)(2,1)}, bf16[4,2,128,1024]{3,2,1,0:T(8,128)(2,1)}, bf16[4,4,2,32,512]{4,3,2,1,0:T(8,128)(2,1)}) custom-call(bf16[128,512]{1,0:T(8,128)(2,1)} %pad_maximum_fusion.6.kv_ref, bf16[128,1024]{1,0:T(8,128)(2,1)} %multiply_convert_fusion.1.lat_ref, bf16[4,2,32,512]{3,2,1,0:T(8,128)(2,1)} %bitcast.136), custom_call_target="tpu_custom_call" | custom-call | tf_op jit(solution)/shard_map/keys_and_latents/pallas_call | solution.py:222
  128.2 1.9 multiply_sine_fusion
  130.1 3.5 fusion.88.q_ref
  133.6 31.5 %attend.1 = (bf16[1024,512]{1,0:T(8,128)(2,1)S(1)}, bf16[4,256,512]{2,1,0:T(8,128)(2,1)S(1)}, f32[4,1,512]{2,1,0:T(1,128)S(1)}) custom-call(f32[1024,512]{1,0:T(8,128)S(1)} %fusion.88.q_ref, bf16[4096,512]{1,0:T(8,128)(2,1)} %bitcast.124, s32[4,1,512]{2,1,0:T(1,128)S(1)} %tile.28.begin_ref, s32[4,1,512]{2,1,0:T(1,128)S(1)} %tile.30.slot_ref, ...), custom_call_target="tpu_custom_call" | custom-call | tf_op jit(solution)/shard_map/attend/pallas_call | solution.py:136
  166.8 4.4 convolution_convert_fusion
  171.2 36.0 %heads_sum_and_cotangent.1 = (f32[128,2048]{1,0:T(8,128)}, bf16[4,2,128,2048]{3,2,1,0:T(8,128)(2,1)}) custom-call(bf16[4,2,128,2048]{3,2,1,0:T(8,128)(2,1)} %bitcast.126, bf16[128,2048]{1,0:T(8,128)(2,1)} %cot_ref.1), custom_call_target="tpu_custom_call" | custom-call | tf_op jit(solution)/shard_map/heads_sum_and_cotangent/pallas_call | solution.py:222
  207.2 1.4 multiply_reduce_fusion.2
  210.3 2.9 fusion.3
  213.2 67.5 %feed_forward.1 = (f32[128,2048]{1,0:T(8,128)}, bf16[4,2,128,512]{3,2,1,0:T(8,128)(2,1)}, bf16[4,2,128,2048]{3,2,1,0:T(8,128)(2,1)}, bf16[2048,1536]{1,0:T(8,128)(2,1)}, bf16[2,4,48,1024]{3,2,1,0:T(8,128)(2,1)}) custom-call(bf16[128,2048]{1,0:T(8,128)(2,1)} %multiply_convert_fusion.two_ref, bf16[128,2048]{1,0:T(8,128)(2,1)} %copy-done.14, ...), custom_call_target="tpu_custom_call" | custom-call | tf_op jit(solution)/shard_map/feed_forward/pallas_call | solution.py:222
  280.7 1.5 multiply_reduce_fusion
  282.2 2.4 fusion.68.ref
  284.6 34.8 %heads_gather_and_branch.1 = (bf16[4,2,128,2048]{3,2,1,0:T(8,128)(2,1)}, f32[128,2048]{1,0:T(8,128)}, bf16[48,2048]{1,0:T(8,128)(2,1)}, bf16[4,128,512]{2,1,0:T(8,128)(2,1)}) custom-call(bf16[128,2048]{1,0:T(8,128)(2,1)} %fusion.68.ref, bf16[4,2,128,2048]{3,2,1,0:T(8,128)(2,1)} %get-tuple-element.63.part_ref, ...), custom_call_target="tpu_custom_call" | custom-call | tf_op jit(solution)/shard_map/heads_gather_and_branch/pallas_call | solution.py:222
  319.5 6.0 %convolution_convert_fusion.1 = bf16[512,2048]{1,0:T(8,128)(2,1)} fusion(bf16[1024,512]{1,0:T(8,128)(2,1)S(1)} %get-tuple-element.56.o_ref, bf16[1024,2048]{1,0:T(8,128)(2,1)} %bitcast.173), kind=kOutput, calls=%fused_computation.36 | convolution fusion | flops 2148532224 | bytes 7340032 | tf_op jit(solution)/shard_map/dot_general | solution.py:29
  325.5 3.3 fusion.18.do_ref
  328.8 40.5 %attend_back.1 = (bf16[1024,512]{1,0:T(8,128)(2,1)}, bf16[4096,512]{1,0:T(8,128)(2,1)}, bf16[4,32,2048]{2,1,0:T(8,128)(2,1)}, bf16[4,128,512]{2,1,0:T(8,128)(2,1...) custom-call(bf16[4,256,512]{2,1,0:T(8,128)(2,1)} %copy-done.5, bf16[1024,512]{1,0:T(8,128)(2,1)} %fusion.18.do_ref, ...), custom_call_target="tpu_custom_call" | custom-call | tf_op jit(solution)/shard_map/attend_back/pallas_call | solution.py:1166
  369.3 4.3 convolution_convert_fusion.3
  373.6 2.7 convolution_convert_fusion.2
  376.3 37.9 %keys_and_latents_sum.1 = (f32[128,512]{1,0:T(8,128)}, f32[128,1024]{1,0:T(8,128)}, bf16[4,4,2,32,128]{4,3,2,1,0:T(8,128)(2,1)}, bf16[32,2048]{1,0:T(8,128)(2,1)...) custom-call(bf16[4,4,2,128,512]{4,3,2,1,0:T(8,128)(2,1)} %bitcast.127, bf16[4,2,128,1024]{3,2,1,0:T(8,128)(2,1)} %bitcast.131, ...), custom_call_target="tpu_custom_call" | custom-call | tf_op jit(solution)/shard_map/keys_and_latents_sum/pallas_call | solution.py:222
  416.3 1.2 multiply_reduce_fusion.3
  417.5 1.3 subtract_convert_fusion
  418.8 6.0 %fusion.29 = (f32[2048]{0:T(1024)S(1)}, f32[128]{0:T(128)S(1)}, f32[128,2048]{1,0:T(8,128)}) fusion(bf16[128,2048]{1,0:T(8,128)(2,1)S(1)} %copy-done.10, f32[128]{0:T(128)S(1)} %add_rsqrt_fusion.2, f32[2048]{0:T(1024)S(1)} %bitcast.163, bf16[2048,1664]{1,0:T(8,128)(2,1)} %bitcast.168, bf16[128,256]{1,0:T(8,128)(2,1)S(1)} %slice.242, ...), kind=kOutput, calls=%fused_computation.61 | convolution fusion | flops 808712064 | bytes 8274944 | tf_op jit(solution)/shard_map/dot_general | solution.py:33
  427.7 30.3 %firsts_gather.1 = (bf16[4,2,128,768]{3,2,1,0:T(8,128)(2,1)}, bf16[4,2,64,1536]{3,2,1,0:T(8,128)(2,1)}, bf16[4,32,2048]{2,1,0:T(8,128)(2,1)}, bf16[4,4,2,32,128]{4,3,2,1,0:T(8,128)(2,1)}) custom-call(bf16[2,128,768]{2,1,0:T(8,128)(2,1)} %bitcast.133, bf16[2,64,1536]{2,1,0:T(8,128)(2,1)} %bitcast.134, bf16[32,2048]{1,0:T(8,128)(2,1)} %get-tuple-element.82.out_ref, ...), custom_call_target="tpu_custom_call" | custom-call | tf_op jit(solution)/shard_map/firsts_gather/pallas_call | solution.py:222
  458.1 3.6 bitcast_convert_fusion
  461.7 24.4 %last_sums.1 = (f32[2,64,768]{2,1,0:T(8,128)}, f32[8,128]{1,0:T(8,128)}) custom-call(bf16[4,2,64,768]{3,2,1,0:T(8,128)(2,1)} %bitcast.145, f32[4,4,2,8,128]{4,3,2,1,0:T(8,128)} %bitcast.150), custom_call_target="tpu_custom_call" | custom-call | tf_op jit(solution)/shard_map/last_sums/pallas_call | solution.py:222
  486.1 1.3 fusion.87
  488.7 2.6 fusion.77
  491.3 2.4 reshape.349
  495.2 3.2 fusion.90
  498.5 1.9 convolution_add_fusion.2
  500.4 1.9 convolution_add_fusion.1
  502.3 1.9 convolution_add_fusion
  505.5 2.2 reshape.348
  509.1 3.2 fusion.89
  512.5 1.9 convolution_add_fusion.5
  514.4 1.9 convolution_add_fusion.4
  516.3 1.9 convolution_add_fusion.3
  522.1 2.1 reshape.350
  524.2 2.1 bitcast_convert_fusion.1
  526.3 2.5 slice_convert_fusion
  528.8 2.7 reshape.352
  531.5 2.5 pad_maximum_fusion.1
  534.1 2.5 pad_maximum_fusion
  536.6 3.5 fusion.25
  (170 shorter events, 29.0 us)
Async XLA Ops:
  7.2 7.2 %copy-start = (bf16[176,2048]{1,0:T(8,128)(2,1)S(1)}, bf16[176,2048]{1,0:T(8,128)(2,1)}, u32[]{:S(2)}) copy-start(bf16[176,2048]{1,0:T(8,128)(2,1)} %param.27) | copy-start | bytes 2162692
  7.2 206.0 %all-gather.5.cloned.1.call-start = ((), (), s32[]{:S(2)}) async-start(), calls=%async_computation.1 | async-start | bytes 3342336 | tf_op jit(solution)/shard_map/all_gather | solution.py:1196
  8.5 2.4 copy-start.15
  10.9 2.4 copy-start.31
  11.0 2.5 copy-start.24
  11.0 2.5 copy-start.25
  11.0 4.1 copy-start.20
  11.0 4.1 copy-start.22
  11.0 4.1 copy-start.23
  13.0 54.0 %copy-start.32 = (s32[1,4]{1,0:T(1,128)S(1)}, s32[1,4]{1,0:T(1,128)}, u32[]{:S(2)}) copy-start(s32[1,4]{1,0:T(1,128)} %param.16) | copy-start | bytes 52
  13.0 54.8 %copy-start.10 = (bf16[128,2048]{1,0:T(8,128)(2,1)S(1)}, bf16[128,2048]{1,0:T(8,128)(2,1)}, u32[]{:S(2)}) copy-start(bf16[128,2048]{1,0:T(8,128)(2,1)} %param.14) | copy-start | bytes 1572868
  64.7 7.5 %copy-start.18 = (bf16[32,4096]{1,0:T(8,128)(2,1)S(1)}, bf16[32,4096]{1,0:T(8,128)(2,1)}, u32[]{:S(2)}) copy-start(bf16[32,4096]{1,0:T(8,128)(2,1)} %param.20) | copy-start | bytes 786436
  64.7 148.5 %all-gather.3.cloned.1.call-start = ((), (), s32[]{:S(2)}) async-start(), calls=%async_computation | async-start | bytes 6684672 | tf_op jit(solution)/shard_map/all_gather | solution.py:1196
  68.2 6.0 %copy-start.14 = (bf16[128,2048]{1,0:T(8,128)(2,1)}, bf16[128,2048]{1,0:T(8,128)(2,1)S(1)}, u32[]{:S(2)}) copy-start(bf16[128,2048]{1,0:T(8,128)(2,1)S(1)} %fusion.21.one_ref) | copy-start | bytes 1572868
  72.1 93.0 %copy-start.11 = (f32[128,1536]{1,0:T(8,128)}, f32[128,1536]{1,0:T(8,128)S(1)}, u32[]{:S(2)}) copy-start(f32[128,1536]{1,0:T(8,128)S(1)} %fusion.16) | copy-start | bytes 2359300
  74.2 91.0 %copy-start.6 = (s32[4,1,512]{2,1,0:T(1,128)}, s32[4,1,512]{2,1,0:T(1,128)S(1)}, u32[]{:S(2)}) copy-start(s32[4,1,512]{2,1,0:T(1,128)S(1)} %tile.30.slot_ref) | copy-start | bytes 24580
  74.2 90.9 %copy-start.7 = (s32[4,1,512]{2,1,0:T(1,128)}, s32[4,1,512]{2,1,0:T(1,128)S(1)}, u32[]{:S(2)}) copy-start(s32[4,1,512]{2,1,0:T(1,128)S(1)} %tile.28.begin_ref) | copy-start | bytes 24580
  130.1 35.1 %copy-start.2 = (f32[4,128,256]{2,1,0:T(8,128)}, f32[4,128,256]{2,1,0:T(8,128)S(1)}, u32[]{:S(2)}) copy-start(f32[4,128,256]{2,1,0:T(8,128)S(1)} %get-tuple-element.131.sin_ref) | copy-start | bytes 1572868
  130.1 35.1 %copy-start.3 = (f32[4,128,256]{2,1,0:T(8,128)}, f32[4,128,256]{2,1,0:T(8,128)S(1)}, u32[]{:S(2)}) copy-start(f32[4,128,256]{2,1,0:T(8,128)S(1)} %get-tuple-element.132.cos_ref) | copy-start | bytes 1572868
  130.1 36.7 %copy-start.27 = (bf16[2,2,4,32,2048]{4,3,2,1,0:T(8,128)(2,1)S(1)}, bf16[2,2,4,32,2048]{4,3,2,1,0:T(8,128)(2,1)}, u32[]{:S(2)}) copy-start(bf16[2,2,4,32,2048]{4,3,2,1,0:T(8,128)(2,1)} %get-tuple-element.57) | copy-start | bytes 6291460
  165.2 1.0 copy-start.5
  166.2 0.6 copy-start.8
  166.8 152.7 %copy-start.4 = (bf16[1024,512]{1,0:T(8,128)(2,1)}, bf16[1024,512]{1,0:T(8,128)(2,1)S(1)}, u32[]{:S(2)}) copy-start(bf16[1024,512]{1,0:T(8,128)(2,1)S(1)} %get-tuple-element.56.o_ref) | copy-start | bytes 3145732
  213.2 69.0 %copy-start.13 = (bf16[128,2048]{1,0:T(8,128)(2,1)S(1)}, bf16[128,2048]{1,0:T(8,128)(2,1)}, u32[]{:S(2)}) copy-start(bf16[128,2048]{1,0:T(8,128)(2,1)} %cot_ref.1) | copy-start | bytes 1572868
  319.4 6.1 %copy-start.26 = (bf16[4,2,128,2048]{3,2,1,0:T(8,128)(2,1)S(1)}, bf16[4,2,128,2048]{3,2,1,0:T(8,128)(2,1)}, u32[]{:S(2)}) copy-start(bf16[4,2,128,2048]{3,2,1,0:T(8,128)(2,1)} %get-tuple-element.68) | copy-start | bytes 12582916
  319.5 6.1 %copy-start.28 = (bf16[2,2,4,32,2048]{4,3,2,1,0:T(8,128)(2,1)S(1)}, bf16[2,2,4,32,2048]{4,3,2,1,0:T(8,128)(2,1)}, u32[]{:S(2)}) copy-start(bf16[2,2,4,32,2048]{4,3,2,1,0:T(8,128)(2,1)} %get-tuple-element.57) | copy-start | bytes 6291460
  369.3 4.3 copy-start.29
  369.3 4.3 copy-start.30
  376.3 40.0 %copy-start.12 = (f32[128,1536]{1,0:T(8,128)S(1)}, f32[128,1536]{1,0:T(8,128)}, u32[]{:S(2)}) copy-start(f32[128,1536]{1,0:T(8,128)} %copy-done.11) | copy-start | bytes 2359300
  417.5 7.3 %copy-start.19 = (bf16[128,1536]{1,0:T(8,128)(2,1)S(1)}, bf16[128,1536]{1,0:T(8,128)(2,1)}, u32[]{:S(2)}) copy-start(bf16[128,1536]{1,0:T(8,128)(2,1)} %get-tuple-element.80) | copy-start | bytes 1179652
  418.8 8.1 %copy-start.21 = (bf16[128,512]{1,0:T(8,128)(2,1)S(1)}, bf16[128,512]{1,0:T(8,128)(2,1)}, u32[]{:S(2)}) copy-start(bf16[128,512]{1,0:T(8,128)(2,1)} %get-tuple-element.81) | copy-start | bytes 393220
  516.3 3.1 copy-start.16
  516.3 4.6 copy-start.17
  522.1 14.5 %copy-start.9 = (f32[128,2048]{1,0:T(8,128)S(1)}, f32[128,2048]{1,0:T(8,128)}, u32[]{:S(2)}) copy-start(f32[128,2048]{1,0:T(8,128)} %get-tuple-element.62) | copy-start | bytes 3145732
  528.8 11.2 %copy-start.1 = (bf16[176,2048]{1,0:T(8,128)(2,1)S(1)}, bf16[176,2048]{1,0:T(8,128)(2,1)}, u32[]{:S(2)}) copy-start(bf16[176,2048]{1,0:T(8,128)(2,1)} %param.27) | copy-start | bytes 2162692
Sparse Core Ops, SparseCore 0:
  64.8 59.8 all-gather.4
  126.9 65.8 all-gather.2

commit v5 on v4

--- a/solution.py
+++ b/solution.py
@@ -81,6 +81,27 @@
 KEYS, VALUES = slice(0, SIZE), slice(SIZE, 2 * SIZE)
 
 
+def sweep(segment, segments, depth, tile):
+    count = segments * segment + depth
+    last = (segment // (segments - 1)) * (depth // (lax.axis_size("z") - 1))
+    guarded = jnp.minimum(count, 1) * (1 - last) + count * last
+    free = count - guarded
+
+    @pl.loop(0, guarded)
+    def _(i):
+        tile(pl.multiple_of(i * BLOCK, BLOCK), BLOCK, True)
+
+    @pl.loop(0, free // 2)
+    def _(i):
+        tile(pl.multiple_of((guarded + 2 * i) * BLOCK, BLOCK), 2 * BLOCK, False)
+
+    @pl.loop(0, free % 2)
+    def _(i):
+        tile(pl.multiple_of((count - 1) * BLOCK, BLOCK), BLOCK, False)
+
+    tile(pl.multiple_of(count * BLOCK, BLOCK), BLOCK, True)
+
+
 def attend_kernel(
     q_ref, kv_ref, begin_ref, slot_ref, live_ref, cos_ref, sin_ref,
     out_ref, qt_ref, lse_ref, vt, peak, total, accum,
@@ -90,8 +111,10 @@
     rows = slot_ref.shape[2]
     tokens = rows // 2
     turned(kv_ref, vt, segments * (segments - 1) + depth + 1, VALUES)
-    for seg in range(segments):
-        here = pl.ds(seg * tokens, tokens)
+
+    @pl.loop(0, segments)
+    def _(seg):
+        here = pl.ds(pl.multiple_of(seg * tokens, tokens), tokens)
         cosine, sine = cos_ref[seg], sin_ref[seg]
         for head in range(2):
             raw = q_ref[here, head * SIZE : (head + 1) * SIZE].T
@@ -102,27 +125,24 @@
             qt_ref[seg, :, head * tokens : (head + 1) * tokens] = (
                 turn.astype(BF) * (SIZE ** -0.5)
             ).astype(BF)
-        query = qt_ref[seg]
-        begin = begin_ref[seg]
-        slot = slot_ref[seg]
         peak[...] = jnp.full_like(peak, MASKED)
         total[...] = jnp.zeros_like(total)
         accum[...] = jnp.zeros_like(accum)
 
-        @pl.loop(0, segments * seg + depth + 1)
-        def _(block):
-            at = pl.multiple_of(block * BLOCK, BLOCK)
-            scores = dot(kv_ref[pl.ds(at, BLOCK), KEYS], query)
-            key = lax.broadcasted_iota(jnp.int32, scores.shape, 0) + at
-            scores = jnp.where((key >= begin) & (key <= slot), scores, MASKED)
+        def tile(at, size, masked):
+            scores = dot(kv_ref[pl.ds(at, size), KEYS], qt_ref[seg])
+            if masked:
+                key = lax.broadcasted_iota(jnp.int32, scores.shape, 0) + at
+                scores = jnp.where((key >= begin_ref[seg]) & (key <= slot_ref[seg]), scores, MASKED)
             before = peak[...]
             now = jnp.maximum(before, jnp.max(scores, axis=0, keepdims=True))
             weights = jnp.exp(scores - now)
             shrink = jnp.exp(before - now)
             peak[...] = now
             total[...] = total[...] * shrink + jnp.sum(weights, axis=0, keepdims=True)
-            accum[...] = accum[...] * shrink + dot(vt[:, pl.ds(at, BLOCK)], weights.astype(BF))
-
+            accum[...] = accum[...] * shrink + dot(vt[:, pl.ds(at, size)], weights.astype(BF))
+
+        sweep(seg, segments, depth, tile)
         lse_ref[seg] = peak[...] + jnp.log(total[...])
         result = accum[...] * (live_ref[seg] / total[...])
         for head in range(2):
@@ -270,7 +290,7 @@
             spot = out.at[along("y", -d), z, c, b]
             self.shared.append(net.send(spot, spot, "c", 1))
 
-    def finish(self):
+    def arrive(self):
         net, out = self.net, self.out
         y, z, c = (lax.axis_index(a) for a in ROW)
         (a, b) = self.parts
@@ -281,6 +301,8 @@
             self.second[1][d - 1].wait_recv()
             spot = out.at[:, along("z", -d), c, b]
             self.shared.append(net.send(spot, spot, "c", 1))
+
+    def finish(self):
         for copy in self.shared:
             copy.wait_recv()
 
@@ -326,14 +348,18 @@
 
 
 STEP = 16
-
-
-def rows_loop(count, body):
-    pl.loop(0, count // STEP)(lambda i: body(pl.ds(pl.multiple_of(i * STEP, STEP), STEP)))
+CHUNK = 32 * 1024
+
+
+def rows_loop(count, width, body):
+    step = STEP
+    while 2 * step * width <= CHUNK and count % (2 * step) == 0:
+        step *= 2
+    pl.loop(0, count // step)(lambda i: body(pl.ds(pl.multiple_of(i * step, STEP), step)))
 
 
 def shifted(rows, first):
-    return pl.ds(pl.multiple_of(rows.start + first, STEP), STEP)
+    return pl.ds(pl.multiple_of(rows.start + first, STEP), rows.size)
 
 
 class RingSum:
@@ -360,7 +386,7 @@
                 value[where, c, at].astype(F32) + near[s, at].astype(F32)
             ).astype(BF)
 
-        rows_loop(count, add)
+        rows_loop(count, value.shape[3], add)
 
     def relay_far(self):
         net = self.net
@@ -392,7 +418,7 @@
                 at = shifted(rows, part.start)
                 go[s, at] = (go[s, at].astype(F32) + relay[i, rows].astype(F32)).astype(BF)
 
-            rows_loop(part.size, add)
+            rows_loop(part.size, go.shape[2], add)
             self.ends.append(net.send(go.at[s, part], come.at[i, part], self.axis, step))
 
     def finish(self):
@@ -407,7 +433,7 @@
                 value[where, c, rows].astype(F32) + near[0, rows].astype(F32)
             ) + (come[0, rows].astype(F32) + come[1, rows].astype(F32))
 
-        rows_loop(self.size, add)
+        rows_loop(self.size, out.shape[1], add)
 
 
 def ring_sum_scratch(size, width):
@@ -443,7 +469,7 @@
                         value[i, j, c, rows].astype(F32) + near[i, j, rows].astype(F32)
                     ).astype(BF)
 
-                rows_loop(self.size, add)
+                rows_loop(self.size, value.shape[4], add)
         a, b = self.parts
         self.ones = [
             [net.send(go.at[along("y", d), :, a], self.first.at[0, d - 1], "y", d) for d in LINE],
@@ -467,7 +493,7 @@
                         + (first[k, 1, j, rows].astype(F32) + first[k, 2, j, rows].astype(F32))
                     ).astype(BF)
 
-                rows_loop(self.parts[k].size, add)
+                rows_loop(self.parts[k].size, mid.shape[3], add)
             self.twos.append(
                 [net.send(mid.at[k, along(axis, d)], self.last.at[k, d - 1], axis, d) for d in LINE]
             )
@@ -486,7 +512,7 @@
                     + (last[k, 1, rows].astype(F32) + last[k, 2, rows].astype(F32))
                 )
 
-            rows_loop(self.parts[k].size, add)
+            rows_loop(self.parts[k].size, out.shape[1], add)
 
 
 def row_sum_scratch(size, width):
@@ -512,61 +538,108 @@
     return jax.ShapeDtypeStruct(dims, kind)
 
 
-def first_weights(first, both, out, down):
+def unit_places(shape_, axis, x, c, share, padded):
+    spot = lax.broadcasted_iota(jnp.int32, shape_, axis)
+    block, inside = spot // padded, spot % padded
+    return jnp.where(inside < share, (2 * block + c) * (4 * share) + x * share + inside, -1)
+
+
+OWN_COLUMNS = 640
+
+
+def first_weights(first, gate, up, out, share, padded):
+    rows_in, wide = gate.shape
+    half_wide = wide // 2
+    half_units = half_wide // (8 * share) * padded
+    units = 2 * half_units
+    rows, width = out.shape
+    quarter = rows // 4
+    lanes = (first.shape[1] - OWN_COLUMNS) // 4
+
     def body(
-        first_ref, both_ref, out_ref, down_ref, first_out, both_out, out_out, down_out, strip, sheet,
+        first_ref, gate_ref, up_ref, out_ref, first_out, both_out, strip_out, both, sends, arrivals, locals_,
+    ):
+        net = Net(sends, arrivals, locals_)
+        x, y, z, c = (lax.axis_index(a) for a in AXES)
+
+        def columns(step):
+            return pl.ds(pl.multiple_of(OWN_COLUMNS + along("x", step) * lanes, 128), lanes)
+
+        def passing(step, h):
+            return first_out.at[pl.ds(2 * h, 2), :, c, :, columns(step)]
+
+        greet(X_RING + Y_LINE + Z_LINE + TWIN)
+        part = RowGather(net, first_ref.at[:, columns(0)], first_out.at[:, :, :, :, columns(0)])
+        every = pl.ds(0, OWN_COLUMNS)
+        whole = RowGather(net, first_ref.at[:, every], first_out.at[:, :, :, :, every])
+        piece = out_ref.at[pl.ds(pl.multiple_of(x * quarter, quarter), quarter)]
+        piece_mine = net.keep(piece, strip_out.at[z])
+        pieces = [net.send(piece, strip_out.at[z], "z", d) for d in LINE]
+        stacked = jnp.concatenate(
+            [ref[:, h * half_wide : (h + 1) * half_wide] for ref in (gate_ref, up_ref) for h in range(2)], axis=0
+        )
+
+        def pick(core):
+            places = unit_places((1, half_units), 1, x, core, share, padded)
+            picks = lax.broadcasted_iota(jnp.int32, (half_wide, half_units), 0) == places
+            picked = dot(stacked, picks.astype(BF)).astype(BF)
+            for i in range(4):
+                both[core, :, i * half_units : (i + 1) * half_units] = (
+                    picked[i * rows_in : (i + 1) * rows_in]
+                )
+
+        pick(0)
+        part.spread()
+        whole.spread()
+        pick(1)
+        both_mine = net.keep(both.at[c], both_out.at[c])
+        both_come = net.send(both.at[1 - c], both_out.at[c], "c", 1)
+        part.arrive()
+        right = [net.send(passing(0, h), passing(0, h), "x", 1) for h in (0, 1)]
+        left = [net.send(passing(0, h), passing(0, h), "x", -1) for h in (1, 0)]
+        whole.arrive()
+        right[0].wait_recv()
+        far = [net.send(passing(-1, 0), passing(-1, 0), "x", 1)]
+        left[0].wait_recv()
+        far.append(net.send(passing(1, 1), passing(1, 1), "x", -1))
+        shared = []
+        for copies, step in ((right, -1), (left, 1)):
+            copies[1].wait_recv()
+            spot = first_out.at[:, :, c, :, columns(step)]
+            shared.append(net.send(spot, spot, "c", 1))
+        for copy in far:
+            copy.wait_recv()
+        spot = first_out.at[:, :, c, :, columns(2)]
+        shared.append(net.send(spot, spot, "c", 1))
+        part.finish()
+        whole.finish()
+        for copy in shared + pieces + [both_come]:
+            copy.wait_recv()
+        both_mine.wait()
+        piece_mine.wait()
+        net.close()
+
+    outs = (shape(4, 4, 2, *first.shape), shape(2, rows_in, 2 * units), shape(4, quarter, width))
+    return comm_call(
+        body, "first_weights", 1, outs, (first, gate, up, out), [pltpu.VMEM((2, rows_in, 2 * units), BF)], 64, 4,
+        [IN_VMEM] * 4, [ANYWHERE] * 3,
+    )
+
+
+def keys_and_latents(key_value, latent, up, strip):
+    def body(
+        kv_ref, lat_ref, up_ref, strip_ref, kv_out, lat_out, up_out, out_out, transit, sheet,
         sends, arrivals, locals_,
     ):
         net = Net(sends, arrivals, locals_)
         x, y, z, c = (lax.axis_index(a) for a in AXES)
-        quarter = out_ref.shape[0] // 4
         greet(X_LINE + Y_LINE + Z_LINE + TWIN)
-        row = RowGather(net, first_ref, first_out)
-        piece = out_ref.at[pl.ds(pl.multiple_of(x * quarter, quarter), quarter)]
-        piece_mine = net.keep(piece, strip.at[z])
-        pieces = [net.send(piece, strip.at[z], "z", d) for d in LINE]
-        both_mine = net.keep(both_ref.at[c], both_out.at[c])
-        both_come = net.send(both_ref.at[1 - c], both_out.at[c], "c", 1)
-        down_mine = net.keep(down_ref, down_out)
-        row.spread()
-        piece_mine.wait()
-        for copy in pieces:
-            copy.wait_recv()
-        strip_mine = net.keep(strip, sheet.at[:, x])
-        strips = [net.send(strip, sheet.at[:, x], "x", d) for d in LINE]
-        row.finish()
-        strip_mine.wait()
-        for copy in strips:
-            copy.wait_recv()
-        half = sheet.shape[0] // 2
-        sheet_keep = net.keep(sheet.at[pl.ds(half * c, half)], out_out.at[:, c])
-        sheet_come = net.send(sheet.at[pl.ds(half * (1 - c), half)], out_out.at[:, c], "c", 1)
-        for copy in (both_mine, sheet_keep, down_mine):
-            copy.wait()
-        for copy in (both_come, sheet_come):
-            copy.wait_recv()
-        net.close()
-
-    rows, width = out.shape
-    quarter = rows // 4
-    outs = (
-        shape(4, 4, 2, *first.shape), shape(*both.shape), shape(2, 2, 4, quarter, width), shape(*down.shape),
-    )
-    scratch = [pltpu.VMEM((4, quarter, width), BF), pltpu.VMEM((4, 4, quarter, width), BF)]
-    return comm_call(
-        body, "first_weights", 1, outs, (first, both, out, down), scratch, 36, 8, [IN_VMEM] * 4, [ANYWHERE] * 4,
-    )
-
-
-def keys_and_latents(key_value, latent, up):
-    def body(kv_ref, lat_ref, up_ref, kv_out, lat_out, up_out, transit, sends, arrivals, locals_):
-        net = Net(sends, arrivals, locals_)
-        y, z, c = (lax.axis_index(a) for a in ROW)
-        greet(Y_LINE + Z_LINE + TWIN)
         up_mine = net.keep(up_ref.at[y], transit.at[y, z])
         ups = [net.send(up_ref.at[along("y", d)], transit.at[y, z], "y", d) for d in LINE]
         row = RowGather(net, kv_ref, kv_out)
         ring = RingGather(net, lat_ref, lat_out, "y")
+        strip_mine = net.keep(strip_ref, sheet.at[:, x])
+        strips = [net.send(strip_ref, sheet.at[:, x], "x", d) for d in LINE]
         up_mine.wait()
         for copy in ups:
             copy.wait_recv()
@@ -574,21 +647,35 @@
         row.spread()
         ring.forward()
         ring.share()
+        row.arrive()
+        strip_mine.wait()
+        for copy in strips:
+            copy.wait_recv()
+        half = sheet.shape[0] // 2
+        sheet_keep = net.keep(sheet.at[pl.ds(half * c, half)], out_out.at[:, c])
+        sheet_come = net.send(sheet.at[pl.ds(half * (1 - c), half)], out_out.at[:, c], "c", 1)
         for copy in ups:
             copy.wait_recv()
         up_keep = net.keep(transit.at[:, :, c], up_out.at[:, :, c])
         up_come = net.send(transit.at[:, :, 1 - c], up_out.at[:, :, c], "c", 1)
+        ring.finish()
         row.finish()
-        ring.finish()
-        up_keep.wait()
-        up_come.wait_recv()
+        for copy in (up_keep, sheet_keep):
+            copy.wait()
+        for copy in (up_come, sheet_come):
+            copy.wait_recv()
         net.close()
 
     _, _, high, thin = up.shape
-    outs = (shape(4, 4, 2, *key_value.shape), shape(4, 2, *latent.shape), shape(4, 4, 2, high, thin))
+    _, quarter, width = strip.shape
+    outs = (
+        shape(4, 4, 2, *key_value.shape), shape(4, 2, *latent.shape), shape(4, 4, 2, high, thin),
+        shape(2, 2, 4, quarter, width),
+    )
+    scratch = [pltpu.VMEM((4, 4, 2, high, thin), BF), pltpu.VMEM((4, 4, quarter, width), BF)]
     return comm_call(
-        body, "keys_and_latents", 2, outs, (key_value, latent, up), [pltpu.VMEM((4, 4, 2, high, thin), BF)], 44, 4,
-        [IN_VMEM] * 3, [ANYWHERE] * 3,
+        body, "keys_and_latents", 2, outs, (key_value, latent, up, strip), scratch, 48, 6,
+        [IN_VMEM] * 4, [ANYWHERE] * 4,
     )
 
 
@@ -623,7 +710,7 @@
 
 
 def add_all(terms, out):
-    rows_loop(out.shape[0], lambda rows: add_up(terms, out, rows))
+    rows_loop(out.shape[0], out.shape[1], lambda rows: add_up(terms, out, rows))
 
 
 def feed_forward(normed_two, normed, grad_out, both, down):
@@ -635,7 +722,7 @@
 
     def body(
         two_ref, one_ref, cot_hbm, both_hbm, down_hbm, sum_out, one_out, branch_out, gb_out, mid_out,
-        two, cot, both, down, hidden, grads, part, near, go, come, gb, gd, down_come,
+        two, cot, both, down, hidden, grads, part, near, go, come, gb, gd, down_come, ahead,
         sends, arrivals, locals_,
     ):
         net = Net(sends, arrivals, locals_)
@@ -654,12 +741,15 @@
             for d in LINE
         ]
 
+        def back(s):
+            return dot_nt(cot[along("x", s)].reshape(2 * size, width), down[...])
+
         def block(s):
             where = along("x", s)
             at = pl.ds(pl.multiple_of(where * 2 * size, 2 * size), 2 * size)
             value = two[where].reshape(2 * size, width)
             pre = dot(value, both[...])
-            grad = dot_nt(cot[where].reshape(2 * size, width), down[...])
+            grad = ahead[s - 1] if s else back(0)
             gate, up = pre[:, :units], pre[:, units:]
             sigma = 1.0 / (1.0 + jnp.exp(-gate))
             gated = gate * sigma
@@ -683,6 +773,8 @@
         cot_load.wait()
         swaps[0] = block(0)
         feed.forward()
+        for s in LINE:
+            ahead[s - 1] = back(s)
         feed.share()
         one_mine.wait()
         spot = one_out.at[y, c]
@@ -767,11 +859,15 @@
         pltpu.VMEM((8, 2 * size, 2 * units), BF),
         pltpu.VMEM((2, 4, 4, high, lanes), BF),
         pltpu.VMEM((2, 3, 4, high, lanes), BF),
+        pltpu.VMEM((3, 2 * size, units), F32),
     ]
     return comm_call(
         body, "feed_forward", 4, outs, (normed_two, normed, grad_out, both, down), scratch, 32, 14,
         [IN_VMEM] * 2 + [ANYWHERE] * 3, [IN_VMEM, ANYWHERE, ANYWHERE, ANYWHERE, IN_VMEM],
     )
+
+
+GB_PARTS = (640, 384, 512)
 
 
 class FirstStep:
@@ -810,7 +906,7 @@
     size, width = value.shape
     _, _, high, lanes = mid.shape
     _, _, tall, wide = gb.shape
-    third = wide // 3
+    skip, third = GB_PARTS[:2]
 
     def body(ref, part_ref, mid_ref, gb_ref, out, part_out, mid_out, gb_out, *rest):
         net = Net(*rest[8:])
@@ -818,7 +914,7 @@
         gathering = RingGather(net, ref, out, "y")
         ring = RingSum(net, part_ref, part_out, "x", *rest[:4])
         halves = [SecondStep(net, mid_ref.at[k], axis, rest[4 + k]) for k, axis in enumerate(("z", "y"))]
-        step = FirstStep(net, gb_ref, pl.ds(third, third), "z", rest[6], rest[7], gb_out)
+        step = FirstStep(net, gb_ref, pl.ds(skip, third), "z", rest[6], rest[7], gb_out)
         ring.relay_far()
         ring.issue()
         gathering.forward()
@@ -852,11 +948,12 @@
     width = partial.shape[3]
     high, lanes = grad_up.shape[3], grad_up.shape[4] // 4
     _, quarter, wide = grad_out.shape
-    tall, third = mids[0].shape[1:]
+    tall, ahead = mids[0].shape[1:]
+    after = mids[1].shape[2]
 
     def body(
-        kv_ref, part_ref, up_ref, out_ref, one_ref, two_ref, down_ref, kv_out, part_out, up_out, out_out, mid_out,
-        down_out, *rest,
+        kv_ref, part_ref, up_ref, out_ref, one_ref, two_ref, down_ref, kv_out, part_out, up_out, out_out, one_out,
+        two_out, down_out, *rest,
     ):
         net = Net(*rest[13:])
         up_come, out_come = rest[9:11]
@@ -888,18 +985,16 @@
         add_all([out_ref.at[z]] + [out_come.at[d] for d in range(3)], out_out)
         for copy in ups:
             copy.wait_recv()
-        for i in range(4):
-
-            @pl.loop(0, 8)
-            def _(k, i=i):
-                j, core = k // 2, k % 2
-                add_all(
-                    [up_ref.at[i, j, core, :, lane(x)]] + [up_come.at[d, i, j, core] for d in range(3)],
-                    up_out.at[i, j, core],
-                )
-
-        halves[0].finish(mid_out.at[:, pl.ds(0, third)])
-        halves[1].finish(mid_out.at[:, pl.ds(2 * third, third)])
+
+        @pl.loop(0, 4)
+        def _(i):
+            up_out[i] = (
+                (up_ref[i, :, :, :, lane(x)].astype(F32) + up_come[0, i].astype(F32))
+                + (up_come[1, i].astype(F32) + up_come[2, i].astype(F32))
+            ).astype(BF)
+
+        halves[0].finish(one_out)
+        halves[1].finish(two_out)
         ring.finish()
         row.finish()
         down_mine.wait()
@@ -909,28 +1004,34 @@
 
     outs = (
         shape(size, thin, kind=F32), shape(size, width, kind=F32), shape(4, 4, 2, high, lanes),
-        shape(quarter, wide), shape(tall, 3 * third), shape(4, *grad_down.shape),
+        shape(quarter, wide), shape(tall, ahead), shape(tall, after), shape(4, *grad_down.shape),
     )
     scratch = [
         pltpu.VMEM((3, 4, 4, 2, high, lanes), BF),
         pltpu.VMEM((3, quarter, wide), BF),
-        pltpu.VMEM((3, tall, third), BF),
-        pltpu.VMEM((3, tall, third), BF),
+        pltpu.VMEM((3, tall, ahead), BF),
+        pltpu.VMEM((3, tall, after), BF),
     ]
     return comm_call(
         body, "keys_and_latents_sum", 7, outs, (grad_kv, partial, grad_up, grad_out, *mids, grad_down),
         row_sum_scratch(size, thin) + ring_sum_scratch(size, width) + scratch, 46, 2,
-        [IN_VMEM] * 7, [IN_VMEM] * 5 + [ANYWHERE],
-    )
-
-
-def firsts_gather(value, both, grad_out, grad_up):
+        [IN_VMEM] * 7, [IN_VMEM] * 6 + [ANYWHERE],
+    )
+
+
+def firsts_gather(value, both, grad_out, grad_up, weights):
+    _, size, part = value.shape
+    tiles = weights.shape[0] // BLOCK
+    tall, wide = grad_out.shape
+    _, _, _, high, lanes = grad_up.shape
+
     def body(
-        ref, both_ref, out_ref, up_ref, gathered, both_out, out_out, up_out, up_come, up_sum, up_y,
-        sends, arrivals, locals_,
+        ref, both_ref, out_ref, up_ref, weights_hbm, gathered, both_out, out_out, up_out, back_out,
+        up_come, up_sum, up_y, weights_ref, sends, arrivals, locals_,
     ):
         net = Net(sends, arrivals, locals_)
         x, y, z, c = (lax.axis_index(a) for a in AXES)
+        load = net.keep(weights_hbm, weights_ref)
         greet(X_LINE + Y_LINE + Z_LINE + TWIN)
         mine = net.keep(ref.at[c], gathered.at[y, c])
         come = net.send(ref.at[1 - c], gathered.at[y, c], "c", 1)
@@ -952,6 +1053,16 @@
         right = [net.send(spot, spot, "x", 1) for spot in (zero, one)]
         left = [net.send(spot, spot, "x", -1) for spot in (one, zero)]
 
+        def back(i):
+            at = pl.ds(pl.multiple_of(i * BLOCK, BLOCK), BLOCK)
+            total = 0.0
+            for core in range(2):
+                columns = slice(core * part, (core + 1) * part)
+                total = total + dot_nt(ref[core], weights_ref[at, columns])
+            back_out[:, at] = total
+
+        load.wait()
+        pl.loop(0, tiles // 2)(back)
         for copy in ups:
             copy.wait_recv()
         for i in range(4):
@@ -981,6 +1092,7 @@
         left[0].wait_recv()
         spot = both_out.at[along("x", 1), 1]
         far.append(net.send(spot, spot, "x", -1))
+        pl.loop(tiles // 2, tiles)(back)
 
         up_near.wait_recv()
         up_mine.wait()
@@ -991,25 +1103,32 @@
         out_mine.wait()
         net.close()
 
-    tall, wide = grad_out.shape
-    _, _, _, high, lanes = grad_up.shape
     outs = (
         shape(4, *value.shape), shape(4, *both.shape), shape(4, tall, wide), shape(4, 4, 2, high, lanes),
+        shape(size, weights.shape[0], kind=F32),
     )
     scratch = [
         pltpu.VMEM((3, 4, 2, high, lanes), BF),
         pltpu.VMEM((4, 2, high, lanes), BF),
         pltpu.VMEM((4, 2, high, lanes), BF),
+        pltpu.VMEM(weights.shape, BF),
     ]
     return comm_call(
-        body, "firsts_gather", 8, outs, (value, both, grad_out, grad_up), scratch, 40, 6,
-        [IN_VMEM] * 4, [ANYWHERE, ANYWHERE, IN_VMEM, IN_VMEM],
-    )
-
-
-def last_sums(grad_first, gains):
+        body, "firsts_gather", 8, outs, (value, both, grad_out, grad_up, weights), scratch, 40, 6,
+        [IN_VMEM] * 4 + [ANYWHERE], [ANYWHERE, ANYWHERE, IN_VMEM, IN_VMEM, IN_VMEM],
+    )
+
+
+def last_sums(grad_first, gains, grad_both, grad_down, grad_up, share):
+    rows = grad_both.shape[2]
+    half_units = grad_both.shape[3] // 4
+    padded, width = grad_down.shape[1:]
+    half_wide = 2 * half_units // padded * 4 * share
+    up_rows, up_lanes = grad_up.shape[3:]
+
     def body(
-        first_ref, gain_ref, first_out, gain_out, wide, first_come, first_x,
+        first_ref, gain_ref, both_ref, down_ref, up_ref, first_out, gain_out, gate_out, up_out, down_out, q_up_out,
+        accum, down_rows, wide, first_come, first_x,
         gain_near, gain_one, gain_come, gain_two, gain_y, gain_three, gain_x, sends, arrivals, locals_,
     ):
         net = Net(sends, arrivals, locals_)
@@ -1024,6 +1143,17 @@
             [net.send(wide.at[core, along("z", d)], first_come.at[d - 1, core], "z", d) for d in LINE]
             for core in range(2)
         ]
+        accum[...] = jnp.zeros_like(accum)
+
+        def put(i):
+            px, pc = i // 2, i % 2
+            places = unit_places((half_units, 1), 0, px, pc, share, padded)
+            picks = lax.broadcasted_iota(jnp.int32, (half_units, half_wide), 1) == places
+            stacked = jnp.concatenate(
+                [both_ref[px, pc, :, k * half_units : (k + 1) * half_units] for k in range(4)], axis=0
+            )
+            accum[...] += dot(stacked, picks.astype(BF))
+
         near.wait_recv()
         gain_one[...] = gain_ref[:, :, c] + gain_near[...]
         comes = [net.send(gain_one.at[:, along("z", d)], gain_come.at[d - 1], "z", d) for d in LINE]
@@ -1034,17 +1164,28 @@
             spot = first_x.at[x, core]
             return [net.send(spot, spot, "x", d) for d in LINE]
 
+        pl.loop(0, 3)(put)
         finals = [onward(0)]
         for copy in comes:
             copy.wait_recv()
         gain_two[...] = (gain_one[:, z] + gain_come[0]) + (gain_come[1] + gain_come[2])
         comes = [net.send(gain_two.at[along("y", d)], gain_y.at[d - 1], "y", d) for d in LINE]
         finals.append(onward(1))
+        pl.loop(3, 8)(put)
         for copy in comes:
             copy.wait_recv()
         gain_three[...] = (gain_two[y] + gain_y[0]) + (gain_y[1] + gain_y[2])
         gain_mine = net.keep(gain_three, gain_x.at[x])
         comes = [net.send(gain_three, gain_x.at[x], "x", d) for d in LINE]
+        for k, target in enumerate((gate_out, gate_out, up_out, up_out)):
+            target[:, (k % 2) * half_wide : (k % 2 + 1) * half_wide] = accum[k * rows : (k + 1) * rows].astype(BF)
+        for px in range(4):
+            down_rows[px * share : (px + 1) * share, :] = down_ref[px].astype(F32)[:share]
+            for py in range(4):
+                for pc in range(2):
+                    at = ((2 * py + pc) * 4 + px) * up_lanes
+                    q_up_out[:, at : at + up_lanes] = up_ref[px, py, pc]
+        down_out[...] = down_rows[...].astype(BF)
         for core in range(2):
             for copy in finals[core]:
                 copy.wait_recv()
@@ -1056,8 +1197,13 @@
         net.close()
 
     _, _, high, lanes = grad_first.shape
-    outs = (shape(2, high, lanes, kind=F32), shape(8, 128, kind=F32))
+    outs = (
+        shape(2, high, lanes, kind=F32), shape(8, 128, kind=F32), shape(rows, 2 * half_wide),
+        shape(rows, 2 * half_wide), shape(4 * share, width), shape(up_rows, 32 * up_lanes),
+    )
     scratch = [
+        pltpu.VMEM((4 * rows, half_wide), F32),
+        pltpu.VMEM((4 * share, width), F32),
         pltpu.VMEM((2, 4, high, lanes), BF),
         pltpu.VMEM((3, 2, high, lanes), BF),
         pltpu.VMEM((4, 2, high, lanes), BF),
@@ -1070,20 +1216,22 @@
         pltpu.VMEM((4, 8, 128), F32),
     ]
     return comm_call(
-        body, "last_sums", 9, outs, (grad_first, gains), scratch, 24, 2, [IN_VMEM] * 2, [IN_VMEM] * 2,
+        body, "last_sums", 9, outs, (grad_first, gains, grad_both, grad_down, grad_up), scratch, 24, 2,
+        [IN_VMEM] * 5, [IN_VMEM] * 6,
     )
 
 
 def attend_back_kernel(
     qt_ref, do_ref, o_ref, kv_ref, begin_ref, slot_ref, lse_ref, cos_ref, sin_ref, go_ref, mid_ref, gb_ref,
     dq_ref, dkv_ref, go_out, one_out, two_out, mid_out,
-    kt, sums, accum, gb_own, gb_come, mid_come, stack, go_come, sends, arrivals, locals_,
+    kt, sums, accum, query, grad_rows, grad_turned, delta, own_one, come_one, own_two, come_two, mid_come, stack, go_come, sends, arrivals, locals_,
 ):
     net = Net(sends, arrivals, locals_)
     x, c = lax.axis_index("x"), lax.axis_index("c")
     greet(X_LINE + Y_LINE + Z_LINE + TWIN)
     half = go_ref.shape[0]
-    third = mid_ref.shape[-1]
+    wide = gb_ref.shape[-1]
+    ahead, _, after = GB_PARTS
     quarter = go_out.shape[1]
 
     def strip(at):
@@ -1092,8 +1240,8 @@
     go_mine = net.keep(go_ref.at[:, c], stack.at[pl.ds(half * c, half)])
     go_near = net.send(go_ref.at[:, 1 - c], stack.at[pl.ds(half * c, half)], "c", 1)
     steps = [
-        FirstStep(net, gb_ref, pl.ds(0, third), "y", gb_own.at[0], gb_come.at[0], one_out),
-        FirstStep(net, gb_ref, pl.ds(2 * third, third), "z", gb_own.at[1], gb_come.at[1], two_out),
+        FirstStep(net, gb_ref, pl.ds(0, ahead), "y", own_one, come_one, one_out),
+        FirstStep(net, gb_ref, pl.ds(wide - after, after), "z", own_two, come_two, two_out),
     ]
     second = SecondStep(net, mid_ref, "y", mid_come)
     go_mine.wait()
@@ -1105,39 +1253,38 @@
     tokens = rows // 2
     sums[...] = jnp.zeros_like(sums)
     turned(kv_ref, kt, segments * (segments - 1) + depth + 1, KEYS)
-    for seg in range(segments):
-        here = pl.ds(seg * tokens, tokens)
+
+    @pl.loop(0, segments)
+    def _(seg):
+        here = pl.ds(pl.multiple_of(seg * tokens, tokens), tokens)
 
         def stacked(ref):
             value = ref[here, :]
             return jnp.concatenate([value[:, :SIZE], value[:, SIZE:]], axis=0)
 
-        query_t = qt_ref[seg]
-        query = query_t.T
         grad = stacked(do_ref)
-        grad_t = grad.T
-        delta = jnp.sum(
-            grad_t.astype(F32) * stacked(o_ref).T.astype(F32), axis=0, keepdims=True
+        query[...] = qt_ref[seg].T
+        grad_rows[...] = grad
+        grad_turned[...] = grad.T
+        delta[...] = jnp.sum(
+            grad_turned[...].astype(F32) * stacked(o_ref).T.astype(F32), axis=0, keepdims=True
         )
-        begin = begin_ref[seg]
-        slot = slot_ref[seg]
-        lse = lse_ref[seg]
         accum[...] = jnp.zeros_like(accum)
 
-        @pl.loop(0, segments * seg + depth + 1)
-        def _(block):
-            at = pl.multiple_of(block * BLOCK, BLOCK)
-            keys = pl.ds(at, BLOCK)
-            scores = dot(kv_ref[keys, KEYS], query_t)
-            key = lax.broadcasted_iota(jnp.int32, scores.shape, 0) + at
-            allowed = (key >= begin) & (key <= slot)
-            probs = jnp.where(allowed, jnp.exp(scores - lse), 0.0)
-            grad_probs = dot(kv_ref[keys, VALUES], grad_t)
-            grad_scores = (probs * (grad_probs - delta)).astype(BF)
-            sums[keys, VALUES] += dot(probs.astype(BF), grad)
-            sums[keys, KEYS] += dot(grad_scores, query)
+        def tile(at, size, masked):
+            keys = pl.ds(at, size)
+            scores = dot(kv_ref[keys, KEYS], qt_ref[seg])
+            probs = jnp.exp(scores - lse_ref[seg])
+            if masked:
+                key = lax.broadcasted_iota(jnp.int32, scores.shape, 0) + at
+                probs = jnp.where((key >= begin_ref[seg]) & (key <= slot_ref[seg]), probs, 0.0)
+            grad_probs = dot(kv_ref[keys, VALUES], grad_turned[...])
+            grad_scores = (probs * (grad_probs - delta[...])).astype(BF)
+            sums[keys, VALUES] += dot(probs.astype(BF), grad_rows[...])
+            sums[keys, KEYS] += dot(grad_scores, query[...])
             accum[...] += dot(kt[:, keys], grad_scores)
 
+        sweep(seg, segments, depth, tile)
         cosine, sine = cos_ref[seg], sin_ref[seg]
         for head in range(2):
             part = accum[:, head * tokens : (head + 1) * tokens] * (SIZE ** -0.5)
@@ -1162,7 +1309,7 @@
     segments, _, rows = slot.shape
     half, _, tall, wide = grad_out.shape
     _, high, third = mid.shape
-    part = jax.ShapeDtypeStruct((4, high, third), BF)
+    ahead, _, after = GB_PARTS
     return pl.pallas_call(
         attend_back_kernel,
         name="attend_back",
@@ -1170,8 +1317,8 @@
             jax.ShapeDtypeStruct(do.shape, BF),
             jax.ShapeDtypeStruct(kv.shape, BF),
             jax.ShapeDtypeStruct((2 * half, tall // 4, wide), BF),
-            part,
-            part,
+            jax.ShapeDtypeStruct((4, high, ahead), BF),
+            jax.ShapeDtypeStruct((4, high, after), BF),
             jax.ShapeDtypeStruct((high, third), BF),
         ),
         in_specs=[IN_VMEM] * 11 + [ANYWHERE],
@@ -1180,8 +1327,14 @@
             pltpu.VMEM((SIZE, kv.shape[0]), BF),
             pltpu.VMEM(kv.shape, F32),
             pltpu.VMEM((SIZE, rows), F32),
-            pltpu.VMEM((2, 4, high, third), BF),
-            pltpu.VMEM((2, 3, 4, high, third), BF),
+            pltpu.VMEM((rows, SIZE), BF),
+            pltpu.VMEM((rows, SIZE), BF),
+            pltpu.VMEM((SIZE, rows), BF),
+            pltpu.VMEM((1, rows), F32),
+            pltpu.VMEM((4, high, ahead), BF),
+            pltpu.VMEM((3, 4, high, ahead), BF),
+            pltpu.VMEM((4, high, after), BF),
+            pltpu.VMEM((3, 4, high, after), BF),
             pltpu.VMEM((3, high, third), BF),
             pltpu.VMEM((2 * half, tall, wide), BF),
             pltpu.VMEM((3, 2 * half, tall // 4, wide), BF),
@@ -1234,34 +1387,16 @@
     per_heads = q_up.shape[1] // members
     q_rows = q_up.shape[0]
 
-    wide = gate_weight.shape[1]
     down_rows = down_weight.shape[0]
     share = down_rows // n_x
     padded = -(-share // 16) * 16
-    source = lax.broadcasted_iota(jnp.int32, (wide // 2, n_c * (span // 4) * padded), 0)
-    target = lax.broadcasted_iota(jnp.int32, source.shape, 1)
-    block_at = target // (padded * (span // 4)) + n_c * ((target // padded) % (span // 4))
-    inside = target % padded
-    picks = (
-        (source == block_at * down_rows + x * share + inside) & (inside < share)
-    ).astype(BF)
-
-    def spread(weight):
-        stacked = jnp.concatenate([weight[:, : wide // 2], weight[:, wide // 2 :]], axis=0)
-        part = dot(stacked, picks).astype(BF)
-        part = part.reshape(2, shard, n_c, -1).transpose(2, 1, 0, 3)
-        return part.reshape(n_c, shard, -1)
-
-    both = jnp.concatenate([spread(gate_weight), spread(up_weight)], axis=2)
-    units = both.shape[-1] // 2
     down_part = lax.dynamic_slice_in_dim(down_weight, x * share, share)
     down_part = jnp.pad(down_part, ((0, padded - share), (0, 0)))
-    first_full, both, out_heads, down_part = first_weights(first, both, out_weight, down_part)
-    out_heads = out_heads.reshape(per_heads, width)
+    first_full, both, out_strip = first_weights(first, gate_weight, up_weight, out_weight, share, padded)
+    units = both.shape[2] // 2
     first_full = first_full.reshape(span * shard, -1)
     both = both.reshape(n_c * shard, 2 * units)
     extra_full = first_full[:, first_width : first_width + 3].astype(F32)
-    first_full = first_full[:, :first_width]
     gain_one = extra_full[:, 0]
     gain_two = extra_full[:, 1]
     gain_latent = extra_full[:, 2].reshape(span, shard)[:, : q_gain.shape[0]].reshape(-1)
@@ -1272,17 +1407,18 @@
     inputs = block_input.astype(F32)
     inverse_one = lax.rsqrt(jnp.mean(inputs * inputs, axis=-1, keepdims=True) + EPSILON)
     normed = (inputs * inverse_one * gain_one).astype(BF)
-    firsts = dot(normed, first_full)
+    firsts = dot(normed, first_full[:, :first_width])
     latent = firsts[:, :latent_width]
     inverse_latent = lax.rsqrt(jnp.mean(latent * latent, axis=-1, keepdims=True) + EPSILON)
     latent_normed = (latent * inverse_latent * gain_latent).astype(BF)
     key_mine = rotate(firsts[:, latent_width : latent_width + SIZE], cosine, sine).astype(BF)
     value_mine = firsts[:, latent_width + SIZE :].astype(BF)
-    key_value, latent_group, up_heads = keys_and_latents(
+    key_value, latent_group, up_heads, out_heads = keys_and_latents(
         jnp.concatenate([key_mine, value_mine], axis=1), latent_normed,
-        q_up.reshape(q_rows, n_y, n_c, per_heads).transpose(1, 2, 0, 3),
+        q_up.reshape(q_rows, n_y, n_c, per_heads).transpose(1, 2, 0, 3), out_strip,
     )
     up_heads = up_heads.reshape(span * q_rows, per_heads)
+    out_heads = out_heads.reshape(per_heads, width)
     key_value = key_value.reshape(span * rows, 2 * SIZE)
     group = members * rows
     latent_group = latent_group.reshape(group, latent_width)
@@ -1303,17 +1439,6 @@
     grad_result = cotangent.astype(F32)
     grad_mid_norm, grad_gain_two = norm_back(middle, inverse_two, gain_two, grad_normed_two)
     grad_middle = grad_result + grad_mid_norm
-
-    def collect(grads):
-        parts = grads.reshape(n_x, n_c, shard, 2, units // 2).transpose(0, 3, 2, 1, 4)
-        parts = parts.reshape(n_x, 2 * shard, n_c * units // 2)
-        whole = 0.0
-        for i in range(n_x):
-            picked = (
-                (source == block_at * down_rows + i * share + inside) & (inside < share)
-            ).astype(BF)
-            whole = whole + dot_nt(parts[i], picked)
-        return jnp.concatenate([whole[:shard], whole[shard:]], axis=1)
 
     grad_both = grad_both.reshape(n_y, n_z, n_c * shard, 2 * units)
     grad_branch, branch_two, grad_down, grad_mid = heads_gather_and_branch(
@@ -1330,14 +1455,13 @@
         cosine_group, sine_group, grad_out.reshape(n_z // n_c, n_c, out_rows, width), grad_mid, grad_both,
     )
     grad_up_heads = dot_tn(latent_group, grad_query_raw).astype(BF)
-    grad_kv, grad_latent_normed, grad_up_heads, grad_out, grad_both, grad_down = keys_and_latents_sum(
+    grad_kv, grad_latent_normed, grad_up_heads, grad_out, grad_one, grad_two, grad_down = keys_and_latents_sum(
         grad_kv.reshape(n_y, n_z, n_c, rows, 2 * SIZE),
         dot_nt(grad_query_raw, up_heads).astype(BF).reshape(n_y, n_c, rows, latent_width),
         grad_up_heads.reshape(n_y, n_z, n_c, q_rows, per_heads),
         grad_out, (grad_one, grad_two), grad_down,
     )
-    third = grad_mid.shape[1]
-    grad_both = jnp.concatenate([grad_both[:, :third], grad_mid, grad_both[:, 2 * third :]], axis=1)
+    grad_both = jnp.concatenate([grad_one, grad_mid, grad_two], axis=1)
     grad_key_raw = unrotate(grad_kv[:, :SIZE], cosine, sine).astype(BF)
     grad_value_raw = grad_kv[:, SIZE:].astype(BF)
     grad_latent_f, grad_gain_latent = norm_back(
@@ -1346,17 +1470,15 @@
     grad_firsts = jnp.concatenate(
         [grad_latent_f.astype(BF), grad_key_raw, grad_value_raw], axis=1
     )
-    grad_normed = dot_nt(grad_firsts, first_full)
+    half_first = first_width // n_c
+    first_part, grad_both, grad_out, grad_up_heads, grad_normed = firsts_gather(
+        grad_firsts.reshape(rows, n_c, half_first).transpose(1, 0, 2),
+        grad_both.reshape(n_c, shard, 2 * units), grad_out, grad_up_heads, first_full,
+    )
+    first_part = first_part.reshape(group, half_first)
+    grad_first = dot_tn(normed_part, first_part).astype(BF)
     grad_input_norm, grad_gain_one = norm_back(inputs, inverse_one, gain_one, grad_normed)
     input_grad = grad_middle + grad_input_norm
-
-    half_first = first_width // n_c
-    first_part, grad_both, grad_out, grad_up_heads = firsts_gather(
-        grad_firsts.reshape(rows, n_c, half_first).transpose(1, 0, 2),
-        grad_both.reshape(n_c, shard, 2 * units), grad_out, grad_up_heads,
-    )
-    first_part = first_part.reshape(group, half_first)
-    grad_first = dot_tn(normed_part, first_part).astype(BF)
     gains = jnp.concatenate(
         [
             grad_gain_one.reshape(span, shard),
@@ -1367,28 +1489,25 @@
     )
     shares = gains.shape[1]
     gains = jnp.pad(gains, ((0, 0), (0, 8 * 128 - shares))).reshape(n_y, n_z, n_c, 8, 128)
-    grad_first, gains = last_sums(grad_first.reshape(n_z, n_c, shard, half_first), gains)
+    grad_first, gains, grad_gate, grad_up, grad_down, grad_q_up = last_sums(
+        grad_first.reshape(n_z, n_c, shard, half_first), gains, grad_both, grad_down, grad_up_heads, share
+    )
     gains = gains.reshape(-1)
     grad_first = jnp.concatenate([grad_first[0], grad_first[1]], axis=1)
-    grad_out = grad_out.reshape(out_rows, width).astype(F32)
-    grad_q_up = grad_up_heads.transpose(3, 1, 2, 0, 4).reshape(q_rows, -1).astype(F32)
-    grad_gate = collect(grad_both[..., :units])
-    grad_up = collect(grad_both[..., units:])
-    grad_down = grad_down[:, :share].reshape(down_rows, width).astype(F32)
     return (
         output,
         input_grad,
         gains[:shard],
         grad_first[:, :latent_width],
         gains[2 * shard : shares],
-        grad_q_up,
+        grad_q_up.astype(F32),
         grad_first[:, latent_width : latent_width + SIZE],
         grad_first[:, latent_width + SIZE :],
-        grad_out,
+        grad_out.reshape(out_rows, width).astype(F32),
         gains[shard : 2 * shard],
-        grad_gate,
-        grad_up,
-        grad_down,
+        grad_gate.astype(F32),
+        grad_up.astype(F32),
+        grad_down.astype(F32),
     )
 
 

time: 557 us -> 476 us (0.85)
  matrix products: 59.7 us -> 31.6 us
  Pallas kernels: 403 us -> 378 us
  local copies, waits for them, and re-layouts: 32.6 us -> 13.2 us
    dot_general x11 -> x2, matrix products: 30 us -> 6.01 us  [dot_nt(): lax.dot_general(left, right, (((1,), (1,)), ((), ())), preferred_element_...]
    pallas_call x8, Pallas kernels: 331 us -> 316 us  [comm_call(): pl.pallas_call(body, name=name, out_shape=outs, in_specs=spaces, out_spec...]
    pallas_call x1, Pallas kernels: 31.5 us -> 17 us  [attend(): pl.pallas_call(attend_kernel, name='attend', out_shape=(jax.ShapeDtypeStr...]
    slice x10 -> x0, local copies, waits for them, and re-layouts: 8.51 us -> none  [the longest x1 2.65 us: on_device(): grad_up = collect(grad_both[..., units:])]
    reshape x10 -> x0, local copies, waits for them, and re-layouts: 7.05 us -> none  [the longest x4 6.28 us: collect(): grads.reshape(n_x, n_c, shard, 2, units // 2).transpose(0, 3, 2, 1, 4)]
    convert_element_type x3 -> x0, local copies, waits for them, and re-layouts: 5.99 us -> none  [the longest x2 3.27 us: on_device(): grad_up_heads.transpose(3, 1, 2, 0, 4).reshape(q_rows, -1).astype(F32)]
    dot_general x5 -> x3, matrix products: 15.7 us -> 11.9 us  [dot(): return jnp.dot(left, right, preferred_element_type=F32)]
  transfers between devices with their start and end apart: 2 -> 2, of which waited for: 0 -> 0; matrix products, arithmetic and copies ran while one was open for 5% -> 6% of each run, Pallas kernels for 22% -> 30%
where the time goes in v5:
time: 476 us; the launch traced here: 470 us
  Pallas kernels  378 us (79%)
  other arithmetic  32.5 us (7%)
  matrix products  31.6 us (7%)
  between operations  15 us (3%)
  local copies, waits for them, and re-layouts  13.2 us (3%)
    pallas_call x8, Pallas kernels, comm_call(): pl.pallas_call(body, name=name, out_shape=outs, in_specs=spaces, out_spec...  316 us
    pallas_call x1, Pallas kernels, attend_back(): pl.pallas_call(attend_back_kernel, name='attend_back', out_shape=(jax.Sha...  45.1 us
    pallas_call x1, Pallas kernels, attend(): pl.pallas_call(attend_kernel, name='attend', out_shape=(jax.ShapeDtypeStr...  17 us
    dot_general x3, matrix products, dot_tn(): lax.dot_general(left, right, (((0,), (0,)), ((), ())), preferred_element_...  13.6 us
    dot_general x3, matrix products, dot(): return jnp.dot(left, right, preferred_element_type=F32)  11.9 us
  transfers between devices with their start and end apart: 2, of which 0 were waited for; matrix products, arithmetic and copies ran while one was open for 6% of the time, Pallas kernels for 30%

profile of v5, /device:TPU:1, one launch (start us, length us, event | category | flops | bytes accessed | tf_op | source)
XLA Modules:
  0.0 470.1 jit_solution(4628317860301607159)
XLA Ops:
  7.3 1.0 copy-done
  10.6 1.6 fusion.15.first_ref
  12.2 45.4 %first_weights.1 = (bf16[4,4,2,64,1664]{4,3,2,1,0:T(8,128)(2,1)}, bf16[2,64,1536]{2,1,0:T(8,128)(2,1)}, bf16[4,32,2048]{2,1,0:T(8,128)(2,1)}) custom-call(bf16[64,1664]{1,0:T(8,128)(2,1)} %fusion.15.first_ref, bf16[64,5632]{1,0:T(8,128)(2,1)} %gate_ref.1, bf16[64,5632]{1,0:T(8,128)(2,1)} %up_ref.1, bf16[128,2048]{1,0:T(8,128)(2,1)} %out_ref.1), custom_call_target="tpu_custom_call" | custom-call | tf_op jit(solution)/shard_map/first_weights/pallas_call | solution.py:242
  58.5 0.7 fusion.35
  59.3 0.7 pad_add_fusion
  60.5 0.8 copy.53
  61.3 1.2 slice_convert_fusion
  62.5 1.4 slice_reduce_fusion
  64.5 4.0 fusion
  69.8 0.8 multiply_convert_fusion.1.lat_ref
  70.6 46.2 %keys_and_latents.1 = (bf16[4,4,2,128,512]{4,3,2,1,0:T(8,128)(2,1)}, bf16[4,2,128,1024]{3,2,1,0:T(8,128)(2,1)}, bf16[4,4,2,32,512]{4,3,2,1,0:T(8,128)(2,1)}, bf16[2,2,4,32,2048]{4,3,2,1,0:T(8,128)(2,1)}) custom-call(bf16[128,512]{1,0:T(8,128)(2,1)} %pad_maximum_fusion.3.kv_ref, bf16[128,1024]{1,0:T(8,128)(2,1)} %multiply_convert_fusion.1.lat_ref, ...), custom_call_target="tpu_custom_call" | custom-call | tf_op jit(solution)/shard_map/keys_and_latents/pallas_call | solution.py:242
  116.8 1.9 multiply_sine_fusion
  118.7 3.5 fusion.39.q_ref
  122.3 17.0 %attend.1 = (bf16[1024,512]{1,0:T(8,128)(2,1)S(1)}, bf16[4,256,512]{2,1,0:T(8,128)(2,1)S(1)}, f32[4,1,512]{2,1,0:T(1,128)S(1)}) custom-call(f32[1024,512]{1,0:T(8,128)S(1)} %fusion.39.q_ref, bf16[4096,512]{1,0:T(8,128)(2,1)} %bitcast.70, s32[4,1,512]{2,1,0:T(1,128)S(1)} %tile.28.begin_ref, s32[4,1,512]{2,1,0:T(1,128)S(1)} %tile.30.slot_ref, ...), custom_call_target="tpu_custom_call" | custom-call | tf_op jit(solution)/shard_map/attend/pallas_call | solution.py:156
  139.4 4.4 convolution_convert_fusion
  143.8 30.3 %heads_sum_and_cotangent.1 = (f32[128,2048]{1,0:T(8,128)}, bf16[4,2,128,2048]{3,2,1,0:T(8,128)(2,1)}) custom-call(bf16[4,2,128,2048]{3,2,1,0:T(8,128)(2,1)} %bitcast.75, bf16[128,2048]{1,0:T(8,128)(2,1)} %cot_ref.1), custom_call_target="tpu_custom_call" | custom-call | tf_op jit(solution)/shard_map/heads_sum_and_cotangent/pallas_call | solution.py:242
  174.1 1.4 multiply_reduce_fusion.2
  176.2 0.9 multiply_convert_fusion.two_ref
  177.2 66.7 %feed_forward.1 = (f32[128,2048]{1,0:T(8,128)}, bf16[4,2,128,512]{3,2,1,0:T(8,128)(2,1)}, bf16[4,2,128,2048]{3,2,1,0:T(8,128)(2,1)}, bf16[2048,1536]{1,0:T(8,128)(2,1)}, bf16[2,4,48,1024]{3,2,1,0:T(8,128)(2,1)}) custom-call(bf16[128,2048]{1,0:T(8,128)(2,1)} %multiply_convert_fusion.two_ref, bf16[128,2048]{1,0:T(8,128)(2,1)} %copy-done.18, ...), custom_call_target="tpu_custom_call" | custom-call | tf_op jit(solution)/shard_map/feed_forward/pallas_call | solution.py:242
  243.9 1.6 multiply_reduce_fusion
  245.5 1.2 fusion.36.ref
  246.7 32.1 %heads_gather_and_branch.1 = (bf16[4,2,128,2048]{3,2,1,0:T(8,128)(2,1)}, f32[128,2048]{1,0:T(8,128)}, bf16[48,2048]{1,0:T(8,128)(2,1)}, bf16[4,128,384]{2,1,0:T(8,128)(2,1)}) custom-call(bf16[128,2048]{1,0:T(8,128)(2,1)} %fusion.36.ref, bf16[4,2,128,2048]{3,2,1,0:T(8,128)(2,1)} %get-tuple-element.69.part_ref, ...), custom_call_target="tpu_custom_call" | custom-call | tf_op jit(solution)/shard_map/heads_gather_and_branch/pallas_call | solution.py:242
  278.9 6.1 %convolution_convert_fusion.1 = bf16[512,2048]{1,0:T(8,128)(2,1)} fusion(bf16[1024,512]{1,0:T(8,128)(2,1)S(1)} %get-tuple-element.63.o_ref, bf16[1024,2048]{1,0:T(8,128)(2,1)} %bitcast.92), kind=kOutput, calls=%fused_computation.3 | convolution fusion | flops 2148532224 | bytes 7340032 | tf_op jit(solution)/shard_map/dot_general | solution.py:29
  285.0 3.3 fusion.2.do_ref
  288.3 45.1 %attend_back.1 = (bf16[1024,512]{1,0:T(8,128)(2,1)}, bf16[4096,512]{1,0:T(8,128)(2,1)}, bf16[4,32,2048]{2,1,0:T(8,128)(2,1)}, bf16[4,128,640]{2,1,0:T(8,128)(2,1...) custom-call(bf16[4,256,512]{2,1,0:T(8,128)(2,1)} %copy-done.5, bf16[1024,512]{1,0:T(8,128)(2,1)} %fusion.2.do_ref, ...), custom_call_target="tpu_custom_call" | custom-call | tf_op jit(solution)/shard_map/attend_back/pallas_call | solution.py:1313
  333.5 4.3 convolution_convert_fusion.3
  337.7 2.7 convolution_convert_fusion.2
  340.4 38.0 %keys_and_latents_sum.1 = (f32[128,512]{1,0:T(8,128)}, f32[128,1024]{1,0:T(8,128)}, bf16[4,4,2,32,128]{4,3,2,1,0:T(8,128)(2,1)}, bf16[32,2048]{1,0:T(8,128)(2,1)...) custom-call(bf16[4,4,2,128,512]{4,3,2,1,0:T(8,128)(2,1)} %bitcast.76, ...), custom_call_target="tpu_custom_call" | custom-call | tf_op jit(solution)/shard_map/keys_and_latents_sum/pallas_call | solution.py:242
  378.4 1.2 fusion.30
  379.6 0.9 slice.138
  380.6 1.2 multiply_reduce_fusion.3
  381.8 1.3 subtract_convert_fusion
  383.4 0.9 copy.46
  384.4 1.7 pad_maximum_fusion.1
  386.1 29.0 %firsts_gather.1 = (bf16[4,2,128,768]{3,2,1,0:T(8,128)(2,1)}, bf16[4,2,64,1536]{3,2,1,0:T(8,128)(2,1)}, bf16[4,32,2048]{2,1,0:T(8,128)(2,1)}, bf16[4,4,2,32,128]{4,3,2,1,0:T(8,128)(2,1)}, f32[128,2048]{1,0:T(8,128)}) custom-call(bf16[2,128,768]{2,1,0:T(8,128)(2,1)} %bitcast.79, bf16[2,64,1536]{2,1,0:T(8,128)(2,1)} %bitcast.80, ...), custom_call_target="tpu_custom_call" | custom-call | tf_op jit(solution)/shard_map/firsts_gather/pallas_call | solution.py:242
  415.1 1.5 fusion.13
  417.5 3.3 bitcast_convert_fusion
  420.8 27.8 %last_sums.1 = (f32[2,64,768]{2,1,0:T(8,128)}, f32[8,128]{1,0:T(8,128)}, bf16[64,5632]{1,0:T(8,128)(2,1)}, bf16[64,5632]{1,0:T(8,128)(2,1)}, bf16[176,2048]{1,0:T(8,128)(2,1)}, /*index=5*/bf16[32,4096]{1,0:T(8,128)(2,1)}) custom-call(bf16[4,2,64,768]{3,2,1,0:T(8,128)(2,1)} %bitcast.84, f32[4,4,2,8,128]{4,3,2,1,0:T(8,128)} %bitcast.85, ...), custom_call_target="tpu_custom_call" | custom-call | tf_op jit(solution)/shard_map/last_sums/pallas_call | solution.py:242
  448.7 1.3 slice.98
  450.0 1.3 fusion.38
  451.3 1.0 slice_bitcast_fusion.1
  453.0 0.7 pad_maximum_fusion.2
  453.7 1.8 convert_element_type.131
  455.6 1.1 bitcast_convert_fusion.1
  456.7 1.2 convert_element_type.134
  457.9 1.2 convert_element_type.135
  459.1 1.3 convert_element_type.136
  461.0 1.8 fusion.9
  (121 shorter events, 8.7 us)
Async XLA Ops:
  7.2 1.1 copy-start
  7.2 50.5 %copy-start.32 = (s32[1,4]{1,0:T(1,128)S(1)}, s32[1,4]{1,0:T(1,128)}, u32[]{:S(2)}) copy-start(s32[1,4]{1,0:T(1,128)} %param.16) | copy-start | bytes 52
  7.2 170.0 %all-gather.5.cloned.1.call-start = ((), (), s32[]{:S(2)}) async-start(), calls=%async_computation.1 | async-start | bytes 3342336 | tf_op jit(solution)/shard_map/all_gather | solution.py:1349
  8.3 52.0 %copy-start.24 = (bf16[32,4096]{1,0:T(8,128)(2,1)S(1)}, bf16[32,4096]{1,0:T(8,128)(2,1)}, u32[]{:S(2)}) copy-start(bf16[32,4096]{1,0:T(8,128)(2,1)} %param.20) | copy-start | bytes 786436
  9.1 168.1 %all-gather.3.cloned.1.call-start = ((), (), s32[]{:S(2)}) async-start(), calls=%async_computation | async-start | bytes 6684672 | tf_op jit(solution)/shard_map/all_gather | solution.py:1349
  60.2 62.1 %copy-start.6 = (s32[4,1,512]{2,1,0:T(1,128)}, s32[4,1,512]{2,1,0:T(1,128)S(1)}, u32[]{:S(2)}) copy-start(s32[4,1,512]{2,1,0:T(1,128)S(1)} %tile.28.begin_ref) | copy-start | bytes 24580
  60.3 62.0 %copy-start.7 = (s32[4,1,512]{2,1,0:T(1,128)}, s32[4,1,512]{2,1,0:T(1,128)S(1)}, u32[]{:S(2)}) copy-start(s32[4,1,512]{2,1,0:T(1,128)S(1)} %tile.30.slot_ref) | copy-start | bytes 24580
  61.3 2.8 copy-start.9
  64.5 4.0 copy-start.18
  68.5 53.8 %copy-start.14 = (f32[128,1536]{1,0:T(8,128)}, f32[128,1536]{1,0:T(8,128)S(1)}, u32[]{:S(2)}) copy-start(f32[128,1536]{1,0:T(8,128)S(1)} %fusion) | copy-start | bytes 2359300
  118.7 3.6 copy-start.2
  118.7 3.6 copy-start.3
  122.3 17.0 %copy-start.27 = (bf16[2,2,4,32,2048]{4,3,2,1,0:T(8,128)(2,1)S(1)}, bf16[2,2,4,32,2048]{4,3,2,1,0:T(8,128)(2,1)}, u32[]{:S(2)}) copy-start(bf16[2,2,4,32,2048]{4,3,2,1,0:T(8,128)(2,1)} %get-tuple-element.64) | copy-start | bytes 6291460
  139.3 4.5 copy-start.5
  139.3 4.5 copy-start.8
  139.3 139.5 %copy-start.4 = (bf16[1024,512]{1,0:T(8,128)(2,1)}, bf16[1024,512]{1,0:T(8,128)(2,1)S(1)}, u32[]{:S(2)}) copy-start(bf16[1024,512]{1,0:T(8,128)(2,1)S(1)} %get-tuple-element.63.o_ref) | copy-start | bytes 3145732
  143.8 30.3 %copy-start.10 = (bf16[128,2048]{1,0:T(8,128)(2,1)S(1)}, bf16[128,2048]{1,0:T(8,128)(2,1)}, u32[]{:S(2)}) copy-start(bf16[128,2048]{1,0:T(8,128)(2,1)} %param.14) | copy-start | bytes 1572868
  243.9 1.7 copy-start.12
  243.9 1.7 copy-start.16
  278.9 6.1 %copy-start.26 = (bf16[4,2,128,2048]{3,2,1,0:T(8,128)(2,1)S(1)}, bf16[4,2,128,2048]{3,2,1,0:T(8,128)(2,1)}, u32[]{:S(2)}) copy-start(bf16[4,2,128,2048]{3,2,1,0:T(8,128)(2,1)} %get-tuple-element.74) | copy-start | bytes 12582916
  278.9 6.1 %copy-start.28 = (bf16[2,2,4,32,2048]{4,3,2,1,0:T(8,128)(2,1)S(1)}, bf16[2,2,4,32,2048]{4,3,2,1,0:T(8,128)(2,1)}, u32[]{:S(2)}) copy-start(bf16[2,2,4,32,2048]{4,3,2,1,0:T(8,128)(2,1)} %get-tuple-element.64) | copy-start | bytes 6291460
  333.4 4.3 copy-start.30
  333.4 4.3 copy-start.31
  340.4 40.2 %copy-start.15 = (f32[128,1536]{1,0:T(8,128)S(1)}, f32[128,1536]{1,0:T(8,128)}, u32[]{:S(2)}) copy-start(f32[128,1536]{1,0:T(8,128)} %copy-done.14) | copy-start | bytes 2359300
  381.8 2.5 copy-start.25
  386.1 31.4 %copy-start.29 = (bf16[4,2,128,512]{3,2,1,0:T(8,128)(2,1)S(1)}, bf16[4,2,128,512]{3,2,1,0:T(8,128)(2,1)}, u32[]{:S(2)}) copy-start(bf16[4,2,128,512]{3,2,1,0:T(8,128)(2,1)} %get-tuple-element.91) | copy-start | bytes 3145732
  448.6 6.9 %copy-start.23 = (bf16[4,32,2048]{2,1,0:T(8,128)(2,1)S(1)}, bf16[4,32,2048]{2,1,0:T(8,128)(2,1)}, u32[]{:S(2)}) copy-start(bf16[4,32,2048]{2,1,0:T(8,128)(2,1)} %get-tuple-element.99) | copy-start | bytes 1572868
  448.7 8.0 %copy-start.22 = (bf16[64,5632]{1,0:T(8,128)(2,1)S(1)}, bf16[64,5632]{1,0:T(8,128)(2,1)}, u32[]{:S(2)}) copy-start(bf16[64,5632]{1,0:T(8,128)(2,1)} %get-tuple-element.100) | copy-start | bytes 2162692
  453.7 4.2 copy-start.21
  456.7 2.4 copy-start.20
  457.9 2.5 copy-start.11
  457.9 2.5 copy-start.13
  457.9 2.5 copy-start.17
  457.9 3.1 copy-start.19
  460.4 2.5 copy-start.1
Sparse Core Ops, SparseCore 0:
  10.8 55.7 all-gather.4
  68.8 71.9 all-gather.2

commit v6 on v5

--- a/solution.py
+++ b/solution.py
@@ -342,9 +342,15 @@
             copy.wait_recv()
         spot = self.out.at[along(self.axis, 2), lax.axis_index("c")]
         self.shared.append(self.net.send(spot, spot, "c", 1))
+        self.arrived()
+
+    def arrived(self):
+        if self.mine is not None:
+            self.mine.wait()
+            self.mine = None
         for copy in self.shared:
             copy.wait_recv()
-        self.mine.wait()
+        self.shared = []
 
 
 STEP = 16
@@ -766,8 +772,7 @@
             return net.send(go.at[s - 1], come.at[s - 1], "x", s)
 
         swaps = {}
-        feed.mine.wait()
-        feed.shared[0].wait_recv()
+        feed.arrived()
         both_load.wait()
         down_load.wait()
         cot_load.wait()
@@ -783,8 +788,7 @@
             ones[d - 1].wait_recv()
             spot = one_out.at[along("y", -d), c]
             shared.append(net.send(spot, spot, "c", 1))
-        feed.shared[1].wait_recv()
-        feed.shared[2].wait_recv()
+        feed.arrived()
         swaps[1] = block(1)
         for copy in feed.far:
             copy.wait_recv()
@@ -867,7 +871,7 @@
     )
 
 
-GB_PARTS = (640, 384, 512)
+Y_COLUMNS = 640
 
 
 class FirstStep:
@@ -902,132 +906,131 @@
         add_all([self.mid.at[here]] + [self.come.at[d] for d in range(3)], out)
 
 
-def heads_gather_and_branch(value, partial, mid, gb):
-    size, width = value.shape
-    _, _, high, lanes = mid.shape
-    _, _, tall, wide = gb.shape
-    skip, third = GB_PARTS[:2]
-
-    def body(ref, part_ref, mid_ref, gb_ref, out, part_out, mid_out, gb_out, *rest):
-        net = Net(*rest[8:])
-        greet(X_RING + Y_LINE + Z_LINE + TWIN)
-        gathering = RingGather(net, ref, out, "y")
-        ring = RingSum(net, part_ref, part_out, "x", *rest[:4])
-        halves = [SecondStep(net, mid_ref.at[k], axis, rest[4 + k]) for k, axis in enumerate(("z", "y"))]
-        step = FirstStep(net, gb_ref, pl.ds(skip, third), "z", rest[6], rest[7], gb_out)
-        ring.relay_far()
-        ring.issue()
-        gathering.forward()
-        ring.pass_on()
-        gathering.share()
-        for k in range(2):
-            halves[k].finish(mid_out.at[:, pl.ds(k * lanes, lanes)])
-        gathering.finish()
-        ring.finish()
-        step.finish()
-        net.close()
-
-    outs = (
-        shape(4, 2, size, width), shape(size, width, kind=F32), shape(high, 2 * lanes), shape(4, tall, third),
-    )
-    scratch = [
-        pltpu.VMEM((3, high, lanes), BF),
-        pltpu.VMEM((3, high, lanes), BF),
-        pltpu.VMEM((4, tall, third), BF),
-        pltpu.VMEM((3, 4, tall, third), BF),
-    ]
-    return comm_call(
-        body, "heads_gather_and_branch", 6, outs, (value, partial, mid, gb),
-        ring_sum_scratch(size, width) + scratch, 30, 3,
-        [IN_VMEM] * 3 + [ANYWHERE], [ANYWHERE] + [IN_VMEM] * 3,
-    )
-
-
-def keys_and_latents_sum(grad_kv, partial, grad_up, grad_out, mids, grad_down):
+def keys_and_latents_sum(
+    grad_kv, grad_query, latent_group, up_heads, grad_out, mids, cosine, sine, latent, inverse, gain,
+):
     _, _, _, size, thin = grad_kv.shape
-    width = partial.shape[3]
-    high, lanes = grad_up.shape[3], grad_up.shape[4] // 4
-    _, quarter, wide = grad_out.shape
+    group, width = latent_group.shape
+    per = up_heads.shape[1]
+    high, lanes = up_heads.shape[0] // 32, per // 4
+    _, out_rows, wide = grad_out.shape
+    quarter = out_rows // 4
     tall, ahead = mids[0].shape[1:]
     after = mids[1].shape[2]
+    part = (width + thin) // 2
 
     def body(
-        kv_ref, part_ref, up_ref, out_ref, one_ref, two_ref, down_ref, kv_out, part_out, up_out, out_out, one_out,
-        two_out, down_out, *rest,
+        kv_ref, query_ref, group_ref, heads_ref, out_ref, one_ref, two_ref, cos_ref, sin_ref, latent_ref, inverse_ref,
+        gain_ref, firsts_out, gain_out, up_out, out_out, one_out, two_out, *rest,
     ):
-        net = Net(*rest[13:])
+        net = Net(*rest[17:])
         up_come, out_come = rest[9:11]
-        x, z = lax.axis_index("x"), lax.axis_index("z")
+        partial, ups_here, kv_sum, part_sum = rest[13:17]
+        x = lax.axis_index("x")
 
         def lane(at):
             return pl.ds(pl.multiple_of(at * lanes, lanes), lanes)
 
+        def strip(at):
+            return pl.ds(pl.multiple_of(at * quarter, quarter), quarter)
+
         greet(X_LINE + Y_LINE + Z_LINE + TWIN)
-        row = RowSum(net, kv_ref, kv_out, *rest[:5])
-        ring = RingSum(net, part_ref, part_out, "y", *rest[5:9])
+        row = RowSum(net, kv_ref, kv_sum, *rest[:5])
+        outs = [net.send(out_ref.at[:, strip(along("x", d))], out_come.at[d - 1], "x", d) for d in LINE]
+        for i in range(4):
+            at = pl.ds(i * 2 * size, 2 * size)
+            partial[i] = dot_nt(query_ref[at, :], heads_ref[...]).astype(BF).reshape(2, size, width)
+        ring = RingSum(net, partial, part_sum, "y", *rest[5:9])
+        ups_here[...] = dot_tn(group_ref[...], query_ref[...]).astype(BF).reshape(4, 4, 2, high, per)
         ups = [
-            net.send(up_ref.at[:, :, :, :, lane(along("x", d))], up_come.at[d - 1], "x", d) for d in LINE
+            net.send(ups_here.at[:, :, :, :, lane(along("x", d))], up_come.at[d - 1], "x", d) for d in LINE
         ]
-        outs = [net.send(out_ref.at[along("z", d)], out_come.at[d - 1], "z", d) for d in LINE]
+        row.start()
         halves = [
             SecondStep(net, mid, axis, come)
             for mid, axis, come in ((one_ref, "z", rest[11]), (two_ref, "y", rest[12]))
         ]
-        down_mine = net.keep(down_ref, down_out.at[x])
-        downs = [net.send(down_ref, down_out.at[x], "x", d) for d in LINE]
-        row.start()
         ring.relay_far()
         ring.issue()
         row.turn()
         ring.pass_on()
-        for copy in outs:
-            copy.wait_recv()
-        add_all([out_ref.at[z]] + [out_come.at[d] for d in range(3)], out_out)
         for copy in ups:
             copy.wait_recv()
 
         @pl.loop(0, 4)
         def _(i):
             up_out[i] = (
-                (up_ref[i, :, :, :, lane(x)].astype(F32) + up_come[0, i].astype(F32))
+                (ups_here[i, :, :, :, lane(x)].astype(F32) + up_come[0, i].astype(F32))
                 + (up_come[1, i].astype(F32) + up_come[2, i].astype(F32))
             ).astype(BF)
 
+        ring.finish()
+        values = latent_ref[...]
+        scale = inverse_ref[...]
+        scaled = part_sum[...] * gain_ref[...]
+        gain_out[...] = jnp.sum(part_sum[...] * values * scale, axis=0, keepdims=True)
+        back = scale * scaled - values * (scale * scale * scale) * jnp.mean(scaled * values, axis=-1, keepdims=True)
+        firsts_out[0] = back[:, :part].astype(BF)
+        firsts_out[1, :, : width - part] = back[:, part:].astype(BF)
+        row.finish()
+        lower, upper = kv_sum[:, :HALF], kv_sum[:, HALF:SIZE]
+        at = width - part
+        firsts_out[1, :, at : at + HALF] = (lower * cos_ref[...] + upper * sin_ref[...]).astype(BF)
+        firsts_out[1, :, at + HALF : at + SIZE] = (upper * cos_ref[...] - lower * sin_ref[...]).astype(BF)
+        firsts_out[1, :, at + SIZE :] = kv_sum[:, SIZE:].astype(BF)
         halves[0].finish(one_out)
         halves[1].finish(two_out)
-        ring.finish()
-        row.finish()
-        down_mine.wait()
-        for copy in downs:
-            copy.wait_recv()
+        for copy in outs:
+            copy.wait_recv()
+        for i in range(4):
+            add_all([out_ref.at[i, strip(x)]] + [out_come.at[d, i] for d in range(3)], out_out.at[i])
         net.close()
 
     outs = (
-        shape(size, thin, kind=F32), shape(size, width, kind=F32), shape(4, 4, 2, high, lanes),
-        shape(quarter, wide), shape(tall, ahead), shape(tall, after), shape(4, *grad_down.shape),
+        shape(2, size, part), shape(1, width, kind=F32), shape(4, 4, 2, high, lanes), shape(4, quarter, wide),
+        shape(tall, ahead), shape(tall, after),
     )
     scratch = [
         pltpu.VMEM((3, 4, 4, 2, high, lanes), BF),
-        pltpu.VMEM((3, quarter, wide), BF),
+        pltpu.VMEM((3, 4, quarter, wide), BF),
         pltpu.VMEM((3, tall, ahead), BF),
         pltpu.VMEM((3, tall, after), BF),
+        pltpu.VMEM((4, 2, size, width), BF),
+        pltpu.VMEM((4, 4, 2, high, per), BF),
+        pltpu.VMEM((size, thin), F32),
+        pltpu.VMEM((size, width), F32),
     ]
     return comm_call(
-        body, "keys_and_latents_sum", 7, outs, (grad_kv, partial, grad_up, grad_out, *mids, grad_down),
+        body, "keys_and_latents_sum", 7, outs,
+        (
+            grad_kv, grad_query, latent_group, up_heads, grad_out, *mids, cosine, sine, latent, inverse, gain,
+        ),
         row_sum_scratch(size, thin) + ring_sum_scratch(size, width) + scratch, 46, 2,
-        [IN_VMEM] * 7, [IN_VMEM] * 6 + [ANYWHERE],
-    )
-
-
-def firsts_gather(value, both, grad_out, grad_up, weights):
+        [IN_VMEM] * 12, [IN_VMEM] * 6,
+    )
+
+
+def last_sums(
+    value, both, grad_out, grad_up, grad_down, normed_part, inputs, inverse, gain_one, gain_two, gain_latent, weights,
+    share,
+):
     _, size, part = value.shape
-    tiles = weights.shape[0] // BLOCK
-    tall, wide = grad_out.shape
+    deep = weights.shape[0]
+    tiles = deep // BLOCK
+    _, tall, wide = grad_out.shape
     _, _, _, high, lanes = grad_up.shape
+    rows = both.shape[1]
+    half_units = both.shape[2] // 4
+    padded, width = grad_down.shape
+    half_wide = 2 * half_units // padded * 4 * share
 
     def body(
-        ref, both_ref, out_ref, up_ref, weights_hbm, gathered, both_out, out_out, up_out, back_out,
-        up_come, up_sum, up_y, weights_ref, sends, arrivals, locals_,
+        ref, both_ref, out_ref, up_ref, down_ref, normed_ref, input_ref, inverse_ref, gain_ref, two_ref, latent_ref,
+        weights_hbm,
+        first_out, gain_out, back_out, out_out, gate_out, up_weight_out, down_out, q_up_out,
+        gathered, both_all, up_all, down_all, out_come, up_come, up_sum, up_y, weights_ref, accum, down_rows,
+        first_here, pair, first_come, first_x, gain_here, gain_near, gain_come, gain_two, gain_y, gain_x,
+        sends, arrivals, locals_,
     ):
         net = Net(sends, arrivals, locals_)
         x, y, z, c = (lax.axis_index(a) for a in AXES)
@@ -1035,11 +1038,11 @@
         greet(X_LINE + Y_LINE + Z_LINE + TWIN)
         mine = net.keep(ref.at[c], gathered.at[y, c])
         come = net.send(ref.at[1 - c], gathered.at[y, c], "c", 1)
-        both_mine = net.keep(both_ref.at[c], both_out.at[x, c])
-        both_come = net.send(both_ref.at[1 - c], both_out.at[x, c], "c", 1)
+        both_mine = net.keep(both_ref.at[c], both_all.at[x, c])
+        both_come = net.send(both_ref.at[1 - c], both_all.at[x, c], "c", 1)
         ups = [net.send(up_ref.at[:, along("z", d)], up_come.at[d - 1], "z", d) for d in LINE]
-        outs = [net.send(out_ref, out_out.at[x], "x", d) for d in LINE]
-        out_mine = net.keep(out_ref, out_out.at[x])
+        outs = [net.send(out_ref.at[along("z", d)], out_come.at[d - 1], "z", d) for d in LINE]
+        down_mine = net.keep(down_ref, down_all.at[x])
 
         mine.wait()
         spot = gathered.at[y, c]
@@ -1049,7 +1052,7 @@
         ahead += [net.send(spot, spot, "y", 1), net.send(spot, spot, "y", -1)]
         both_mine.wait()
         both_come.wait_recv()
-        zero, one = both_out.at[x, 0], both_out.at[x, 1]
+        zero, one = both_all.at[x, 0], both_all.at[x, 1]
         right = [net.send(spot, spot, "x", 1) for spot in (zero, one)]
         left = [net.send(spot, spot, "x", -1) for spot in (one, zero)]
 
@@ -1066,10 +1069,10 @@
         for copy in ups:
             copy.wait_recv()
         for i in range(4):
-            for core in range(2):
-                add_all(
-                    [up_ref.at[i, z, core]] + [up_come.at[d, i, core] for d in range(3)], up_sum.at[i, core]
-                )
+            up_sum[i] = (
+                (up_ref[i, z].astype(F32) + up_come[0, i].astype(F32))
+                + (up_come[1, i].astype(F32) + up_come[2, i].astype(F32))
+            ).astype(BF)
         ups = [net.send(up_sum.at[along("y", d)], up_y.at[y], "y", d) for d in LINE]
         up_mine = net.keep(up_sum.at[y], up_y.at[y])
 
@@ -1080,269 +1083,291 @@
         spot = gathered.at[along("y", 1), 1 - c]
         ahead.append(net.send(spot, spot, "y", -1))
 
+        pl.loop(tiles // 2, tiles)(back)
+        values = input_ref[...].astype(F32)
+        scale = inverse_ref[...]
+        grad = back_out[...]
+        gain_own = jnp.sum(grad * values * scale, axis=0, keepdims=True)
+        scaled = grad * gain_ref[...]
+        back_out[...] = scale * scaled - values * (scale * scale * scale) * jnp.mean(
+            scaled * values, axis=-1, keepdims=True
+        )
+        gain_here[...] = jnp.zeros_like(gain_here)
+        for i in range(16):
+            gain_here[i // 4, i % 4, 0:1, :] = gain_own[:, i * 128 : (i + 1) * 128]
+            gain_here[i // 4, i % 4, 1:2, :] = two_ref[:, i * 128 : (i + 1) * 128]
+            gain_here[i // 4, i % 4, 2:3, :] = latent_ref[:, i // 2 * 128 : (i // 2 + 1) * 128]
+        near = net.send(gain_here, gain_near, "c", 1)
+
+        right[0].wait_recv()
+        spot = both_all.at[along("x", -1), 0]
+        far = [net.send(spot, spot, "x", 1)]
+        left[0].wait_recv()
+        spot = both_all.at[along("x", 1), 1]
+        far.append(net.send(spot, spot, "x", -1))
+
+        for copy in [ahead[i] for i in (1, 2, 4, 5)]:
+            copy.wait_recv()
+        first_here[...] = (
+            dot_tn(normed_ref[...], gathered[...].reshape(8 * size, part)).astype(BF).reshape(4, 2, rows, part)
+        )
+        first_near = net.send(first_here.at[:, 1 - c], pair.at[c], "c", 1)
+        first_mine = net.keep(first_here.at[:, c], pair.at[c])
+
+        for copy in outs:
+            copy.wait_recv()
+        add_all([out_ref.at[z]] + [out_come.at[d] for d in range(3)], out_out.at[x])
+        spot = out_out.at[x]
+        outs = [net.send(spot, spot, "x", d) for d in LINE]
         up_mine.wait()
         for copy in ups:
             copy.wait_recv()
-        up_near = net.send(up_y.at[:, 1 - c], up_out.at[x, :, c], "c", 1)
-        up_mine = net.keep(up_y.at[:, c], up_out.at[x, :, c])
-
-        right[0].wait_recv()
-        spot = both_out.at[along("x", -1), 0]
-        far = [net.send(spot, spot, "x", 1)]
-        left[0].wait_recv()
-        spot = both_out.at[along("x", 1), 1]
-        far.append(net.send(spot, spot, "x", -1))
-        pl.loop(tiles // 2, tiles)(back)
-
-        up_near.wait_recv()
-        up_mine.wait()
-        spot = up_out.at[x]
-        ups = [net.send(spot, spot, "x", d) for d in LINE]
-        for copy in [ahead[i] for i in (1, 2, 4, 5)] + [right[1], left[1]] + far + outs + ups:
-            copy.wait_recv()
-        out_mine.wait()
-        net.close()
-
-    outs = (
-        shape(4, *value.shape), shape(4, *both.shape), shape(4, tall, wide), shape(4, 4, 2, high, lanes),
-        shape(size, weights.shape[0], kind=F32),
-    )
-    scratch = [
-        pltpu.VMEM((3, 4, 2, high, lanes), BF),
-        pltpu.VMEM((4, 2, high, lanes), BF),
-        pltpu.VMEM((4, 2, high, lanes), BF),
-        pltpu.VMEM(weights.shape, BF),
-    ]
-    return comm_call(
-        body, "firsts_gather", 8, outs, (value, both, grad_out, grad_up, weights), scratch, 40, 6,
-        [IN_VMEM] * 4 + [ANYWHERE], [ANYWHERE, ANYWHERE, IN_VMEM, IN_VMEM, IN_VMEM],
-    )
-
-
-def last_sums(grad_first, gains, grad_both, grad_down, grad_up, share):
-    rows = grad_both.shape[2]
-    half_units = grad_both.shape[3] // 4
-    padded, width = grad_down.shape[1:]
-    half_wide = 2 * half_units // padded * 4 * share
-    up_rows, up_lanes = grad_up.shape[3:]
-
-    def body(
-        first_ref, gain_ref, both_ref, down_ref, up_ref, first_out, gain_out, gate_out, up_out, down_out, q_up_out,
-        accum, down_rows, wide, first_come, first_x,
-        gain_near, gain_one, gain_come, gain_two, gain_y, gain_three, gain_x, sends, arrivals, locals_,
-    ):
-        net = Net(sends, arrivals, locals_)
-        x, y, z, c = (lax.axis_index(a) for a in AXES)
-        greet(X_LINE + Y_LINE + Z_LINE + TWIN)
-        first_near = net.send(first_ref.at[:, 1 - c], wide.at[c], "c", 1)
-        first_mine = net.keep(first_ref.at[:, c], wide.at[c])
-        near = net.send(gain_ref.at[:, :, 1 - c], gain_near, "c", 1)
+        up_near = net.send(up_y.at[:, 1 - c], up_all.at[x, :, c], "c", 1)
+        up_mine = net.keep(up_y.at[:, c], up_all.at[x, :, c])
+
         first_mine.wait()
         first_near.wait_recv()
         firsts = [
-            [net.send(wide.at[core, along("z", d)], first_come.at[d - 1, core], "z", d) for d in LINE]
+            [net.send(pair.at[core, along("z", d)], first_come.at[d - 1, core], "z", d) for d in LINE]
             for core in range(2)
         ]
+        near.wait_recv()
+        gain_near[...] = gain_here[...] + gain_near[...]
+        comes = [net.send(gain_near.at[:, along("z", d)], gain_come.at[d - 1], "z", d) for d in LINE]
+        up_near.wait_recv()
+        up_mine.wait()
+        spot = up_all.at[x]
+        ups = [net.send(spot, spot, "x", d) for d in LINE]
+        downs = [net.send(down_ref, down_all.at[x], "x", d) for d in LINE]
+
         accum[...] = jnp.zeros_like(accum)
 
-        def put(i):
-            px, pc = i // 2, i % 2
-            places = unit_places((half_units, 1), 0, px, pc, share, padded)
-            picks = lax.broadcasted_iota(jnp.int32, (half_units, half_wide), 1) == places
-            stacked = jnp.concatenate(
-                [both_ref[px, pc, :, k * half_units : (k + 1) * half_units] for k in range(4)], axis=0
-            )
-            accum[...] += dot(stacked, picks.astype(BF))
-
-        near.wait_recv()
-        gain_one[...] = gain_ref[:, :, c] + gain_near[...]
-        comes = [net.send(gain_one.at[:, along("z", d)], gain_come.at[d - 1], "z", d) for d in LINE]
+        def put(px):
+            for pc in range(2):
+                places = unit_places((half_units, 1), 0, px, pc, share, padded)
+                picks = lax.broadcasted_iota(jnp.int32, (half_units, half_wide), 1) == places
+                stacked = jnp.concatenate(
+                    [both_all[px, pc, :, k * half_units : (k + 1) * half_units] for k in range(4)], axis=0
+                )
+                accum[...] += dot(stacked, picks.astype(BF))
+
+        for copy in (right[1], left[1]):
+            copy.wait_recv()
+        put(x)
+        put(along("x", 1))
+
         def onward(core):
             for copy in firsts[core]:
                 copy.wait_recv()
-            add_all([wide.at[core, z]] + [first_come.at[d, core] for d in range(3)], first_x.at[x, core])
+            add_all([pair.at[core, z]] + [first_come.at[d, core] for d in range(3)], first_x.at[x, core])
             spot = first_x.at[x, core]
             return [net.send(spot, spot, "x", d) for d in LINE]
 
-        pl.loop(0, 3)(put)
         finals = [onward(0)]
         for copy in comes:
             copy.wait_recv()
-        gain_two[...] = (gain_one[:, z] + gain_come[0]) + (gain_come[1] + gain_come[2])
+        gain_two[...] = (gain_near[:, z] + gain_come[0]) + (gain_come[1] + gain_come[2])
         comes = [net.send(gain_two.at[along("y", d)], gain_y.at[d - 1], "y", d) for d in LINE]
         finals.append(onward(1))
-        pl.loop(3, 8)(put)
+        put(along("x", -1))
         for copy in comes:
             copy.wait_recv()
-        gain_three[...] = (gain_two[y] + gain_y[0]) + (gain_y[1] + gain_y[2])
-        gain_mine = net.keep(gain_three, gain_x.at[x])
-        comes = [net.send(gain_three, gain_x.at[x], "x", d) for d in LINE]
-        for k, target in enumerate((gate_out, gate_out, up_out, up_out)):
+        gain_x[x] = (gain_two[y] + gain_y[0]) + (gain_y[1] + gain_y[2])
+        spot = gain_x.at[x]
+        comes = [net.send(spot, spot, "x", d) for d in LINE]
+        for copy in far:
+            copy.wait_recv()
+        put(along("x", 2))
+        for k, target in enumerate((gate_out, gate_out, up_weight_out, up_weight_out)):
             target[:, (k % 2) * half_wide : (k % 2 + 1) * half_wide] = accum[k * rows : (k + 1) * rows].astype(BF)
+        for copy in outs + ups + downs:
+            copy.wait_recv()
+        down_mine.wait()
         for px in range(4):
-            down_rows[px * share : (px + 1) * share, :] = down_ref[px].astype(F32)[:share]
+            down_rows[px * share : (px + 1) * share, :] = down_all[px].astype(F32)[:share]
             for py in range(4):
                 for pc in range(2):
-                    at = ((2 * py + pc) * 4 + px) * up_lanes
-                    q_up_out[:, at : at + up_lanes] = up_ref[px, py, pc]
+                    at = ((2 * py + pc) * 4 + px) * lanes
+                    q_up_out[:, at : at + lanes] = up_all[px, py, pc]
         down_out[...] = down_rows[...].astype(BF)
         for core in range(2):
             for copy in finals[core]:
                 copy.wait_recv()
             add_all([first_x.at[i, core] for i in range(4)], first_out.at[core])
-        gain_mine.wait()
         for copy in comes:
             copy.wait_recv()
         gain_out[...] = (gain_x[0] + gain_x[1]) + (gain_x[2] + gain_x[3])
         net.close()
 
-    _, _, high, lanes = grad_first.shape
     outs = (
-        shape(2, high, lanes, kind=F32), shape(8, 128, kind=F32), shape(rows, 2 * half_wide),
-        shape(rows, 2 * half_wide), shape(4 * share, width), shape(up_rows, 32 * up_lanes),
+        shape(2, rows, part, kind=F32), shape(8, 128, kind=F32), shape(size, deep, kind=F32), shape(4, tall, wide),
+        shape(rows, 2 * half_wide), shape(rows, 2 * half_wide), shape(4 * share, width), shape(high, 32 * lanes),
     )
     scratch = [
+        pltpu.VMEM((4, 2, size, part), BF),
+        pltpu.VMEM((4, *both.shape), BF),
+        pltpu.VMEM((4, 4, 2, high, lanes), BF),
+        pltpu.VMEM((4, padded, width), BF),
+        pltpu.VMEM((3, tall, wide), BF),
+        pltpu.VMEM((3, 4, 2, high, lanes), BF),
+        pltpu.VMEM((4, 2, high, lanes), BF),
+        pltpu.VMEM((4, 2, high, lanes), BF),
+        pltpu.VMEM(weights.shape, BF),
         pltpu.VMEM((4 * rows, half_wide), F32),
         pltpu.VMEM((4 * share, width), F32),
-        pltpu.VMEM((2, 4, high, lanes), BF),
-        pltpu.VMEM((3, 2, high, lanes), BF),
-        pltpu.VMEM((4, 2, high, lanes), BF),
+        pltpu.VMEM((4, 2, rows, part), BF),
+        pltpu.VMEM((2, 4, rows, part), BF),
+        pltpu.VMEM((3, 2, rows, part), BF),
+        pltpu.VMEM((4, 2, rows, part), BF),
         pltpu.VMEM((4, 4, 8, 128), F32),
         pltpu.VMEM((4, 4, 8, 128), F32),
         pltpu.VMEM((3, 4, 8, 128), F32),
         pltpu.VMEM((4, 8, 128), F32),
         pltpu.VMEM((3, 8, 128), F32),
-        pltpu.VMEM((8, 128), F32),
         pltpu.VMEM((4, 8, 128), F32),
     ]
     return comm_call(
-        body, "last_sums", 9, outs, (grad_first, gains, grad_both, grad_down, grad_up), scratch, 24, 2,
-        [IN_VMEM] * 5, [IN_VMEM] * 6,
-    )
-
-
-def attend_back_kernel(
-    qt_ref, do_ref, o_ref, kv_ref, begin_ref, slot_ref, lse_ref, cos_ref, sin_ref, go_ref, mid_ref, gb_ref,
-    dq_ref, dkv_ref, go_out, one_out, two_out, mid_out,
-    kt, sums, accum, query, grad_rows, grad_turned, delta, own_one, come_one, own_two, come_two, mid_come, stack, go_come, sends, arrivals, locals_,
+        body, "last_sums", 8, outs,
+        (
+            value, both, grad_out, grad_up, grad_down, normed_part, inputs, inverse, gain_one, gain_two, gain_latent,
+            weights,
+        ),
+        scratch, 64, 8, [IN_VMEM] * 11 + [ANYWHERE], [IN_VMEM] * 8,
+    )
+
+
+def heads_back(
+    grad_branch, branch, mixed, qt, kv, out_heads, begin, slot, lse, live, cosine, sine, mid_down, gb,
 ):
-    net = Net(sends, arrivals, locals_)
-    x, c = lax.axis_index("x"), lax.axis_index("c")
-    greet(X_LINE + Y_LINE + Z_LINE + TWIN)
-    half = go_ref.shape[0]
-    wide = gb_ref.shape[-1]
-    ahead, _, after = GB_PARTS
-    quarter = go_out.shape[1]
-
-    def strip(at):
-        return pl.ds(pl.multiple_of(at * quarter, quarter), quarter)
-
-    go_mine = net.keep(go_ref.at[:, c], stack.at[pl.ds(half * c, half)])
-    go_near = net.send(go_ref.at[:, 1 - c], stack.at[pl.ds(half * c, half)], "c", 1)
-    steps = [
-        FirstStep(net, gb_ref, pl.ds(0, ahead), "y", own_one, come_one, one_out),
-        FirstStep(net, gb_ref, pl.ds(wide - after, after), "z", own_two, come_two, two_out),
+    segments, _, rows = slot.shape
+    tokens = rows // 2
+    size, width = grad_branch.shape
+    _, high, down_lanes = mid_down.shape[1:]
+    tall, wide = gb.shape[2:]
+    ahead, after = Y_COLUMNS, wide - Y_COLUMNS
+    half = out_heads.shape[0] // (2 * size)
+
+    def body(
+        grad_ref, branch_ref, mixed_ref, qt_ref, kv_ref, out_ref, begin_ref, slot_ref, lse_ref, live_ref, cos_ref,
+        sin_ref, mid_ref, gb_ref,
+        dq_ref, dkv_ref, stack, branch_out, down_out, one_out, two_out,
+        grads, kt, sums, accum, query, grad_rows, grad_turned, delta, go_send, near, relay, come, go,
+        own_one, come_one, own_two, come_two, down_one, down_two, sends, arrivals, locals_,
+    ):
+        net = Net(sends, arrivals, locals_)
+        y, z, c = (lax.axis_index(a) for a in ROW)
+        greet(X_RING + Y_LINE + Z_LINE + TWIN)
+        gathering = RingGather(net, grad_ref, grads, "y")
+        two = FirstStep(net, gb_ref, pl.ds(ahead, after), "z", own_two, come_two, two_out)
+        halves = [
+            SecondStep(net, mid_ref.at[k], axis, (down_one, down_two)[k]) for k, axis in enumerate(("z", "y"))
+        ]
+        ring = RingSum(net, branch_ref, branch_out, "x", near, relay, come, go)
+        sums[...] = jnp.zeros_like(sums)
+        turned(kv_ref, kt, segments * (segments - 1) + z + 1, KEYS)
+
+        def segment(step):
+            seg = along("y", step)
+            here = pl.ds(pl.multiple_of(seg * tokens, tokens), tokens)
+            grad = dot_nt(grads[seg].reshape(tokens, width), out_ref[...]).astype(BF) * live_ref[here, :].astype(BF)
+            grad = jnp.concatenate([grad[:, :SIZE], grad[:, SIZE:]], axis=0)
+            value = mixed_ref[here, :]
+            value = jnp.concatenate([value[:, :SIZE], value[:, SIZE:]], axis=0)
+            query[...] = qt_ref[seg].T
+            grad_rows[...] = grad
+            grad_turned[...] = grad.T
+            delta[...] = jnp.sum(grad_turned[...].astype(F32) * value.T.astype(F32), axis=0, keepdims=True)
+            accum[...] = jnp.zeros_like(accum)
+
+            def tile(at, count, masked):
+                keys = pl.ds(at, count)
+                scores = dot(kv_ref[keys, KEYS], qt_ref[seg])
+                probs = jnp.exp(scores - lse_ref[seg])
+                if masked:
+                    key = lax.broadcasted_iota(jnp.int32, scores.shape, 0) + at
+                    probs = jnp.where((key >= begin_ref[seg]) & (key <= slot_ref[seg]), probs, 0.0)
+                grad_probs = dot(kv_ref[keys, VALUES], grad_turned[...])
+                grad_scores = (probs * (grad_probs - delta[...])).astype(BF)
+                sums[keys, VALUES] += dot(probs.astype(BF), grad_rows[...])
+                sums[keys, KEYS] += dot(grad_scores, query[...])
+                accum[...] += dot(kt[:, keys], grad_scores)
+
+            sweep(seg, segments, z, tile)
+            cos_here, sin_here = cos_ref[seg], sin_ref[seg]
+            for head in range(2):
+                part = accum[:, head * tokens : (head + 1) * tokens] * (SIZE ** -0.5)
+                lower, upper = part[:HALF], part[HALF:]
+                turn = jnp.concatenate(
+                    [lower * cos_here + upper * sin_here, upper * cos_here - lower * sin_here], axis=0
+                )
+                dq_ref[here, head * SIZE : (head + 1) * SIZE] = turn.T.astype(BF)
+
+        gathering.arrived()
+        segment(0)
+        gathering.forward()
+        one = FirstStep(net, gb_ref, pl.ds(0, ahead), "y", own_one, come_one, one_out)
+        ring.relay_far()
+        ring.issue()
+        gathering.share()
+        gathering.arrived()
+        pl.loop(0, 2)(lambda i: segment(1 + 2 * i))
+        ring.pass_on()
+        gathering.finish()
+
+        for k in range(4):
+            columns = slice(k * width // 4, (k + 1) * width // 4)
+            part = dot_tn(mixed_ref[...], grads[...].reshape(segments * tokens, width)[:, columns]).astype(BF)
+            part = part.reshape(half, 2, size, width // 4)
+            for h in range(half):
+
+                @pl.when(c == 0)
+                def _(h=h, part=part, columns=columns):
+                    stack[h, :, columns] = part[h, 0]
+                    go_send[h, :, columns] = part[h, 1]
+
+                @pl.when(c == 1)
+                def _(h=h, part=part, columns=columns):
+                    stack[half + h, :, columns] = part[h, 1]
+                    go_send[h, :, columns] = part[h, 0]
+
+        go_come = net.send(go_send, stack.at[pl.ds(half * c, half)], "c", 1)
+        segment(2)
+        dkv_ref[...] = sums[...].astype(BF)
+        for k in range(2):
+            halves[k].finish(down_out.at[:, pl.ds(k * down_lanes, down_lanes)])
+        ring.finish()
+        go_come.wait_recv()
+        one.finish()
+        two.finish()
+        net.close()
+
+    outs = (
+        shape(*mixed.shape), shape(*kv.shape), shape(2 * half, size, width), shape(size, width, kind=F32),
+        shape(high, 2 * down_lanes), shape(4, tall, ahead), shape(4, tall, after),
+    )
+    scratch = [
+        pltpu.VMEM((4, 2, size, width), BF),
+        pltpu.VMEM((SIZE, kv.shape[0]), BF),
+        pltpu.VMEM(kv.shape, F32),
+        pltpu.VMEM((SIZE, rows), F32),
+        pltpu.VMEM((rows, SIZE), BF),
+        pltpu.VMEM((rows, SIZE), BF),
+        pltpu.VMEM((SIZE, rows), BF),
+        pltpu.VMEM((1, rows), F32),
+        pltpu.VMEM((half, size, width), BF),
+    ] + ring_sum_scratch(size, width) + [
+        pltpu.VMEM((4, tall, ahead), BF),
+        pltpu.VMEM((3, 4, tall, ahead), BF),
+        pltpu.VMEM((4, tall, after), BF),
+        pltpu.VMEM((3, 4, tall, after), BF),
+        pltpu.VMEM((3, high, down_lanes), BF),
+        pltpu.VMEM((3, high, down_lanes), BF),
     ]
-    second = SecondStep(net, mid_ref, "y", mid_come)
-    go_mine.wait()
-    go_near.wait_recv()
-    go_sends = [net.send(stack.at[:, strip(along("x", d))], go_come.at[d - 1], "x", d) for d in LINE]
-    depth = lax.axis_index("z")
-    segments = slot_ref.shape[0]
-    rows = slot_ref.shape[2]
-    tokens = rows // 2
-    sums[...] = jnp.zeros_like(sums)
-    turned(kv_ref, kt, segments * (segments - 1) + depth + 1, KEYS)
-
-    @pl.loop(0, segments)
-    def _(seg):
-        here = pl.ds(pl.multiple_of(seg * tokens, tokens), tokens)
-
-        def stacked(ref):
-            value = ref[here, :]
-            return jnp.concatenate([value[:, :SIZE], value[:, SIZE:]], axis=0)
-
-        grad = stacked(do_ref)
-        query[...] = qt_ref[seg].T
-        grad_rows[...] = grad
-        grad_turned[...] = grad.T
-        delta[...] = jnp.sum(
-            grad_turned[...].astype(F32) * stacked(o_ref).T.astype(F32), axis=0, keepdims=True
-        )
-        accum[...] = jnp.zeros_like(accum)
-
-        def tile(at, size, masked):
-            keys = pl.ds(at, size)
-            scores = dot(kv_ref[keys, KEYS], qt_ref[seg])
-            probs = jnp.exp(scores - lse_ref[seg])
-            if masked:
-                key = lax.broadcasted_iota(jnp.int32, scores.shape, 0) + at
-                probs = jnp.where((key >= begin_ref[seg]) & (key <= slot_ref[seg]), probs, 0.0)
-            grad_probs = dot(kv_ref[keys, VALUES], grad_turned[...])
-            grad_scores = (probs * (grad_probs - delta[...])).astype(BF)
-            sums[keys, VALUES] += dot(probs.astype(BF), grad_rows[...])
-            sums[keys, KEYS] += dot(grad_scores, query[...])
-            accum[...] += dot(kt[:, keys], grad_scores)
-
-        sweep(seg, segments, depth, tile)
-        cosine, sine = cos_ref[seg], sin_ref[seg]
-        for head in range(2):
-            part = accum[:, head * tokens : (head + 1) * tokens] * (SIZE ** -0.5)
-            lower, upper = part[:HALF], part[HALF:]
-            turn = jnp.concatenate(
-                [lower * cosine + upper * sine, upper * cosine - lower * sine], axis=0
-            )
-            dq_ref[here, head * SIZE : (head + 1) * SIZE] = turn.T.astype(BF)
-
-    dkv_ref[...] = sums[...].astype(BF)
-    second.finish(mid_out)
-    for copy in go_sends:
-        copy.wait_recv()
-    for i in range(2 * half):
-        add_all([stack.at[i, strip(x)]] + [go_come.at[d, i] for d in range(3)], go_out.at[i])
-    for step in steps:
-        step.finish()
-    net.close()
-
-
-def attend_back(qt, do, o, kv, begin, slot, lse, cosine, sine, grad_out, mid, gb):
-    segments, _, rows = slot.shape
-    half, _, tall, wide = grad_out.shape
-    _, high, third = mid.shape
-    ahead, _, after = GB_PARTS
-    return pl.pallas_call(
-        attend_back_kernel,
-        name="attend_back",
-        out_shape=(
-            jax.ShapeDtypeStruct(do.shape, BF),
-            jax.ShapeDtypeStruct(kv.shape, BF),
-            jax.ShapeDtypeStruct((2 * half, tall // 4, wide), BF),
-            jax.ShapeDtypeStruct((4, high, ahead), BF),
-            jax.ShapeDtypeStruct((4, high, after), BF),
-            jax.ShapeDtypeStruct((high, third), BF),
-        ),
-        in_specs=[IN_VMEM] * 11 + [ANYWHERE],
-        out_specs=[IN_VMEM] * 6,
-        scratch_shapes=[
-            pltpu.VMEM((SIZE, kv.shape[0]), BF),
-            pltpu.VMEM(kv.shape, F32),
-            pltpu.VMEM((SIZE, rows), F32),
-            pltpu.VMEM((rows, SIZE), BF),
-            pltpu.VMEM((rows, SIZE), BF),
-            pltpu.VMEM((SIZE, rows), BF),
-            pltpu.VMEM((1, rows), F32),
-            pltpu.VMEM((4, high, ahead), BF),
-            pltpu.VMEM((3, 4, high, ahead), BF),
-            pltpu.VMEM((4, high, after), BF),
-            pltpu.VMEM((3, 4, high, after), BF),
-            pltpu.VMEM((3, high, third), BF),
-            pltpu.VMEM((2 * half, tall, wide), BF),
-            pltpu.VMEM((3, 2 * half, tall // 4, wide), BF),
-        ] + semaphores(14, 3),
-        compiler_params=pltpu.CompilerParams(
-            collective_id=10, has_side_effects=True, vmem_limit_bytes=60 << 20
-        ),
-    )(qt, do, o, kv, begin, slot, lse, cosine, sine, grad_out, mid, gb)
+    return comm_call(
+        body, "heads_back", 6, outs,
+        (grad_branch, branch, mixed, qt, kv, out_heads, begin, slot, lse, live, cosine, sine, mid_down, gb),
+        scratch, 36, 3, [IN_VMEM] * 13 + [ANYWHERE], [IN_VMEM] * 7,
+    )
 
 
 def gather(value, axes):
@@ -1441,70 +1466,36 @@
     grad_middle = grad_result + grad_mid_norm
 
     grad_both = grad_both.reshape(n_y, n_z, n_c * shard, 2 * units)
-    grad_branch, branch_two, grad_down, grad_mid = heads_gather_and_branch(
-        grad_middle.astype(BF), branch_part, grad_down, grad_both
-    )
-    grad_branch = grad_branch.reshape(group, width)
+    out_rows = out_weight.shape[0]
+    grad_query_raw, grad_kv, grad_out, branch_two, grad_down, grad_one, grad_two = heads_back(
+        grad_middle.astype(BF), branch_part, mixed, queries_t, key_value, out_heads, begin_lanes, slot_lanes, lse,
+        live_group[:, None], cosine_group, sine_group, grad_down, grad_both,
+    )
     output = (middle + branch_two).astype(BF)
-    grad_mixed = dot_nt(grad_branch, out_heads).astype(BF)
-    grad_attended = grad_mixed * live_group[:, None].astype(BF)
-    grad_out = dot_tn(mixed, grad_branch).astype(BF)
-    out_rows = out_weight.shape[0]
-    grad_query_raw, grad_kv, grad_out, grad_one, grad_two, grad_mid = attend_back(
-        queries_t, grad_attended, mixed, key_value, begin_lanes, slot_lanes, lse,
-        cosine_group, sine_group, grad_out.reshape(n_z // n_c, n_c, out_rows, width), grad_mid, grad_both,
-    )
-    grad_up_heads = dot_tn(latent_group, grad_query_raw).astype(BF)
-    grad_kv, grad_latent_normed, grad_up_heads, grad_out, grad_one, grad_two, grad_down = keys_and_latents_sum(
-        grad_kv.reshape(n_y, n_z, n_c, rows, 2 * SIZE),
-        dot_nt(grad_query_raw, up_heads).astype(BF).reshape(n_y, n_c, rows, latent_width),
-        grad_up_heads.reshape(n_y, n_z, n_c, q_rows, per_heads),
-        grad_out, (grad_one, grad_two), grad_down,
-    )
-    grad_both = jnp.concatenate([grad_one, grad_mid, grad_two], axis=1)
-    grad_key_raw = unrotate(grad_kv[:, :SIZE], cosine, sine).astype(BF)
-    grad_value_raw = grad_kv[:, SIZE:].astype(BF)
-    grad_latent_f, grad_gain_latent = norm_back(
-        latent, inverse_latent, gain_latent, grad_latent_normed
-    )
-    grad_firsts = jnp.concatenate(
-        [grad_latent_f.astype(BF), grad_key_raw, grad_value_raw], axis=1
-    )
-    half_first = first_width // n_c
-    first_part, grad_both, grad_out, grad_up_heads, grad_normed = firsts_gather(
-        grad_firsts.reshape(rows, n_c, half_first).transpose(1, 0, 2),
-        grad_both.reshape(n_c, shard, 2 * units), grad_out, grad_up_heads, first_full,
-    )
-    first_part = first_part.reshape(group, half_first)
-    grad_first = dot_tn(normed_part, first_part).astype(BF)
-    grad_input_norm, grad_gain_one = norm_back(inputs, inverse_one, gain_one, grad_normed)
+    grad_firsts, grad_gain_latent, grad_up_heads, grad_out, grad_one, grad_two = keys_and_latents_sum(
+        grad_kv.reshape(n_y, n_z, n_c, rows, 2 * SIZE), grad_query_raw, latent_group, up_heads, grad_out,
+        (grad_one, grad_two), cosine, sine, latent, inverse_latent, gain_latent[None, :],
+    )
+    grad_both = jnp.concatenate([grad_one, grad_two], axis=1)
+
+    grad_first, gains, grad_input_norm, grad_out, grad_gate, grad_up, grad_down, grad_q_up = last_sums(
+        grad_firsts, grad_both.reshape(n_c, shard, 2 * units), grad_out, grad_up_heads, grad_down, normed_part,
+        block_input, inverse_one, gain_one[None, :], grad_gain_two[None, :], grad_gain_latent, first_full, share,
+    )
     input_grad = grad_middle + grad_input_norm
-    gains = jnp.concatenate(
-        [
-            grad_gain_one.reshape(span, shard),
-            grad_gain_two.reshape(span, shard),
-            grad_gain_latent.reshape(span, -1),
-        ],
-        axis=1,
-    )
-    shares = gains.shape[1]
-    gains = jnp.pad(gains, ((0, 0), (0, 8 * 128 - shares))).reshape(n_y, n_z, n_c, 8, 128)
-    grad_first, gains, grad_gate, grad_up, grad_down, grad_q_up = last_sums(
-        grad_first.reshape(n_z, n_c, shard, half_first), gains, grad_both, grad_down, grad_up_heads, share
-    )
-    gains = gains.reshape(-1)
     grad_first = jnp.concatenate([grad_first[0], grad_first[1]], axis=1)
+    latent_shard = q_gain.shape[0]
     return (
         output,
         input_grad,
-        gains[:shard],
+        lax.dynamic_slice(gains[0], (c * shard,), (shard,)),
         grad_first[:, :latent_width],
-        gains[2 * shard : shares],
+        lax.dynamic_slice(gains[2], ((z % 2 * n_c + c) * latent_shard,), (latent_shard,)),
         grad_q_up.astype(F32),
         grad_first[:, latent_width : latent_width + SIZE],
         grad_first[:, latent_width + SIZE :],
         grad_out.reshape(out_rows, width).astype(F32),
-        gains[shard : 2 * shard],
+        lax.dynamic_slice(gains[1], (c * shard,), (shard,)),
         grad_gate.astype(F32),
         grad_up.astype(F32),
         grad_down.astype(F32),

time: 476 us -> 446 us (0.937)
  matrix products: 31.6 us -> 11.9 us
  Pallas kernels: 378 us -> 370 us
    pallas_call x1 -> x0, Pallas kernels: 45.1 us -> none  [attend_back(): pl.pallas_call(attend_back_kernel, name='attend_back', out_shape=(jax.Sha...]
    pallas_call x8 -> x7, Pallas kernels: 316 us -> 353 us  [comm_call(): pl.pallas_call(body, name=name, out_shape=outs, in_specs=spaces, out_spec...]
    dot_general x5 -> x0, matrix products: 19.6 us -> none  [the longest x3 13.6 us: dot_tn(): lax.dot_general(left, right, (((0,), (0,)), ((), ())), preferred_element_...]
  transfers between devices with their start and end apart: 2 -> 2, of which waited for: 0 -> 0; matrix products, arithmetic and copies ran while one was open for 6% -> 7% of each run, Pallas kernels for 30% -> 31%
where the time goes in v6:
time: 446 us; the launch traced here: 439 us
  Pallas kernels  370 us (83%)
  other arithmetic  29.7 us (7%)
  between operations  14.6 us (3%)
  local copies, waits for them, and re-layouts  12.8 us (3%)
  matrix products  11.9 us (3%)
    pallas_call x7, Pallas kernels, comm_call(): pl.pallas_call(body, name=name, out_shape=outs, in_specs=spaces, out_spec...  353 us
    pallas_call x1, Pallas kernels, attend(): pl.pallas_call(attend_kernel, name='attend', out_shape=(jax.ShapeDtypeStr...  17 us
    dot_general x3, matrix products, dot(): return jnp.dot(left, right, preferred_element_type=F32)  11.9 us
  transfers between devices with their start and end apart: 2, of which 0 were waited for; matrix products, arithmetic and copies ran while one was open for 7% of the time, Pallas kernels for 31%

profile of v6, /device:TPU:1, one launch (start us, length us, event | category | flops | bytes accessed | tf_op | source)
XLA Modules:
  0.0 439.4 jit_solution(443256614084563191)
XLA Ops:
  7.2 1.0 copy-done
  8.4 0.7 pad.15
  9.1 0.7 convert.27
  9.8 0.7 convert_bitcast_fusion
  10.6 1.6 fusion.6.first_ref
  12.3 45.5 %first_weights.1 = (bf16[4,4,2,64,1664]{4,3,2,1,0:T(8,128)(2,1)}, bf16[2,64,1536]{2,1,0:T(8,128)(2,1)}, bf16[4,32,2048]{2,1,0:T(8,128)(2,1)}) custom-call(bf16[64,1664]{1,0:T(8,128)(2,1)} %fusion.6.first_ref, bf16[64,5632]{1,0:T(8,128)(2,1)} %gate_ref.1, bf16[64,5632]{1,0:T(8,128)(2,1)} %up_ref.1, bf16[128,2048]{1,0:T(8,128)(2,1)} %out_ref.1), custom_call_target="tpu_custom_call" | custom-call | tf_op jit(solution)/shard_map/first_weights/pallas_call | solution.py:242
  57.8 1.1 slice_convert_fusion
  59.0 1.4 slice_reduce_fusion
  60.6 0.7 broadcast_in_dim_reshape.2.gain_ref
  61.4 0.6 slice.70
  62.4 4.0 fusion
  66.6 0.8 copy.53
  67.5 0.7 pad_add_fusion
  68.5 0.7 fusion.10
  69.2 1.0 copy.51
  70.3 0.8 fusion.18
  71.1 0.7 copy.47.inverse_ref
  71.8 0.7 copy.48.inverse_ref
  72.7 1.0 subtract_convert_fusion
  73.7 0.7 pad_maximum_fusion.2.kv_ref
  74.3 0.8 multiply_convert_fusion.1.lat_ref
  75.2 45.4 %keys_and_latents.1 = (bf16[4,4,2,128,512]{4,3,2,1,0:T(8,128)(2,1)}, bf16[4,2,128,1024]{3,2,1,0:T(8,128)(2,1)}, bf16[4,4,2,32,512]{4,3,2,1,0:T(8,128)(2,1)}, bf16[2,2,4,32,2048]{4,3,2,1,0:T(8,128)(2,1)}) custom-call(bf16[128,512]{1,0:T(8,128)(2,1)} %pad_maximum_fusion.2.kv_ref, bf16[128,1024]{1,0:T(8,128)(2,1)} %multiply_convert_fusion.1.lat_ref, ...), custom_call_target="tpu_custom_call" | custom-call | tf_op jit(solution)/shard_map/keys_and_latents/pallas_call | solution.py:242
  120.6 1.9 multiply_sine_fusion
  122.5 3.6 fusion.21.q_ref
  126.1 17.0 %attend.1 = (bf16[1024,512]{1,0:T(8,128)(2,1)S(1)}, bf16[4,256,512]{2,1,0:T(8,128)(2,1)S(1)}, f32[4,1,512]{2,1,0:T(1,128)S(1)}) custom-call(f32[1024,512]{1,0:T(8,128)S(1)} %fusion.21.q_ref, bf16[4096,512]{1,0:T(8,128)(2,1)} %bitcast.60, s32[4,1,512]{2,1,0:T(1,128)S(1)} %tile.28.begin_ref, s32[4,1,512]{2,1,0:T(1,128)S(1)} %tile.30.slot_ref, ...), custom_call_target="tpu_custom_call" | custom-call | tf_op jit(solution)/shard_map/attend/pallas_call | solution.py:156
  143.1 4.4 %convolution_convert_fusion = bf16[1024,2048]{1,0:T(8,128)(2,1)} fusion(bf16[1024,512]{1,0:T(8,128)(2,1)S(1)} %get-tuple-element.56.mixed_ref, bf16[512,2048]{1,0:T(8,128)(2,1)S(1)} %bitcast.69), kind=kOutput, calls=%fused_computation.2 | convolution fusion | flops 2149580800 | bytes 7340032 | tf_op jit(solution)/shard_map/dot_general | solution.py:25
  147.6 30.1 %heads_sum_and_cotangent.1 = (f32[128,2048]{1,0:T(8,128)}, bf16[4,2,128,2048]{3,2,1,0:T(8,128)(2,1)}) custom-call(bf16[4,2,128,2048]{3,2,1,0:T(8,128)(2,1)} %bitcast.66, bf16[128,2048]{1,0:T(8,128)(2,1)} %cot_ref.1), custom_call_target="tpu_custom_call" | custom-call | tf_op jit(solution)/shard_map/heads_sum_and_cotangent/pallas_call | solution.py:242
  177.6 1.4 multiply_reduce_fusion.2
  179.1 1.0 multiply_convert_fusion.two_ref
  180.1 68.2 %feed_forward.1 = (f32[128,2048]{1,0:T(8,128)}, bf16[4,2,128,512]{3,2,1,0:T(8,128)(2,1)}, bf16[4,2,128,2048]{3,2,1,0:T(8,128)(2,1)}, bf16[2048,1536]{1,0:T(8,128)(2,1)}, bf16[2,4,48,1024]{3,2,1,0:T(8,128)(2,1)}) custom-call(bf16[128,2048]{1,0:T(8,128)(2,1)} %multiply_convert_fusion.two_ref, bf16[128,2048]{1,0:T(8,128)(2,1)} %copy-done.13, ...), custom_call_target="tpu_custom_call" | custom-call | tf_op jit(solution)/shard_map/feed_forward/pallas_call | solution.py:242
  248.3 2.1 multiply_reduce_fusion
  250.4 2.4 fusion.17.grad_ref
  252.8 64.4 %heads_back.1 = (bf16[1024,512]{1,0:T(8,128)(2,1)}, bf16[4096,512]{1,0:T(8,128)(2,1)}, bf16[4,128,2048]{2,1,0:T(8,128)(2,1)}, f32[128,2048]{1,0:T(8,128)}, bf16[...) custom-call(bf16[128,2048]{1,0:T(8,128)(2,1)} %fusion.17.grad_ref, ...), custom_call_target="tpu_custom_call" | custom-call | tf_op jit(solution)/shard_map/heads_back/pallas_call | solution.py:242
  317.2 48.5 %keys_and_latents_sum.1 = (bf16[2,128,768]{2,1,0:T(8,128)(2,1)}, f32[1,1024]{1,0:T(1,128)}, bf16[4,4,2,32,128]{4,3,2,1,0:T(8,128)(2,1)}, bf16[4,32,2048]{2,1,0:T...) custom-call(bf16[4,4,2,128,512]{4,3,2,1,0:T(8,128)(2,1)} %bitcast.67, ...), custom_call_target="tpu_custom_call" | custom-call | tf_op jit(solution)/shard_map/keys_and_latents_sum/pallas_call | solution.py:242
  365.8 1.8 pad_maximum_fusion
  367.6 51.1 %last_sums.1 = (f32[2,64,768]{2,1,0:T(8,128)}, f32[8,128]{1,0:T(8,128)}, f32[128,2048]{1,0:T(8,128)}, bf16[4,32,2048]{2,1,0:T(8,128)(2,1)}, bf16[64,5632]{1,0:T(...) custom-call(bf16[2,128,768]{2,1,0:T(8,128)(2,1)} %get-tuple-element.73.ref, ...), custom_call_target="tpu_custom_call" | custom-call | tf_op jit(solution)/shard_map/last_sums/pallas_call | solution.py:242
  418.7 1.2 slice_bitcast_fusion.1
  419.9 0.7 fusion.19
  420.5 0.7 pad_maximum_fusion.1
  421.3 2.5 convert_element_type.104
  423.7 1.2 convert_element_type.105
  424.9 1.3 convert_element_type.106
  426.2 1.1 bitcast_convert_fusion
  427.3 0.8 convert_element_type.101
  428.1 0.8 fusion.20
  428.9 0.6 fusion.11
  430.1 1.7 fusion.16
  431.8 0.6 fusion.12
  (85 shorter events, 2.4 us)
Async XLA Ops:
  7.2 1.1 copy-start
  7.2 172.9 %all-gather.5.cloned.1.call-start = ((), (), s32[]{:S(2)}) async-start(), calls=%async_computation.1 | async-start | bytes 3342336 | tf_op jit(solution)/shard_map/all_gather | solution.py:1374
  8.4 52.9 %copy-start.22 = (s32[1,4]{1,0:T(1,128)S(1)}, s32[1,4]{1,0:T(1,128)}, u32[]{:S(2)}) copy-start(s32[1,4]{1,0:T(1,128)} %param.16) | copy-start | bytes 52
  8.4 53.6 %copy-start.10 = (bf16[128,2048]{1,0:T(8,128)(2,1)S(1)}, bf16[128,2048]{1,0:T(8,128)(2,1)}, u32[]{:S(2)}) copy-start(bf16[128,2048]{1,0:T(8,128)(2,1)} %input_ref.1) | copy-start | bytes 1572868
  9.1 171.0 %all-gather.3.cloned.1.call-start = ((), (), s32[]{:S(2)}) async-start(), calls=%async_computation | async-start | bytes 6684672 | tf_op jit(solution)/shard_map/all_gather | solution.py:1374
  60.4 6.0 %copy-start.21 = (f32[2048]{0:T(1024)}, f32[2048]{0:T(1024)S(1)}, u32[]{:S(2)}) copy-start(f32[2048]{0:T(1024)S(1)} %get-tuple-element.93) | copy-start | bytes 24580
  62.4 4.0 copy-start.13
  62.4 4.0 copy-start.20
  68.4 57.6 %copy-start.6 = (s32[4,1,512]{2,1,0:T(1,128)}, s32[4,1,512]{2,1,0:T(1,128)S(1)}, u32[]{:S(2)}) copy-start(s32[4,1,512]{2,1,0:T(1,128)S(1)} %tile.30.slot_ref) | copy-start | bytes 24580
  68.5 57.6 %copy-start.7 = (s32[4,1,512]{2,1,0:T(1,128)}, s32[4,1,512]{2,1,0:T(1,128)S(1)}, u32[]{:S(2)}) copy-start(s32[4,1,512]{2,1,0:T(1,128)S(1)} %tile.28.begin_ref) | copy-start | bytes 24580
  122.4 3.6 copy-start.2
  122.5 3.6 copy-start.3
  126.0 17.1 %copy-start.12 = (bf16[2,2,4,32,2048]{4,3,2,1,0:T(8,128)(2,1)S(1)}, bf16[2,2,4,32,2048]{4,3,2,1,0:T(8,128)(2,1)}, u32[]{:S(2)}) copy-start(bf16[2,2,4,32,2048]{4,3,2,1,0:T(8,128)(2,1)} %get-tuple-element.57) | copy-start | bytes 6291460
  143.1 4.5 %copy-start.4 = (bf16[1024,512]{1,0:T(8,128)(2,1)}, bf16[1024,512]{1,0:T(8,128)(2,1)S(1)}, u32[]{:S(2)}) copy-start(bf16[1024,512]{1,0:T(8,128)(2,1)S(1)} %get-tuple-element.56.mixed_ref) | copy-start | bytes 3145732
  143.1 4.5 %copy-start.5 = (bf16[4,256,512]{2,1,0:T(8,128)(2,1)}, bf16[4,256,512]{2,1,0:T(8,128)(2,1)S(1)}, u32[]{:S(2)}) copy-start(bf16[4,256,512]{2,1,0:T(8,128)(2,1)S(1)} %get-tuple-element.63.qt_ref) | copy-start | bytes 3145732
  143.1 4.4 %copy-start.8 = (f32[4,1,512]{2,1,0:T(1,128)}, f32[4,1,512]{2,1,0:T(1,128)S(1)}, u32[]{:S(2)}) copy-start(f32[4,1,512]{2,1,0:T(1,128)S(1)} %get-tuple-element.64.lse_ref) | copy-start | bytes 24580
  180.1 70.3 %copy-start.11 = (bf16[128,2048]{1,0:T(8,128)(2,1)S(1)}, bf16[128,2048]{1,0:T(8,128)(2,1)}, u32[]{:S(2)}) copy-start(bf16[128,2048]{1,0:T(8,128)(2,1)} %cot_ref.1) | copy-start | bytes 1572868
  418.6 5.1 %copy-start.17 = (bf16[64,5632]{1,0:T(8,128)(2,1)S(1)}, bf16[64,5632]{1,0:T(8,128)(2,1)}, u32[]{:S(2)}) copy-start(bf16[64,5632]{1,0:T(8,128)(2,1)} %get-tuple-element.87) | copy-start | bytes 2162692
  418.7 6.3 %copy-start.16 = (bf16[176,2048]{1,0:T(8,128)(2,1)S(1)}, bf16[176,2048]{1,0:T(8,128)(2,1)}, u32[]{:S(2)}) copy-start(bf16[176,2048]{1,0:T(8,128)(2,1)} %get-tuple-element.88) | copy-start | bytes 2162692
  418.7 7.5 %copy-start.18 = (bf16[4,32,2048]{2,1,0:T(8,128)(2,1)S(1)}, bf16[4,32,2048]{2,1,0:T(8,128)(2,1)}, u32[]{:S(2)}) copy-start(bf16[4,32,2048]{2,1,0:T(8,128)(2,1)} %get-tuple-element.85) | copy-start | bytes 1572868
  421.2 6.0 %copy-start.19 = (bf16[32,4096]{1,0:T(8,128)(2,1)S(1)}, bf16[32,4096]{1,0:T(8,128)(2,1)}, u32[]{:S(2)}) copy-start(bf16[32,4096]{1,0:T(8,128)(2,1)} %get-tuple-element.84) | copy-start | bytes 786436
  421.2 8.8 %copy-start.9 = (f32[128,2048]{1,0:T(8,128)S(1)}, f32[128,2048]{1,0:T(8,128)}, u32[]{:S(2)}) copy-start(f32[128,2048]{1,0:T(8,128)} %get-tuple-element.61) | copy-start | bytes 3145732
  421.2 8.8 %copy-start.14 = (f32[128,2048]{1,0:T(8,128)S(1)}, f32[128,2048]{1,0:T(8,128)}, u32[]{:S(2)}) copy-start(f32[128,2048]{1,0:T(8,128)} %get-tuple-element.67) | copy-start | bytes 3145732
  421.2 8.8 %copy-start.15 = (f32[128,2048]{1,0:T(8,128)S(1)}, f32[128,2048]{1,0:T(8,128)}, u32[]{:S(2)}) copy-start(f32[128,2048]{1,0:T(8,128)} %get-tuple-element.81) | copy-start | bytes 3145732
  426.2 6.2 %copy-start.1 = (bf16[176,2048]{1,0:T(8,128)(2,1)S(1)}, bf16[176,2048]{1,0:T(8,128)(2,1)}, u32[]{:S(2)}) copy-start(bf16[176,2048]{1,0:T(8,128)(2,1)} %param.27) | copy-start | bytes 2162692
Sparse Core Ops, SparseCore 0:
  10.2 55.7 all-gather.4
  68.2 71.3 all-gather.2

commit v7 on v6

--- a/solution.py
+++ b/solution.py
@@ -33,44 +33,6 @@
     return lax.dot_general(left, right, (((1,), (1,)), ((), ())), preferred_element_type=F32)
 
 
-def norm_back(values, inverse, gain, grad):
-    scaled = grad * gain
-    grad_values = inverse * scaled - values * inverse * inverse * inverse * jnp.mean(
-        scaled * values, axis=-1, keepdims=True
-    )
-    return grad_values, jnp.sum(grad * values * inverse, axis=0)
-
-
-def places_of(lengths_row, slots):
-    ends = jnp.cumsum(lengths_row)
-    begins = jnp.concatenate([ends - lengths_row, ends[-1:]])
-    begin = jnp.max(jnp.where(slots[:, None] >= begins[None, :], begins[None, :], 0), axis=1)
-    live = (slots < ends[-1]).astype(F32)
-    return begin, live
-
-
-def tables(position):
-    freq = jnp.exp(jnp.arange(HALF, dtype=F32) * (-math.log(10000.0) / HALF))
-    angle = position.astype(F32)[:, None] * freq[None, :]
-    return jnp.cos(angle), jnp.sin(angle)
-
-
-def tables_across(position):
-    freq = jnp.exp(jnp.arange(HALF, dtype=F32) * (-math.log(10000.0) / HALF))
-    angle = position.astype(F32)[..., None, :] * freq[:, None]
-    return jnp.cos(angle), jnp.sin(angle)
-
-
-def rotate(values, cosine, sine):
-    lower, upper = values[..., :HALF], values[..., HALF:]
-    return jnp.concatenate([lower * cosine - upper * sine, upper * cosine + lower * sine], axis=-1)
-
-
-def unrotate(grad, cosine, sine):
-    lower, upper = grad[..., :HALF], grad[..., HALF:]
-    return jnp.concatenate([lower * cosine + upper * sine, upper * cosine - lower * sine], axis=-1)
-
-
 def turned(source, target, count, columns):
     @pl.loop(0, count)
     def _(block):
@@ -100,77 +62,6 @@
         tile(pl.multiple_of((count - 1) * BLOCK, BLOCK), BLOCK, False)
 
     tile(pl.multiple_of(count * BLOCK, BLOCK), BLOCK, True)
-
-
-def attend_kernel(
-    q_ref, kv_ref, begin_ref, slot_ref, live_ref, cos_ref, sin_ref,
-    out_ref, qt_ref, lse_ref, vt, peak, total, accum,
-):
-    depth = lax.axis_index("z")
-    segments = slot_ref.shape[0]
-    rows = slot_ref.shape[2]
-    tokens = rows // 2
-    turned(kv_ref, vt, segments * (segments - 1) + depth + 1, VALUES)
-
-    @pl.loop(0, segments)
-    def _(seg):
-        here = pl.ds(pl.multiple_of(seg * tokens, tokens), tokens)
-        cosine, sine = cos_ref[seg], sin_ref[seg]
-        for head in range(2):
-            raw = q_ref[here, head * SIZE : (head + 1) * SIZE].T
-            lower, upper = raw[:HALF], raw[HALF:]
-            turn = jnp.concatenate(
-                [lower * cosine - upper * sine, upper * cosine + lower * sine], axis=0
-            )
-            qt_ref[seg, :, head * tokens : (head + 1) * tokens] = (
-                turn.astype(BF) * (SIZE ** -0.5)
-            ).astype(BF)
-        peak[...] = jnp.full_like(peak, MASKED)
-        total[...] = jnp.zeros_like(total)
-        accum[...] = jnp.zeros_like(accum)
-
-        def tile(at, size, masked):
-            scores = dot(kv_ref[pl.ds(at, size), KEYS], qt_ref[seg])
-            if masked:
-                key = lax.broadcasted_iota(jnp.int32, scores.shape, 0) + at
-                scores = jnp.where((key >= begin_ref[seg]) & (key <= slot_ref[seg]), scores, MASKED)
-            before = peak[...]
-            now = jnp.maximum(before, jnp.max(scores, axis=0, keepdims=True))
-            weights = jnp.exp(scores - now)
-            shrink = jnp.exp(before - now)
-            peak[...] = now
-            total[...] = total[...] * shrink + jnp.sum(weights, axis=0, keepdims=True)
-            accum[...] = accum[...] * shrink + dot(vt[:, pl.ds(at, size)], weights.astype(BF))
-
-        sweep(seg, segments, depth, tile)
-        lse_ref[seg] = peak[...] + jnp.log(total[...])
-        result = accum[...] * (live_ref[seg] / total[...])
-        for head in range(2):
-            out_ref[here, head * SIZE : (head + 1) * SIZE] = (
-                result[:, head * tokens : (head + 1) * tokens].T.astype(BF)
-            )
-
-
-def attend(q, kv, begin, slot, live, cosine, sine):
-    segments, _, rows = slot.shape
-    return pl.pallas_call(
-        attend_kernel,
-        name="attend",
-        out_shape=(
-            jax.ShapeDtypeStruct(q.shape, BF),
-            jax.ShapeDtypeStruct((segments, SIZE, rows), BF),
-            jax.ShapeDtypeStruct((segments, 1, rows), F32),
-        ),
-        in_specs=[pl.BlockSpec(memory_space=pltpu.VMEM)] * 7,
-        out_specs=[pl.BlockSpec(memory_space=pltpu.VMEM)] * 3,
-        scratch_shapes=[
-            pltpu.VMEM((SIZE, kv.shape[0]), BF),
-            pltpu.VMEM((1, rows), F32),
-            pltpu.VMEM((1, rows), F32),
-            pltpu.VMEM((SIZE, rows), F32),
-        ],
-        compiler_params=pltpu.CompilerParams(vmem_limit_bytes=48 << 20),
-    )(q, kv, begin, slot, live, cosine, sine)
 
 
 MESH_IDS = pl.DeviceIdType.MESH
@@ -553,7 +444,7 @@
 OWN_COLUMNS = 640
 
 
-def first_weights(first, gate, up, out, share, padded):
+def first_weights(first, gate, up, out, inputs, lengths, latent_width, share, padded):
     rows_in, wide = gate.shape
     half_wide = wide // 2
     half_units = half_wide // (8 * share) * padded
@@ -563,7 +454,10 @@
     lanes = (first.shape[1] - OWN_COLUMNS) // 4
 
     def body(
-        first_ref, gate_ref, up_ref, out_ref, first_out, both_out, strip_out, both, sends, arrivals, locals_,
+        first_ref, gate_ref, up_ref, out_ref, input_ref, length_ref,
+        first_hbm, both_out, strip_out, normed_out, kv_out, lat_out, latent_out, inverse_out, latent_inverse_out,
+        gain_one_out, gain_two_out, gain_latent_out, cos_ref, sin_ref, cos_group, sin_group, begin_out, slot_out,
+        live_out, live_rows, first_out, both, sends, arrivals, locals_,
     ):
         net = Net(sends, arrivals, locals_)
         x, y, z, c = (lax.axis_index(a) for a in AXES)
@@ -574,13 +468,6 @@
         def passing(step, h):
             return first_out.at[pl.ds(2 * h, 2), :, c, :, columns(step)]
 
-        greet(X_RING + Y_LINE + Z_LINE + TWIN)
-        part = RowGather(net, first_ref.at[:, columns(0)], first_out.at[:, :, :, :, columns(0)])
-        every = pl.ds(0, OWN_COLUMNS)
-        whole = RowGather(net, first_ref.at[:, every], first_out.at[:, :, :, :, every])
-        piece = out_ref.at[pl.ds(pl.multiple_of(x * quarter, quarter), quarter)]
-        piece_mine = net.keep(piece, strip_out.at[z])
-        pieces = [net.send(piece, strip_out.at[z], "z", d) for d in LINE]
         stacked = jnp.concatenate(
             [ref[:, h * half_wide : (h + 1) * half_wide] for ref in (gate_ref, up_ref) for h in range(2)], axis=0
         )
@@ -594,16 +481,58 @@
                     picked[i * rows_in : (i + 1) * rows_in]
                 )
 
+        greet(X_RING + Y_LINE + Z_LINE + TWIN)
+        part = RowGather(net, first_ref.at[:, columns(0)], first_out.at[:, :, :, :, columns(0)])
         pick(0)
         part.spread()
+        every = pl.ds(0, OWN_COLUMNS)
+        whole = RowGather(net, first_ref.at[:, every], first_out.at[:, :, :, :, every])
+        piece = out_ref.at[pl.ds(pl.multiple_of(x * quarter, quarter), quarter)]
+        piece_mine = net.keep(piece, strip_out.at[z])
+        pieces = [net.send(piece, strip_out.at[z], "z", d) for d in LINE]
+        pick(1)
         whole.spread()
-        pick(1)
+
+        begins = [0]
+        for i in range(length_ref.shape[1]):
+            begins.append(begins[-1] + length_ref[0, i])
+
+        def begin_of(slots):
+            begin = jnp.zeros_like(slots)
+            for value in begins[1:]:
+                begin = jnp.where(slots >= value, value, begin)
+            return begin
+
+        def angles(slots, axis):
+            feature = lax.broadcasted_iota(jnp.int32, slots.shape, axis).astype(F32)
+            return (slots - begin_of(slots)).astype(F32) * jnp.exp(feature * (-math.log(10000.0) / HALF))
+
+        slots = lax.broadcasted_iota(jnp.int32, (size, HALF), 0) + ((y * 4 + z) * 2 + c) * size
+        angle = angles(slots, 1)
+        cos_ref[...] = jnp.cos(angle)
+        sin_ref[...] = jnp.sin(angle)
         both_mine = net.keep(both.at[c], both_out.at[c])
         both_come = net.send(both.at[1 - c], both_out.at[c], "c", 1)
         part.arrive()
         right = [net.send(passing(0, h), passing(0, h), "x", 1) for h in (0, 1)]
         left = [net.send(passing(0, h), passing(0, h), "x", -1) for h in (1, 0)]
         whole.arrive()
+
+        @pl.loop(0, 4)
+        def _(seg):
+            base = (seg * 4 + z) * 2 * size
+            angle = angles(lax.broadcasted_iota(jnp.int32, (HALF, 2 * size), 1) + base, 0)
+            cos_group[seg] = jnp.cos(angle)
+            sin_group[seg] = jnp.sin(angle)
+            slots = lax.broadcasted_iota(jnp.int32, (1, 4 * size), 1) % (2 * size) + base
+            slot_out[seg] = slots
+            begin_out[seg] = begin_of(slots)
+            live_out[seg] = (slots < begins[-1]).astype(F32)
+            slots = lax.broadcasted_iota(jnp.int32, (2 * size, 1), 0) + base
+            live_rows[pl.ds(pl.multiple_of(seg * 2 * size, 2 * size), 2 * size), :] = (
+                (slots < begins[-1]).astype(F32)
+            )
+
         right[0].wait_recv()
         far = [net.send(passing(-1, 0), passing(-1, 0), "x", 1)]
         left[0].wait_recv()
@@ -621,15 +550,68 @@
         whole.finish()
         for copy in shared + pieces + [both_come]:
             copy.wait_recv()
+        keep = net.keep(first_out, first_hbm)
+
+        gains = pl.ds(first_width, 128)
+        for i in range(16):
+            for k, target in enumerate((gain_one_out, gain_two_out)):
+                target[:, i * 128 : (i + 1) * 128] = (
+                    first_out[i // 4, i % 4, 0, k : k + 1, gains].astype(F32)
+                    + first_out[i // 4, i % 4, 1, k : k + 1, gains].astype(F32)
+                )
+        for i in range(8):
+            total = 0.0
+            for k in range(4):
+                total = total + first_out[i // 2, i % 2 * 2 + k // 2, k % 2, 2:3, gains].astype(F32)
+            gain_latent_out[:, i * 128 : (i + 1) * 128] = total
+        values = input_ref[...].astype(F32)
+        inverse = lax.rsqrt(jnp.mean(values * values, axis=-1, keepdims=True) + EPSILON)
+        inverse_out[...] = inverse
+        normed_out[...] = (values * inverse * gain_one_out[...]).astype(BF)
+        firsts = dot(normed_out[...], first_out[...].reshape(32 * rows_in, first_width + 128)[:, :first_width])
+        latent = firsts[:, :latent_width]
+        latent_out[...] = latent
+        inverse = lax.rsqrt(jnp.mean(latent * latent, axis=-1, keepdims=True) + EPSILON)
+        latent_inverse_out[...] = inverse
+        lat_out[...] = (latent * inverse * gain_latent_out[...]).astype(BF)
+        lower, upper = firsts[:, latent_width : latent_width + HALF], firsts[:, latent_width + HALF : latent_width + SIZE]
+        kv_out[:, :HALF] = (lower * cos_ref[...] - upper * sin_ref[...]).astype(BF)
+        kv_out[:, HALF:SIZE] = (upper * cos_ref[...] + lower * sin_ref[...]).astype(BF)
+        kv_out[:, SIZE:] = firsts[:, latent_width + SIZE :].astype(BF)
         both_mine.wait()
         piece_mine.wait()
+        keep.wait()
         net.close()
 
-    outs = (shape(4, 4, 2, *first.shape), shape(2, rows_in, 2 * units), shape(4, quarter, width))
+    size, deep = inputs.shape
+    first_width = first.shape[1] - 128
+    whole = (4, 4, 2, *first.shape)
+    outs = (
+        shape(*whole), shape(2, rows_in, 2 * units), shape(4, quarter, width), shape(size, deep),
+        shape(size, 2 * SIZE), shape(size, latent_width), shape(size, latent_width, kind=F32),
+        shape(size, 1, kind=F32), shape(size, 1, kind=F32), shape(1, deep, kind=F32), shape(1, deep, kind=F32),
+        shape(1, latent_width, kind=F32), shape(size, HALF, kind=F32), shape(size, HALF, kind=F32),
+        shape(4, HALF, 2 * size, kind=F32), shape(4, HALF, 2 * size, kind=F32),
+        shape(4, 1, 4 * size, kind=jnp.int32), shape(4, 1, 4 * size, kind=jnp.int32), shape(4, 1, 4 * size, kind=F32),
+        shape(8 * size, 1, kind=F32),
+    )
+    scratch = [pltpu.VMEM(whole, BF), pltpu.VMEM((2, rows_in, 2 * units), BF)]
     return comm_call(
-        body, "first_weights", 1, outs, (first, gate, up, out), [pltpu.VMEM((2, rows_in, 2 * units), BF)], 64, 4,
-        [IN_VMEM] * 4, [ANYWHERE] * 3,
-    )
+        body, "first_weights", 1, outs, (first, gate, up, out, inputs, lengths), scratch, 64, 5,
+        [IN_VMEM] * 5 + [pl.BlockSpec(memory_space=pltpu.SMEM)], [ANYWHERE] * 3 + [IN_VMEM] * 17,
+    )
+
+
+def gain_rows(norm_gain, ffn_gain, q_gain):
+    z, c = lax.axis_index("z"), lax.axis_index("c")
+    rows = norm_gain.shape[0]
+
+    def spot(values, at):
+        count = 128 // values.shape[0]
+        return jnp.concatenate([values * (at == i).astype(F32) for i in range(count)])
+
+    block = jnp.stack([spot(norm_gain, c), spot(ffn_gain, c), spot(q_gain, z % 2 * 2 + c)])
+    return jnp.pad(block.astype(BF), ((0, rows - 3), (0, 0)))
 
 
 def keys_and_latents(key_value, latent, up, strip):
@@ -685,29 +667,6 @@
     )
 
 
-def heads_sum_and_cotangent(partial, cotangent):
-    def body(part_ref, cot_ref, out_ref, cot_out, near, relay, come, go, sends, arrivals, locals_):
-        net = Net(sends, arrivals, locals_)
-        greet(X_RING + Y_RING + TWIN)
-        ring = RingSum(net, part_ref, out_ref, "y", near, relay, come, go)
-        feed = RingGather(net, cot_ref, cot_out, "x")
-        ring.relay_far()
-        ring.issue()
-        feed.forward()
-        ring.pass_on()
-        feed.share()
-        ring.finish()
-        feed.finish()
-        net.close()
-
-    size, width = cotangent.shape
-    outs = (shape(size, width, kind=F32), shape(4, 2, size, width))
-    return comm_call(
-        body, "heads_sum_and_cotangent", 3, outs, (partial, cotangent), ring_sum_scratch(size, width), 20, 2,
-        [IN_VMEM, IN_VMEM], [IN_VMEM, ANYWHERE],
-    )
-
-
 def add_up(terms, out, rows):
     total = terms[0][rows].astype(F32)
     for term in terms[1:]:
@@ -719,7 +678,115 @@
     rows_loop(out.shape[0], out.shape[1], lambda rows: add_up(terms, out, rows))
 
 
-def feed_forward(normed_two, normed, grad_out, both, down):
+def attend(
+    latent, up_heads, kv, begin, slot, live, cosine, sine, out_heads, inputs, gain, cotangent,
+):
+    segments, _, rows = slot.shape
+    tokens = rows // 2
+    size, width = inputs.shape
+
+    def body(
+        lat_ref, up_ref, kv_ref, begin_ref, slot_ref, live_ref, cos_ref, sin_ref, heads_ref, input_ref, gain_ref,
+        cot_ref,
+        mixed_out, qt_ref, lse_ref, middle_out, inverse_out, two_out, cot_out,
+        vt, peak, total, accum, part, near, go, come, sends, arrivals, locals_,
+    ):
+        net = Net(sends, arrivals, locals_)
+        y, z, c = (lax.axis_index(a) for a in ROW)
+        greet(X_RING + Y_LINE + TWIN)
+        feed = RingGather(net, cot_ref, cot_out, "x")
+        turned(kv_ref, vt, segments * (segments - 1) + z + 1, VALUES)
+
+        def segment(step):
+            seg = along("y", step)
+            here = pl.ds(pl.multiple_of(seg * tokens, tokens), tokens)
+            cos_here, sin_here = cos_ref[seg], sin_ref[seg]
+            for head in range(2):
+                columns = slice(head * SIZE, (head + 1) * SIZE)
+                raw = dot(lat_ref[here, :], up_ref[:, columns]).T
+                lower, upper = raw[:HALF], raw[HALF:]
+                turn = jnp.concatenate(
+                    [lower * cos_here - upper * sin_here, upper * cos_here + lower * sin_here], axis=0
+                )
+                qt_ref[seg, :, head * tokens : (head + 1) * tokens] = (
+                    turn.astype(BF) * (SIZE ** -0.5)
+                ).astype(BF)
+            peak[...] = jnp.full_like(peak, MASKED)
+            total[...] = jnp.zeros_like(total)
+            accum[...] = jnp.zeros_like(accum)
+
+            def tile(at, count, masked):
+                scores = dot(kv_ref[pl.ds(at, count), KEYS], qt_ref[seg])
+                if masked:
+                    key = lax.broadcasted_iota(jnp.int32, scores.shape, 0) + at
+                    scores = jnp.where((key >= begin_ref[seg]) & (key <= slot_ref[seg]), scores, MASKED)
+                before = peak[...]
+                now = jnp.maximum(before, jnp.max(scores, axis=0, keepdims=True))
+                weights = jnp.exp(scores - now)
+                shrink = jnp.exp(before - now)
+                peak[...] = now
+                total[...] = total[...] * shrink + jnp.sum(weights, axis=0, keepdims=True)
+                accum[...] = accum[...] * shrink + dot(vt[:, pl.ds(at, count)], weights.astype(BF))
+
+            sweep(seg, segments, z, tile)
+            lse_ref[seg] = peak[...] + jnp.log(total[...])
+            result = accum[...] * (live_ref[seg] / total[...])
+            for head in range(2):
+                mixed_out[here, head * SIZE : (head + 1) * SIZE] = (
+                    result[:, head * tokens : (head + 1) * tokens].T.astype(BF)
+                )
+            part[seg] = dot(mixed_out[here, :], heads_ref[...]).astype(BF).reshape(2, size, width)
+            return net.send(part.at[seg, 1 - c], near.at[step], "c", 1)
+
+        def pair(step):
+            swaps[step].wait_recv()
+            add_all([part.at[along("y", step), c], near.at[step]], go.at[step - 1])
+            return net.send(go.at[step - 1], come.at[step - 1], "y", step)
+
+        swaps = {2: segment(2)}
+        feed.forward()
+        swaps[1] = segment(1)
+        ends = [pair(2)]
+        feed.share()
+        swaps[3] = segment(3)
+        ends.append(pair(1))
+        ends.append(pair(3))
+        feed.finish()
+        swaps[0] = segment(0)
+        swaps[0].wait_recv()
+        for copy in ends:
+            copy.wait_recv()
+        add_all(
+            [input_ref, part.at[y, c], near.at[0], come.at[0], come.at[1], come.at[2]], middle_out
+        )
+        values = middle_out[...]
+        inverse = lax.rsqrt(jnp.mean(values * values, axis=-1, keepdims=True) + EPSILON)
+        inverse_out[...] = inverse
+        two_out[...] = (values * inverse * gain_ref[...]).astype(BF)
+        net.close()
+
+    outs = (
+        shape(segments * tokens, 2 * SIZE), shape(segments, SIZE, rows), shape(segments, 1, rows, kind=F32),
+        shape(size, width, kind=F32), shape(size, 1, kind=F32), shape(size, width), shape(4, 2, size, width),
+    )
+    scratch = [
+        pltpu.VMEM((SIZE, kv.shape[0]), BF),
+        pltpu.VMEM((1, rows), F32),
+        pltpu.VMEM((1, rows), F32),
+        pltpu.VMEM((SIZE, rows), F32),
+        pltpu.VMEM((4, 2, size, width), BF),
+        pltpu.VMEM((4, size, width), BF),
+        pltpu.VMEM((3, size, width), BF),
+        pltpu.VMEM((3, size, width), BF),
+    ]
+    return comm_call(
+        body, "attend", 3, outs,
+        (latent, up_heads, kv, begin, slot, live, cosine, sine, out_heads, inputs, gain, cotangent),
+        scratch, 20, 2, [IN_VMEM] * 12, [IN_VMEM] * 6 + [ANYWHERE],
+    )
+
+
+def feed_forward(normed_two, normed, grad_out, both, down, middle, inverse, gain):
     size, width = normed_two.shape
     units = down.shape[0]
     tall = width // 4
@@ -727,7 +794,8 @@
     high = units // 16
 
     def body(
-        two_ref, one_ref, cot_hbm, both_hbm, down_hbm, sum_out, one_out, branch_out, gb_out, mid_out,
+        two_ref, one_ref, middle_ref, inverse_ref, gain_ref, cot_hbm, both_hbm, down_hbm,
+        middle_out, grad_out_, gain_out, one_out, branch_out, gb_out, mid_out,
         two, cot, both, down, hidden, grads, part, near, go, come, gb, gd, down_come, ahead,
         sends, arrivals, locals_,
     ):
@@ -832,7 +900,16 @@
         swaps[0].wait_recv()
         for copy in ends:
             copy.wait_recv()
-        add_all([part.at[x, c], near.at[0], come.at[0], come.at[1], come.at[2]], sum_out)
+        add_all([part.at[x, c], near.at[0], come.at[0], come.at[1], come.at[2]], middle_out)
+        values, scale, grad = middle_ref[...], inverse_ref[...], middle_out[...]
+        gain_out[...] = jnp.sum(grad * values * scale, axis=0, keepdims=True)
+        scaled = grad * gain_ref[...]
+        grad = cot[x, c].astype(F32) + (
+            scale * scaled
+            - values * (scale * scale * scale) * jnp.mean(scaled * values, axis=-1, keepdims=True)
+        )
+        middle_out[...] = grad
+        grad_out_[...] = grad.astype(BF)
         for copy in shared:
             copy.wait_recv()
         for copy in first:
@@ -846,7 +923,8 @@
         net.close()
 
     outs = (
-        shape(size, width, kind=F32), shape(4, 2, size, tall), shape(4, 2, size, width), shape(width, 2 * units),
+        shape(size, width, kind=F32), shape(size, width), shape(1, width, kind=F32), shape(4, 2, size, tall),
+        shape(4, 2, size, width), shape(width, 2 * units),
         shape(2, 4, high, lanes),
     )
     scratch = [
@@ -866,12 +944,12 @@
         pltpu.VMEM((3, 2 * size, units), F32),
     ]
     return comm_call(
-        body, "feed_forward", 4, outs, (normed_two, normed, grad_out, both, down), scratch, 32, 14,
-        [IN_VMEM] * 2 + [ANYWHERE] * 3, [IN_VMEM, ANYWHERE, ANYWHERE, ANYWHERE, IN_VMEM],
-    )
-
-
-Y_COLUMNS = 640
+        body, "feed_forward", 4, outs, (normed_two, normed, middle, inverse, gain, grad_out, both, down), scratch,
+        32, 14, [IN_VMEM] * 5 + [ANYWHERE] * 3, [IN_VMEM] * 3 + [ANYWHERE] * 3 + [IN_VMEM],
+    )
+
+
+Y_COLUMNS = 512
 
 
 class FirstStep:
@@ -906,184 +984,150 @@
         add_all([self.mid.at[here]] + [self.come.at[d] for d in range(3)], out)
 
 
-def keys_and_latents_sum(
-    grad_kv, grad_query, latent_group, up_heads, grad_out, mids, cosine, sine, latent, inverse, gain,
+def last_sums(
+    grad_kv, grad_query, latent_group, up_heads, grad_out, grad_both, grad_down, cosine, sine, latent,
+    latent_inverse, latent_gain, normed_part, inputs, inverse, gain_one, gain_two, weights, share,
 ):
     _, _, _, size, thin = grad_kv.shape
-    group, width = latent_group.shape
+    group, latent_width = latent_group.shape
     per = up_heads.shape[1]
     high, lanes = up_heads.shape[0] // 32, per // 4
     _, out_rows, wide = grad_out.shape
     quarter = out_rows // 4
-    tall, ahead = mids[0].shape[1:]
-    after = mids[1].shape[2]
-    part = (width + thin) // 2
-
-    def body(
-        kv_ref, query_ref, group_ref, heads_ref, out_ref, one_ref, two_ref, cos_ref, sin_ref, latent_ref, inverse_ref,
-        gain_ref, firsts_out, gain_out, up_out, out_out, one_out, two_out, *rest,
-    ):
-        net = Net(*rest[17:])
-        up_come, out_come = rest[9:11]
-        partial, ups_here, kv_sum, part_sum = rest[13:17]
-        x = lax.axis_index("x")
-
-        def lane(at):
-            return pl.ds(pl.multiple_of(at * lanes, lanes), lanes)
-
-        def strip(at):
-            return pl.ds(pl.multiple_of(at * quarter, quarter), quarter)
-
-        greet(X_LINE + Y_LINE + Z_LINE + TWIN)
-        row = RowSum(net, kv_ref, kv_sum, *rest[:5])
-        outs = [net.send(out_ref.at[:, strip(along("x", d))], out_come.at[d - 1], "x", d) for d in LINE]
-        for i in range(4):
-            at = pl.ds(i * 2 * size, 2 * size)
-            partial[i] = dot_nt(query_ref[at, :], heads_ref[...]).astype(BF).reshape(2, size, width)
-        ring = RingSum(net, partial, part_sum, "y", *rest[5:9])
-        ups_here[...] = dot_tn(group_ref[...], query_ref[...]).astype(BF).reshape(4, 4, 2, high, per)
-        ups = [
-            net.send(ups_here.at[:, :, :, :, lane(along("x", d))], up_come.at[d - 1], "x", d) for d in LINE
-        ]
-        row.start()
-        halves = [
-            SecondStep(net, mid, axis, come)
-            for mid, axis, come in ((one_ref, "z", rest[11]), (two_ref, "y", rest[12]))
-        ]
-        ring.relay_far()
-        ring.issue()
-        row.turn()
-        ring.pass_on()
-        for copy in ups:
-            copy.wait_recv()
-
-        @pl.loop(0, 4)
-        def _(i):
-            up_out[i] = (
-                (ups_here[i, :, :, :, lane(x)].astype(F32) + up_come[0, i].astype(F32))
-                + (up_come[1, i].astype(F32) + up_come[2, i].astype(F32))
-            ).astype(BF)
-
-        ring.finish()
-        values = latent_ref[...]
-        scale = inverse_ref[...]
-        scaled = part_sum[...] * gain_ref[...]
-        gain_out[...] = jnp.sum(part_sum[...] * values * scale, axis=0, keepdims=True)
-        back = scale * scaled - values * (scale * scale * scale) * jnp.mean(scaled * values, axis=-1, keepdims=True)
-        firsts_out[0] = back[:, :part].astype(BF)
-        firsts_out[1, :, : width - part] = back[:, part:].astype(BF)
-        row.finish()
-        lower, upper = kv_sum[:, :HALF], kv_sum[:, HALF:SIZE]
-        at = width - part
-        firsts_out[1, :, at : at + HALF] = (lower * cos_ref[...] + upper * sin_ref[...]).astype(BF)
-        firsts_out[1, :, at + HALF : at + SIZE] = (upper * cos_ref[...] - lower * sin_ref[...]).astype(BF)
-        firsts_out[1, :, at + SIZE :] = kv_sum[:, SIZE:].astype(BF)
-        halves[0].finish(one_out)
-        halves[1].finish(two_out)
-        for copy in outs:
-            copy.wait_recv()
-        for i in range(4):
-            add_all([out_ref.at[i, strip(x)]] + [out_come.at[d, i] for d in range(3)], out_out.at[i])
-        net.close()
-
-    outs = (
-        shape(2, size, part), shape(1, width, kind=F32), shape(4, 4, 2, high, lanes), shape(4, quarter, wide),
-        shape(tall, ahead), shape(tall, after),
-    )
-    scratch = [
-        pltpu.VMEM((3, 4, 4, 2, high, lanes), BF),
-        pltpu.VMEM((3, 4, quarter, wide), BF),
-        pltpu.VMEM((3, tall, ahead), BF),
-        pltpu.VMEM((3, tall, after), BF),
-        pltpu.VMEM((4, 2, size, width), BF),
-        pltpu.VMEM((4, 4, 2, high, per), BF),
-        pltpu.VMEM((size, thin), F32),
-        pltpu.VMEM((size, width), F32),
-    ]
-    return comm_call(
-        body, "keys_and_latents_sum", 7, outs,
-        (
-            grad_kv, grad_query, latent_group, up_heads, grad_out, *mids, cosine, sine, latent, inverse, gain,
-        ),
-        row_sum_scratch(size, thin) + ring_sum_scratch(size, width) + scratch, 46, 2,
-        [IN_VMEM] * 12, [IN_VMEM] * 6,
-    )
-
-
-def last_sums(
-    value, both, grad_out, grad_up, grad_down, normed_part, inputs, inverse, gain_one, gain_two, gain_latent, weights,
-    share,
-):
-    _, size, part = value.shape
+    tall, ahead_columns = grad_both[0].shape[1:]
+    after_columns = grad_both[1].shape[2]
+    both_columns = ahead_columns + after_columns
+    rows = tall // 2
+    half_units = both_columns // 4
+    _, _, padded, down_lanes = grad_down.shape
+    width = 2 * down_lanes
+    half_wide = 2 * half_units // padded * 4 * share
+    part = (latent_width + thin) // 2
     deep = weights.shape[0]
     tiles = deep // BLOCK
-    _, tall, wide = grad_out.shape
-    _, _, _, high, lanes = grad_up.shape
-    rows = both.shape[1]
-    half_units = both.shape[2] // 4
-    padded, width = grad_down.shape
-    half_wide = 2 * half_units // padded * 4 * share
 
     def body(
-        ref, both_ref, out_ref, up_ref, down_ref, normed_ref, input_ref, inverse_ref, gain_ref, two_ref, latent_ref,
-        weights_hbm,
+        kv_ref, query_ref, group_ref, heads_ref, out_ref, one_ref, two_ref, down_ref, cos_ref, sin_ref, latent_ref,
+        latent_inverse_ref, latent_gain_ref, normed_ref, input_ref, inverse_ref, gain_ref, gain_two_ref, weights_hbm,
         first_out, gain_out, back_out, out_out, gate_out, up_weight_out, down_out, q_up_out,
+        row_near, row_go, row_first, row_mid, row_last, ring_near, ring_relay, ring_come, ring_go,
+        partial, ups_here, kv_sum, part_sum, up_come_x, out_come_x, one_come, two_come, down_come, both_here,
+        up_kept, out_kept, firsts,
         gathered, both_all, up_all, down_all, out_come, up_come, up_sum, up_y, weights_ref, accum, down_rows,
-        first_here, pair, first_come, first_x, gain_here, gain_near, gain_come, gain_two, gain_y, gain_x,
+        first_here, pair, first_come, first_x, gain_here, gain_near, gain_come, gain_z, gain_y, gain_x,
         sends, arrivals, locals_,
     ):
         net = Net(sends, arrivals, locals_)
         x, y, z, c = (lax.axis_index(a) for a in AXES)
+
+        def lane(at):
+            return pl.ds(pl.multiple_of(at * lanes, lanes), lanes)
+
+        def strip(at):
+            return pl.ds(pl.multiple_of(at * quarter, quarter), quarter)
+
         load = net.keep(weights_hbm, weights_ref)
         greet(X_LINE + Y_LINE + Z_LINE + TWIN)
-        mine = net.keep(ref.at[c], gathered.at[y, c])
-        come = net.send(ref.at[1 - c], gathered.at[y, c], "c", 1)
-        both_mine = net.keep(both_ref.at[c], both_all.at[x, c])
-        both_come = net.send(both_ref.at[1 - c], both_all.at[x, c], "c", 1)
-        ups = [net.send(up_ref.at[:, along("z", d)], up_come.at[d - 1], "z", d) for d in LINE]
-        outs = [net.send(out_ref.at[along("z", d)], out_come.at[d - 1], "z", d) for d in LINE]
-        down_mine = net.keep(down_ref, down_all.at[x])
-
+        row = RowSum(net, kv_ref, kv_sum, row_near, row_go, row_first, row_mid, row_last)
+        outs = [net.send(out_ref.at[:, strip(along("x", d))], out_come_x.at[d - 1], "x", d) for d in LINE]
+        for i in range(4):
+            at = pl.ds(i * 2 * size, 2 * size)
+            partial[i] = dot_nt(query_ref[at, :], heads_ref[...]).astype(BF).reshape(2, size, latent_width)
+        ring = RingSum(net, partial, part_sum, "y", ring_near, ring_relay, ring_come, ring_go)
+        row.start()
+        ring.relay_far()
+        ring.issue()
+        ups_here[...] = dot_tn(group_ref[...], query_ref[...]).astype(BF).reshape(4, 4, 2, high, per)
+        ups = [
+            net.send(ups_here.at[:, :, :, :, lane(along("x", d))], up_come_x.at[d - 1], "x", d) for d in LINE
+        ]
+        row.turn()
+        ring.pass_on()
+        halves = [
+            SecondStep(net, mid, axis, come)
+            for mid, axis, come in (
+                (one_ref, "z", one_come), (two_ref, "y", two_come), (down_ref.at[0], "z", down_come.at[0]),
+                (down_ref.at[1], "y", down_come.at[1]),
+            )
+        ]
+
+        ring.finish()
+        values = latent_ref[...]
+        scale = latent_inverse_ref[...]
+        scaled = part_sum[...] * latent_gain_ref[...]
+        gain_latent = jnp.sum(part_sum[...] * values * scale, axis=0, keepdims=True)
+        back = scale * scaled - values * (scale * scale * scale) * jnp.mean(scaled * values, axis=-1, keepdims=True)
+        firsts[0] = back[:, :part].astype(BF)
+        firsts[1, :, : latent_width - part] = back[:, part:].astype(BF)
+        row.finish()
+        lower, upper = kv_sum[:, :HALF], kv_sum[:, HALF:SIZE]
+        at = latent_width - part
+        firsts[1, :, at : at + HALF] = (lower * cos_ref[...] + upper * sin_ref[...]).astype(BF)
+        firsts[1, :, at + HALF : at + SIZE] = (upper * cos_ref[...] - lower * sin_ref[...]).astype(BF)
+        firsts[1, :, at + SIZE :] = kv_sum[:, SIZE:].astype(BF)
+
+        mine = net.keep(firsts.at[c], gathered.at[y, c])
+        come = net.send(firsts.at[1 - c], gathered.at[y, c], "c", 1)
         mine.wait()
         spot = gathered.at[y, c]
         ahead = [net.send(spot, spot, "y", 1), net.send(spot, spot, "y", -1)]
         come.wait_recv()
         spot = gathered.at[y, 1 - c]
         ahead += [net.send(spot, spot, "y", 1), net.send(spot, spot, "y", -1)]
+        halves[0].finish(both_here.at[:, pl.ds(0, ahead_columns)])
+        halves[1].finish(both_here.at[:, pl.ds(ahead_columns, after_columns)])
+        own_rows = pl.ds(pl.multiple_of(c * rows, rows), rows)
+        other_rows = pl.ds(pl.multiple_of((1 - c) * rows, rows), rows)
+        both_mine = net.keep(both_here.at[own_rows], both_all.at[x, c])
+        both_come = net.send(both_here.at[other_rows], both_all.at[x, c], "c", 1)
         both_mine.wait()
         both_come.wait_recv()
         zero, one = both_all.at[x, 0], both_all.at[x, 1]
         right = [net.send(spot, spot, "x", 1) for spot in (zero, one)]
         left = [net.send(spot, spot, "x", -1) for spot in (one, zero)]
 
-        def back(i):
+        for copy in ups:
+            copy.wait_recv()
+        for i in range(4):
+            up_kept[i] = (
+                (ups_here[i, :, :, :, lane(x)].astype(F32) + up_come_x[0, i].astype(F32))
+                + (up_come_x[1, i].astype(F32) + up_come_x[2, i].astype(F32))
+            ).astype(BF)
+        ups = [net.send(up_kept.at[:, along("z", d)], up_come.at[d - 1], "z", d) for d in LINE]
+        for copy in outs:
+            copy.wait_recv()
+        for i in range(4):
+            add_all([out_ref.at[i, strip(x)]] + [out_come_x.at[d, i] for d in range(3)], out_kept.at[i])
+        outs = [net.send(out_kept.at[along("z", d)], out_come.at[d - 1], "z", d) for d in LINE]
+
+        def back_tile(i):
             at = pl.ds(pl.multiple_of(i * BLOCK, BLOCK), BLOCK)
             total = 0.0
             for core in range(2):
                 columns = slice(core * part, (core + 1) * part)
-                total = total + dot_nt(ref[core], weights_ref[at, columns])
+                total = total + dot_nt(firsts[core], weights_ref[at, columns])
             back_out[:, at] = total
 
         load.wait()
-        pl.loop(0, tiles // 2)(back)
-        for copy in ups:
-            copy.wait_recv()
-        for i in range(4):
-            up_sum[i] = (
-                (up_ref[i, z].astype(F32) + up_come[0, i].astype(F32))
-                + (up_come[1, i].astype(F32) + up_come[2, i].astype(F32))
-            ).astype(BF)
-        ups = [net.send(up_sum.at[along("y", d)], up_y.at[y], "y", d) for d in LINE]
-        up_mine = net.keep(up_sum.at[y], up_y.at[y])
-
+        pl.loop(0, tiles // 2)(back_tile)
         ahead[0].wait_recv()
         spot = gathered.at[along("y", -1), c]
         ahead.append(net.send(spot, spot, "y", 1))
         ahead[3].wait_recv()
         spot = gathered.at[along("y", 1), 1 - c]
         ahead.append(net.send(spot, spot, "y", -1))
-
-        pl.loop(tiles // 2, tiles)(back)
+        pl.loop(tiles // 2, tiles)(back_tile)
+
+        for copy in ups:
+            copy.wait_recv()
+        for i in range(4):
+            up_sum[i] = (
+                (up_kept[i, z].astype(F32) + up_come[0, i].astype(F32))
+                + (up_come[1, i].astype(F32) + up_come[2, i].astype(F32))
+            ).astype(BF)
+        ups = [net.send(up_sum.at[along("y", d)], up_y.at[y], "y", d) for d in LINE]
+        up_mine = net.keep(up_sum.at[y], up_y.at[y])
+
         values = input_ref[...].astype(F32)
         scale = inverse_ref[...]
         grad = back_out[...]
@@ -1095,8 +1139,8 @@
         gain_here[...] = jnp.zeros_like(gain_here)
         for i in range(16):
             gain_here[i // 4, i % 4, 0:1, :] = gain_own[:, i * 128 : (i + 1) * 128]
-            gain_here[i // 4, i % 4, 1:2, :] = two_ref[:, i * 128 : (i + 1) * 128]
-            gain_here[i // 4, i % 4, 2:3, :] = latent_ref[:, i // 2 * 128 : (i // 2 + 1) * 128]
+            gain_here[i // 4, i % 4, 1:2, :] = gain_two_ref[:, i * 128 : (i + 1) * 128]
+            gain_here[i // 4, i % 4, 2:3, :] = gain_latent[:, i // 2 * 128 : (i // 2 + 1) * 128]
         near = net.send(gain_here, gain_near, "c", 1)
 
         right[0].wait_recv()
@@ -1105,6 +1149,10 @@
         left[0].wait_recv()
         spot = both_all.at[along("x", 1), 1]
         far.append(net.send(spot, spot, "x", -1))
+        for k in (2, 3):
+            halves[k].finish(down_all.at[x, :, pl.ds((k - 2) * down_lanes, down_lanes)])
+        spot = down_all.at[x]
+        downs = [net.send(spot, spot, "x", d) for d in LINE]
 
         for copy in [ahead[i] for i in (1, 2, 4, 5)]:
             copy.wait_recv()
@@ -1116,7 +1164,7 @@
 
         for copy in outs:
             copy.wait_recv()
-        add_all([out_ref.at[z]] + [out_come.at[d] for d in range(3)], out_out.at[x])
+        add_all([out_kept.at[z]] + [out_come.at[d] for d in range(3)], out_out.at[x])
         spot = out_out.at[x]
         outs = [net.send(spot, spot, "x", d) for d in LINE]
         up_mine.wait()
@@ -1127,7 +1175,7 @@
 
         first_mine.wait()
         first_near.wait_recv()
-        firsts = [
+        weight_sends = [
             [net.send(pair.at[core, along("z", d)], first_come.at[d - 1, core], "z", d) for d in LINE]
             for core in range(2)
         ]
@@ -1138,7 +1186,6 @@
         up_mine.wait()
         spot = up_all.at[x]
         ups = [net.send(spot, spot, "x", d) for d in LINE]
-        downs = [net.send(down_ref, down_all.at[x], "x", d) for d in LINE]
 
         accum[...] = jnp.zeros_like(accum)
 
@@ -1157,7 +1204,7 @@
         put(along("x", 1))
 
         def onward(core):
-            for copy in firsts[core]:
+            for copy in weight_sends[core]:
                 copy.wait_recv()
             add_all([pair.at[core, z]] + [first_come.at[d, core] for d in range(3)], first_x.at[x, core])
             spot = first_x.at[x, core]
@@ -1166,13 +1213,13 @@
         finals = [onward(0)]
         for copy in comes:
             copy.wait_recv()
-        gain_two[...] = (gain_near[:, z] + gain_come[0]) + (gain_come[1] + gain_come[2])
-        comes = [net.send(gain_two.at[along("y", d)], gain_y.at[d - 1], "y", d) for d in LINE]
+        gain_z[...] = (gain_near[:, z] + gain_come[0]) + (gain_come[1] + gain_come[2])
+        comes = [net.send(gain_z.at[along("y", d)], gain_y.at[d - 1], "y", d) for d in LINE]
         finals.append(onward(1))
         put(along("x", -1))
         for copy in comes:
             copy.wait_recv()
-        gain_x[x] = (gain_two[y] + gain_y[0]) + (gain_y[1] + gain_y[2])
+        gain_x[x] = (gain_z[y] + gain_y[0]) + (gain_y[1] + gain_y[2])
         spot = gain_x.at[x]
         comes = [net.send(spot, spot, "x", d) for d in LINE]
         for copy in far:
@@ -1182,7 +1229,6 @@
             target[:, (k % 2) * half_wide : (k % 2 + 1) * half_wide] = accum[k * rows : (k + 1) * rows].astype(BF)
         for copy in outs + ups + downs:
             copy.wait_recv()
-        down_mine.wait()
         for px in range(4):
             down_rows[px * share : (px + 1) * share, :] = down_all[px].astype(F32)[:share]
             for py in range(4):
@@ -1200,15 +1246,29 @@
         net.close()
 
     outs = (
-        shape(2, rows, part, kind=F32), shape(8, 128, kind=F32), shape(size, deep, kind=F32), shape(4, tall, wide),
-        shape(rows, 2 * half_wide), shape(rows, 2 * half_wide), shape(4 * share, width), shape(high, 32 * lanes),
-    )
-    scratch = [
+        shape(2, rows, part, kind=F32), shape(8, 128, kind=F32), shape(size, deep, kind=F32),
+        shape(4, quarter, wide), shape(rows, 2 * half_wide), shape(rows, 2 * half_wide), shape(4 * share, width),
+        shape(high, 32 * lanes),
+    )
+    scratch = row_sum_scratch(size, thin) + ring_sum_scratch(size, latent_width) + [
+        pltpu.VMEM((4, 2, size, latent_width), BF),
+        pltpu.VMEM((4, 4, 2, high, per), BF),
+        pltpu.VMEM((size, thin), F32),
+        pltpu.VMEM((size, latent_width), F32),
+        pltpu.VMEM((3, 4, 4, 2, high, lanes), BF),
+        pltpu.VMEM((3, 4, quarter, wide), BF),
+        pltpu.VMEM((3, tall, ahead_columns), BF),
+        pltpu.VMEM((3, tall, after_columns), BF),
+        pltpu.VMEM((2, 3, padded, down_lanes), BF),
+        pltpu.VMEM((tall, both_columns), BF),
+        pltpu.VMEM((4, 4, 2, high, lanes), BF),
+        pltpu.VMEM((4, quarter, wide), BF),
+        pltpu.VMEM((2, size, part), BF),
         pltpu.VMEM((4, 2, size, part), BF),
-        pltpu.VMEM((4, *both.shape), BF),
+        pltpu.VMEM((4, 2, rows, both_columns), BF),
         pltpu.VMEM((4, 4, 2, high, lanes), BF),
         pltpu.VMEM((4, padded, width), BF),
-        pltpu.VMEM((3, tall, wide), BF),
+        pltpu.VMEM((3, quarter, wide), BF),
         pltpu.VMEM((3, 4, 2, high, lanes), BF),
         pltpu.VMEM((4, 2, high, lanes), BF),
         pltpu.VMEM((4, 2, high, lanes), BF),
@@ -1227,41 +1287,37 @@
         pltpu.VMEM((4, 8, 128), F32),
     ]
     return comm_call(
-        body, "last_sums", 8, outs,
+        body, "last_sums", 7, outs,
         (
-            value, both, grad_out, grad_up, grad_down, normed_part, inputs, inverse, gain_one, gain_two, gain_latent,
-            weights,
+            grad_kv, grad_query, latent_group, up_heads, grad_out, *grad_both, grad_down, cosine, sine, latent,
+            latent_inverse, latent_gain, normed_part, inputs, inverse, gain_one, gain_two, weights,
         ),
-        scratch, 64, 8, [IN_VMEM] * 11 + [ANYWHERE], [IN_VMEM] * 8,
+        scratch, 104, 8, [IN_VMEM] * 18 + [ANYWHERE], [IN_VMEM] * 8,
     )
 
 
 def heads_back(
-    grad_branch, branch, mixed, qt, kv, out_heads, begin, slot, lse, live, cosine, sine, mid_down, gb,
+    grad_branch, branch, mixed, qt, kv, out_heads, begin, slot, lse, live, cosine, sine, gb,
 ):
     segments, _, rows = slot.shape
     tokens = rows // 2
     size, width = grad_branch.shape
-    _, high, down_lanes = mid_down.shape[1:]
     tall, wide = gb.shape[2:]
     ahead, after = Y_COLUMNS, wide - Y_COLUMNS
     half = out_heads.shape[0] // (2 * size)
 
     def body(
         grad_ref, branch_ref, mixed_ref, qt_ref, kv_ref, out_ref, begin_ref, slot_ref, lse_ref, live_ref, cos_ref,
-        sin_ref, mid_ref, gb_ref,
-        dq_ref, dkv_ref, stack, branch_out, down_out, one_out, two_out,
+        sin_ref, gb_ref,
+        dq_ref, dkv_ref, stack, branch_out, one_out, two_out,
         grads, kt, sums, accum, query, grad_rows, grad_turned, delta, go_send, near, relay, come, go,
-        own_one, come_one, own_two, come_two, down_one, down_two, sends, arrivals, locals_,
+        own_one, come_one, own_two, come_two, sends, arrivals, locals_,
     ):
         net = Net(sends, arrivals, locals_)
         y, z, c = (lax.axis_index(a) for a in ROW)
         greet(X_RING + Y_LINE + Z_LINE + TWIN)
         gathering = RingGather(net, grad_ref, grads, "y")
         two = FirstStep(net, gb_ref, pl.ds(ahead, after), "z", own_two, come_two, two_out)
-        halves = [
-            SecondStep(net, mid_ref.at[k], axis, (down_one, down_two)[k]) for k, axis in enumerate(("z", "y"))
-        ]
         ring = RingSum(net, branch_ref, branch_out, "x", near, relay, come, go)
         sums[...] = jnp.zeros_like(sums)
         turned(kv_ref, kt, segments * (segments - 1) + z + 1, KEYS)
@@ -1333,8 +1389,6 @@
         go_come = net.send(go_send, stack.at[pl.ds(half * c, half)], "c", 1)
         segment(2)
         dkv_ref[...] = sums[...].astype(BF)
-        for k in range(2):
-            halves[k].finish(down_out.at[:, pl.ds(k * down_lanes, down_lanes)])
         ring.finish()
         go_come.wait_recv()
         one.finish()
@@ -1343,7 +1397,7 @@
 
     outs = (
         shape(*mixed.shape), shape(*kv.shape), shape(2 * half, size, width), shape(size, width, kind=F32),
-        shape(high, 2 * down_lanes), shape(4, tall, ahead), shape(4, tall, after),
+        shape(4, tall, ahead), shape(4, tall, after),
     )
     scratch = [
         pltpu.VMEM((4, 2, size, width), BF),
@@ -1360,14 +1414,72 @@
         pltpu.VMEM((3, 4, tall, ahead), BF),
         pltpu.VMEM((4, tall, after), BF),
         pltpu.VMEM((3, 4, tall, after), BF),
-        pltpu.VMEM((3, high, down_lanes), BF),
-        pltpu.VMEM((3, high, down_lanes), BF),
     ]
     return comm_call(
         body, "heads_back", 6, outs,
-        (grad_branch, branch, mixed, qt, kv, out_heads, begin, slot, lse, live, cosine, sine, mid_down, gb),
-        scratch, 36, 3, [IN_VMEM] * 13 + [ANYWHERE], [IN_VMEM] * 7,
-    )
+        (grad_branch, branch, mixed, qt, kv, out_heads, begin, slot, lse, live, cosine, sine, gb),
+        scratch, 30, 3, [IN_VMEM] * 12 + [ANYWHERE], [IN_VMEM] * 6,
+    )
+
+
+def results(middle, branch, grad_middle, grad_norm, first, gate, up, down, out, q_up, latent_width):
+    size, width = middle.shape
+    rows, part = first.shape[1:]
+    spare = latent_width - part
+    kinds = [BF] + [F32] * 9
+    shapes = [
+        (size, width), (size, width), (rows, latent_width), (rows, SIZE), (rows, SIZE), gate.shape, up.shape,
+        down.shape, (4 * out.shape[1], out.shape[2]), q_up.shape,
+    ]
+    count = len(shapes)
+
+    def body(
+        middle_ref, branch_ref, grad_ref, norm_ref, first_ref, gate_ref, up_ref, down_ref, out_ref, q_up_ref, *rest,
+    ):
+        targets, made, done = rest[:count], rest[count : 2 * count], rest[2 * count]
+        copies = []
+
+        def ready(i):
+            copy = pltpu.make_async_copy(made[i], targets[i], done.at[i])
+            copy.start()
+            copies.append(copy)
+
+        made[5][...] = gate_ref[...].astype(F32)
+        ready(5)
+        made[6][...] = up_ref[...].astype(F32)
+        ready(6)
+        made[7][...] = down_ref[...].astype(F32)
+        ready(7)
+        for i in range(4):
+            quarter = out_ref.shape[1]
+            made[8][i * quarter : (i + 1) * quarter, :] = out_ref[i].astype(F32)
+        ready(8)
+        made[1][...] = grad_ref[...] + norm_ref[...]
+        ready(1)
+        made[0][...] = (middle_ref[...] + branch_ref[...]).astype(BF)
+        ready(0)
+        made[9][...] = q_up_ref[...].astype(F32)
+        ready(9)
+        made[2][:, :part] = first_ref[0]
+        made[2][:, part:] = first_ref[1, :, :spare]
+        ready(2)
+        made[3][...] = first_ref[1, :, spare : spare + SIZE]
+        ready(3)
+        made[4][...] = first_ref[1, :, spare + SIZE :]
+        ready(4)
+        for copy in copies:
+            copy.wait()
+
+    return pl.pallas_call(
+        body,
+        name="results",
+        out_shape=tuple(shape(*dims, kind=kind) for dims, kind in zip(shapes, kinds)),
+        in_specs=[IN_VMEM] * 10,
+        out_specs=[ANYWHERE] * count,
+        scratch_shapes=[pltpu.VMEM(dims, kind) for dims, kind in zip(shapes, kinds)]
+        + [pltpu.SemaphoreType.DMA((count,))],
+        compiler_params=pltpu.CompilerParams(vmem_limit_bytes=56 << 20),
+    )(middle, branch, grad_middle, grad_norm, first, gate, up, down, out, q_up)
 
 
 def gather(value, axes):
@@ -1384,30 +1496,11 @@
     x, y, z, c = (lax.axis_index(a) for a in ("x", "y", "z", "c"))
     span = n_y * n_z * n_c
     members = n_y * n_c
-    lengths_row = lengths[0]
-
-    mine = (y * n_z + z) * n_c + c
-    slots_mine = mine * rows + jnp.arange(rows, dtype=jnp.int32)
-    begin_mine, _ = places_of(lengths_row, slots_mine)
-    cosine, sine = tables(slots_mine - begin_mine)
-    strip = n_c * rows
-    slots_group = (
-        (jnp.arange(n_y, dtype=jnp.int32)[:, None] * n_z + z) * strip
-        + jnp.arange(strip, dtype=jnp.int32)[None, :]
-    ).reshape(-1)
-    begin_group, live_group = places_of(lengths_row, slots_group)
-    cosine_group, sine_group = tables_across((slots_group - begin_group).reshape(n_y, strip))
-    begin_lanes = jnp.tile(begin_group.reshape(n_y, 1, strip), (1, 1, 2))
-    slot_lanes = jnp.tile(slots_group.reshape(n_y, 1, strip), (1, 1, 2))
-    live_lanes = jnp.tile(live_group.reshape(n_y, 1, strip), (1, 1, 2))
 
     shard = norm_gain.shape[0]
-    extra = jnp.stack(
-        [norm_gain, ffn_gain, jnp.pad(q_gain, (0, shard - q_gain.shape[0]))], axis=1
-    ).astype(BF)
     first_width = latent_width + 2 * SIZE
     first = jnp.concatenate(
-        [q_down, key_weight, value_weight, jnp.pad(extra, ((0, 0), (0, 125)))], axis=1
+        [q_down, key_weight, value_weight, gain_rows(norm_gain, ffn_gain, q_gain)], axis=1
     )
     per_heads = q_up.shape[1] // members
     q_rows = q_up.shape[0]
@@ -1417,88 +1510,69 @@
     padded = -(-share // 16) * 16
     down_part = lax.dynamic_slice_in_dim(down_weight, x * share, share)
     down_part = jnp.pad(down_part, ((0, padded - share), (0, 0)))
-    first_full, both, out_strip = first_weights(first, gate_weight, up_weight, out_weight, share, padded)
+    (
+        first_full, both, out_strip, normed, key_value, latent_normed, latent, inverse_one, inverse_latent, gain_one,
+        gain_two, gain_latent, cosine, sine, cosine_group, sine_group, begin_lanes, slot_lanes, live_lanes, live_rows,
+    ) = first_weights(
+        first, gate_weight, up_weight, out_weight, block_input, lengths, latent_width, share, padded
+    )
     units = both.shape[2] // 2
     first_full = first_full.reshape(span * shard, -1)
     both = both.reshape(n_c * shard, 2 * units)
-    extra_full = first_full[:, first_width : first_width + 3].astype(F32)
-    gain_one = extra_full[:, 0]
-    gain_two = extra_full[:, 1]
-    gain_latent = extra_full[:, 2].reshape(span, shard)[:, : q_gain.shape[0]].reshape(-1)
-
     both_full = gather(both, ("y", "z"))
     down_use = gather(down_part, ("y", "z"))
 
-    inputs = block_input.astype(F32)
-    inverse_one = lax.rsqrt(jnp.mean(inputs * inputs, axis=-1, keepdims=True) + EPSILON)
-    normed = (inputs * inverse_one * gain_one).astype(BF)
-    firsts = dot(normed, first_full[:, :first_width])
-    latent = firsts[:, :latent_width]
-    inverse_latent = lax.rsqrt(jnp.mean(latent * latent, axis=-1, keepdims=True) + EPSILON)
-    latent_normed = (latent * inverse_latent * gain_latent).astype(BF)
-    key_mine = rotate(firsts[:, latent_width : latent_width + SIZE], cosine, sine).astype(BF)
-    value_mine = firsts[:, latent_width + SIZE :].astype(BF)
     key_value, latent_group, up_heads, out_heads = keys_and_latents(
-        jnp.concatenate([key_mine, value_mine], axis=1), latent_normed,
-        q_up.reshape(q_rows, n_y, n_c, per_heads).transpose(1, 2, 0, 3), out_strip,
+        key_value, latent_normed, q_up.reshape(q_rows, n_y, n_c, per_heads).transpose(1, 2, 0, 3), out_strip,
     )
     up_heads = up_heads.reshape(span * q_rows, per_heads)
     out_heads = out_heads.reshape(per_heads, width)
     key_value = key_value.reshape(span * rows, 2 * SIZE)
     group = members * rows
     latent_group = latent_group.reshape(group, latent_width)
-    mixed, queries_t, lse = attend(
-        dot(latent_group, up_heads), key_value, begin_lanes, slot_lanes, live_lanes,
-        cosine_group, sine_group,
-    )
-    branch, grad_feed = heads_sum_and_cotangent(
-        dot(mixed, out_heads).astype(BF).reshape(n_y, n_c, rows, width), cotangent
-    )
-    middle = inputs + branch
-
-    inverse_two = lax.rsqrt(jnp.mean(middle * middle, axis=-1, keepdims=True) + EPSILON)
-    grad_normed_two, normed_part, branch_part, grad_both, grad_down = feed_forward(
-        (middle * inverse_two * gain_two).astype(BF), normed, grad_feed, both_full, down_use
+    mixed, queries_t, lse, middle, inverse_two, normed_two, grad_feed = attend(
+        latent_group, up_heads, key_value, begin_lanes, slot_lanes, live_lanes, cosine_group, sine_group, out_heads,
+        block_input, gain_two, cotangent,
+    )
+
+    grad_middle, grad_branch, grad_gain_two, normed_part, branch_part, grad_both, grad_down = feed_forward(
+        normed_two, normed, grad_feed, both_full, down_use, middle, inverse_two, gain_two
     )
     normed_part = normed_part.reshape(group, -1)
-    grad_result = cotangent.astype(F32)
-    grad_mid_norm, grad_gain_two = norm_back(middle, inverse_two, gain_two, grad_normed_two)
-    grad_middle = grad_result + grad_mid_norm
 
     grad_both = grad_both.reshape(n_y, n_z, n_c * shard, 2 * units)
     out_rows = out_weight.shape[0]
-    grad_query_raw, grad_kv, grad_out, branch_two, grad_down, grad_one, grad_two = heads_back(
-        grad_middle.astype(BF), branch_part, mixed, queries_t, key_value, out_heads, begin_lanes, slot_lanes, lse,
-        live_group[:, None], cosine_group, sine_group, grad_down, grad_both,
-    )
-    output = (middle + branch_two).astype(BF)
-    grad_firsts, grad_gain_latent, grad_up_heads, grad_out, grad_one, grad_two = keys_and_latents_sum(
+    grad_query_raw, grad_kv, grad_out, branch_two, grad_one, grad_two = heads_back(
+        grad_branch, branch_part, mixed, queries_t, key_value, out_heads, begin_lanes, slot_lanes, lse,
+        live_rows, cosine_group, sine_group, grad_both,
+    )
+
+    grad_first, gains, grad_input_norm, grad_out, grad_gate, grad_up, grad_down, grad_q_up = last_sums(
         grad_kv.reshape(n_y, n_z, n_c, rows, 2 * SIZE), grad_query_raw, latent_group, up_heads, grad_out,
-        (grad_one, grad_two), cosine, sine, latent, inverse_latent, gain_latent[None, :],
-    )
-    grad_both = jnp.concatenate([grad_one, grad_two], axis=1)
-
-    grad_first, gains, grad_input_norm, grad_out, grad_gate, grad_up, grad_down, grad_q_up = last_sums(
-        grad_firsts, grad_both.reshape(n_c, shard, 2 * units), grad_out, grad_up_heads, grad_down, normed_part,
-        block_input, inverse_one, gain_one[None, :], grad_gain_two[None, :], grad_gain_latent, first_full, share,
-    )
-    input_grad = grad_middle + grad_input_norm
-    grad_first = jnp.concatenate([grad_first[0], grad_first[1]], axis=1)
+        (grad_one, grad_two), grad_down, cosine, sine, latent, inverse_latent, gain_latent, normed_part, block_input,
+        inverse_one, gain_one, grad_gain_two, first_full, share,
+    )
+    (
+        output, input_grad, grad_q_down, grad_key, grad_value, grad_gate, grad_up, grad_down, grad_out, grad_q_up,
+    ) = results(
+        middle, branch_two, grad_middle, grad_input_norm, grad_first, grad_gate, grad_up, grad_down, grad_out,
+        grad_q_up, latent_width,
+    )
     latent_shard = q_gain.shape[0]
     return (
         output,
         input_grad,
         lax.dynamic_slice(gains[0], (c * shard,), (shard,)),
-        grad_first[:, :latent_width],
+        grad_q_down,
         lax.dynamic_slice(gains[2], ((z % 2 * n_c + c) * latent_shard,), (latent_shard,)),
-        grad_q_up.astype(F32),
-        grad_first[:, latent_width : latent_width + SIZE],
-        grad_first[:, latent_width + SIZE :],
-        grad_out.reshape(out_rows, width).astype(F32),
+        grad_q_up,
+        grad_key,
+        grad_value,
+        grad_out,
         lax.dynamic_slice(gains[1], (c * shard,), (shard,)),
-        grad_gate.astype(F32),
-        grad_up.astype(F32),
-        grad_down.astype(F32),
+        grad_gate,
+        grad_up,
+        grad_down,
     )
 
 

time: 446 us -> 412 us (0.924)
  other arithmetic: 29.7 us -> 3.23 us
  matrix products: 11.9 us -> 0 us
  Pallas kernels: 370 us -> 381 us
  local copies, waits for them, and re-layouts: 12.8 us -> 5.3 us
    pallas_call x7 -> x6, Pallas kernels: 353 us -> 375 us  [comm_call(): pl.pallas_call(body, name=name, out_shape=outs, in_specs=spaces, out_spec...]
    convert_element_type x12 -> x0, other arithmetic: 12.4 us -> none  [the longest x1 2.45 us: on_device(): grad_gate.astype(F32)]
    dot_general x3 -> x0, matrix products: 11.9 us -> none  [dot(): return jnp.dot(left, right, preferred_element_type=F32)]
    pallas_call x1, Pallas kernels: 17 us -> 6.39 us  [results(): pl.pallas_call(body, name='results', out_shape=tuple((shape(*dims, kind=k...]
  transfers between devices with their start and end apart: 2 -> 2, of which waited for: 0 -> 0; matrix products, arithmetic and copies ran while one was open for 7% -> 1% of each run, Pallas kernels for 31% -> 38%
where the time goes in v7:
time: 412 us; the launch traced here: 404 us
  Pallas kernels  381 us (92%)
  between operations  14.4 us (3%)
  local copies, waits for them, and re-layouts  5.3 us (1%)
    pallas_call x6, Pallas kernels, comm_call(): pl.pallas_call(body, name=name, out_shape=outs, in_specs=spaces, out_spec...  375 us
  transfers between devices with their start and end apart: 2, of which 0 were waited for; matrix products, arithmetic and copies ran while one was open for 1% of the time, Pallas kernels for 38%

profile of v7, /device:TPU:1, one launch (start us, length us, event | category | flops | bytes accessed | tf_op | source)
XLA Modules:
  0.0 404.3 jit_solution(9260600988632677415)
XLA Ops:
  7.2 0.0 copy-start
  7.2 0.0 copy-start.2
  7.2 0.0 all-gather.5.cloned.1.call-start
  7.3 1.0 copy-done
  8.3 0.1 constant_dynamic-slice_fusion.3
  8.4 0.7 pad.9
  9.0 0.0 all-gather.5.cloned.1.call-update
  9.1 0.0 all-gather.3.cloned.1.call-start
  9.2 0.7 multiply_convert_fusion.5
  9.8 0.1 maximum_bitcast_fusion.1
  9.9 0.1 maximum_bitcast_fusion
  10.0 0.7 multiply_convert_fusion.3
  10.7 0.1 maximum_bitcast_fusion.2
  10.7 1.6 pad_maximum_fusion.first_ref
  12.4 51.5 %first_weights.1 = (bf16[4,4,2,64,1664]{4,3,2,1,0:T(8,128)(2,1)}, bf16[2,64,1536]{2,1,0:T(8,128)(2,1)}, bf16[4,32,2048]{2,1,0:T(8,128)(2,1)}, bf16[128,2048]{1,0...) custom-call(bf16[64,1664]{1,0:T(8,128)(2,1)} %pad_maximum_fusion.fir, ...), custom_call_target="tpu_custom_call" | custom-call | tf_op jit(solution)/shard_map/first_weights/pallas_call | solution.py:133
  63.9 0.0 all-gather.3.cloned.1.call-update
  63.9 0.0 copy-done.2
  63.9 0.2 reshape.59
  64.1 0.8 copy.29
  64.9 47.7 %keys_and_latents.1 = (bf16[4,4,2,128,512]{4,3,2,1,0:T(8,128)(2,1)}, bf16[4,2,128,1024]{3,2,1,0:T(8,128)(2,1)}, bf16[4,4,2,32,512]{4,3,2,1,0:T(8,128)(2,1)}, bf16[2,2,4,32,2048]{4,3,2,1,0:T(8,128)(2,1)}) custom-call(bf16[128,512]{1,0:T(8,128)(2,1)} %get-tuple-element.75.kv_ref, bf16[128,1024]{1,0:T(8,128)(2,1)} %get-tuple-element.76.lat_ref, ...), custom_call_target="tpu_custom_call" | custom-call | tf_op jit(solution)/shard_map/keys_and_latents/pallas_call | solution.py:133
  112.6 53.3 %attend.1 = (bf16[1024,512]{1,0:T(8,128)(2,1)}, bf16[4,256,512]{2,1,0:T(8,128)(2,1)}, f32[4,1,512]{2,1,0:T(1,128)}, f32[128,2048]{1,0:T(8,128)}, f32[128,1]{1,0:...) custom-call(bf16[1024,1024]{1,0:T(8,128)(2,1)} %bitcast.26, bf16[1024,512]{1,0:T(8,128)(2,1)} %bitcast.33, ...), custom_call_target="tpu_custom_call" | custom-call | tf_op jit(solution)/shard_map/attend/pallas_call | solution.py:133
  165.9 0.0 all-gather.5.cloned.1.call-done.down_hbm
  165.9 0.0 all-gather.3.cloned.1.call-done.both_hbm
  166.0 65.5 %feed_forward.1 = (f32[128,2048]{1,0:T(8,128)}, bf16[128,2048]{1,0:T(8,128)(2,1)}, f32[1,2048]{1,0:T(1,128)}, bf16[4,2,128,512]{3,2,1,0:T(8,128)(2,1)}, bf16[4,2...) custom-call(bf16[128,2048]{1,0:T(8,128)(2,1)} %get-tuple-element.89.two_ref, ...), custom_call_target="tpu_custom_call" | custom-call | tf_op jit(solution)/shard_map/feed_forward/pallas_call | solution.py:133
  231.5 58.8 %heads_back.1 = (bf16[1024,512]{1,0:T(8,128)(2,1)}, bf16[4096,512]{1,0:T(8,128)(2,1)}, bf16[4,128,2048]{2,1,0:T(8,128)(2,1)}, f32[128,2048]{1,0:T(8,128)}, bf16[...) custom-call(bf16[128,2048]{1,0:T(8,128)(2,1)} %get-tuple-element.94.grad_ref, ...), custom_call_target="tpu_custom_call" | custom-call | tf_op jit(solution)/shard_map/heads_back/pallas_call | solution.py:133
  290.3 0.0 copy-start.1
  290.3 98.0 %last_sums.1 = (f32[2,64,768]{2,1,0:T(8,128)}, f32[8,128]{1,0:T(8,128)}, f32[128,2048]{1,0:T(8,128)}, bf16[4,32,2048]{2,1,0:T(8,128)(2,1)}, bf16[64,5632]{1,0:T(...) custom-call(bf16[4,4,2,128,512]{4,3,2,1,0:T(8,128)(2,1)} %bitcast.32, ...), custom_call_target="tpu_custom_call" | custom-call | tf_op jit(solution)/shard_map/last_sums/pallas_call | solution.py:133
  388.3 0.8 fusion.8
  389.1 0.6 fusion.7
  389.7 0.6 fusion.5
  390.3 0.6 fusion.6
  390.8 6.4 %results.1 = (bf16[128,2048]{1,0:T(8,128)(2,1)}, f32[128,2048]{1,0:T(8,128)}, f32[64,1024]{1,0:T(8,128)}, f32[64,256]{1,0:T(8,128)}, f32[64,256]{1,0:T(8,128)}, ...) custom-call(f32[128,2048]{1,0:T(8,128)} %get-tuple-element.88.middle, ...), custom_call_target="tpu_custom_call" | custom-call | tf_op jit(solution)/shard_map/results/pallas_call | solution.py:1473
  397.2 0.0 copy-done.1
  (1 shorter events, 0.0 us)
Async XLA Ops:
  7.2 1.1 copy-start
  7.2 56.7 %copy-start.2 = (bf16[32,4096]{1,0:T(8,128)(2,1)S(1)}, bf16[32,4096]{1,0:T(8,128)(2,1)}, u32[]{:S(2)}) copy-start(bf16[32,4096]{1,0:T(8,128)(2,1)} %param.20) | copy-start | bytes 786436
  7.2 158.7 %all-gather.5.cloned.1.call-start = ((), (), s32[]{:S(2)}) async-start(), calls=%async_computation.1 | async-start | bytes 3342336 | tf_op jit(solution)/shard_map/all_gather | solution.py:1486
  9.1 156.9 %all-gather.3.cloned.1.call-start = ((), (), s32[]{:S(2)}) async-start(), calls=%async_computation | async-start | bytes 6684672 | tf_op jit(solution)/shard_map/all_gather | solution.py:1486
  290.3 107.0 %copy-start.1 = (bf16[176,2048]{1,0:T(8,128)(2,1)S(1)}, bf16[176,2048]{1,0:T(8,128)(2,1)}, u32[]{:S(2)}) copy-start(bf16[176,2048]{1,0:T(8,128)(2,1)} %param.27) | copy-start | bytes 2162692
Sparse Core Ops, SparseCore 0:
  10.8 54.6 all-gather.4
  67.6 87.1 all-gather.2

commit v8 on v7

--- a/solution.py
+++ b/solution.py
@@ -949,7 +949,7 @@
     )
 
 
-Y_COLUMNS = 512
+Y_COLUMNS = 640
 
 
 class FirstStep:
@@ -1030,6 +1030,13 @@
         greet(X_LINE + Y_LINE + Z_LINE + TWIN)
         row = RowSum(net, kv_ref, kv_sum, row_near, row_go, row_first, row_mid, row_last)
         outs = [net.send(out_ref.at[:, strip(along("x", d))], out_come_x.at[d - 1], "x", d) for d in LINE]
+        halves = [
+            SecondStep(net, mid, axis, come)
+            for mid, axis, come in (
+                (one_ref, "z", one_come), (two_ref, "y", two_come), (down_ref.at[0], "z", down_come.at[0]),
+                (down_ref.at[1], "y", down_come.at[1]),
+            )
+        ]
         for i in range(4):
             at = pl.ds(i * 2 * size, 2 * size)
             partial[i] = dot_nt(query_ref[at, :], heads_ref[...]).astype(BF).reshape(2, size, latent_width)
@@ -1041,15 +1048,31 @@
         ups = [
             net.send(ups_here.at[:, :, :, :, lane(along("x", d))], up_come_x.at[d - 1], "x", d) for d in LINE
         ]
+        halves[0].finish(both_here.at[:, pl.ds(0, ahead_columns)])
+        halves[1].finish(both_here.at[:, pl.ds(ahead_columns, after_columns)])
+        own_rows = pl.ds(pl.multiple_of(c * rows, rows), rows)
+        other_rows = pl.ds(pl.multiple_of((1 - c) * rows, rows), rows)
+        both_mine = net.keep(both_here.at[own_rows], both_all.at[x, c])
+        both_come = net.send(both_here.at[other_rows], both_all.at[x, c], "c", 1)
         row.turn()
         ring.pass_on()
-        halves = [
-            SecondStep(net, mid, axis, come)
-            for mid, axis, come in (
-                (one_ref, "z", one_come), (two_ref, "y", two_come), (down_ref.at[0], "z", down_come.at[0]),
-                (down_ref.at[1], "y", down_come.at[1]),
-            )
-        ]
+        both_mine.wait()
+        both_come.wait_recv()
+        zero, one = both_all.at[x, 0], both_all.at[x, 1]
+        right = [net.send(spot, spot, "x", 1) for spot in (zero, one)]
+        left = [net.send(spot, spot, "x", -1) for spot in (one, zero)]
+        accum[...] = jnp.zeros_like(accum)
+
+        def put(px):
+            for pc in range(2):
+                places = unit_places((half_units, 1), 0, px, pc, share, padded)
+                picks = lax.broadcasted_iota(jnp.int32, (half_units, half_wide), 1) == places
+                stacked = jnp.concatenate(
+                    [both_all[px, pc, :, k * half_units : (k + 1) * half_units] for k in range(4)], axis=0
+                )
+                accum[...] += dot(stacked, picks.astype(BF))
+
+        put(x)
 
         ring.finish()
         values = latent_ref[...]
@@ -1074,17 +1097,13 @@
         come.wait_recv()
         spot = gathered.at[y, 1 - c]
         ahead += [net.send(spot, spot, "y", 1), net.send(spot, spot, "y", -1)]
-        halves[0].finish(both_here.at[:, pl.ds(0, ahead_columns)])
-        halves[1].finish(both_here.at[:, pl.ds(ahead_columns, after_columns)])
-        own_rows = pl.ds(pl.multiple_of(c * rows, rows), rows)
-        other_rows = pl.ds(pl.multiple_of((1 - c) * rows, rows), rows)
-        both_mine = net.keep(both_here.at[own_rows], both_all.at[x, c])
-        both_come = net.send(both_here.at[other_rows], both_all.at[x, c], "c", 1)
-        both_mine.wait()
-        both_come.wait_recv()
-        zero, one = both_all.at[x, 0], both_all.at[x, 1]
-        right = [net.send(spot, spot, "x", 1) for spot in (zero, one)]
-        left = [net.send(spot, spot, "x", -1) for spot in (one, zero)]
+
+        right[0].wait_recv()
+        spot = both_all.at[along("x", -1), 0]
+        far = [net.send(spot, spot, "x", 1)]
+        left[0].wait_recv()
+        spot = both_all.at[along("x", 1), 1]
+        far.append(net.send(spot, spot, "x", -1))
 
         for copy in ups:
             copy.wait_recv()
@@ -1143,12 +1162,6 @@
             gain_here[i // 4, i % 4, 2:3, :] = gain_latent[:, i // 2 * 128 : (i // 2 + 1) * 128]
         near = net.send(gain_here, gain_near, "c", 1)
 
-        right[0].wait_recv()
-        spot = both_all.at[along("x", -1), 0]
-        far = [net.send(spot, spot, "x", 1)]
-        left[0].wait_recv()
-        spot = both_all.at[along("x", 1), 1]
-        far.append(net.send(spot, spot, "x", -1))
         for k in (2, 3):
             halves[k].finish(down_all.at[x, :, pl.ds((k - 2) * down_lanes, down_lanes)])
         spot = down_all.at[x]
@@ -1187,20 +1200,8 @@
         spot = up_all.at[x]
         ups = [net.send(spot, spot, "x", d) for d in LINE]
 
-        accum[...] = jnp.zeros_like(accum)
-
-        def put(px):
-            for pc in range(2):
-                places = unit_places((half_units, 1), 0, px, pc, share, padded)
-                picks = lax.broadcasted_iota(jnp.int32, (half_units, half_wide), 1) == places
-                stacked = jnp.concatenate(
-                    [both_all[px, pc, :, k * half_units : (k + 1) * half_units] for k in range(4)], axis=0
-                )
-                accum[...] += dot(stacked, picks.astype(BF))
-
         for copy in (right[1], left[1]):
             copy.wait_recv()
-        put(x)
         put(along("x", 1))
 
         def onward(core):

time: 412 us -> 405 us (0.983)
  Pallas kernels: 381 us -> 374 us
    pallas_call x6, Pallas kernels: 375 us -> 368 us  [comm_call(): pl.pallas_call(body, name=name, out_shape=outs, in_specs=spaces, out_spec...]
where the time goes in v8:
time: 405 us; the launch traced here: 397 us
  Pallas kernels  374 us (92%)
  between operations  14.4 us (4%)
  local copies, waits for them, and re-layouts  5.3 us (1%)
    pallas_call x6, Pallas kernels, comm_call(): pl.pallas_call(body, name=name, out_shape=outs, in_specs=spaces, out_spec...  368 us
  transfers between devices with their start and end apart: 2, of which 0 were waited for; matrix products, arithmetic and copies ran while one was open for 1% of the time, Pallas kernels for 38%

profile of v8, /device:TPU:1, one launch (start us, length us, event | category | flops | bytes accessed | tf_op | source)
XLA Modules:
  0.0 397.0 jit_solution(13379522177187074057)
XLA Ops:
  7.2 0.0 copy-start
  7.2 0.0 copy-start.2
  7.2 0.0 all-gather.5.cloned.1.call-start
  7.3 1.0 copy-done
  8.3 0.1 constant_dynamic-slice_fusion.3
  8.4 0.7 pad.9
  9.0 0.0 all-gather.5.cloned.1.call-update
  9.1 0.0 all-gather.3.cloned.1.call-start
  9.2 0.7 multiply_convert_fusion.5
  9.8 0.1 maximum_bitcast_fusion.1
  9.9 0.1 maximum_bitcast_fusion
  10.0 0.7 multiply_convert_fusion.3
  10.7 0.1 maximum_bitcast_fusion.2
  10.7 1.6 pad_maximum_fusion.first_ref
  12.4 51.5 %first_weights.1 = (bf16[4,4,2,64,1664]{4,3,2,1,0:T(8,128)(2,1)}, bf16[2,64,1536]{2,1,0:T(8,128)(2,1)}, bf16[4,32,2048]{2,1,0:T(8,128)(2,1)}, bf16[128,2048]{1,0...) custom-call(bf16[64,1664]{1,0:T(8,128)(2,1)} %pad_maximum_fusion.fir, ...), custom_call_target="tpu_custom_call" | custom-call | tf_op jit(solution)/shard_map/first_weights/pallas_call | solution.py:133
  63.9 0.0 all-gather.3.cloned.1.call-update
  63.9 0.0 copy-done.2
  63.9 0.2 reshape.59
  64.1 0.8 copy.29
  64.9 47.7 %keys_and_latents.1 = (bf16[4,4,2,128,512]{4,3,2,1,0:T(8,128)(2,1)}, bf16[4,2,128,1024]{3,2,1,0:T(8,128)(2,1)}, bf16[4,4,2,32,512]{4,3,2,1,0:T(8,128)(2,1)}, bf16[2,2,4,32,2048]{4,3,2,1,0:T(8,128)(2,1)}) custom-call(bf16[128,512]{1,0:T(8,128)(2,1)} %get-tuple-element.75.kv_ref, bf16[128,1024]{1,0:T(8,128)(2,1)} %get-tuple-element.76.lat_ref, ...), custom_call_target="tpu_custom_call" | custom-call | tf_op jit(solution)/shard_map/keys_and_latents/pallas_call | solution.py:133
  112.6 53.3 %attend.1 = (bf16[1024,512]{1,0:T(8,128)(2,1)}, bf16[4,256,512]{2,1,0:T(8,128)(2,1)}, f32[4,1,512]{2,1,0:T(1,128)}, f32[128,2048]{1,0:T(8,128)}, f32[128,1]{1,0:...) custom-call(bf16[1024,1024]{1,0:T(8,128)(2,1)} %bitcast.26, bf16[1024,512]{1,0:T(8,128)(2,1)} %bitcast.33, ...), custom_call_target="tpu_custom_call" | custom-call | tf_op jit(solution)/shard_map/attend/pallas_call | solution.py:133
  165.9 0.0 all-gather.5.cloned.1.call-done.down_hbm
  165.9 0.0 all-gather.3.cloned.1.call-done.both_hbm
  166.0 65.5 %feed_forward.1 = (f32[128,2048]{1,0:T(8,128)}, bf16[128,2048]{1,0:T(8,128)(2,1)}, f32[1,2048]{1,0:T(1,128)}, bf16[4,2,128,512]{3,2,1,0:T(8,128)(2,1)}, bf16[4,2...) custom-call(bf16[128,2048]{1,0:T(8,128)(2,1)} %get-tuple-element.89.two_ref, ...), custom_call_target="tpu_custom_call" | custom-call | tf_op jit(solution)/shard_map/feed_forward/pallas_call | solution.py:133
  231.5 58.7 %heads_back.1 = (bf16[1024,512]{1,0:T(8,128)(2,1)}, bf16[4096,512]{1,0:T(8,128)(2,1)}, bf16[4,128,2048]{2,1,0:T(8,128)(2,1)}, f32[128,2048]{1,0:T(8,128)}, bf16[...) custom-call(bf16[128,2048]{1,0:T(8,128)(2,1)} %get-tuple-element.94.grad_ref, ...), custom_call_target="tpu_custom_call" | custom-call | tf_op jit(solution)/shard_map/heads_back/pallas_call | solution.py:133
  290.2 0.0 copy-start.1
  290.2 90.8 %last_sums.1 = (f32[2,64,768]{2,1,0:T(8,128)}, f32[8,128]{1,0:T(8,128)}, f32[128,2048]{1,0:T(8,128)}, bf16[4,32,2048]{2,1,0:T(8,128)(2,1)}, bf16[64,5632]{1,0:T(...) custom-call(bf16[4,4,2,128,512]{4,3,2,1,0:T(8,128)(2,1)} %bitcast.32, ...), custom_call_target="tpu_custom_call" | custom-call | tf_op jit(solution)/shard_map/last_sums/pallas_call | solution.py:133
  381.1 0.8 fusion.8
  381.8 0.6 fusion.7
  382.4 0.6 fusion.5
  383.0 0.6 fusion.6
  383.6 6.4 %results.1 = (bf16[128,2048]{1,0:T(8,128)(2,1)}, f32[128,2048]{1,0:T(8,128)}, f32[64,1024]{1,0:T(8,128)}, f32[64,256]{1,0:T(8,128)}, f32[64,256]{1,0:T(8,128)}, ...) custom-call(f32[128,2048]{1,0:T(8,128)} %get-tuple-element.88.middle, ...), custom_call_target="tpu_custom_call" | custom-call | tf_op jit(solution)/shard_map/results/pallas_call | solution.py:1474
  390.0 0.0 copy-done.1
  (1 shorter events, 0.0 us)
Async XLA Ops:
  7.2 1.1 copy-start
  7.2 56.7 %copy-start.2 = (bf16[32,4096]{1,0:T(8,128)(2,1)S(1)}, bf16[32,4096]{1,0:T(8,128)(2,1)}, u32[]{:S(2)}) copy-start(bf16[32,4096]{1,0:T(8,128)(2,1)} %param.20) | copy-start | bytes 786436
  7.2 158.7 %all-gather.5.cloned.1.call-start = ((), (), s32[]{:S(2)}) async-start(), calls=%async_computation.1 | async-start | bytes 3342336 | tf_op jit(solution)/shard_map/all_gather | solution.py:1487
  9.1 156.9 %all-gather.3.cloned.1.call-start = ((), (), s32[]{:S(2)}) async-start(), calls=%async_computation | async-start | bytes 6684672 | tf_op jit(solution)/shard_map/all_gather | solution.py:1487
  290.2 99.8 %copy-start.1 = (bf16[176,2048]{1,0:T(8,128)(2,1)S(1)}, bf16[176,2048]{1,0:T(8,128)(2,1)}, u32[]{:S(2)}) copy-start(bf16[176,2048]{1,0:T(8,128)(2,1)} %param.27) | copy-start | bytes 2162692
Sparse Core Ops, SparseCore 0:
  10.8 54.6 all-gather.4
  67.6 87.1 all-gather.2

commit v9 on v8

--- a/solution.py
+++ b/solution.py
@@ -444,23 +444,34 @@
 OWN_COLUMNS = 640
 
 
-def first_weights(first, gate, up, out, inputs, lengths, latent_width, share, padded):
+def first_weights(weights, gate, up, out, inputs, lengths, share, padded):
     rows_in, wide = gate.shape
     half_wide = wide // 2
     half_units = half_wide // (8 * share) * padded
     units = 2 * half_units
     rows, width = out.shape
     quarter = rows // 4
-    lanes = (first.shape[1] - OWN_COLUMNS) // 4
-
-    def body(
-        first_ref, gate_ref, up_ref, out_ref, input_ref, length_ref,
+    first_width = sum(w.shape[1] for w in weights) - 128
+    latent_width = weights[0].shape[1]
+    lanes = (first_width + 128 - OWN_COLUMNS) // 4
+    pieces_in = len(weights)
+
+    def body(*refs):
+        kernel(refs[:pieces_in], *refs[pieces_in:])
+
+    def kernel(
+        weight_refs, gate_ref, up_ref, out_ref, input_ref, length_ref,
         first_hbm, both_out, strip_out, normed_out, kv_out, lat_out, latent_out, inverse_out, latent_inverse_out,
         gain_one_out, gain_two_out, gain_latent_out, cos_ref, sin_ref, cos_group, sin_group, begin_out, slot_out,
-        live_out, live_rows, first_out, both, sends, arrivals, locals_,
+        live_out, live_rows, first_ref, first_out, both, sends, arrivals, locals_,
     ):
         net = Net(sends, arrivals, locals_)
         x, y, z, c = (lax.axis_index(a) for a in AXES)
+
+        at = 0
+        for ref in weight_refs:
+            first_ref[:, at : at + ref.shape[1]] = ref[...]
+            at += ref.shape[1]
 
         def columns(step):
             return pl.ds(pl.multiple_of(OWN_COLUMNS + along("x", step) * lanes, 128), lanes)
@@ -584,8 +595,7 @@
         net.close()
 
     size, deep = inputs.shape
-    first_width = first.shape[1] - 128
-    whole = (4, 4, 2, *first.shape)
+    whole = (4, 4, 2, rows_in, first_width + 128)
     outs = (
         shape(*whole), shape(2, rows_in, 2 * units), shape(4, quarter, width), shape(size, deep),
         shape(size, 2 * SIZE), shape(size, latent_width), shape(size, latent_width, kind=F32),
@@ -595,10 +605,12 @@
         shape(4, 1, 4 * size, kind=jnp.int32), shape(4, 1, 4 * size, kind=jnp.int32), shape(4, 1, 4 * size, kind=F32),
         shape(8 * size, 1, kind=F32),
     )
-    scratch = [pltpu.VMEM(whole, BF), pltpu.VMEM((2, rows_in, 2 * units), BF)]
+    scratch = [
+        pltpu.VMEM((rows_in, first_width + 128), BF), pltpu.VMEM(whole, BF), pltpu.VMEM((2, rows_in, 2 * units), BF),
+    ]
     return comm_call(
-        body, "first_weights", 1, outs, (first, gate, up, out, inputs, lengths), scratch, 64, 5,
-        [IN_VMEM] * 5 + [pl.BlockSpec(memory_space=pltpu.SMEM)], [ANYWHERE] * 3 + [IN_VMEM] * 17,
+        body, "first_weights", 1, outs, (*weights, gate, up, out, inputs, lengths), scratch, 64, 5,
+        [IN_VMEM] * (pieces_in + 4) + [pl.BlockSpec(memory_space=pltpu.SMEM)], [ANYWHERE] * 3 + [IN_VMEM] * 17,
     )
 
 
@@ -626,22 +638,28 @@
         ups = [net.send(up_ref.at[along("y", d)], transit.at[y, z], "y", d) for d in LINE]
         row = RowGather(net, kv_ref, kv_out)
         ring = RingGather(net, lat_ref, lat_out, "y")
-        strip_mine = net.keep(strip_ref, sheet.at[:, x])
-        strips = [net.send(strip_ref, sheet.at[:, x], "x", d) for d in LINE]
+        half = strip_ref.shape[0] // 2
+        strip_mine = net.keep(strip_ref.at[pl.ds(half * c, half)], sheet.at[:, c])
+        strip_come = net.send(strip_ref.at[pl.ds(half * (1 - c), half)], sheet.at[:, c], "c", 1)
         up_mine.wait()
         for copy in ups:
             copy.wait_recv()
         ups = [net.send(transit.at[:, z], transit.at[:, z], "z", d) for d in LINE]
+        strip_mine.wait()
+        strip_come.wait_recv()
+        sheet_keep = net.keep(sheet, out_out.at[:, :, x])
+        right = [net.send(sheet.at[h], out_out.at[h, :, x], "x", 1) for h in (0, 1)]
+        left = [net.send(sheet.at[h], out_out.at[h, :, x], "x", -1) for h in (1, 0)]
         row.spread()
         ring.forward()
+        right[0].wait_recv()
+        spot = out_out.at[0, :, along("x", -1)]
+        far = [net.send(spot, spot, "x", 1)]
+        left[0].wait_recv()
+        spot = out_out.at[1, :, along("x", 1)]
+        far.append(net.send(spot, spot, "x", -1))
         ring.share()
         row.arrive()
-        strip_mine.wait()
-        for copy in strips:
-            copy.wait_recv()
-        half = sheet.shape[0] // 2
-        sheet_keep = net.keep(sheet.at[pl.ds(half * c, half)], out_out.at[:, c])
-        sheet_come = net.send(sheet.at[pl.ds(half * (1 - c), half)], out_out.at[:, c], "c", 1)
         for copy in ups:
             copy.wait_recv()
         up_keep = net.keep(transit.at[:, :, c], up_out.at[:, :, c])
@@ -650,7 +668,7 @@
         row.finish()
         for copy in (up_keep, sheet_keep):
             copy.wait()
-        for copy in (up_come, sheet_come):
+        for copy in [up_come, right[1], left[1]] + far:
             copy.wait_recv()
         net.close()
 
@@ -660,9 +678,9 @@
         shape(4, 4, 2, *key_value.shape), shape(4, 2, *latent.shape), shape(4, 4, 2, high, thin),
         shape(2, 2, 4, quarter, width),
     )
-    scratch = [pltpu.VMEM((4, 4, 2, high, thin), BF), pltpu.VMEM((4, 4, quarter, width), BF)]
+    scratch = [pltpu.VMEM((4, 4, 2, high, thin), BF), pltpu.VMEM((2, 2, quarter, width), BF)]
     return comm_call(
-        body, "keys_and_latents", 2, outs, (key_value, latent, up, strip), scratch, 48, 6,
+        body, "keys_and_latents", 2, outs, (key_value, latent, up, strip), scratch, 52, 6,
         [IN_VMEM] * 4, [ANYWHERE] * 4,
     )
 
@@ -1499,10 +1517,6 @@
     members = n_y * n_c
 
     shard = norm_gain.shape[0]
-    first_width = latent_width + 2 * SIZE
-    first = jnp.concatenate(
-        [q_down, key_weight, value_weight, gain_rows(norm_gain, ffn_gain, q_gain)], axis=1
-    )
     per_heads = q_up.shape[1] // members
     q_rows = q_up.shape[0]
 
@@ -1515,7 +1529,8 @@
         first_full, both, out_strip, normed, key_value, latent_normed, latent, inverse_one, inverse_latent, gain_one,
         gain_two, gain_latent, cosine, sine, cosine_group, sine_group, begin_lanes, slot_lanes, live_lanes, live_rows,
     ) = first_weights(
-        first, gate_weight, up_weight, out_weight, block_input, lengths, latent_width, share, padded
+        (q_down, key_weight, value_weight, gain_rows(norm_gain, ffn_gain, q_gain)), gate_weight, up_weight, out_weight,
+        block_input, lengths, share, padded
     )
     units = both.shape[2] // 2
     first_full = first_full.reshape(span * shard, -1)

time: 405 us -> 403 us (level)
  no operation moved by 1% of the time
where the time goes in v9:
time: 403 us; the launch traced here: 395 us
  Pallas kernels  373 us (93%)
  between operations  14.4 us (4%)
  local copies, waits for them, and re-layouts  5.3 us (1%)
    pallas_call x6, Pallas kernels, comm_call(): pl.pallas_call(body, name=name, out_shape=outs, in_specs=spaces, out_spec...  366 us
  transfers between devices with their start and end apart: 2, of which 0 were waited for; matrix products, arithmetic and copies ran while one was open for 1% of the time, Pallas kernels for 38%

profile of v9, /device:TPU:1, one launch (start us, length us, event | category | flops | bytes accessed | tf_op | source)
XLA Modules:
  0.0 394.8 jit_solution(4730230613425468989)
XLA Ops:
  7.2 0.0 copy-start
  7.2 0.0 copy-start.2
  7.2 0.0 all-gather.5.cloned.1.call-start
  7.3 1.0 copy-done
  8.3 0.1 constant_dynamic-slice_fusion.3
  8.4 0.7 pad.9
  9.0 0.0 all-gather.5.cloned.1.call-update
  9.1 0.0 all-gather.3.cloned.1.call-start
  9.2 0.7 multiply_convert_fusion.5
  9.8 0.1 maximum_bitcast_fusion.1
  9.9 0.1 maximum_bitcast_fusion
  10.0 0.7 multiply_convert_fusion.3
  10.7 0.1 maximum_bitcast_fusion.2
  10.7 0.6 fusion.4.refs_3_
  11.3 51.5 %first_weights.1 = (bf16[4,4,2,64,1664]{4,3,2,1,0:T(8,128)(2,1)}, bf16[2,64,1536]{2,1,0:T(8,128)(2,1)}, bf16[4,32,2048]{2,1,0:T(8,128)(2,1)}, bf16[128,2048]{1,0...) custom-call(bf16[64,1024]{1,0:T(8,128)(2,1)} %refs_0_.1, ...), custom_call_target="tpu_custom_call" | custom-call | tf_op jit(solution)/shard_map/first_weights/pallas_call | solution.py:133
  62.9 0.0 all-gather.3.cloned.1.call-update
  62.9 0.0 copy-done.2
  62.9 0.2 reshape.59
  63.1 0.8 copy.29
  63.9 43.4 %keys_and_latents.1 = (bf16[4,4,2,128,512]{4,3,2,1,0:T(8,128)(2,1)}, bf16[4,2,128,1024]{3,2,1,0:T(8,128)(2,1)}, bf16[4,4,2,32,512]{4,3,2,1,0:T(8,128)(2,1)}, bf16[2,2,4,32,2048]{4,3,2,1,0:T(8,128)(2,1)}) custom-call(bf16[128,512]{1,0:T(8,128)(2,1)} %get-tuple-element.75.kv_ref, bf16[128,1024]{1,0:T(8,128)(2,1)} %get-tuple-element.76.lat_ref, ...), custom_call_target="tpu_custom_call" | custom-call | tf_op jit(solution)/shard_map/keys_and_latents/pallas_call | solution.py:133
  107.3 56.3 %attend.1 = (bf16[1024,512]{1,0:T(8,128)(2,1)}, bf16[4,256,512]{2,1,0:T(8,128)(2,1)}, f32[4,1,512]{2,1,0:T(1,128)}, f32[128,2048]{1,0:T(8,128)}, f32[128,1]{1,0:...) custom-call(bf16[1024,1024]{1,0:T(8,128)(2,1)} %bitcast.26, bf16[1024,512]{1,0:T(8,128)(2,1)} %bitcast.33, ...), custom_call_target="tpu_custom_call" | custom-call | tf_op jit(solution)/shard_map/attend/pallas_call | solution.py:133
  163.6 0.0 all-gather.5.cloned.1.call-done.down_hbm
  163.6 0.0 all-gather.3.cloned.1.call-done.both_hbm
  163.6 65.7 %feed_forward.1 = (f32[128,2048]{1,0:T(8,128)}, bf16[128,2048]{1,0:T(8,128)(2,1)}, f32[1,2048]{1,0:T(1,128)}, bf16[4,2,128,512]{3,2,1,0:T(8,128)(2,1)}, bf16[4,2...) custom-call(bf16[128,2048]{1,0:T(8,128)(2,1)} %get-tuple-element.89.two_ref, ...), custom_call_target="tpu_custom_call" | custom-call | tf_op jit(solution)/shard_map/feed_forward/pallas_call | solution.py:133
  229.3 58.7 %heads_back.1 = (bf16[1024,512]{1,0:T(8,128)(2,1)}, bf16[4096,512]{1,0:T(8,128)(2,1)}, bf16[4,128,2048]{2,1,0:T(8,128)(2,1)}, f32[128,2048]{1,0:T(8,128)}, bf16[...) custom-call(bf16[128,2048]{1,0:T(8,128)(2,1)} %get-tuple-element.94.grad_ref, ...), custom_call_target="tpu_custom_call" | custom-call | tf_op jit(solution)/shard_map/heads_back/pallas_call | solution.py:133
  288.0 0.0 copy-start.1
  288.0 90.8 %last_sums.1 = (f32[2,64,768]{2,1,0:T(8,128)}, f32[8,128]{1,0:T(8,128)}, f32[128,2048]{1,0:T(8,128)}, bf16[4,32,2048]{2,1,0:T(8,128)(2,1)}, bf16[64,5632]{1,0:T(...) custom-call(bf16[4,4,2,128,512]{4,3,2,1,0:T(8,128)(2,1)} %bitcast.32, ...), custom_call_target="tpu_custom_call" | custom-call | tf_op jit(solution)/shard_map/last_sums/pallas_call | solution.py:133
  378.9 0.8 fusion.8
  379.7 0.6 fusion.7
  380.2 0.6 fusion.5
  380.8 0.6 fusion.6
  381.4 6.4 %results.1 = (bf16[128,2048]{1,0:T(8,128)(2,1)}, f32[128,2048]{1,0:T(8,128)}, f32[64,1024]{1,0:T(8,128)}, f32[64,256]{1,0:T(8,128)}, f32[64,256]{1,0:T(8,128)}, ...) custom-call(f32[128,2048]{1,0:T(8,128)} %get-tuple-element.88.middle, ...), custom_call_target="tpu_custom_call" | custom-call | tf_op jit(solution)/shard_map/results/pallas_call | solution.py:1492
  387.8 0.0 copy-done.1
Async XLA Ops:
  7.2 1.1 copy-start
  7.2 55.7 %copy-start.2 = (bf16[32,4096]{1,0:T(8,128)(2,1)S(1)}, bf16[32,4096]{1,0:T(8,128)(2,1)}, u32[]{:S(2)}) copy-start(bf16[32,4096]{1,0:T(8,128)(2,1)} %param.20) | copy-start | bytes 786436
  7.2 156.4 %all-gather.5.cloned.1.call-start = ((), (), s32[]{:S(2)}) async-start(), calls=%async_computation.1 | async-start | bytes 3342336 | tf_op jit(solution)/shard_map/all_gather | solution.py:1505
  9.1 154.6 %all-gather.3.cloned.1.call-start = ((), (), s32[]{:S(2)}) async-start(), calls=%async_computation | async-start | bytes 6684672 | tf_op jit(solution)/shard_map/all_gather | solution.py:1505
  288.0 99.8 %copy-start.1 = (bf16[176,2048]{1,0:T(8,128)(2,1)S(1)}, bf16[176,2048]{1,0:T(8,128)(2,1)}, u32[]{:S(2)}) copy-start(bf16[176,2048]{1,0:T(8,128)(2,1)} %param.27) | copy-start | bytes 2162692
Sparse Core Ops, SparseCore 0:
  10.8 54.2 all-gather.4
  67.2 85.8 all-gather.2
